TPU v7x, 512 devices: a whole 4x4x16 slice. The times are simulated.
512 devices in a mesh: row: 32 (over y, x, core), col: 16 (over z).
Axes of the slice: x: 4, y: 4, z: 16, core: 2. Of those that a mesh axis runs over, the one named last changes fastest.
Arguments:
- feats: bfloat16 [1024, 32768], P('col', 'row'), may hold values from -6 to 6
- w_self: bfloat16 [1024, 1024], P('col'), may hold values from -0.1875 to 0.1875
- w_neigh: bfloat16 [1024, 1024], P('col'), may hold values from -0.375 to 0.375
- cotangent: bfloat16 [1024, 32768], P('col', 'row'), may hold values from -6 to 6
- loc_nbr: int32 [32768, 8], P('row'), may hold values from 0 to 1023
- send_rows: int32 [32, 32, 128], P('row'), may hold values from 0 to 1023
- recv_node: int32 [32, 32, 128], P('row'), may hold values from -1 to 1023, as said below
- hub_rows: int32 [512], P('row'), may hold values from 0 to 1023
- hub_nbr: int32 [32768, 2], P('row'), may hold values from 0 to 511
Outputs:
- hidden_out: bfloat16 [1024, 32768], P('col', 'row')
- grad_feats: bfloat16 [1024, 32768], P('col', 'row')
- grad_self: float32 [1024, 1024], P('col')
- grad_neigh: float32 [1024, 1024], P('col')
Inputs may be any that keep to these rules, and one draw needn't show every extreme that they name: `recv_node`: for receiver block d and sender block s, the first c slots hold rows of block d and the rest hold -1, with 1 <= c <= 128; in every draw one receiver block gets all 128 slots from every sender block.
All inputs are finite; a program needn't handle non-finite values.
Results may differ from a plain program's by a relative error of at most 0.0075.
Values may be sent and summed in bfloat16 or wider, within the bound.
No kernel may reach another device: no remote copies, remote signals or barrier semaphores. Data moves between devices by JAX's collectives and lax.ppermute only.
A program may use at most 64 MiB of HBM per device.

v0:
```python
import jax
import jax.numpy as jnp
from jax import lax
from jax.sharding import PartitionSpec as P


def silu_slope(preact):
    sigmoid_part = jax.nn.sigmoid(preact)
    return sigmoid_part * (1.0 + preact * (1.0 - sigmoid_part))


def spread_sum(values, indices, segments):
    repeats = indices.shape[1]
    spread = jnp.broadcast_to(values[:, None, :], (values.shape[0], repeats, values.shape[1]))
    return jax.ops.segment_sum(
        spread.reshape(-1, values.shape[1]).astype(jnp.float32), indices.reshape(-1), segments
    )


def per_device(feats, w_self, w_neigh, cotangent, loc_nbr, send_rows, recv_node, hub_rows, hub_nbr):
    node_rows = feats.T
    node_count, narrow = node_rows.shape
    peer_count = lax.axis_size("row")
    outgoing = feats[:, send_rows.reshape(-1)].reshape(narrow, peer_count, -1)
    incoming = lax.all_to_all(outgoing, "row", split_axis=1, concat_axis=1, tiled=True)
    hub_table = lax.all_gather(feats[:, hub_rows], "row", axis=1, tiled=True)
    targets = recv_node.reshape(-1)
    live_slots = targets >= 0
    slot_rows = jnp.where(live_slots, targets, node_count)
    local_sum = jnp.sum(node_rows[loc_nbr], axis=1, dtype=jnp.float32)
    hub_sum = jnp.sum(hub_table.T[hub_nbr], axis=1, dtype=jnp.float32)
    remote_sum = jax.ops.segment_sum(
        incoming.reshape(narrow, -1).T.astype(jnp.float32), slot_rows, node_count + 1
    )[:node_count]
    arrivals = jax.ops.segment_sum(live_slots.astype(jnp.float32), slot_rows, node_count + 1)[
        :node_count
    ]
    degree = loc_nbr.shape[1] + hub_nbr.shape[1] + arrivals
    neighbour_mean = ((local_sum + hub_sum + remote_sum) / degree[:, None]).astype(jnp.bfloat16)
    joined = jnp.concatenate([node_rows, neighbour_mean], axis=1)
    weights = jnp.concatenate([w_self, w_neigh], axis=0)
    partial_product = jnp.dot(joined, weights, preferred_element_type=jnp.float32)
    preact = lax.psum_scatter(partial_product, "col", scatter_dimension=1, tiled=True)
    hidden_out = jax.nn.silu(preact).astype(jnp.bfloat16)
    slopes = (cotangent.T.astype(jnp.float32) * silu_slope(preact)).astype(jnp.bfloat16)
    block_cols = lax.all_gather(slopes, "col", axis=1, tiled=True)
    back_sum = lax.dot_general(
        block_cols, weights, (((1,), (1,)), ((), ())), preferred_element_type=jnp.float32
    )
    weight_part = lax.dot_general(
        joined, block_cols, (((0,), (0,)), ((), ())), preferred_element_type=jnp.float32
    )
    weight_sum = weight_part
    back_sum, weight_sum = (back_sum, weight_sum)
    share_back = (back_sum[:, narrow:] / degree[:, None]).astype(jnp.bfloat16)
    hub_terms = spread_sum(share_back, hub_nbr, hub_table.shape[1])
    hub_count = hub_rows.shape[0]
    weight_total, hub_total = lax.psum((weight_sum, hub_terms), "row")
    owned_hubs = lax.dynamic_slice_in_dim(
        hub_total, lax.axis_index("row") * hub_count, hub_count, 0
    )
    share_padded = jnp.concatenate([share_back, jnp.zeros((1, narrow), jnp.bfloat16)], axis=0)
    slot_values = share_padded[slot_rows].T.reshape(narrow, peer_count, -1)
    returned = lax.all_to_all(slot_values, "row", split_axis=1, concat_axis=1, tiled=True)
    remote_grad = jax.ops.segment_sum(
        returned.reshape(narrow, -1).T.astype(jnp.float32), send_rows.reshape(-1), node_count
    )
    local_grad = spread_sum(share_back, loc_nbr, node_count)
    hub_grad = jax.ops.segment_sum(owned_hubs, hub_rows, node_count)
    grad_feats = (back_sum[:, :narrow] + local_grad + remote_grad + hub_grad).astype(jnp.bfloat16)
    return (hidden_out.T, grad_feats.T, weight_total[:narrow], weight_total[narrow:])


def solution(mesh):
    return jax.shard_map(
        per_device,
        mesh=mesh,
        in_specs=(
            P("col", "row"),
            P("col", None),
            P("col", None),
            P("col", "row"),
            P("row", None),
            P("row", None, None),
            P("row", None, None),
            P("row"),
            P("row", None),
        ),
        out_specs=(P("col", "row"), P("col", "row"), P("col", None), P("col", None)),
        check_vma=False,
    )
```

profile of v0, /device:TPU:1, one launch (start us, length us, event | category | flops | bytes accessed | tf_op | source)
XLA Modules:
  0.0 496.0 jit_solution(391836456921918905)
XLA Ops:
  7.2 0.7 compare_select_fusion.1
  7.9 1.1 copy.51
  9.0 12.1 %gather_fusion.3 = bf16[4096,64]{1,0:T(8,128)(2,1)S(1)} fusion(bf16[64,1024]{0,1:T(8,128)(2,1)S(1)} %copy.51, s32[4096]{0:T(1024)S(1)} %broadcast_clamp_fusion.2), kind=kCustom, calls=%fused_computation.3 | custom fusion | bytes 1064960 | tf_op jit(solution)/shard_map/gather | solution.py:24
  21.2 1.1 copy.56
  22.3 10.4 %all-to-all-start = ((bf16[64,32,128]{2,0,1:T(8,128)(2,1)}), bf16[64,32,128]{2,0,1:T(8,128)(2,1)S(1)}, u32[]{:S(2)}, u32[]{:S(2)}) async-start(bf16[64,32,128]{2,0,1:T(8,128)(2,1)} %copy.56), calls=%async_computation | async-start | bytes 1048576 | tf_op jit(solution)/shard_map/all_to_all | solution.py:25
  32.9 0.6 gather_fusion.1
  33.5 25.7 %all-gather = bf16[64,512]{0,1:T(8,128)(2,1)S(1)} all-gather(bf16[64,16]{0,1:T(8,128)(2,1)S(1)} %bitcast.60), channel_id=2, replica_groups=mesh['row'=32,'col'=16] {'row'}, dimensions={1}, use_global_device_ids=true | all-gather | bytes 67584 | tf_op jit(solution)/shard_map/all_gather | solution.py:26
  60.4 24.0 %gather_fusion = bf16[8192,64]{1,0:T(8,128)(2,1)S(1)} fusion(bf16[1024,64]{1,0:T(8,128)(2,1)S(1)} %copy.50, s32[8192]{0:T(1024)S(1)} %broadcast_clamp_fusion), kind=kCustom, calls=%fused_computation | custom fusion | bytes 2129920 | tf_op jit(solution)/shard_map/gather | solution.py:30
  84.4 2.2 convert_reduce_fusion
  86.6 6.2 %gather_fusion.2 = bf16[2048,64]{1,0:T(8,128)(2,1)S(1)} fusion(bf16[512,64]{1,0:T(8,128)(2,1)S(1)} %bitcast.52, s32[2048]{0:T(1024)S(1)} %broadcast_clamp_fusion.3), kind=kCustom, calls=%fused_computation.2 | custom fusion | bytes 532480 | tf_op jit(solution)/shard_map/gather | solution.py:31
  92.8 1.5 convert_reduce_fusion.1
  94.7 28.6 %scatter_custom_fusion.1 = f32[1025]{0:T(1024)S(1)} fusion(s32[4096]{0:T(1024)S(1)} %bitcast.64, f32[4096]{0:T(1024)S(1)} %convert_bitcast_fusion.3, f32[]{:T(128)} %constant.13.clone.1), kind=kCustom, calls=%fused_computation.54 | custom fusion | flops 4096 | bytes 4104 | tf_op jit(solution)/shard_map/scatter-add | solution.py:35
  123.4 2.0 copy.58
  125.4 26.8 %scatter_custom_fusion = f32[1025,64]{1,0:T(8,128)S(1)} fusion(s32[4096]{0:T(1024)S(1)} %bitcast.65, f32[4096,64]{1,0:T(8,128)} %copy.58, f32[]{:T(128)} %constant.13.clone.1), kind=kCustom, calls=%fused_computation.20 | custom fusion | flops 262144 | bytes 262912 | tf_op jit(solution)/shard_map/scatter-add | solution.py:32
  152.5 2.7 fusion.10
  155.2 70.5 %reduce-scatter.2.cloned.1.call-done = f32[1024,64]{0,1:T(8,128)} async-done(((f32[1024,1024]{0,1:T(8,128)}), f32[1024,64]{0,1:T(8,128)}) %reduce-scatter.2.cloned.1.call-update) | async-done | bytes 262160 | tf_op jit(solution)/shard_map/reduce_scatter | solution.py:43
  225.7 1.8 fusion.6
  228.2 71.9 %all-gather.3.cloned.1.call-done = bf16[1024,1024]{0,1:T(8,128)(2,1)} async-done(((bf16[1024,64]{0,1:T(8,128)(2,1)}), bf16[1024,1024]{0,1:T(8,128)(2,1)}) %all-gather.3.cloned.1.call-update) | async-done | bytes 2097168 | tf_op jit(solution)/shard_map/all_gather | solution.py:46
  300.1 2.0 fusion.21
  302.3 1.3 broadcast_in_dim.53
  303.7 12.5 %scatter_custom_fusion.4 = f32[512,64]{1,0:T(8,128)} fusion(s32[2048]{0:T(1024)S(1)} %reshape.180, f32[2048,64]{1,0:T(8,128)} %bitcast.59, f32[]{:T(128)} %constant.13.clone.1), kind=kCustom, calls=%fused_computation.35 | custom fusion | flops 131072 | bytes 131584 | tf_op jit(solution)/shard_map/scatter-add | solution.py:15
  316.2 1.6 fusion.9
  318.1 12.1 %gather_fusion.4 = bf16[4096,64]{1,0:T(8,128)(2,1)S(1)} fusion(bf16[1025,64]{1,0:T(8,128)(2,1)S(1)} %concatenate.11.clone, s32[4096]{0:T(1024)S(1)} %broadcast_clamp_fusion.1), kind=kCustom, calls=%fused_computation.4 | custom fusion | bytes 1064960 | tf_op jit(solution)/shard_map/gather | solution.py:63
  330.2 1.2 copy.64
  331.4 16.6 %all-to-all-start.1 = ((bf16[64,32,128]{2,0,1:T(8,128)(2,1)}), bf16[64,32,128]{2,0,1:T(8,128)(2,1)S(1)}, u32[]{:S(2)}, u32[]{:S(2)}) async-start(bf16[64,32,128]{2,0,1:T(8,128)(2,1)} %copy.64), calls=%async_computation.2 | async-start | bytes 1048576 | tf_op jit(solution)/shard_map/all_to_all | solution.py:64
  348.6 44.4 %scatter_custom_fusion.2 = f32[1024,64]{1,0:T(8,128)S(1)} fusion(f32[1024,64]{1,0:T(8,128)S(1)} %copy.62, s32[8192]{0:T(1024)S(1)} %reshape.164, f32[1024,64]{1,0:T(8,128)S(1)} %copy.61), kind=kCustom, calls=%fused_computation.12 | custom fusion | flops 524288 | bytes 786432 | tf_op jit(solution)/shard_map/scatter-add | solution.py:15
  393.0 67.9 %all-reduce.4.cloned.1.call-done = (f32[512,64]{1,0:T(8,128)}, f32[128,1024]{1,0:T(8,128)}) async-done(((f32[512,64]{1,0:T(8,128)}, f32[128,1024]{1,0:T(8,128)}), (f32[512,64]{1,0:T(8,128)}, f32[128,1024]{1,0:T(8,128)})) %all-reduce.4.cloned.1.call-update) | async-done | bytes 655376 | tf_op jit(solution)/shard_map/psum | solution.py:58
  460.8 1.9 fusion.20
  462.8 2.0 copy.66
  464.7 22.8 %scatter_custom_fusion.3 = f32[1024,64]{1,0:T(8,128)S(1)} fusion(s32[4096]{0:T(1024)} %bitcast.67, f32[4096,64]{1,0:T(8,128)} %copy.66, f32[]{:T(128)} %constant.13.clone.1), kind=kCustom, calls=%fused_computation.28 | custom fusion | flops 262144 | bytes 262656 | tf_op jit(solution)/shard_map/scatter-add | solution.py:65
  487.6 1.0 scatter_custom_fusion.5
  488.7 0.8 copy.69
  (64 shorter events, 4.0 us)
Async XLA Ops:
  21.1 11.7 %copy-start.9 = (s32[16]{0:T(128)S(1)}, s32[16]{0:T(128)}, u32[]{:S(2)}) copy-start(s32[16]{0:T(128)} %param.16) | copy-start | bytes 196
  21.2 11.7 %copy-start.8 = (s32[1024,2]{0,1:T(2,128)S(1)}, s32[1024,2]{0,1:T(2,128)}, u32[]{:S(2)}) copy-start(s32[1024,2]{0,1:T(2,128)} %param.17) | copy-start | bytes 24580
  21.2 11.7 %copy-start.7 = (s32[1,32,128]{2,1,0:T(8,128)S(1)}, s32[1,32,128]{2,1,0:T(8,128)}, u32[]{:S(2)}) copy-start(s32[1,32,128]{2,1,0:T(8,128)} %param.15) | copy-start | bytes 49156
  21.2 11.7 %copy-start.4 = (s32[1024,8]{0,1:T(8,128)S(1)}, s32[1024,8]{0,1:T(8,128)}, u32[]{:S(2)}) copy-start(s32[1024,8]{0,1:T(8,128)} %param.13) | copy-start | bytes 98308
  21.2 38.0 %copy-start.1 = (bf16[64,1024]{1,0:T(8,128)(2,1)S(1)}, bf16[64,1024]{1,0:T(8,128)(2,1)}, u32[]{:S(2)}) copy-start(bf16[64,1024]{1,0:T(8,128)(2,1)} %param.9) | copy-start | bytes 393220
  22.3 101.0 %all-to-all-start = ((bf16[64,32,128]{2,0,1:T(8,128)(2,1)}), bf16[64,32,128]{2,0,1:T(8,128)(2,1)S(1)}, u32[]{:S(2)}, u32[]{:S(2)}) async-start(bf16[64,32,128]{2,0,1:T(8,128)(2,1)} %copy.56), calls=%async_computation | async-start | bytes 1048576 | tf_op jit(solution)/shard_map/all_to_all | solution.py:25
  32.7 192.9 %reduce-scatter.2.cloned.1.call-start = ((), (), s32[]{:S(2)}) async-start(), calls=%async_computation.3 | async-start | bytes 4456448 | tf_op jit(solution)/shard_map/reduce_scatter | solution.py:43
  92.8 1.7 copy-start.2
  92.8 30.5 %copy-start.5 = (bf16[64,1024]{1,0:T(8,128)(2,1)S(1)}, bf16[64,1024]{1,0:T(8,128)(2,1)}, u32[]{:S(2)}) copy-start(bf16[64,1024]{1,0:T(8,128)(2,1)} %param.10) | copy-start | bytes 393220
  92.8 30.5 %copy-start.6 = (bf16[64,1024]{1,0:T(8,128)(2,1)S(1)}, bf16[64,1024]{1,0:T(8,128)(2,1)}, u32[]{:S(2)}) copy-start(bf16[64,1024]{1,0:T(8,128)(2,1)} %param.11) | copy-start | bytes 393220
  155.2 70.5 %copy-start.3 = (bf16[64,1024]{1,0:T(8,128)(2,1)S(1)}, bf16[64,1024]{1,0:T(8,128)(2,1)}, u32[]{:S(2)}) copy-start(bf16[64,1024]{1,0:T(8,128)(2,1)} %param.12) | copy-start | bytes 393220
  155.2 144.9 %all-gather.3.cloned.1.call-start = ((), (), s32[]{:S(2)}) async-start(), calls=%async_computation.4 | async-start | bytes 2228224 | tf_op jit(solution)/shard_map/all_gather | solution.py:46
  227.5 233.4 %all-reduce.4.cloned.1.call-start = ((), (), s32[]{:S(2)}) async-start(), calls=%async_computation.5 | async-start | bytes 1572864 | tf_op jit(solution)/shard_map/psum | solution.py:58
  302.1 14.0 %copy-start = (bf16[1024,1024]{0,1:T(8,128)(2,1)S(1)}, bf16[1024,1024]{0,1:T(8,128)(2,1)}, u32[]{:S(2)}) copy-start(bf16[1024,1024]{0,1:T(8,128)(2,1)} %all-gather.3.cloned.1.call-done) | copy-start | bytes 6291460
  331.4 131.4 %all-to-all-start.1 = ((bf16[64,32,128]{2,0,1:T(8,128)(2,1)}), bf16[64,32,128]{2,0,1:T(8,128)(2,1)S(1)}, u32[]{:S(2)}, u32[]{:S(2)}) async-start(bf16[64,32,128]{2,0,1:T(8,128)(2,1)} %copy.64), calls=%async_computation.2 | async-start | bytes 1048576 | tf_op jit(solution)/shard_map/all_to_all | solution.py:64
Sparse Core Ops, SparseCore 0:
  155.3 70.3 reduce-scatter.1
  228.3 71.6 all-gather.2
  317.9 142.8 all-reduce.3
where the time goes:
time: 496 us
  waiting for transfers between devices  210 us (42%)
  other arithmetic  143 us (29%)
  local copies, waits for them, and re-layouts  69.6 us (14%)
  starting transfers between devices  27.3 us (6%)
  blocking collectives  25.7 us (5%)
  between operations  14.2 us (3%)
  matrix products  6.35 us (1%)
    all_gather x1, waiting for transfers between devices, per_device(): block_cols = lax.all_gather(slopes, 'col', axis=1, tiled=True)  71.9 us
    reduce_scatter x1, waiting for transfers between devices, per_device(): lax.psum_scatter(partial_product, 'col', scatter_dimension=1, tiled=True)  70.5 us
    psum x1, waiting for transfers between devices, per_device(): weight_total, hub_total = lax.psum((weight_sum, hub_terms), 'row')  67.9 us
    scatter-add x2, other arithmetic, spread_sum(): jax.ops.segment_sum(spread.reshape(-1, values.shape[1]).astype(jnp.float3...  56.9 us
    scatter-add x1, other arithmetic, per_device(): jax.ops.segment_sum(live_slots.astype(jnp.float32), slot_rows, node_count...  28.6 us
    scatter-add x1, other arithmetic, per_device(): jax.ops.segment_sum(incoming.reshape(narrow, -1).T.astype(jnp.float32), s...  26.8 us
    all_gather x1, blocking collectives, per_device(): hub_table = lax.all_gather(feats[:, hub_rows], 'row', axis=1, tiled=True)  25.7 us
    gather x1, local copies, waits for them, and re-layouts, per_device(): local_sum = jnp.sum(node_rows[loc_nbr], axis=1, dtype=jnp.float32)  24 us
  transfers between devices with their start and end apart: 5, of which 3 were waited for; matrix products, arithmetic and copies ran while one was open for 25% of the time, Pallas kernels for 0%

commit v1 on v0

v1 whole, which is shorter than its diff:
```python
import jax
import jax.numpy as jnp
from jax import lax
from jax.experimental import pallas as pl
from jax.experimental.pallas import tpu as pltpu
from jax.sharding import PartitionSpec as P

NODES = 1024
FEATS = 64
PEERS = 32
SLOTS = 128
HUBS_OWN = 16
HUBS = 512
ROWS = 80
BF16 = jnp.bfloat16
F32 = jnp.float32
NT = (((1,), (1,)), ((), ()))
NN = (((1,), (0,)), ((), ()))
MIB = 1 << 20


def params():
    return pltpu.CompilerParams(vmem_limit_bytes=48 * MIB)


def cost(flops, moved):
    return pl.CostEstimate(flops=flops, bytes_accessed=moved, transcendentals=0)


def whole(shape):
    return pl.BlockSpec(shape, lambda *_: (0,) * len(shape))


def one_hot(mask):
    return jnp.where(mask, 1.0, 0.0).astype(BF16)


def matmul(a, b, dims):
    return lax.dot_general(a, b, dims, preferred_element_type=F32)


def gather_kernel(x_ref, send_ref, hub_ref, out_ref):
    x = x_ref[...]
    node = lax.broadcasted_iota(jnp.int32, (NODES, 2 * SLOTS), 0)
    hub_node = lax.broadcasted_iota(jnp.int32, (NODES, SLOTS), 0)
    hub_feats = matmul(x, one_hot(hub_node == hub_ref[...]), NN)
    hub_rows = hub_feats.T[:HUBS_OWN, :]
    hub_block = jnp.concatenate([hub_rows, jnp.zeros_like(hub_rows)], axis=1).astype(BF16)
    for pair in range(PEERS // 2):
        picked = matmul(x, one_hot(node == send_ref[pair : pair + 1, :]), NN).astype(BF16)
        out_ref[2 * pair, :FEATS, :] = picked[:, :SLOTS]
        out_ref[2 * pair + 1, :FEATS, :] = picked[:, SLOTS:]
        out_ref[2 * pair, FEATS:, :] = hub_block
        out_ref[2 * pair + 1, FEATS:, :] = hub_block


def gather_slots(feats, send_pairs, hub_lanes):
    return pl.pallas_call(
        gather_kernel,
        out_shape=jax.ShapeDtypeStruct((PEERS, ROWS, SLOTS), BF16),
        compiler_params=params(),
        cost_estimate=cost(2 * 256 * 4096 * 1024, 1 << 20),
        name="gather_slots",
    )(feats, send_pairs, hub_lanes)


BUILD = 128


def build_kernel(loc_ref, recv_ref, hub_ref, local_ref, slot_ref, hubs_ref, degree_ref):
    first = pl.program_id(0) * BUILD
    node = lax.broadcasted_iota(jnp.int32, (BUILD, 2 * SLOTS), 0) + first
    for pair in range(PEERS // 2):
        slot_ref[:, 2 * SLOTS * pair : 2 * SLOTS * (pair + 1)] = one_hot(
            node == recv_ref[pair : pair + 1, :]
        )
    lane = lax.broadcasted_iota(jnp.int32, (BUILD, NODES), 1)
    counts = jnp.zeros((BUILD, NODES), F32)
    for k in range(loc_ref.shape[1]):
        counts = counts + jnp.where(lane == loc_ref[:, k : k + 1], 1.0, 0.0)
    local_ref[...] = counts.astype(BF16)
    hub_lane = lax.broadcasted_iota(jnp.int32, (BUILD, HUBS), 1)
    hub_counts = jnp.zeros((BUILD, HUBS), F32)
    for k in range(hub_ref.shape[1]):
        hub_counts = hub_counts + jnp.where(hub_lane == hub_ref[:, k : k + 1], 1.0, 0.0)
    hubs_ref[...] = hub_counts.astype(BF16)
    arrivals = matmul(jnp.ones((8, PEERS * SLOTS), BF16), slot_ref[...], NT)
    degree_ref[...] = arrivals + float(loc_ref.shape[1] + hub_ref.shape[1])


def build_counts(loc_nbr, recv_pairs, hub_nbr):
    return pl.pallas_call(
        build_kernel,
        grid=(NODES // BUILD,),
        in_specs=[
            pl.BlockSpec((BUILD, loc_nbr.shape[1]), lambda i: (i, 0)),
            whole((PEERS // 2, 2 * SLOTS)),
            pl.BlockSpec((BUILD, hub_nbr.shape[1]), lambda i: (i, 0)),
        ],
        out_specs=[
            pl.BlockSpec((BUILD, NODES), lambda i: (i, 0)),
            pl.BlockSpec((BUILD, PEERS * SLOTS), lambda i: (i, 0)),
            pl.BlockSpec((BUILD, HUBS), lambda i: (i, 0)),
            pl.BlockSpec((8, BUILD), lambda i: (0, i)),
        ],
        out_shape=[
            jax.ShapeDtypeStruct((NODES, NODES), BF16),
            jax.ShapeDtypeStruct((NODES, PEERS * SLOTS), BF16),
            jax.ShapeDtypeStruct((NODES, HUBS), BF16),
            jax.ShapeDtypeStruct((8, NODES), F32),
        ],
        compiler_params=params(),
        cost_estimate=cost(1 << 30, 24 << 20),
        name="build_counts",
    )(loc_nbr, recv_pairs, hub_nbr)


AGG = 256


def aggregate_kernel(x_ref, inc_ref, local_ref, slot_ref, hubs_ref, degree_ref, out_ref, slots, table):
    @pl.when(pl.program_id(0) == 0)
    def _():
        for peer in range(PEERS):
            slots[:, SLOTS * peer : SLOTS * (peer + 1)] = inc_ref[peer, :FEATS, :]
        rows = inc_ref[:, FEATS:, :].astype(F32).reshape(HUBS, SLOTS)
        table[...] = rows.T[:FEATS, :].astype(BF16)

    total = (
        matmul(x_ref[...], local_ref[...], NT)
        + matmul(slots[...], slot_ref[...], NT)
        + matmul(table[...], hubs_ref[...], NT)
    )
    out_ref[...] = (total / degree_ref[0:1, :]).astype(BF16)


def aggregate(feats, incoming, local, slot, hubs, degree):
    return pl.pallas_call(
        aggregate_kernel,
        grid=(NODES // AGG,),
        in_specs=[
            whole((FEATS, NODES)),
            whole((PEERS, ROWS, SLOTS)),
            pl.BlockSpec((AGG, NODES), lambda i: (i, 0)),
            pl.BlockSpec((AGG, PEERS * SLOTS), lambda i: (i, 0)),
            pl.BlockSpec((AGG, HUBS), lambda i: (i, 0)),
            pl.BlockSpec((8, AGG), lambda i: (0, i)),
        ],
        out_specs=pl.BlockSpec((FEATS, AGG), lambda i: (0, i)),
        out_shape=jax.ShapeDtypeStruct((FEATS, NODES), BF16),
        scratch_shapes=[pltpu.VMEM((FEATS, PEERS * SLOTS), BF16), pltpu.VMEM((FEATS, HUBS), BF16)],
        compiler_params=params(),
        cost_estimate=cost(2 * 256 * 5632 * 1024, 12 << 20),
        name="aggregate",
    )(feats, incoming, local, slot, hubs, degree)


def return_kernel(share_ref, slot_ref, hubs_ref, out_ref):
    share = share_ref[...]
    values = matmul(share, slot_ref[...], NN).astype(BF16)
    for peer in range(8):
        out_ref[peer, :FEATS, :] = values[:, SLOTS * peer : SLOTS * (peer + 1)]
    terms = matmul(share, hubs_ref[...], NN).T
    high = terms.astype(BF16)
    low = (terms - high.astype(F32)).astype(BF16)
    both = jnp.concatenate([high.astype(F32), low.astype(F32)], axis=1)
    out_ref[:, FEATS:, :] = both.reshape(8, HUBS_OWN, SLOTS).astype(BF16)


def return_slots(share, slot, hubs):
    return pl.pallas_call(
        return_kernel,
        grid=(PEERS // 8,),
        in_specs=[
            whole((FEATS, NODES)),
            pl.BlockSpec((NODES, 8 * SLOTS), lambda i: (0, i)),
            pl.BlockSpec((NODES, 8 * HUBS_OWN), lambda i: (0, i)),
        ],
        out_specs=pl.BlockSpec((8, ROWS, SLOTS), lambda i: (i, 0, 0)),
        out_shape=jax.ShapeDtypeStruct((PEERS, ROWS, SLOTS), BF16),
        compiler_params=params(),
        cost_estimate=cost(2 * 256 * 4608 * 1024, 10 << 20),
        name="return_slots",
    )(share, slot, hubs)


SPREAD = 256


def spread_kernel(back_ref, send_ref, hub_ref, base_ref, out_ref, slots, hub_total):
    @pl.when(pl.program_id(0) == 0)
    def _():
        for peer in range(PEERS):
            slots[:, SLOTS * peer : SLOTS * (peer + 1)] = back_ref[peer, :FEATS, :]
        sums = jnp.sum(back_ref[:, FEATS:, :].astype(F32), axis=0)
        total = sums[:, :FEATS] + sums[:, FEATS:]
        high = total.astype(BF16).astype(F32)
        stacked = jnp.concatenate(
            [high, total - high, jnp.zeros((SLOTS - 2 * HUBS_OWN, FEATS), F32)], axis=0
        )
        hub_total[...] = stacked.T.astype(BF16)

    first = pl.program_id(0) * SPREAD
    node = lax.broadcasted_iota(jnp.int32, (SPREAD, 2 * SLOTS), 0) + first
    grad = base_ref[...]
    for pair in range(PEERS // 2):
        grad = grad + matmul(
            slots[:, 2 * SLOTS * pair : 2 * SLOTS * (pair + 1)],
            one_hot(node == send_ref[pair : pair + 1, :]),
            NT,
        )
    hub_node = lax.broadcasted_iota(jnp.int32, (SPREAD, SLOTS), 0) + first
    grad = grad + matmul(hub_total[...], one_hot(hub_node == hub_ref[...]), NT)
    out_ref[...] = grad.astype(BF16)


def spread_grads(returned, send_pairs, hub_lanes, base):
    return pl.pallas_call(
        spread_kernel,
        grid=(NODES // SPREAD,),
        in_specs=[
            whole((PEERS, ROWS, SLOTS)),
            whole((PEERS // 2, 2 * SLOTS)),
            whole((1, SLOTS)),
            pl.BlockSpec((FEATS, SPREAD), lambda i: (0, i)),
        ],
        out_specs=pl.BlockSpec((FEATS, SPREAD), lambda i: (0, i)),
        out_shape=jax.ShapeDtypeStruct((FEATS, NODES), BF16),
        scratch_shapes=[pltpu.VMEM((FEATS, PEERS * SLOTS), BF16), pltpu.VMEM((FEATS, SLOTS), BF16)],
        compiler_params=params(),
        cost_estimate=cost(2 * 256 * 4224 * 1024, 2 << 20),
        name="spread_grads",
    )(returned, send_pairs, hub_lanes, base)


def silu_slope(preact):
    sigmoid_part = jax.nn.sigmoid(preact)
    return sigmoid_part * (1.0 + preact * (1.0 - sigmoid_part))


def per_device(feats, w_self, w_neigh, cotangent, loc_nbr, send_rows, recv_node, hub_rows, hub_nbr):
    send_pairs = send_rows.reshape(PEERS // 2, 2 * SLOTS)
    recv_pairs = recv_node.reshape(PEERS // 2, 2 * SLOTS)
    hub_lanes = jnp.concatenate(
        [hub_rows, hub_rows, jnp.full((SLOTS - 2 * HUBS_OWN,), -1, jnp.int32)]
    )[None, :]
    outgoing = gather_slots(feats, send_pairs, hub_lanes)
    incoming = lax.all_to_all(outgoing, "row", 0, 0, tiled=True)
    local, slot, hubs, degree = build_counts(loc_nbr, recv_pairs, hub_nbr)
    agg = aggregate(feats, incoming, local, slot, hubs, degree)
    joined = jnp.concatenate([feats, agg], axis=0)
    weights = jnp.concatenate([w_self, w_neigh], axis=0)
    partial_product = lax.dot_general(
        weights, joined, (((0,), (0,)), ((), ())), preferred_element_type=F32
    )
    preact = lax.psum_scatter(partial_product, "col", scatter_dimension=0, tiled=True)
    hidden_out = jax.nn.silu(preact).astype(BF16)
    slopes = (cotangent.astype(F32) * silu_slope(preact)).astype(BF16)
    block_rows = lax.all_gather(slopes, "col", axis=0, tiled=True)
    back_sum = matmul(weights, block_rows, NN)
    share = (back_sum[FEATS:] / degree[0:1, :]).astype(BF16)
    returned = lax.all_to_all(return_slots(share, slot, hubs), "row", 0, 0, tiled=True)
    weight_part = matmul(joined, block_rows, NT)
    pieces = weight_part.reshape(16, 8, 2, 512).transpose(0, 2, 1, 3).reshape(PEERS, 8, 512)
    pieces = lax.all_to_all(pieces, "row", 0, 0, tiled=True)
    piece = jnp.sum(pieces, axis=0, keepdims=True)
    pieces = lax.all_to_all(jnp.broadcast_to(piece, pieces.shape), "row", 0, 0, tiled=True)
    weight_total = pieces.reshape(16, 2, 8, 512).transpose(0, 2, 1, 3).reshape(2 * FEATS, 1024)
    base = back_sum[:FEATS] + matmul(share, local, NN)
    grad_feats = spread_grads(returned, send_pairs, hub_lanes, base)
    return (hidden_out, grad_feats, weight_total[:FEATS], weight_total[FEATS:])


def solution(mesh):
    return jax.shard_map(
        per_device,
        mesh=mesh,
        in_specs=(
            P("col", "row"),
            P("col", None),
            P("col", None),
            P("col", "row"),
            P("row", None),
            P("row", None, None),
            P("row", None, None),
            P("row"),
            P("row", None),
        ),
        out_specs=(P("col", "row"), P("col", "row"), P("col", None), P("col", None)),
        check_vma=False,
    )
```

time: 496 us -> 270 us (0.54)
  other arithmetic: 143 us -> 3.72 us
  local copies, waits for them, and re-layouts: 69.6 us -> 11.6 us
  waiting for transfers between devices: 210 us -> 164 us
  Pallas kernels: 0 us -> 26.8 us
  blocking collectives: 25.7 us -> 0 us
  starting transfers between devices: 27.3 us -> 38.1 us
    scatter-add x6 -> x0, other arithmetic: 136 us -> none  [the longest x2 56.9 us: spread_sum(): jax.ops.segment_sum(spread.reshape(-1, values.shape[1]).astype(jnp.float3...]
    psum x1 -> x0, waiting for transfers between devices: 67.9 us -> none  [per_device(): weight_total, hub_total = lax.psum((weight_sum, hub_terms), 'row')]
    gather x5 -> x0, local copies, waits for them, and re-layouts: 55 us -> none  [the longest x1 24 us: per_device(): local_sum = jnp.sum(node_rows[loc_nbr], axis=1, dtype=jnp.float32)]
    pallas_call x0 -> x5, Pallas kernels: none -> 26.8 us  [the longest x1 8.12 us: build_counts(): pl.pallas_call(build_kernel, grid=(NODES // BUILD,), in_specs=[pl.BlockSp...]
    all_gather x1 -> x0, blocking collectives: 25.7 us -> none  [per_device(): hub_table = lax.all_gather(feats[:, hub_rows], 'row', axis=1, tiled=True)]
    all_to_all x2 -> x4, waiting for transfers between devices: 0.01 us -> 20.2 us  [the longest x1 11.8 us: per_device(): lax.all_to_all(return_slots(share, slot, hubs), 'row', 0, 0, tiled=True)]
    all_to_all x2 -> x4, starting transfers between devices: 27 us -> 38 us  [the longest x1 16.9 us: per_device(): pieces = lax.all_to_all(pieces, 'row', 0, 0, tiled=True)]
    dot_general x3 -> x4, matrix products: 6.35 us -> 10.5 us  [the longest x3 6.79 us: matmul(): return lax.dot_general(a, b, dims, preferred_element_type=F32)]
  transfers between devices with their start and end apart: 5 -> 6, of which waited for: 3 -> 5; matrix products, arithmetic and copies ran while one was open for 25% -> 3% of each run, Pallas kernels for 0% -> 7%
where the time goes in v1:
time: 270 us; the launch traced here: 269 us
  waiting for transfers between devices  164 us (61%)
  starting transfers between devices  38.1 us (14%)
  Pallas kernels  26.8 us (10%)
  between operations  14.2 us (5%)
  local copies, waits for them, and re-layouts  11.6 us (4%)
  matrix products  10.5 us (4%)
  other arithmetic  3.72 us (1%)
    all_gather x1, waiting for transfers between devices, per_device(): block_rows = lax.all_gather(slopes, 'col', axis=0, tiled=True)  72 us
    reduce_scatter x1, waiting for transfers between devices, per_device(): lax.psum_scatter(partial_product, 'col', scatter_dimension=0, tiled=True)  71.9 us
    all_to_all x1, starting transfers between devices, per_device(): pieces = lax.all_to_all(pieces, 'row', 0, 0, tiled=True)  16.9 us
    all_to_all x1, waiting for transfers between devices, per_device(): lax.all_to_all(return_slots(share, slot, hubs), 'row', 0, 0, tiled=True)  11.8 us
    all_to_all x1, starting transfers between devices, per_device(): incoming = lax.all_to_all(outgoing, 'row', 0, 0, tiled=True)  11.1 us
    pallas_call x1, Pallas kernels, build_counts(): pl.pallas_call(build_kernel, grid=(NODES // BUILD,), in_specs=[pl.BlockSp...  8.12 us
    unnamed x25, local copies, waits for them, and re-layouts  7.43 us
    dot_general x3, matrix products, matmul(): return lax.dot_general(a, b, dims, preferred_element_type=F32)  6.79 us
  transfers between devices with their start and end apart: 6, of which 5 were waited for; matrix products, arithmetic and copies ran while one was open for 3% of the time, Pallas kernels for 7%

profile of v1, /device:TPU:1, one launch (start us, length us, event | category | flops | bytes accessed | tf_op | source)
XLA Modules:
  0.0 268.9 jit_solution(9081464976076808446)
XLA Ops:
  7.2 0.7 reshape.27.send_ref
  7.9 0.8 add_bitcast_fusion.hub_ref
  8.7 0.9 copy-done.1
  9.6 2.5 gather_slots.1
  12.1 11.1 %all-to-all-start = ((bf16[32,80,128]{2,1,0:T(8,128)(2,1)}), bf16[32,80,128]{2,1,0:T(8,128)(2,1)}, u32[]{:S(2)}, u32[]{:S(2)}) async-start(bf16[32,80,128]{2,1,0:T(8,128)(2,1)} %gather_slots.1), calls=%async_computation | async-start | bytes 1310720 | tf_op jit(solution)/shard_map/all_to_all | solution.py:248
  23.3 1.0 copy.13.loc_ref
  24.3 1.0 copy.14.hub_ref
  25.3 1.0 copy-done.3
  26.4 1.0 copy-done.4
  27.4 8.1 %build_counts.1 = (bf16[1024,1024]{1,0:T(8,128)(2,1)S(1)}, bf16[1024,4096]{1,0:T(8,128)(2,1)}, bf16[1024,512]{1,0:T(8,128)(2,1)S(1)}, f32[8,1024]{1,0:T(8,128)S(1)}) custom-call(s32[1024,8]{1,0:T(8,128)S(1)} %copy-done.3, s32[16,256]{1,0:T(8,128)S(1)} %reshape.28.recv_ref, s32[1024,2]{1,0:T(8,128)S(1)} %copy-done.4), custom_call_target="tpu_custom_call" | custom-call | flops 1073741824 | bytes 25165824 | tf_op jit(solution)/shard_map/build_counts/pallas_call | solution.py:92
  36.2 0.7 constant_dynamic-update-slice_fusion
  36.9 6.6 %aggregate.1 = bf16[64,1024]{1,0:T(8,128)(2,1)S(1)} custom-call(bf16[64,1024]{1,0:T(8,128)(2,1)S(1)} %copy-done.2, bf16[32,80,128]{2,1,0:T(8,128)(2,1)} %all-to-all-done.inc_ref, bf16[1024,1024]{1,0:T(8,128)(2,1)S(1)} %get-tuple-element.8.local_ref, bf16[1024,4096]{1,0:T(8,128)(2,1)} %get-tuple-element.9.slot_ref, ...), custom_call_target="tpu_custom_call" | custom-call | flops 2952790016 | bytes 12582912 | tf_op jit(solution)/shard_map/aggregate/pallas_call | solution.py:138
  43.5 3.7 %fusion.2 = f32[1024,1024]{1,0:T(8,128)} fusion(bf16[128,1024]{1,0:T(8,128)(2,1)} %constant_dynamic-update-slice_fusion, bf16[64,1024]{1,0:T(8,128)(2,1)S(1)} %aggregate.1, bf16[64,1024]{1,0:T(8,128)(2,1)S(1)} %copy-done.2), kind=kOutput, calls=%fused_computation.8 | convolution fusion | flops 268959744 | bytes 4718592 | tf_op jit(solution)/shard_map/dot_general | solution.py:253
  47.2 71.9 %reduce-scatter.2.cloned.1.call-done = f32[64,1024]{1,0:T(8,128)} async-done(((f32[1024,1024]{1,0:T(8,128)}), f32[64,1024]{1,0:T(8,128)}) %reduce-scatter.2.cloned.1.call-update) | async-done | bytes 262160 | tf_op jit(solution)/shard_map/reduce_scatter | solution.py:256
  119.2 1.8 multiply_convert_fusion
  121.0 72.0 %all-gather.2.cloned.1.call-done = bf16[1024,1024]{1,0:T(8,128)(2,1)} async-done(((bf16[64,1024]{1,0:T(8,128)(2,1)}), bf16[1024,1024]{1,0:T(8,128)(2,1)}) %all-gather.2.cloned.1.call-update) | async-done | bytes 2097168 | tf_op jit(solution)/shard_map/all_gather | solution.py:259
  193.0 3.2 %fusion.1 = f32[128,1024]{1,0:T(8,128)} fusion(bf16[1024,1024]{1,0:T(8,128)(2,1)} %all-gather.2.cloned.1.call-done, bf16[64,1024]{1,0:T(8,128)(2,1)S(1)} %aggregate.1, bf16[64,1024]{1,0:T(8,128)(2,1)S(1)} %copy-done.2), kind=kOutput, calls=%fused_computation.7 | convolution fusion | flops 268959744 | bytes 2883584 | tf_op jit(solution)/shard_map/dot_general | solution.py:39
  196.2 16.9 %all-to-all-start.2 = ((f32[32,8,512]{2,1,0:T(8,128)}), f32[32,8,512]{2,1,0:T(8,128)}, u32[]{:S(2)}, u32[]{:S(2)}) async-start(f32[32,8,512]{2,1,0:T(8,128)} %bitcast.19), calls=%async_computation.3 | async-start | bytes 1048576 | tf_op jit(solution)/shard_map/all_to_all | solution.py:265
  213.1 2.1 fusion.6
  215.3 0.8 copy-done.5
  216.2 5.5 %return_slots.1 = bf16[32,80,128]{2,1,0:T(8,128)(2,1)S(1)} custom-call(bf16[64,1024]{1,0:T(8,128)(2,1)S(1)} %fusion.share_ref, bf16[1024,4096]{1,0:T(8,128)(2,1)} %get-tuple-element.9.slot_ref, bf16[1024,512]{1,0:T(8,128)(2,1)S(1)} %get-tuple-element.10.hubs_ref), custom_call_target="tpu_custom_call" | custom-call | flops 2415919104 | bytes 10485760 | tf_op jit(solution)/shard_map/return_slots/pallas_call | solution.py:171
  221.7 0.9 copy-done
  222.6 2.2 all-to-all-done.2
  224.7 5.2 %all-to-all-start.1 = ((bf16[32,80,128]{2,1,0:T(8,128)(2,1)}), bf16[32,80,128]{2,1,0:T(8,128)(2,1)S(1)}, u32[]{:S(2)}, u32[]{:S(2)}) async-start(bf16[32,80,128]{2,1,0:T(8,128)(2,1)} %copy-done), calls=%async_computation.2 | async-start | bytes 1310720 | tf_op jit(solution)/shard_map/all_to_all | solution.py:262
  230.0 1.1 reduce_sum.9
  231.0 11.8 %all-to-all-done.1.back_ref = bf16[32,80,128]{2,1,0:T(8,128)(2,1)S(1)} async-done(((bf16[32,80,128]{2,1,0:T(8,128)(2,1)}), bf16[32,80,128]{2,1,0:T(8,128)(2,1)S(1)}, u32[]{:S(2)}, u32[]{:S(2)}) %all-to-all-start.1) | async-done | bytes 655392 | tf_op jit(solution)/shard_map/all_to_all | solution.py:262
  242.9 0.9 broadcast_in_dim.14
  243.7 4.7 %all-to-all-start.3 = ((f32[32,8,512]{2,1,0:T(8,128)}), f32[32,8,512]{2,1,0:T(8,128)}, u32[]{:S(2)}, u32[]{:S(2)}) async-start(f32[32,8,512]{2,1,0:T(8,128)} %broadcast_in_dim.14), calls=%async_computation.4 | async-start | bytes 1048576 | tf_op jit(solution)/shard_map/all_to_all | solution.py:267
  248.5 1.4 convolution_add_fusion.base_ref
  249.9 4.1 %spread_grads.1 = bf16[64,1024]{1,0:T(8,128)(2,1)} custom-call(bf16[32,80,128]{2,1,0:T(8,128)(2,1)S(1)} %all-to-all-done.1.back_ref, s32[16,256]{1,0:T(8,128)S(1)} %reshape.27.send_ref, s32[1,128]{1,0:T(1,128)S(1)} %add_bitcast_fusion.hub_ref, f32[64,1024]{1,0:T(8,128)S(1)} %convolution_add_fusion.base_ref), custom_call_target="tpu_custom_call" | custom-call | flops 2214592512 | bytes 2097152 | tf_op jit(solution)/shard_map/spread_grads/pallas_call | solution.py:218
  254.0 6.2 %all-to-all-done.3 = f32[32,8,512]{2,1,0:T(8,128)} async-done(((f32[32,8,512]{2,1,0:T(8,128)}), f32[32,8,512]{2,1,0:T(8,128)}, u32[]{:S(2)}, u32[]{:S(2)}) %all-to-all-start.3) | async-done | bytes 524320 | tf_op jit(solution)/shard_map/all_to_all | solution.py:267
  260.2 1.9 fusion.5
  (27 shorter events, 0.9 us)
Async XLA Ops:
  8.7 0.9 copy-start.1
  9.6 13.6 %copy-start.9 = (s32[1,32,128]{2,1,0:T(8,128)S(1)}, s32[1,32,128]{2,1,0:T(8,128)}, u32[]{:S(2)}) copy-start(s32[1,32,128]{2,1,0:T(8,128)} %param.15) | copy-start | bytes 49156
  9.6 13.7 %copy-start.8 = (s32[1024,8]{0,1:T(8,128)S(1)}, s32[1024,8]{0,1:T(8,128)}, u32[]{:S(2)}) copy-start(s32[1024,8]{0,1:T(8,128)} %param.13) | copy-start | bytes 98308
  9.6 14.7 %copy-start.10 = (s32[1024,2]{0,1:T(2,128)S(1)}, s32[1024,2]{0,1:T(2,128)}, u32[]{:S(2)}) copy-start(s32[1024,2]{0,1:T(2,128)} %param.17) | copy-start | bytes 24580
  12.1 24.8 %all-to-all-start = ((bf16[32,80,128]{2,1,0:T(8,128)(2,1)}), bf16[32,80,128]{2,1,0:T(8,128)(2,1)}, u32[]{:S(2)}, u32[]{:S(2)}) async-start(bf16[32,80,128]{2,1,0:T(8,128)(2,1)} %gather_slots.1), calls=%async_computation | async-start | bytes 1310720 | tf_op jit(solution)/shard_map/all_to_all | solution.py:248
  23.2 96.0 %reduce-scatter.2.cloned.1.call-start = ((), (), s32[]{:S(2)}) async-start(), calls=%async_computation.5 | async-start | bytes 4456448 | tf_op jit(solution)/shard_map/reduce_scatter | solution.py:256
  25.3 1.0 copy-start.3
  26.4 1.0 copy-start.4
  27.4 8.1 %copy-start.6 = (bf16[64,1024]{1,0:T(8,128)(2,1)S(1)}, bf16[64,1024]{1,0:T(8,128)(2,1)}, u32[]{:S(2)}) copy-start(bf16[64,1024]{1,0:T(8,128)(2,1)} %param.10) | copy-start | bytes 393220
  27.4 8.8 %copy-start.7 = (bf16[64,1024]{1,0:T(8,128)(2,1)S(1)}, bf16[64,1024]{1,0:T(8,128)(2,1)}, u32[]{:S(2)}) copy-start(bf16[64,1024]{1,0:T(8,128)(2,1)} %param.11) | copy-start | bytes 393220
  27.4 9.5 %copy-start.2 = (bf16[64,1024]{1,0:T(8,128)(2,1)S(1)}, bf16[64,1024]{1,0:T(8,128)(2,1)}, u32[]{:S(2)}) copy-start(bf16[64,1024]{1,0:T(8,128)(2,1)} %x_ref.3) | copy-start | bytes 393220
  47.2 145.8 %all-gather.2.cloned.1.call-start = ((), (), s32[]{:S(2)}) async-start(), calls=%async_computation.6 | async-start | bytes 2228224 | tf_op jit(solution)/shard_map/all_gather | solution.py:259
  196.2 28.5 %all-to-all-start.2 = ((f32[32,8,512]{2,1,0:T(8,128)}), f32[32,8,512]{2,1,0:T(8,128)}, u32[]{:S(2)}, u32[]{:S(2)}) async-start(f32[32,8,512]{2,1,0:T(8,128)} %bitcast.19), calls=%async_computation.3 | async-start | bytes 1048576 | tf_op jit(solution)/shard_map/all_to_all | solution.py:265
  215.3 0.9 copy-start.5
  221.7 0.9 copy-start
  224.7 18.1 %all-to-all-start.1 = ((bf16[32,80,128]{2,1,0:T(8,128)(2,1)}), bf16[32,80,128]{2,1,0:T(8,128)(2,1)S(1)}, u32[]{:S(2)}, u32[]{:S(2)}) async-start(bf16[32,80,128]{2,1,0:T(8,128)(2,1)} %copy-done), calls=%async_computation.2 | async-start | bytes 1310720 | tf_op jit(solution)/shard_map/all_to_all | solution.py:262
  243.7 16.5 %all-to-all-start.3 = ((f32[32,8,512]{2,1,0:T(8,128)}), f32[32,8,512]{2,1,0:T(8,128)}, u32[]{:S(2)}, u32[]{:S(2)}) async-start(f32[32,8,512]{2,1,0:T(8,128)} %broadcast_in_dim.14), calls=%async_computation.4 | async-start | bytes 1048576 | tf_op jit(solution)/shard_map/all_to_all | solution.py:267
Sparse Core Ops, SparseCore 0:
  47.3 71.8 reduce-scatter.1
  121.8 71.1 all-gather.1

commit v2 on v1

v2 whole, which is shorter than its diff:
```python
import jax
import jax.numpy as jnp
from jax import lax
from jax.experimental import pallas as pl
from jax.experimental.pallas import tpu as pltpu
from jax.sharding import PartitionSpec as P

NODES = 1024
FEATS = 64
PEERS = 32
SLOTS = 128
HUBS_OWN = 16
HUBS = 512
ROWS = 80
LAYERS = 16
OWN = 64
OUTS = 1024
BF16 = jnp.bfloat16
F32 = jnp.float32
NT = (((1,), (1,)), ((), ()))
NN = (((1,), (0,)), ((), ()))
MIB = 1 << 20


def params():
    return pltpu.CompilerParams(vmem_limit_bytes=48 * MIB)


def cost(flops, moved):
    return pl.CostEstimate(flops=flops, bytes_accessed=moved, transcendentals=0)


def whole(shape):
    return pl.BlockSpec(shape, lambda *_: (0,) * len(shape))


def one_hot(mask):
    return jnp.where(mask, 1.0, 0.0).astype(BF16)


def matmul(a, b, dims):
    return lax.dot_general(a, b, dims, preferred_element_type=F32)


def pair_lanes(ref, pair):
    return jnp.concatenate([ref[2 * pair : 2 * pair + 1, :], ref[2 * pair + 1 : 2 * pair + 2, :]], axis=1)


def gather_kernel(x_ref, send_ref, hub_ref, out_ref):
    x = x_ref[...]
    node = lax.broadcasted_iota(jnp.int32, (NODES, 2 * SLOTS), 0)
    hub_node = lax.broadcasted_iota(jnp.int32, (NODES, HUBS_OWN), 0)
    hub_feats = matmul(x, one_hot(hub_node == hub_ref[...]), NN)
    hub_rows = hub_feats.T
    hub_block = jnp.concatenate([hub_rows, jnp.zeros_like(hub_rows)], axis=1).astype(BF16)
    for pair in range(PEERS // 2):
        picked = matmul(x, one_hot(node == pair_lanes(send_ref, pair)), NN).astype(BF16)
        out_ref[2 * pair, :FEATS, :] = picked[:, :SLOTS]
        out_ref[2 * pair + 1, :FEATS, :] = picked[:, SLOTS:]
        out_ref[2 * pair, FEATS:, :] = hub_block
        out_ref[2 * pair + 1, FEATS:, :] = hub_block


def gather_slots(feats, send_lanes, hub_own):
    return pl.pallas_call(
        gather_kernel,
        out_shape=jax.ShapeDtypeStruct((PEERS, ROWS, SLOTS), BF16),
        compiler_params=params(),
        cost_estimate=cost(2 * 256 * 4096 * 1024, 1 << 20),
        name="gather_slots",
    )(feats, send_lanes, hub_own)


BUILD = 128


def build_kernel(loc_ref, recv_ref, hub_ref, local_ref, slot_ref, hubs_ref, degree_ref):
    first = pl.program_id(0) * BUILD
    node = lax.broadcasted_iota(jnp.int32, (BUILD, 2 * SLOTS), 0) + first
    for pair in range(PEERS // 2):
        slot_ref[:, 2 * SLOTS * pair : 2 * SLOTS * (pair + 1)] = one_hot(
            node == pair_lanes(recv_ref, pair)
        )
    lane = lax.broadcasted_iota(jnp.int32, (BUILD, NODES), 1)
    counts = jnp.zeros((BUILD, NODES), F32)
    for k in range(loc_ref.shape[1]):
        counts = counts + jnp.where(lane == loc_ref[:, k : k + 1], 1.0, 0.0)
    local_ref[...] = counts.astype(BF16)
    hub_lane = lax.broadcasted_iota(jnp.int32, (BUILD, HUBS), 1)
    hub_counts = jnp.zeros((BUILD, HUBS), F32)
    for k in range(hub_ref.shape[1]):
        hub_counts = hub_counts + jnp.where(hub_lane == hub_ref[:, k : k + 1], 1.0, 0.0)
    hubs_ref[...] = hub_counts.astype(BF16)
    arrivals = matmul(jnp.ones((8, PEERS * SLOTS), BF16), slot_ref[...], NT)
    degree_ref[...] = arrivals + float(loc_ref.shape[1] + hub_ref.shape[1])


def build_counts(loc_nbr, recv_lanes, hub_nbr):
    return pl.pallas_call(
        build_kernel,
        grid=(NODES // BUILD,),
        in_specs=[
            pl.BlockSpec((BUILD, loc_nbr.shape[1]), lambda i: (i, 0)),
            whole((PEERS, SLOTS)),
            pl.BlockSpec((BUILD, hub_nbr.shape[1]), lambda i: (i, 0)),
        ],
        out_specs=[
            pl.BlockSpec((BUILD, NODES), lambda i: (i, 0)),
            pl.BlockSpec((BUILD, PEERS * SLOTS), lambda i: (i, 0)),
            pl.BlockSpec((BUILD, HUBS), lambda i: (i, 0)),
            pl.BlockSpec((8, BUILD), lambda i: (0, i)),
        ],
        out_shape=[
            jax.ShapeDtypeStruct((NODES, NODES), BF16),
            jax.ShapeDtypeStruct((NODES, PEERS * SLOTS), BF16),
            jax.ShapeDtypeStruct((NODES, HUBS), BF16),
            jax.ShapeDtypeStruct((8, NODES), F32),
        ],
        compiler_params=params(),
        cost_estimate=cost(1 << 30, 24 << 20),
        name="build_counts",
    )(loc_nbr, recv_lanes, hub_nbr)


AGG = 256


def fold_halves(block):
    return jnp.concatenate([block[: OWN // 2, :], block[OWN // 2 :, :]], axis=1)


def aggregate_kernel(
    x_ref, inc_ref, local_ref, slot_ref, hubs_ref, degree_ref, x_tile_ref, cot_ref, out_ref, slots, table
):
    @pl.when(pl.program_id(0) == 0)
    def _():
        for peer in range(PEERS):
            slots[:, SLOTS * peer : SLOTS * (peer + 1)] = inc_ref[peer, :FEATS, :]
        rows = inc_ref[:, FEATS:, :].astype(F32).reshape(HUBS, SLOTS)
        table[...] = rows.T[:FEATS, :].astype(BF16)

    total = (
        matmul(x_ref[...], local_ref[...], NT)
        + matmul(slots[...], slot_ref[...], NT)
        + matmul(table[...], hubs_ref[...], NT)
    )
    mean = (total / degree_ref[0:1, :]).T
    nodes = jnp.concatenate([x_tile_ref[...].astype(F32).T, mean], axis=1).astype(BF16)
    slopes = cot_ref[...].astype(F32).T
    for layer in range(AGG // OWN):
        out_ref[layer, :OWN, :] = nodes[OWN * layer : OWN * (layer + 1), :]
        out_ref[layer, OWN:, :] = fold_halves(slopes[OWN * layer : OWN * (layer + 1), :]).astype(BF16)


def aggregate(feats, incoming, local, slot, hubs, degree, cotangent):
    return pl.pallas_call(
        aggregate_kernel,
        grid=(NODES // AGG,),
        in_specs=[
            whole((FEATS, NODES)),
            whole((PEERS, ROWS, SLOTS)),
            pl.BlockSpec((AGG, NODES), lambda i: (i, 0)),
            pl.BlockSpec((AGG, PEERS * SLOTS), lambda i: (i, 0)),
            pl.BlockSpec((AGG, HUBS), lambda i: (i, 0)),
            pl.BlockSpec((8, AGG), lambda i: (0, i)),
            pl.BlockSpec((FEATS, AGG), lambda i: (0, i)),
            pl.BlockSpec((FEATS, AGG), lambda i: (0, i)),
        ],
        out_specs=pl.BlockSpec((AGG // OWN, 96, SLOTS), lambda i: (i, 0, 0)),
        out_shape=jax.ShapeDtypeStruct((LAYERS, 96, SLOTS), BF16),
        scratch_shapes=[pltpu.VMEM((FEATS, PEERS * SLOTS), BF16), pltpu.VMEM((FEATS, HUBS), BF16)],
        compiler_params=params(),
        cost_estimate=cost(2 * 256 * 5632 * 1024, 12 << 20),
        name="aggregate",
    )(feats, incoming, local, slot, hubs, degree, feats, cotangent)


PIECE = 16
TILE = 256


def regroup_kernel(inc_ref, out_ref):
    group = lax.broadcasted_iota(jnp.int32, (OWN, SLOTS), 1) // PIECE
    for half in range(2):
        blocks = [inc_ref[8 * half + i, :OWN, :].astype(F32) for i in range(8)]
        for slice_of in range(8):
            tile = jnp.zeros((OWN, SLOTS), F32)
            for i in range(8):
                moved = blocks[i]
                if i != slice_of:
                    moved = pltpu.roll(moved, (PIECE * (i - slice_of)) % SLOTS, 1)
                tile = jnp.where(group == i, moved, tile)
            tile = tile.astype(BF16)
            for outs in range(4):
                out_ref[4 * slice_of + outs, :, SLOTS * half : SLOTS * (half + 1)] = tile


def regroup(node_block):
    return pl.pallas_call(
        regroup_kernel,
        out_shape=jax.ShapeDtypeStruct((PEERS, OWN, TILE), BF16),
        compiler_params=params(),
        cost_estimate=cost(1 << 24, 2 << 20),
        name="regroup",
    )(node_block)


def forward_kernel(inc_ref, weights_ref, slopes_ref, hidden_ref, flat_ref):
    joined = jnp.concatenate([inc_ref[layer, :OWN, :] for layer in range(LAYERS)], axis=1)
    preact = matmul(joined, weights_ref[...], NN)
    sigmoid_part = jax.nn.sigmoid(preact)
    hidden = preact * sigmoid_part
    slope = sigmoid_part * (1.0 + preact * (1.0 - sigmoid_part))
    half = OWN // 2
    for pair in range(LAYERS // 2):
        even = inc_ref[2 * pair, OWN:, :].astype(F32)
        odd = inc_ref[2 * pair + 1, OWN:, :].astype(F32)
        top = jnp.concatenate([even[:, :FEATS], odd[:, :FEATS]], axis=1)
        bottom = jnp.concatenate([even[:, FEATS:], odd[:, FEATS:]], axis=1)
        lanes = slice(SLOTS * pair, SLOTS * (pair + 1))
        slopes = (jnp.concatenate([top, bottom], axis=0) * slope[:, lanes]).astype(BF16)
        flat_ref[:, lanes] = slopes
        for slice_of in range(8):
            column = SLOTS * (pair % 2)
            slopes_ref[4 * slice_of + pair // 2, :, column : column + SLOTS] = slopes
        tile = hidden[:, lanes]
        hidden_ref[2 * pair] = fold_halves(tile[:, :FEATS]).astype(BF16)
        hidden_ref[2 * pair + 1] = fold_halves(tile[:, FEATS:]).astype(BF16)


def forward(node_block, weights):
    return pl.pallas_call(
        forward_kernel,
        out_shape=[
            jax.ShapeDtypeStruct((PEERS, OWN, TILE), BF16),
            jax.ShapeDtypeStruct((LAYERS, OWN // 2, SLOTS), BF16),
            jax.ShapeDtypeStruct((OWN, OUTS), BF16),
        ],
        compiler_params=params(),
        cost_estimate=cost(2 * 256 * 2048 * 1024, 6 << 20),
        name="forward",
    )(node_block, weights)


def backward_kernel(slopes_ref, weights_ref, degree_ref, out_ref):
    back = matmul(slopes_ref[...], weights_ref[...], NT)
    direct = lax.broadcasted_iota(jnp.int32, (OWN, SLOTS), 1) < FEATS
    divisor = jnp.where(direct, 1.0, degree_ref[...])
    for layer in range(LAYERS):
        out_ref[layer] = (back[:, SLOTS * layer : SLOTS * (layer + 1)] / divisor).astype(BF16)


def backward(slopes, weights, own_degree):
    return pl.pallas_call(
        backward_kernel,
        out_shape=jax.ShapeDtypeStruct((LAYERS, OWN, SLOTS), BF16),
        compiler_params=params(),
        cost_estimate=cost(2 * 256 * 2048 * 1024, 6 << 20),
        name="backward",
    )(slopes, weights, own_degree)


def weight_kernel(joined_ref, slopes_ref, back_ref, hidden_ref, out_ref):
    part = matmul(joined_ref[...], slopes_ref[...], NN).astype(BF16)
    for layer in range(LAYERS):
        out_ref[layer, :OWN, :] = back_ref[layer]
        out_ref[layer, OWN:96, :] = hidden_ref[layer]
        out_ref[layer, 96:112, :] = part[PIECE * layer : PIECE * (layer + 1), :SLOTS]
        out_ref[layer, 112:, :] = part[PIECE * layer : PIECE * (layer + 1), SLOTS:]


def weight_parts(joined_cols, slopes_rows, back, hidden):
    return pl.pallas_call(
        weight_kernel,
        out_shape=jax.ShapeDtypeStruct((LAYERS, SLOTS, SLOTS), BF16),
        compiler_params=params(),
        cost_estimate=cost(2 * 256 * 2048 * 256, 3 << 20),
        name="weight_parts",
    )(joined_cols, slopes_rows, back, hidden)


RETURN_ROWS = 112


def return_kernel(back_ref, slot_ref, hubs_ref, out_ref, share, sums):
    @pl.when(pl.program_id(0) == 0)
    def _():
        rows = back_ref[:, :OWN, :].astype(F32).reshape(NODES, SLOTS)
        share[...] = rows.T[FEATS:, :].astype(BF16)
        sums[...] = jnp.sum(back_ref[:, 96:, :].astype(F32), axis=0).astype(BF16)

    values = matmul(share[...], slot_ref[...], NN).astype(BF16)
    for peer in range(8):
        out_ref[peer, :FEATS, :] = values[:, SLOTS * peer : SLOTS * (peer + 1)]
        out_ref[peer, ROWS:, :] = sums[...]
    terms = matmul(share[...], hubs_ref[...], NN).T
    high = terms.astype(BF16).astype(F32)
    both = jnp.concatenate([high, terms - high], axis=1)
    out_ref[:, FEATS:ROWS, :] = both.reshape(8, HUBS_OWN, SLOTS).astype(BF16)


def return_slots(back_block, slot, hubs):
    return pl.pallas_call(
        return_kernel,
        grid=(PEERS // 8,),
        in_specs=[
            whole((LAYERS, SLOTS, SLOTS)),
            pl.BlockSpec((NODES, 8 * SLOTS), lambda i: (0, i)),
            pl.BlockSpec((NODES, 8 * HUBS_OWN), lambda i: (0, i)),
        ],
        out_specs=pl.BlockSpec((8, RETURN_ROWS, SLOTS), lambda i: (i, 0, 0)),
        out_shape=jax.ShapeDtypeStruct((PEERS, RETURN_ROWS, SLOTS), BF16),
        scratch_shapes=[pltpu.VMEM((FEATS, NODES), BF16), pltpu.VMEM((32, SLOTS), BF16)],
        compiler_params=params(),
        cost_estimate=cost(2 * 256 * 4608 * 1024, 10 << 20),
        name="return_slots",
    )(back_block, slot, hubs)


def local_kernel(back_ref, local_ref, base_ref, hidden_ref):
    columns = back_ref[:, :OWN, :].astype(F32).reshape(NODES, SLOTS).T
    share = columns[FEATS:, :].astype(BF16)
    base_ref[...] = columns[:FEATS, :] + matmul(share, local_ref[...], NN)
    folded = back_ref[:, OWN:96, :].astype(F32)
    rows = jnp.concatenate([folded[:, :, :FEATS], folded[:, :, FEATS:]], axis=1)
    hidden_ref[...] = rows.reshape(NODES, FEATS).T.astype(BF16)


def local_grads(back_block, local):
    return pl.pallas_call(
        local_kernel,
        out_shape=[
            jax.ShapeDtypeStruct((FEATS, NODES), F32),
            jax.ShapeDtypeStruct((FEATS, NODES), BF16),
        ],
        compiler_params=params(),
        cost_estimate=cost(2 * 256 * 1024 * 1024, 3 << 20),
        name="local_grads",
    )(back_block, local)


SPREAD = 256


def spread_kernel(back_ref, send_ref, hub_ref, base_ref, out_ref, self_ref, neigh_ref, slots, hub_total):
    @pl.when(pl.program_id(0) == 0)
    def _():
        for peer in range(PEERS):
            slots[:, SLOTS * peer : SLOTS * (peer + 1)] = back_ref[peer, :FEATS, :]
            grads = back_ref[peer, ROWS:, :].astype(F32)
            slice_of, outs = peer // 4, peer % 4
            weight_ref = self_ref if slice_of < 4 else neigh_ref
            row = PIECE * (slice_of % 4)
            weight_ref[row : row + PIECE, TILE * outs : TILE * outs + SLOTS] = grads[:PIECE, :]
            weight_ref[row : row + PIECE, TILE * outs + SLOTS : TILE * (outs + 1)] = grads[PIECE:, :]
        sums = jnp.sum(back_ref[:, FEATS:ROWS, :].astype(F32), axis=0)
        total = sums[:, :FEATS] + sums[:, FEATS:]
        high = total.astype(BF16).astype(F32)
        stacked = jnp.concatenate(
            [high, total - high, jnp.zeros((SLOTS - 2 * HUBS_OWN, FEATS), F32)], axis=0
        )
        hub_total[...] = stacked.T.astype(BF16)

    first = pl.program_id(0) * SPREAD
    node = lax.broadcasted_iota(jnp.int32, (SPREAD, 2 * SLOTS), 0) + first
    grad = base_ref[...]
    for pair in range(PEERS // 2):
        grad = grad + matmul(
            slots[:, 2 * SLOTS * pair : 2 * SLOTS * (pair + 1)],
            one_hot(node == pair_lanes(send_ref, pair)),
            NT,
        )
    hub_node = lax.broadcasted_iota(jnp.int32, (SPREAD, SLOTS), 0) + first
    grad = grad + matmul(hub_total[...], one_hot(hub_node == hub_ref[...]), NT)
    out_ref[...] = grad.astype(BF16)


def spread_grads(returned, send_lanes, hub_lanes, base):
    return pl.pallas_call(
        spread_kernel,
        grid=(NODES // SPREAD,),
        in_specs=[
            whole((PEERS, RETURN_ROWS, SLOTS)),
            whole((PEERS, SLOTS)),
            whole((1, SLOTS)),
            pl.BlockSpec((FEATS, SPREAD), lambda i: (0, i)),
        ],
        out_specs=[
            pl.BlockSpec((FEATS, SPREAD), lambda i: (0, i)),
            whole((FEATS, OUTS)),
            whole((FEATS, OUTS)),
        ],
        out_shape=[
            jax.ShapeDtypeStruct((FEATS, NODES), BF16),
            jax.ShapeDtypeStruct((FEATS, OUTS), F32),
            jax.ShapeDtypeStruct((FEATS, OUTS), F32),
        ],
        scratch_shapes=[pltpu.VMEM((FEATS, PEERS * SLOTS), BF16), pltpu.VMEM((FEATS, SLOTS), BF16)],
        compiler_params=params(),
        cost_estimate=cost(2 * 256 * 4224 * 1024, 2 << 20),
        name="spread_grads",
    )(returned, send_lanes, hub_lanes, base)


def exchange(blocks, axis):
    return lax.all_to_all(blocks, axis, 0, 0, tiled=True)


def per_device(feats, w_self, w_neigh, cotangent, loc_nbr, send_rows, recv_node, hub_rows, hub_nbr):
    send_lanes = send_rows.reshape(PEERS, SLOTS)
    recv_lanes = recv_node.reshape(PEERS, SLOTS)
    hub_lanes = jnp.concatenate(
        [hub_rows, hub_rows, jnp.full((SLOTS - 2 * HUBS_OWN,), -1, jnp.int32)]
    )[None, :]
    weights = lax.all_gather(jnp.concatenate([w_self, w_neigh], axis=0), "col", axis=0, tiled=True)
    incoming = exchange(gather_slots(feats, send_lanes, hub_rows[None, :]), "row")
    local, slot, hubs, degree = build_counts(loc_nbr, recv_lanes, hub_nbr)
    node_block = exchange(
        aggregate(feats, incoming, local, slot, hubs, degree, cotangent), "col"
    )
    own_degree = lax.dynamic_slice_in_dim(degree[0], OWN * lax.axis_index("col"), OWN)[:, None]
    joined_cols = exchange(regroup(node_block), "row").reshape(PEERS * OWN, TILE).T
    slopes_out, hidden, slopes = forward(node_block, weights)
    slopes_rows = exchange(slopes_out, "row").reshape(PEERS * OWN, TILE)
    back = backward(slopes, weights, own_degree)
    back_block = exchange(weight_parts(joined_cols, slopes_rows, back, hidden), "col")
    returned = exchange(return_slots(back_block, slot, hubs), "row")
    base, hidden_out = local_grads(back_block, local)
    grad_feats, grad_self, grad_neigh = spread_grads(returned, send_lanes, hub_lanes, base)
    return (hidden_out, grad_feats, grad_self, grad_neigh)


def solution(mesh):
    return jax.shard_map(
        per_device,
        mesh=mesh,
        in_specs=(
            P("col", "row"),
            P("col", None),
            P("col", None),
            P("col", "row"),
            P("row", None),
            P("row", None, None),
            P("row", None, None),
            P("row"),
            P("row", None),
        ),
        out_specs=(P("col", "row"), P("col", "row"), P("col", None), P("col", None)),
        check_vma=False,
    )
```

time: 270 us -> 219 us (0.81)
  waiting for transfers between devices: 164 us -> 34.7 us
  blocking collectives: 0 us -> 65.5 us
  matrix products: 10.5 us -> 0 us
  local copies, waits for them, and re-layouts: 11.6 us -> 21.6 us
  Pallas kernels: 26.8 us -> 34.1 us
  starting transfers between devices: 38.1 us -> 45 us
    reduce_scatter x1 -> x0, waiting for transfers between devices: 71.9 us -> none  [per_device(): lax.psum_scatter(partial_product, 'col', scatter_dimension=0, tiled=True)]
    all_to_all x0 -> x2, blocking collectives: none -> 65.5 us  [exchange(): return lax.all_to_all(blocks, axis, 0, 0, tiled=True)]
    all_gather x1, waiting for transfers between devices: 72 us -> 7.94 us  [per_device(): lax.all_gather(jnp.concatenate([w_self, w_neigh], axis=0), 'col', axis=0,...]
    unnamed x25 -> x52, local copies, waits for them, and re-layouts: 7.43 us -> 18.4 us
    dot_general x4 -> x0, matrix products: 10.5 us -> none  [the longest x3 6.79 us: matmul(): return lax.dot_general(a, b, dims, preferred_element_type=F32)]
    all_to_all x4, starting transfers between devices: 38 us -> 45 us  [exchange(): return lax.all_to_all(blocks, axis, 0, 0, tiled=True)]
    all_to_all x4, waiting for transfers between devices: 20.2 us -> 26.7 us  [exchange(): return lax.all_to_all(blocks, axis, 0, 0, tiled=True)]
    pallas_call x1 -> x6, Pallas kernels: 5.51 us -> 12 us  [the longest x1 6.43 us: return_slots(): pl.pallas_call(return_kernel, grid=(PEERS // 8,), in_specs=[whole((LAYERS...]
  transfers between devices with their start and end apart: 6 -> 5, of which waited for: 5 -> 5; matrix products, arithmetic and copies ran while one was open for 3% -> 3% of each run, Pallas kernels for 7% -> 11%
where the time goes in v2:
time: 219 us; the launch traced here: 218 us
  blocking collectives  65.5 us (30%)
  starting transfers between devices  45 us (21%)
  waiting for transfers between devices  34.7 us (16%)
  Pallas kernels  34.1 us (16%)
  local copies, waits for them, and re-layouts  21.6 us (10%)
  between operations  14.2 us (6%)
  other arithmetic  3.01 us (1%)
    all_to_all x2, blocking collectives, exchange(): return lax.all_to_all(blocks, axis, 0, 0, tiled=True)  65.5 us
    all_to_all x4, starting transfers between devices, exchange(): return lax.all_to_all(blocks, axis, 0, 0, tiled=True)  45 us
    all_to_all x4, waiting for transfers between devices, exchange(): return lax.all_to_all(blocks, axis, 0, 0, tiled=True)  26.7 us
    unnamed x52, local copies, waits for them, and re-layouts  18.4 us
    pallas_call x1, Pallas kernels, build_counts(): pl.pallas_call(build_kernel, grid=(NODES // BUILD,), in_specs=[pl.BlockSp...  8.12 us
    all_gather x1, waiting for transfers between devices, per_device(): lax.all_gather(jnp.concatenate([w_self, w_neigh], axis=0), 'col', axis=0,...  7.94 us
    pallas_call x1, Pallas kernels, aggregate(): pl.pallas_call(aggregate_kernel, grid=(NODES // AGG,), in_specs=[whole((F...  7.47 us
    pallas_call x1, Pallas kernels, return_slots(): pl.pallas_call(return_kernel, grid=(PEERS // 8,), in_specs=[whole((LAYERS...  6.43 us
  transfers between devices with their start and end apart: 5, of which 5 were waited for; matrix products, arithmetic and copies ran while one was open for 3% of the time, Pallas kernels for 11%

profile of v2, /device:TPU:1, one launch (start us, length us, event | category | flops | bytes accessed | tf_op | source)
XLA Modules:
  0.0 218.1 jit_solution(3262441203124643494)
XLA Ops:
  7.2 1.7 pad_maximum_fusion
  11.2 2.5 %gather_slots.1 = bf16[32,80,128]{2,1,0:T(8,128)(2,1)} custom-call(bf16[64,1024]{1,0:T(8,128)(2,1)S(1)} %copy-done.6, s32[32,128]{1,0:T(8,128)S(1)} %bitcast.13, s32[1,16]{1,0:T(1,128)S(1)} %bitcast.15), custom_call_target="tpu_custom_call" | custom-call | flops 2147483648 | bytes 1048576 | tf_op jit(solution)/shard_map/gather_slots/pallas_call | solution.py:65
  13.7 11.2 %all-to-all-start = ((bf16[32,80,128]{2,1,0:T(8,128)(2,1)}), bf16[32,80,128]{2,1,0:T(8,128)(2,1)}, u32[]{:S(2)}, u32[]{:S(2)}) async-start(bf16[32,80,128]{2,1,0:T(8,128)(2,1)} %gather_slots.1), calls=%async_computation | async-start | bytes 1310720 | tf_op jit(solution)/shard_map/all_to_all | solution.py:406
  24.9 1.0 copy.17.loc_ref
  26.0 1.0 copy.18.hub_ref
  27.0 1.0 copy-done.8
  28.0 1.0 copy-done.9
  29.1 8.1 %build_counts.1 = (bf16[1024,1024]{1,0:T(8,128)(2,1)S(1)}, bf16[1024,4096]{1,0:T(8,128)(2,1)}, bf16[1024,512]{1,0:T(8,128)(2,1)S(1)}, f32[8,1024]{1,0:T(8,128)S(1)}) custom-call(s32[1024,8]{1,0:T(8,128)S(1)} %copy-done.8, s32[32,128]{1,0:T(8,128)S(1)} %bitcast.12, s32[1024,2]{1,0:T(8,128)S(1)} %copy-done.9), custom_call_target="tpu_custom_call" | custom-call | flops 1073741824 | bytes 25165824 | tf_op jit(solution)/shard_map/build_counts/pallas_call | solution.py:99
  38.0 7.5 %aggregate.1 = bf16[16,96,128]{2,1,0:T(8,128)(2,1)S(1)} custom-call(bf16[64,1024]{1,0:T(8,128)(2,1)S(1)} %copy-done.7, bf16[32,80,128]{2,1,0:T(8,128)(2,1)} %all-to-all-done.inc_ref, bf16[1024,1024]{1,0:T(8,128)(2,1)S(1)} %get-tuple-element.16.local_ref, bf16[1024,4096]{1,0:T(8,128)(2,1)} %get-tuple-element.17.slot_ref, ...), custom_call_target="tpu_custom_call" | custom-call | flops 2952790016 | bytes 12582912 | tf_op jit(solution)/shard_map/aggregate/pallas_call | solution.py:156
  45.5 36.4 %all_to_all.30.inc_ref = bf16[16,96,128]{2,1,0:T(8,128)(2,1)S(1)} all-to-all(bf16[16,96,128]{2,1,0:T(8,128)(2,1)S(1)} %aggregate.1), channel_id=1, replica_groups=mesh['row'=32,'col'=16] {'col'}, dimensions={0} | all-to-all | bytes 786432 | tf_op jit(solution)/shard_map/all_to_all | solution.py:406
  81.8 1.5 regroup.1
  83.4 11.7 %all-to-all-start.2 = ((bf16[32,64,256]{2,1,0:T(8,128)(2,1)}), bf16[32,64,256]{2,1,0:T(8,128)(2,1)}, u32[]{:S(2)}, u32[]{:S(2)}) async-start(bf16[32,64,256]{2,1,0:T(8,128)(2,1)} %regroup.1), calls=%async_computation.2 | async-start | bytes 2097152 | tf_op jit(solution)/shard_map/all_to_all | solution.py:406
  95.1 7.9 %all-gather.2.cloned.1.call-done.weights_ref = bf16[2048,1024]{1,0:T(8,128)(2,1)} async-done(((bf16[128,1024]{1,0:T(8,128)(2,1)}), bf16[2048,1024]{1,0:T(8,128)(2,1)}) %all-gather.2.cloned.1.call-update) | async-done | bytes 4194320 | tf_op jit(solution)/shard_map/all_gather | solution.py:415
  103.0 2.2 %copy-done = bf16[2048,1024]{1,0:T(8,128)(2,1)S(1)} copy-done((bf16[2048,1024]{1,0:T(8,128)(2,1)S(1)}, bf16[2048,1024]{1,0:T(8,128)(2,1)}, u32[]{:S(2)}) %copy-start) | copy-done | bytes 4194328
  105.2 1.1 forward.1
  106.3 1.0 copy-done.5
  108.6 3.7 %all-to-all-done.2 = bf16[32,64,256]{2,1,0:T(8,128)(2,1)} async-done(((bf16[32,64,256]{2,1,0:T(8,128)(2,1)}), bf16[32,64,256]{2,1,0:T(8,128)(2,1)}, u32[]{:S(2)}, u32[]{:S(2)}) %all-to-all-start.2) | async-done | bytes 1048608 | tf_op jit(solution)/shard_map/all_to_all | solution.py:406
  112.3 11.2 %all-to-all-start.3 = ((bf16[32,64,256]{2,1,0:T(8,128)(2,1)}), bf16[32,64,256]{2,1,0:T(8,128)(2,1)S(1)}, u32[]{:S(2)}, u32[]{:S(2)}) async-start(bf16[32,64,256]{2,1,0:T(8,128)(2,1)} %copy-done.5), calls=%async_computation.3 | async-start | bytes 2097152 | tf_op jit(solution)/shard_map/all_to_all | solution.py:406
  124.5 2.3 %copy.19 = bf16[2048,256]{0,1:T(8,128)(2,1)} copy(bf16[2048,256]{1,0:T(8,128)(2,1)} %bitcast.3) | data formatting | bytes 2097152 | tf_op jit(solution)/shard_map/reshape | solution.py:422
  126.7 2.2 %copy-done.1 = bf16[2048,1024]{1,0:T(8,128)(2,1)S(1)} copy-done((bf16[2048,1024]{1,0:T(8,128)(2,1)S(1)}, bf16[2048,1024]{1,0:T(8,128)(2,1)}, u32[]{:S(2)}) %copy-start.1) | copy-done | bytes 4194328
  128.9 0.9 copy-done.14
  129.8 1.4 backward.1.back_ref
  131.2 9.5 %all-to-all-done.3 = bf16[32,64,256]{2,1,0:T(8,128)(2,1)S(1)} async-done(((bf16[32,64,256]{2,1,0:T(8,128)(2,1)}), bf16[32,64,256]{2,1,0:T(8,128)(2,1)S(1)}, u32[]{:S(2)}, u32[]{:S(2)}) %all-to-all-start.3) | async-done | bytes 1048608 | tf_op jit(solution)/shard_map/all_to_all | solution.py:406
  140.7 1.2 copy-done.2
  143.3 29.2 %all_to_all.31.back_ref = bf16[16,128,128]{2,1,0:T(8,128)(2,1)S(1)} all-to-all(bf16[16,128,128]{2,1,0:T(8,128)(2,1)S(1)} %weight_parts.1), channel_id=1, replica_groups=mesh['row'=32,'col'=16] {'col'}, dimensions={0} | all-to-all | bytes 1048576 | tf_op jit(solution)/shard_map/all_to_all | solution.py:406
  172.4 6.4 %return_slots.1 = bf16[32,112,128]{2,1,0:T(8,128)(2,1)} custom-call(bf16[16,128,128]{2,1,0:T(8,128)(2,1)S(1)} %all_to_all.31.back_ref, bf16[1024,4096]{1,0:T(8,128)(2,1)} %get-tuple-element.17.slot_ref, bf16[1024,512]{1,0:T(8,128)(2,1)S(1)} %copy-done.4), custom_call_target="tpu_custom_call" | custom-call | flops 2415919104 | bytes 10485760 | tf_op jit(solution)/shard_map/return_slots/pallas_call | solution.py:303
  178.9 10.9 %all-to-all-start.5 = ((bf16[32,112,128]{2,1,0:T(8,128)(2,1)}), bf16[32,112,128]{2,1,0:T(8,128)(2,1)S(1)}, u32[]{:S(2)}, u32[]{:S(2)}) async-start(bf16[32,112,128]{2,1,0:T(8,128)(2,1)} %return_slots.1), calls=%async_computation.5 | async-start | bytes 1835008 | tf_op jit(solution)/shard_map/all_to_all | solution.py:406
  189.8 1.3 add_bitcast_fusion.hub_ref
  191.1 1.1 local_grads.1
  192.9 12.7 %all-to-all-done.5.back_ref = bf16[32,112,128]{2,1,0:T(8,128)(2,1)S(1)} async-done(((bf16[32,112,128]{2,1,0:T(8,128)(2,1)}), bf16[32,112,128]{2,1,0:T(8,128)(2,1)S(1)}, u32[]{:S(2)}, u32[]{:S(2)}) %all-to-all-start.5) | async-done | bytes 917536 | tf_op jit(solution)/shard_map/all_to_all | solution.py:406
  205.6 0.9 copy-done.17
  207.2 4.0 %spread_grads.1 = (bf16[64,1024]{1,0:T(8,128)(2,1)}, f32[64,1024]{1,0:T(8,128)}, f32[64,1024]{1,0:T(8,128)}) custom-call(bf16[32,112,128]{2,1,0:T(8,128)(2,1)S(1)} %all-to-all-done.5.back_ref, s32[32,128]{1,0:T(8,128)S(1)} %bitcast.14, s32[1,128]{1,0:T(1,128)S(1)} %copy-done.22, f32[64,1024]{1,0:T(8,128)S(1)} %copy-done.17), custom_call_target="tpu_custom_call" | custom-call | flops 2214592512 | bytes 2097152 | tf_op jit(solution)/shard_map/spread_grads/pallas_call | solution.py:379
  (50 shorter events, 8.1 us)
Async XLA Ops:
  7.2 95.9 %all-gather.2.cloned.1.call-start = ((), (), s32[]{:S(2)}) async-start(), calls=%async_computation.6 | async-start | bytes 4456448 | tf_op jit(solution)/shard_map/all_gather | solution.py:415
  8.9 0.9 copy-start.6
  9.8 0.7 copy-start.19
  10.5 0.7 copy-start.21
  11.2 13.7 %copy-start.23 = (s32[1024,8]{0,1:T(8,128)S(1)}, s32[1024,8]{0,1:T(8,128)}, u32[]{:S(2)}) copy-start(s32[1024,8]{0,1:T(8,128)} %param.13) | copy-start | bytes 98308
  11.2 14.7 %copy-start.24 = (s32[1024,2]{0,1:T(2,128)S(1)}, s32[1024,2]{0,1:T(2,128)}, u32[]{:S(2)}) copy-start(s32[1024,2]{0,1:T(2,128)} %param.17) | copy-start | bytes 24580
  11.2 15.8 %copy-start.18 = (s32[1,32,128]{2,1,0:T(8,128)S(1)}, s32[1,32,128]{2,1,0:T(8,128)}, u32[]{:S(2)}) copy-start(s32[1,32,128]{2,1,0:T(8,128)} %param.15) | copy-start | bytes 49156
  13.7 24.3 %copy-start.7 = (bf16[64,1024]{1,0:T(8,128)(2,1)S(1)}, bf16[64,1024]{1,0:T(8,128)(2,1)}, u32[]{:S(2)}) copy-start(bf16[64,1024]{1,0:T(8,128)(2,1)} %x_tile_ref.1) | copy-start | bytes 393220
  13.7 24.3 %copy-start.10 = (bf16[64,1024]{1,0:T(8,128)(2,1)S(1)}, bf16[64,1024]{1,0:T(8,128)(2,1)}, u32[]{:S(2)}) copy-start(bf16[64,1024]{1,0:T(8,128)(2,1)} %cot_ref.1) | copy-start | bytes 393220
  13.7 24.3 %all-to-all-start = ((bf16[32,80,128]{2,1,0:T(8,128)(2,1)}), bf16[32,80,128]{2,1,0:T(8,128)(2,1)}, u32[]{:S(2)}, u32[]{:S(2)}) async-start(bf16[32,80,128]{2,1,0:T(8,128)(2,1)} %gather_slots.1), calls=%async_computation | async-start | bytes 1310720 | tf_op jit(solution)/shard_map/all_to_all | solution.py:406
  27.0 1.0 copy-start.8
  28.0 1.0 copy-start.9
  37.2 0.8 copy-start.15
  37.2 8.3 %copy-start.3 = (bf16[1024,512]{1,0:T(8,128)(2,1)}, bf16[1024,512]{1,0:T(8,128)(2,1)S(1)}, u32[]{:S(2)}) copy-start(bf16[1024,512]{1,0:T(8,128)(2,1)S(1)} %get-tuple-element.18.hubs_ref) | copy-start | bytes 3145732
  83.4 28.9 %all-to-all-start.2 = ((bf16[32,64,256]{2,1,0:T(8,128)(2,1)}), bf16[32,64,256]{2,1,0:T(8,128)(2,1)}, u32[]{:S(2)}, u32[]{:S(2)}) async-start(bf16[32,64,256]{2,1,0:T(8,128)(2,1)} %regroup.1), calls=%async_computation.2 | async-start | bytes 2097152 | tf_op jit(solution)/shard_map/all_to_all | solution.py:406
  103.0 2.2 %copy-start = (bf16[2048,1024]{1,0:T(8,128)(2,1)S(1)}, bf16[2048,1024]{1,0:T(8,128)(2,1)}, u32[]{:S(2)}) copy-start(bf16[2048,1024]{1,0:T(8,128)(2,1)} %all-gather.2.cloned.1.call-done.weights_ref) | copy-start | bytes 12582916
  106.3 1.0 copy-start.5
  107.3 0.7 copy-start.11
  107.9 0.7 copy-start.13
  112.3 28.4 %all-to-all-start.3 = ((bf16[32,64,256]{2,1,0:T(8,128)(2,1)}), bf16[32,64,256]{2,1,0:T(8,128)(2,1)S(1)}, u32[]{:S(2)}, u32[]{:S(2)}) async-start(bf16[32,64,256]{2,1,0:T(8,128)(2,1)} %copy-done.5), calls=%async_computation.3 | async-start | bytes 2097152 | tf_op jit(solution)/shard_map/all_to_all | solution.py:406
  126.7 2.2 %copy-start.1 = (bf16[2048,1024]{1,0:T(8,128)(2,1)S(1)}, bf16[2048,1024]{1,0:T(8,128)(2,1)}, u32[]{:S(2)}) copy-start(bf16[2048,1024]{1,0:T(8,128)(2,1)} %all-gather.2.cloned.1.call-done.weights_ref) | copy-start | bytes 12582916
  128.9 0.9 copy-start.14
  140.7 1.2 copy-start.2
  141.9 0.9 copy-start.12
  142.8 29.6 %copy-start.4 = (bf16[1024,512]{1,0:T(8,128)(2,1)S(1)}, bf16[1024,512]{1,0:T(8,128)(2,1)}, u32[]{:S(2)}) copy-start(bf16[1024,512]{1,0:T(8,128)(2,1)} %copy-done.3) | copy-start | bytes 3145732
  178.9 26.8 %copy-start.20 = (s32[1,32,128]{2,1,0:T(8,128)S(1)}, s32[1,32,128]{2,1,0:T(8,128)}, u32[]{:S(2)}) copy-start(s32[1,32,128]{2,1,0:T(8,128)} %param.14) | copy-start | bytes 49156
  178.9 26.8 %all-to-all-start.5 = ((bf16[32,112,128]{2,1,0:T(8,128)(2,1)}), bf16[32,112,128]{2,1,0:T(8,128)(2,1)S(1)}, u32[]{:S(2)}, u32[]{:S(2)}) async-start(bf16[32,112,128]{2,1,0:T(8,128)(2,1)} %return_slots.1), calls=%async_computation.5 | async-start | bytes 1835008 | tf_op jit(solution)/shard_map/all_to_all | solution.py:406
  192.2 0.7 copy-start.16
  205.6 1.0 copy-start.17
  206.6 0.7 copy-start.22
Sparse Core Ops, SparseCore 0:
  10.7 92.3 all-gather.1

commit v3 on v2

v3 whole, which is shorter than its diff:
```python
import jax
import jax.numpy as jnp
from jax import lax
from jax.experimental import pallas as pl
from jax.experimental.pallas import tpu as pltpu
from jax.sharding import PartitionSpec as P

NODES = 1024
FEATS = 64
PEERS = 32
SLOTS = 128
HUBS_OWN = 16
HUBS = 512
ROWS = 80
LAYERS = 16
OWN = 64
OUTS = 1024
BF16 = jnp.bfloat16
F32 = jnp.float32
NT = (((1,), (1,)), ((), ()))
NN = (((1,), (0,)), ((), ()))
MIB = 1 << 20


def params(mib):
    return pltpu.CompilerParams(vmem_limit_bytes=mib * MIB)


def cost(flops, moved):
    return pl.CostEstimate(flops=flops, bytes_accessed=moved, transcendentals=0)


def whole(shape):
    return pl.BlockSpec(shape, lambda *_: (0,) * len(shape))


def one_hot(mask):
    return jnp.where(mask, 1.0, 0.0).astype(BF16)


def matmul(a, b, dims):
    return lax.dot_general(a, b, dims, preferred_element_type=F32)


def pair_lanes(ref, pair):
    return jnp.concatenate([ref[2 * pair : 2 * pair + 1, :], ref[2 * pair + 1 : 2 * pair + 2, :]], axis=1)


def gather_kernel(x_ref, send_ref, hub_ref, out_ref):
    x = x_ref[...]
    node = lax.broadcasted_iota(jnp.int32, (NODES, 2 * SLOTS), 0)
    hub_node = lax.broadcasted_iota(jnp.int32, (NODES, HUBS_OWN), 0)
    hub_feats = matmul(x, one_hot(hub_node == hub_ref[...]), NN)
    hub_rows = hub_feats.T
    hub_block = jnp.concatenate([hub_rows, jnp.zeros_like(hub_rows)], axis=1).astype(BF16)
    for pair in range(PEERS // 2):
        picked = matmul(x, one_hot(node == pair_lanes(send_ref, pair)), NN).astype(BF16)
        out_ref[2 * pair, :FEATS, :] = picked[:, :SLOTS]
        out_ref[2 * pair + 1, :FEATS, :] = picked[:, SLOTS:]
        out_ref[2 * pair, FEATS:, :] = hub_block
        out_ref[2 * pair + 1, FEATS:, :] = hub_block


def gather_slots(feats, send_lanes, hub_own):
    return pl.pallas_call(
        gather_kernel,
        out_shape=jax.ShapeDtypeStruct((PEERS, ROWS, SLOTS), BF16),
        compiler_params=params(8),
        cost_estimate=cost(2 * 256 * 4096 * 1024, 1 << 20),
        name="gather_slots",
    )(feats, send_lanes, hub_own)


BUILD = 128


def build_kernel(loc_ref, hub_ref, local_ref, hubs_ref):
    lane = lax.broadcasted_iota(jnp.int32, (BUILD, NODES), 1)
    counts = jnp.zeros((BUILD, NODES), F32)
    for k in range(loc_ref.shape[1]):
        counts = counts + jnp.where(lane == loc_ref[:, k : k + 1], 1.0, 0.0)
    local_ref[...] = counts.astype(BF16)
    hub_lane = lax.broadcasted_iota(jnp.int32, (BUILD, HUBS), 1)
    hub_counts = jnp.zeros((BUILD, HUBS), F32)
    for k in range(hub_ref.shape[1]):
        hub_counts = hub_counts + jnp.where(hub_lane == hub_ref[:, k : k + 1], 1.0, 0.0)
    hubs_ref[...] = hub_counts.astype(BF16)


def build_counts(loc_nbr, hub_nbr):
    return pl.pallas_call(
        build_kernel,
        grid=(NODES // BUILD,),
        in_specs=[
            pl.BlockSpec((BUILD, loc_nbr.shape[1]), lambda i: (i, 0)),
            pl.BlockSpec((BUILD, hub_nbr.shape[1]), lambda i: (i, 0)),
        ],
        out_specs=[
            pl.BlockSpec((BUILD, NODES), lambda i: (i, 0)),
            pl.BlockSpec((BUILD, HUBS), lambda i: (i, 0)),
        ],
        out_shape=[
            jax.ShapeDtypeStruct((NODES, NODES), BF16),
            jax.ShapeDtypeStruct((NODES, HUBS), BF16),
        ],
        compiler_params=params(8),
        cost_estimate=cost(1 << 30, 12 << 20),
        name="build_counts",
    )(loc_nbr, hub_nbr)


AGG = 256


def fold_halves(block):
    return jnp.concatenate([block[: OWN // 2, :], block[OWN // 2 :, :]], axis=1)


NEIGHBOURS = 10.0


def aggregate_kernel(
    x_ref, inc_ref, recv_ref, local_ref, hubs_ref, cot_ref, out_ref, degree_ref, slots, table
):
    for peer in range(PEERS):
        slots[:FEATS, SLOTS * peer : SLOTS * (peer + 1)] = inc_ref[peer, :FEATS, :]
    slots[FEATS:, :] = jnp.ones((16, PEERS * SLOTS), BF16)
    rows = inc_ref[:, FEATS:, :].astype(F32).reshape(HUBS, SLOTS)
    table[...] = rows.T[:FEATS, :].astype(BF16)
    for tile in range(NODES // AGG):
        lanes = slice(AGG * tile, AGG * (tile + 1))
        node = lax.broadcasted_iota(jnp.int32, (AGG, 2 * SLOTS), 0) + AGG * tile
        remote = jnp.zeros((ROWS, AGG), F32)
        for pair in range(PEERS // 2):
            remote = remote + matmul(
                slots[:, 2 * SLOTS * pair : 2 * SLOTS * (pair + 1)],
                one_hot(node == pair_lanes(recv_ref, pair)),
                NT,
            )
        total = (
            remote[:FEATS, :]
            + matmul(x_ref[...], local_ref[lanes, :], NT)
            + matmul(table[...], hubs_ref[lanes, :], NT)
        )
        degree = remote[FEATS : FEATS + 8, :] + NEIGHBOURS
        degree_ref[:, lanes] = degree
        mean = (total / degree[0:1, :]).T
        nodes = jnp.concatenate([x_ref[:, lanes].astype(F32).T, mean], axis=1).astype(BF16)
        slopes = cot_ref[:, lanes].astype(F32).T
        for part in range(AGG // OWN):
            layer = AGG // OWN * tile + part
            out_ref[layer, :OWN, :] = nodes[OWN * part : OWN * (part + 1), :]
            out_ref[layer, OWN:, :] = fold_halves(slopes[OWN * part : OWN * (part + 1), :]).astype(BF16)


def aggregate(feats, incoming, recv_lanes, local, hubs, cotangent):
    return pl.pallas_call(
        aggregate_kernel,
        out_shape=[
            jax.ShapeDtypeStruct((LAYERS, 96, SLOTS), BF16),
            jax.ShapeDtypeStruct((8, NODES), F32),
        ],
        scratch_shapes=[pltpu.VMEM((ROWS, PEERS * SLOTS), BF16), pltpu.VMEM((FEATS, HUBS), BF16)],
        compiler_params=params(16),
        cost_estimate=cost(2 * 256 * 5632 * 1024, 5 << 20),
        name="aggregate",
    )(feats, incoming, recv_lanes, local, hubs, cotangent)


PIECE = 16
TILE = 256


def regroup_kernel(inc_ref, out_ref):
    group = lax.broadcasted_iota(jnp.int32, (OWN, SLOTS), 1) // PIECE
    for half in range(2):
        blocks = [inc_ref[8 * half + i, :OWN, :].astype(F32) for i in range(8)]
        for slice_of in range(8):
            tile = jnp.zeros((OWN, SLOTS), F32)
            for i in range(8):
                moved = blocks[i]
                if i != slice_of:
                    moved = pltpu.roll(moved, (PIECE * (i - slice_of)) % SLOTS, 1)
                tile = jnp.where(group == i, moved, tile)
            tile = tile.astype(BF16)
            for outs in range(4):
                out_ref[4 * slice_of + outs, :, SLOTS * half : SLOTS * (half + 1)] = tile


def regroup(node_block):
    return pl.pallas_call(
        regroup_kernel,
        out_shape=jax.ShapeDtypeStruct((PEERS, OWN, TILE), BF16),
        compiler_params=params(6),
        cost_estimate=cost(1 << 24, 2 << 20),
        name="regroup",
    )(node_block)


HALF = OUTS // 2


def forward_kernel(inc_ref, own_ref, other_ref, slopes_ref, hidden_ref, flat_ref, halves):
    core = lax.axis_index("row") % 2
    joined = jnp.concatenate([inc_ref[layer, :OWN, :] for layer in range(LAYERS)], axis=1)
    halves[core] = matmul(joined, own_ref[...], NN)
    halves[1 - core] = matmul(joined, other_ref[...], NN)
    for pair in range(LAYERS // 2):
        side, start = pair // 4, SLOTS * (pair % 4)
        preact = halves[side, :, start : start + SLOTS]
        sigmoid_part = jax.nn.sigmoid(preact)
        hidden = preact * sigmoid_part
        slope = sigmoid_part * (1.0 + preact * (1.0 - sigmoid_part))
        even = inc_ref[2 * pair, OWN:, :].astype(F32)
        odd = inc_ref[2 * pair + 1, OWN:, :].astype(F32)
        top = jnp.concatenate([even[:, :FEATS], odd[:, :FEATS]], axis=1)
        bottom = jnp.concatenate([even[:, FEATS:], odd[:, FEATS:]], axis=1)
        slopes = (jnp.concatenate([top, bottom], axis=0) * slope).astype(BF16)
        flat_ref[side, :, start : start + SLOTS] = slopes
        for slice_of in range(8):
            column = SLOTS * (pair % 2)
            slopes_ref[4 * slice_of + pair // 2, :, column : column + SLOTS] = slopes
        hidden_ref[2 * pair] = fold_halves(hidden[:, :FEATS]).astype(BF16)
        hidden_ref[2 * pair + 1] = fold_halves(hidden[:, FEATS:]).astype(BF16)


def forward(node_block, own, other):
    return pl.pallas_call(
        forward_kernel,
        out_shape=[
            jax.ShapeDtypeStruct((PEERS, OWN, TILE), BF16),
            jax.ShapeDtypeStruct((LAYERS, OWN // 2, SLOTS), BF16),
            jax.ShapeDtypeStruct((2, OWN, HALF), BF16),
        ],
        scratch_shapes=[pltpu.VMEM((2, OWN, HALF), F32)],
        compiler_params=params(12),
        cost_estimate=cost(2 * 256 * 2048 * 1024, 6 << 20),
        name="forward",
    )(node_block, own, other)


def backward_kernel(slopes_ref, own_ref, other_ref, degree_ref, out_ref):
    core = lax.axis_index("row") % 2
    back = matmul(slopes_ref[core], own_ref[...], NT) + matmul(
        slopes_ref[1 - core], other_ref[...], NT
    )
    direct = lax.broadcasted_iota(jnp.int32, (OWN, SLOTS), 1) < FEATS
    divisor = jnp.where(direct, 1.0, degree_ref[...])
    for layer in range(LAYERS):
        out_ref[layer] = (back[:, SLOTS * layer : SLOTS * (layer + 1)] / divisor).astype(BF16)


def backward(slopes, own, other, own_degree):
    return pl.pallas_call(
        backward_kernel,
        out_shape=jax.ShapeDtypeStruct((LAYERS, OWN, SLOTS), BF16),
        compiler_params=params(12),
        cost_estimate=cost(2 * 256 * 2048 * 1024, 6 << 20),
        name="backward",
    )(slopes, own, other, own_degree)


def weight_kernel(joined_ref, slopes_ref, back_ref, hidden_ref, out_ref):
    part = matmul(joined_ref[...], slopes_ref[...], NN).astype(BF16)
    for layer in range(LAYERS):
        out_ref[layer, :OWN, :] = back_ref[layer]
        out_ref[layer, OWN:96, :] = hidden_ref[layer]
        out_ref[layer, 96:112, :] = part[PIECE * layer : PIECE * (layer + 1), :SLOTS]
        out_ref[layer, 112:, :] = part[PIECE * layer : PIECE * (layer + 1), SLOTS:]


def weight_parts(joined_cols, slopes_rows, back, hidden):
    return pl.pallas_call(
        weight_kernel,
        out_shape=jax.ShapeDtypeStruct((LAYERS, SLOTS, SLOTS), BF16),
        compiler_params=params(8),
        cost_estimate=cost(2 * 256 * 2048 * 256, 3 << 20),
        name="weight_parts",
    )(joined_cols, slopes_rows, back, hidden)


RETURN_ROWS = 112


def return_kernel(back_ref, recv_ref, hubs_ref, out_ref):
    rows = back_ref[:, :OWN, :].astype(F32).reshape(NODES, SLOTS)
    share = rows.T[FEATS:, :].astype(BF16)
    sums = jnp.sum(back_ref[:, 96:, :].astype(F32), axis=0).astype(BF16)
    terms = matmul(share, hubs_ref[...], NN).T
    high = terms.astype(BF16).astype(F32)
    both = jnp.concatenate([high, terms - high], axis=1)
    out_ref[:, FEATS:ROWS, :] = both.reshape(PEERS, HUBS_OWN, SLOTS).astype(BF16)
    node = lax.broadcasted_iota(jnp.int32, (NODES, 2 * SLOTS), 0)
    for pair in range(PEERS // 2):
        values = matmul(share, one_hot(node == pair_lanes(recv_ref, pair)), NN).astype(BF16)
        out_ref[2 * pair, :FEATS, :] = values[:, :SLOTS]
        out_ref[2 * pair + 1, :FEATS, :] = values[:, SLOTS:]
        out_ref[2 * pair, ROWS:, :] = sums
        out_ref[2 * pair + 1, ROWS:, :] = sums


def return_slots(back_block, recv_lanes, hubs):
    return pl.pallas_call(
        return_kernel,
        out_shape=jax.ShapeDtypeStruct((PEERS, RETURN_ROWS, SLOTS), BF16),
        compiler_params=params(12),
        cost_estimate=cost(2 * 256 * 4608 * 1024, 3 << 20),
        name="return_slots",
    )(back_block, recv_lanes, hubs)


def local_kernel(back_ref, local_ref, base_ref, hidden_ref):
    columns = back_ref[:, :OWN, :].astype(F32).reshape(NODES, SLOTS).T
    share = columns[FEATS:, :].astype(BF16)
    base_ref[...] = columns[:FEATS, :] + matmul(share, local_ref[...], NN)
    folded = back_ref[:, OWN:96, :].astype(F32)
    rows = jnp.concatenate([folded[:, :, :FEATS], folded[:, :, FEATS:]], axis=1)
    hidden_ref[...] = rows.reshape(NODES, FEATS).T.astype(BF16)


def local_grads(back_block, local):
    return pl.pallas_call(
        local_kernel,
        out_shape=[
            jax.ShapeDtypeStruct((FEATS, NODES), F32),
            jax.ShapeDtypeStruct((FEATS, NODES), BF16),
        ],
        compiler_params=params(8),
        cost_estimate=cost(2 * 256 * 1024 * 1024, 3 << 20),
        name="local_grads",
    )(back_block, local)


SPREAD = 256


def spread_kernel(back_ref, send_ref, hub_ref, base_ref, out_ref, self_ref, neigh_ref, slots, hub_total):
    @pl.when(pl.program_id(0) == 0)
    def _():
        for peer in range(PEERS):
            slots[:, SLOTS * peer : SLOTS * (peer + 1)] = back_ref[peer, :FEATS, :]
            grads = back_ref[peer, ROWS:, :].astype(F32)
            slice_of, outs = peer // 4, peer % 4
            weight_ref = self_ref if slice_of < 4 else neigh_ref
            row = PIECE * (slice_of % 4)
            weight_ref[row : row + PIECE, TILE * outs : TILE * outs + SLOTS] = grads[:PIECE, :]
            weight_ref[row : row + PIECE, TILE * outs + SLOTS : TILE * (outs + 1)] = grads[PIECE:, :]
        sums = jnp.sum(back_ref[:, FEATS:ROWS, :].astype(F32), axis=0)
        total = sums[:, :FEATS] + sums[:, FEATS:]
        high = total.astype(BF16).astype(F32)
        hub_total[0] = high.T.astype(BF16)
        hub_total[1] = (total - high).T.astype(BF16)

    first = pl.program_id(0) * SPREAD
    node = lax.broadcasted_iota(jnp.int32, (SPREAD, 2 * SLOTS), 0) + first
    grad = base_ref[...]
    for pair in range(PEERS // 2):
        grad = grad + matmul(
            slots[:, 2 * SLOTS * pair : 2 * SLOTS * (pair + 1)],
            one_hot(node == pair_lanes(send_ref, pair)),
            NT,
        )
    hub_node = lax.broadcasted_iota(jnp.int32, (SPREAD, HUBS_OWN), 0) + first
    hub_hot = one_hot(hub_node == hub_ref[...])
    grad = grad + matmul(hub_total[0], hub_hot, NT) + matmul(hub_total[1], hub_hot, NT)
    out_ref[...] = grad.astype(BF16)


def spread_grads(returned, send_lanes, hub_own, base):
    return pl.pallas_call(
        spread_kernel,
        grid=(NODES // SPREAD,),
        in_specs=[
            whole((PEERS, RETURN_ROWS, SLOTS)),
            whole((PEERS, SLOTS)),
            whole((1, HUBS_OWN)),
            pl.BlockSpec((FEATS, SPREAD), lambda i: (0, i)),
        ],
        out_specs=[
            pl.BlockSpec((FEATS, SPREAD), lambda i: (0, i)),
            whole((FEATS, OUTS)),
            whole((FEATS, OUTS)),
        ],
        out_shape=[
            jax.ShapeDtypeStruct((FEATS, NODES), BF16),
            jax.ShapeDtypeStruct((FEATS, OUTS), F32),
            jax.ShapeDtypeStruct((FEATS, OUTS), F32),
        ],
        scratch_shapes=[pltpu.VMEM((FEATS, PEERS * SLOTS), BF16), pltpu.VMEM((2, FEATS, HUBS_OWN), BF16)],
        compiler_params=params(8),
        cost_estimate=cost(2 * 256 * 4224 * 1024, 2 << 20),
        name="spread_grads",
    )(returned, send_lanes, hub_own, base)


def exchange(blocks, axis):
    return lax.all_to_all(blocks, axis, 0, 0, tiled=True)


def per_device(feats, w_self, w_neigh, cotangent, loc_nbr, send_rows, recv_node, hub_rows, hub_nbr):
    send_lanes = send_rows.reshape(PEERS, SLOTS)
    recv_lanes = recv_node.reshape(PEERS, SLOTS)
    hub_own = hub_rows[None, :]
    core = lax.axis_index("row") % 2
    own_half = lax.dynamic_slice_in_dim(
        jnp.concatenate([w_self, w_neigh], axis=0), HALF * core, HALF, 1
    )
    own = lax.all_gather(own_half, "col", axis=0, tiled=True)
    other = lax.ppermute(own, "row", [(i, i ^ 1) for i in range(PEERS)])
    incoming = exchange(gather_slots(feats, send_lanes, hub_own), "row")
    local, hubs = build_counts(loc_nbr, hub_nbr)
    outgoing, degree = aggregate(feats, incoming, recv_lanes, local, hubs, cotangent)
    node_block = exchange(outgoing, "col")
    own_degree = lax.dynamic_slice_in_dim(degree[0], OWN * lax.axis_index("col"), OWN)[:, None]
    joined_cols = exchange(regroup(node_block), "row").reshape(PEERS * OWN, TILE).T
    slopes_out, hidden, slopes = forward(node_block, own, other)
    slopes_rows = exchange(slopes_out, "row").reshape(PEERS * OWN, TILE)
    back = backward(slopes, own, other, own_degree)
    back_block = exchange(weight_parts(joined_cols, slopes_rows, back, hidden), "col")
    returned = exchange(return_slots(back_block, recv_lanes, hubs), "row")
    base, hidden_out = local_grads(back_block, local)
    grad_feats, grad_self, grad_neigh = spread_grads(returned, send_lanes, hub_own, base)
    return (hidden_out, grad_feats, grad_self, grad_neigh)


def solution(mesh):
    return jax.shard_map(
        per_device,
        mesh=mesh,
        in_specs=(
            P("col", "row"),
            P("col", None),
            P("col", None),
            P("col", "row"),
            P("row", None),
            P("row", None, None),
            P("row", None, None),
            P("row"),
            P("row", None),
        ),
        out_specs=(P("col", "row"), P("col", "row"), P("col", None), P("col", None)),
        check_vma=False,
    )
```

time: 219 us -> 229 us (1.046)
  waiting for transfers between devices: 34.7 us -> 78 us
  blocking collectives: 65.5 us -> 30.2 us
  starting transfers between devices: 45 us -> 57 us
  Pallas kernels: 34.1 us -> 27.4 us
  local copies, waits for them, and re-layouts: 21.6 us -> 19 us
    all_to_all x2 -> x1, blocking collectives: 65.5 us -> 30.2 us  [exchange(): return lax.all_to_all(blocks, axis, 0, 0, tiled=True)]
    all_gather x1, waiting for transfers between devices: 7.94 us -> 36.4 us  [per_device(): own = lax.all_gather(own_half, 'col', axis=0, tiled=True)]
    all_to_all x4 -> x5, waiting for transfers between devices: 26.7 us -> 41.6 us  [exchange(): return lax.all_to_all(blocks, axis, 0, 0, tiled=True)]
    ppermute x0 -> x1, starting transfers between devices: none -> 11.6 us  [per_device(): other = lax.ppermute(own, 'row', [(i, i ^ 1) for i in range(PEERS)])]
    pallas_call x2, Pallas kernels: 13.9 us -> 6.71 us  [the longest x1 4.7 us: aggregate(): pl.pallas_call(aggregate_kernel, out_shape=[jax.ShapeDtypeStruct((LAYERS,...]
    pallas_call x1, Pallas kernels: 8.12 us -> 5.37 us  [build_counts(): pl.pallas_call(build_kernel, grid=(NODES // BUILD,), in_specs=[pl.BlockSp...]
    unnamed x52 -> x54, local copies, waits for them, and re-layouts: 18.4 us -> 16.5 us
    all_to_all x4 -> x5, starting transfers between devices: 45 us -> 45.3 us  [exchange(): return lax.all_to_all(blocks, axis, 0, 0, tiled=True)]
  transfers between devices with their start and end apart: 5 -> 7, of which waited for: 5 -> 5; matrix products, arithmetic and copies ran while one was open for 3% -> 2% of each run, Pallas kernels for 11% -> 9%
where the time goes in v3:
time: 229 us; the launch traced here: 227 us
  waiting for transfers between devices  78 us (34%)
  starting transfers between devices  57 us (25%)
  blocking collectives  30.2 us (13%)
  Pallas kernels  27.4 us (12%)
  local copies, waits for them, and re-layouts  19 us (8%)
  between operations  14.3 us (6%)
    all_to_all x5, starting transfers between devices, exchange(): return lax.all_to_all(blocks, axis, 0, 0, tiled=True)  45.3 us
    all_to_all x5, waiting for transfers between devices, exchange(): return lax.all_to_all(blocks, axis, 0, 0, tiled=True)  41.6 us
    all_gather x1, waiting for transfers between devices, per_device(): own = lax.all_gather(own_half, 'col', axis=0, tiled=True)  36.4 us
    all_to_all x1, blocking collectives, exchange(): return lax.all_to_all(blocks, axis, 0, 0, tiled=True)  30.2 us
    unnamed x54, local copies, waits for them, and re-layouts  16.5 us
    ppermute x1, starting transfers between devices, per_device(): other = lax.ppermute(own, 'row', [(i, i ^ 1) for i in range(PEERS)])  11.6 us
    pallas_call x1, Pallas kernels, build_counts(): pl.pallas_call(build_kernel, grid=(NODES // BUILD,), in_specs=[pl.BlockSp...  5.37 us
    pallas_call x1, Pallas kernels, aggregate(): pl.pallas_call(aggregate_kernel, out_shape=[jax.ShapeDtypeStruct((LAYERS,...  4.7 us
  transfers between devices with their start and end apart: 7, of which 5 were waited for; matrix products, arithmetic and copies ran while one was open for 2% of the time, Pallas kernels for 9%

profile of v3, /device:TPU:1, one launch (start us, length us, event | category | flops | bytes accessed | tf_op | source)
XLA Modules:
  0.0 227.4 jit_solution(7290067032238341274)
XLA Ops:
  7.2 1.5 fusion
  11.1 2.5 %gather_slots.1 = bf16[32,80,128]{2,1,0:T(8,128)(2,1)} custom-call(bf16[64,1024]{1,0:T(8,128)(2,1)S(1)} %copy-done.13, s32[32,128]{1,0:T(8,128)S(1)} %bitcast.12, s32[1,16]{1,0:T(1,128)S(1)} %bitcast.14), custom_call_target="tpu_custom_call" | custom-call | flops 2147483648 | bytes 1048576 | tf_op jit(solution)/shard_map/gather_slots/pallas_call | solution.py:65
  13.6 10.4 %all-to-all-start = ((bf16[32,80,128]{2,1,0:T(8,128)(2,1)}), bf16[32,80,128]{2,1,0:T(8,128)(2,1)S(1)}, u32[]{:S(2)}, u32[]{:S(2)}) async-start(bf16[32,80,128]{2,1,0:T(8,128)(2,1)} %gather_slots.1), calls=%async_computation | async-start | bytes 1310720 | tf_op jit(solution)/shard_map/all_to_all | solution.py:397
  24.2 1.0 copy.18.hub_ref
  25.3 1.0 copy-done.6
  26.3 5.4 %build_counts.1 = (bf16[1024,1024]{1,0:T(8,128)(2,1)S(1)}, bf16[1024,512]{1,0:T(8,128)(2,1)S(1)}) custom-call(s32[1024,8]{1,0:T(8,128)S(1)} %copy.17.loc_ref, s32[1024,2]{1,0:T(8,128)S(1)} %copy-done.6), custom_call_target="tpu_custom_call" | custom-call | flops 1073741824 | bytes 12582912 | tf_op jit(solution)/shard_map/build_counts/pallas_call | solution.py:91
  31.7 1.0 copy-done.21
  32.7 4.4 %all-to-all-done.inc_ref = bf16[32,80,128]{2,1,0:T(8,128)(2,1)S(1)} async-done(((bf16[32,80,128]{2,1,0:T(8,128)(2,1)}), bf16[32,80,128]{2,1,0:T(8,128)(2,1)S(1)}, u32[]{:S(2)}, u32[]{:S(2)}) %all-to-all-start) | async-done | bytes 655392 | tf_op jit(solution)/shard_map/all_to_all | solution.py:397
  37.0 1.2 copy-done.22
  38.3 4.7 %aggregate.1 = (bf16[16,96,128]{2,1,0:T(8,128)(2,1)}, f32[8,1024]{1,0:T(8,128)S(1)}) custom-call(bf16[64,1024]{1,0:T(8,128)(2,1)S(1)} %copy-done.14, bf16[32,80,128]{2,1,0:T(8,128)(2,1)S(1)} %all-to-all-done.inc_ref, s32[32,128]{1,0:T(8,128)S(1)} %bitcast.10, bf16[1024,1024]{1,0:T(8,128)(2,1)S(1)} %get-tuple-element.16.local_ref, ...), custom_call_target="tpu_custom_call" | custom-call | flops 2952790016 | bytes 5242880 | tf_op jit(solution)/shard_map/aggregate/pallas_call | solution.py:157
  43.0 13.0 %all-to-all-start.1 = ((bf16[16,96,128]{2,1,0:T(8,128)(2,1)}), bf16[16,96,128]{2,1,0:T(8,128)(2,1)S(1)}, u32[]{:S(2)}, u32[]{:S(2)}) async-start(bf16[16,96,128]{2,1,0:T(8,128)(2,1)} %get-tuple-element.18), calls=%async_computation.1 | async-start | bytes 786432 | tf_op jit(solution)/shard_map/all_to_all | solution.py:397
  55.9 36.4 %all-gather.2.cloned.1.call-done.own_ref = bf16[2048,512]{1,0:T(8,128)(2,1)} async-done(((bf16[128,512]{1,0:T(8,128)(2,1)}), bf16[2048,512]{1,0:T(8,128)(2,1)}) %all-gather.2.cloned.1.call-update) | async-done | bytes 2097168 | tf_op jit(solution)/shard_map/all_gather | solution.py:408
  92.4 11.6 %collective-permute-start = (bf16[2048,512]{1,0:T(8,128)(2,1)}, bf16[2048,512]{1,0:T(8,128)(2,1)}, u32[]{:S(2)}, u32[]{:S(2)}) collective-permute-start(bf16[2048,512]{1,0:T(8,128)(2,1)} %all-gather.2.cloned.1.call-done.own_ref), channel_id=1, source_target_pairs={{0,16},{16,0},{32,48},{48,32},{64,80},{80,64},{96,112},{112,96},{1... | collective-permute-start | bytes 6291464 | tf_op jit(solution)/shard_map/ppermute | solution.py:409
  104.0 1.5 regroup.1
  105.5 7.1 %all-to-all-start.2 = ((bf16[32,64,256]{2,1,0:T(8,128)(2,1)}), bf16[32,64,256]{2,1,0:T(8,128)(2,1)}, u32[]{:S(2)}, u32[]{:S(2)}) async-start(bf16[32,64,256]{2,1,0:T(8,128)(2,1)} %regroup.1), calls=%async_computation.2 | async-start | bytes 2097152 | tf_op jit(solution)/shard_map/all_to_all | solution.py:397
  112.6 2.7 %forward.1 = (bf16[32,64,256]{2,1,0:T(8,128)(2,1)S(1)}, bf16[16,32,128]{2,1,0:T(8,128)(2,1)S(1)}, bf16[2,64,512]{2,1,0:T(8,128)(2,1)S(1)}) custom-call(bf16[16,96,128]{2,1,0:T(8,128)(2,1)S(1)} %all-to-all-done.1.inc_ref, bf16[2048,512]{1,0:T(8,128)(2,1)S(1)} %copy-done, bf16[2048,512]{1,0:T(8,128)(2,1)} %collective-permute-done.other_ref), custom_call_target="tpu_custom_call" | custom-call | flops 1073741824 | bytes 6291456 | tf_op jit(solution)/shard_map/forward/pallas_call | solution.py:228
  115.3 1.0 copy-done.4
  117.6 12.2 %all-to-all-done.2 = bf16[32,64,256]{2,1,0:T(8,128)(2,1)} async-done(((bf16[32,64,256]{2,1,0:T(8,128)(2,1)}), bf16[32,64,256]{2,1,0:T(8,128)(2,1)}, u32[]{:S(2)}, u32[]{:S(2)}) %all-to-all-start.2) | async-done | bytes 1048608 | tf_op jit(solution)/shard_map/all_to_all | solution.py:397
  129.8 4.0 %all-to-all-start.3 = ((bf16[32,64,256]{2,1,0:T(8,128)(2,1)}), bf16[32,64,256]{2,1,0:T(8,128)(2,1)S(1)}, u32[]{:S(2)}, u32[]{:S(2)}) async-start(bf16[32,64,256]{2,1,0:T(8,128)(2,1)} %copy-done.4), calls=%async_computation.3 | async-start | bytes 2097152 | tf_op jit(solution)/shard_map/all_to_all | solution.py:397
  134.0 2.3 copy.19
  137.2 3.0 %backward.1.back_ref = bf16[16,64,128]{2,1,0:T(8,128)(2,1)S(1)} custom-call(bf16[2,64,512]{2,1,0:T(8,128)(2,1)S(1)} %copy-done.10, bf16[2048,512]{1,0:T(8,128)(2,1)S(1)} %copy-done, bf16[2048,512]{1,0:T(8,128)(2,1)} %collective-permute-done.other_ref, f32[64,1]{1,0:T(8,128)S(1)} %copy.20.degree_ref), custom_call_target="tpu_custom_call" | custom-call | flops 1073741824 | bytes 6291456 | tf_op jit(solution)/shard_map/backward/pallas_call | solution.py:254
  140.1 11.0 %all-to-all-done.3 = bf16[32,64,256]{2,1,0:T(8,128)(2,1)S(1)} async-done(((bf16[32,64,256]{2,1,0:T(8,128)(2,1)}), bf16[32,64,256]{2,1,0:T(8,128)(2,1)S(1)}, u32[]{:S(2)}, u32[]{:S(2)}) %all-to-all-start.3) | async-done | bytes 1048608 | tf_op jit(solution)/shard_map/all_to_all | solution.py:397
  151.1 1.2 copy-done.1
  153.7 30.2 %all_to_all.30.back_ref = bf16[16,128,128]{2,1,0:T(8,128)(2,1)S(1)} all-to-all(bf16[16,128,128]{2,1,0:T(8,128)(2,1)S(1)} %weight_parts.1), channel_id=1, replica_groups=mesh['row'=32,'col'=16] {'col'}, dimensions={0} | all-to-all | bytes 1048576 | tf_op jit(solution)/shard_map/all_to_all | solution.py:397
  183.9 1.2 copy-done.23
  185.1 2.0 return_slots.1
  187.2 0.9 copy-done.5
  188.1 10.9 %all-to-all-start.5 = ((bf16[32,112,128]{2,1,0:T(8,128)(2,1)}), bf16[32,112,128]{2,1,0:T(8,128)(2,1)S(1)}, u32[]{:S(2)}, u32[]{:S(2)}) async-start(bf16[32,112,128]{2,1,0:T(8,128)(2,1)} %copy-done.5), calls=%async_computation.5 | async-start | bytes 1835008 | tf_op jit(solution)/shard_map/all_to_all | solution.py:397
  199.0 1.1 local_grads.1
  200.8 14.0 %all-to-all-done.5.back_ref = bf16[32,112,128]{2,1,0:T(8,128)(2,1)S(1)} async-done(((bf16[32,112,128]{2,1,0:T(8,128)(2,1)}), bf16[32,112,128]{2,1,0:T(8,128)(2,1)S(1)}, u32[]{:S(2)}, u32[]{:S(2)}) %all-to-all-start.5) | async-done | bytes 917536 | tf_op jit(solution)/shard_map/all_to_all | solution.py:397
  214.8 0.9 copy-done.12
  216.5 4.1 %spread_grads.1 = (bf16[64,1024]{1,0:T(8,128)(2,1)}, f32[64,1024]{1,0:T(8,128)}, f32[64,1024]{1,0:T(8,128)}) custom-call(bf16[32,112,128]{2,1,0:T(8,128)(2,1)S(1)} %all-to-all-done.5.back_ref, s32[32,128]{1,0:T(8,128)S(1)} %bitcast.13, s32[1,16]{1,0:T(1,128)S(1)} %bitcast.15, f32[64,1024]{1,0:T(8,128)S(1)} %copy-done.12), custom_call_target="tpu_custom_call" | custom-call | flops 2214592512 | bytes 2097152 | tf_op jit(solution)/shard_map/spread_grads/pallas_call | solution.py:370
  (53 shorter events, 7.7 us)
Async XLA Ops:
  7.2 85.2 %all-gather.2.cloned.1.call-start = ((), (), s32[]{:S(2)}) async-start(), calls=%async_computation.6 | async-start | bytes 2228224 | tf_op jit(solution)/shard_map/all_gather | solution.py:408
  8.8 0.9 copy-start.13
  9.7 0.7 copy-start.17
  10.4 0.7 copy-start.19
  11.1 12.9 %copy-start.24 = (s32[1024,8]{0,1:T(8,128)S(1)}, s32[1024,8]{0,1:T(8,128)}, u32[]{:S(2)}) copy-start(s32[1024,8]{0,1:T(8,128)} %param.13) | copy-start | bytes 98308
  11.1 13.1 %copy-start.25 = (s32[1024,2]{0,1:T(2,128)S(1)}, s32[1024,2]{0,1:T(2,128)}, u32[]{:S(2)}) copy-start(s32[1024,2]{0,1:T(2,128)} %param.17) | copy-start | bytes 24580
  13.6 23.5 %all-to-all-start = ((bf16[32,80,128]{2,1,0:T(8,128)(2,1)}), bf16[32,80,128]{2,1,0:T(8,128)(2,1)S(1)}, u32[]{:S(2)}, u32[]{:S(2)}) async-start(bf16[32,80,128]{2,1,0:T(8,128)(2,1)} %gather_slots.1), calls=%async_computation | async-start | bytes 1310720 | tf_op jit(solution)/shard_map/all_to_all | solution.py:397
  25.3 1.0 copy-start.6
  26.3 10.7 %copy-start.14 = (bf16[64,1024]{1,0:T(8,128)(2,1)S(1)}, bf16[64,1024]{1,0:T(8,128)(2,1)}, u32[]{:S(2)}) copy-start(bf16[64,1024]{1,0:T(8,128)(2,1)} %x_ref.3) | copy-start | bytes 393220
  26.3 10.7 %copy-start.15 = (bf16[64,1024]{1,0:T(8,128)(2,1)S(1)}, bf16[64,1024]{1,0:T(8,128)(2,1)}, u32[]{:S(2)}) copy-start(bf16[64,1024]{1,0:T(8,128)(2,1)} %cot_ref.1) | copy-start | bytes 393220
  26.3 10.7 %copy-start.16 = (s32[1,32,128]{2,1,0:T(8,128)S(1)}, s32[1,32,128]{2,1,0:T(8,128)}, u32[]{:S(2)}) copy-start(s32[1,32,128]{2,1,0:T(8,128)} %param.15) | copy-start | bytes 49156
  31.7 1.0 copy-start.21
  32.7 10.3 %copy-start.2 = (bf16[1024,1024]{1,0:T(8,128)(2,1)}, bf16[1024,1024]{1,0:T(8,128)(2,1)S(1)}, u32[]{:S(2)}) copy-start(bf16[1024,1024]{1,0:T(8,128)(2,1)S(1)} %get-tuple-element.16.local_ref) | copy-start | bytes 6291460
  37.0 1.2 copy-start.22
  43.0 61.0 %all-to-all-start.1 = ((bf16[16,96,128]{2,1,0:T(8,128)(2,1)}), bf16[16,96,128]{2,1,0:T(8,128)(2,1)S(1)}, u32[]{:S(2)}, u32[]{:S(2)}) async-start(bf16[16,96,128]{2,1,0:T(8,128)(2,1)} %get-tuple-element.18), calls=%async_computation.1 | async-start | bytes 786432 | tf_op jit(solution)/shard_map/all_to_all | solution.py:397
  92.4 20.3 %copy-start = (bf16[2048,512]{1,0:T(8,128)(2,1)S(1)}, bf16[2048,512]{1,0:T(8,128)(2,1)}, u32[]{:S(2)}) copy-start(bf16[2048,512]{1,0:T(8,128)(2,1)} %all-gather.2.cloned.1.call-done.own_ref) | copy-start | bytes 6291460
  92.4 20.3 %collective-permute-start = (bf16[2048,512]{1,0:T(8,128)(2,1)}, bf16[2048,512]{1,0:T(8,128)(2,1)}, u32[]{:S(2)}, u32[]{:S(2)}) collective-permute-start(bf16[2048,512]{1,0:T(8,128)(2,1)} %all-gather.2.cloned.1.call-done.own_ref), channel_id=1, source_target_pairs={{0,16},{16,0},{32,48},{48,32},{64,80},{80,64},{96,112},{112,96},{1... | collective-permute-start | bytes 6291464 | tf_op jit(solution)/shard_map/ppermute | solution.py:409
  105.5 24.3 %all-to-all-start.2 = ((bf16[32,64,256]{2,1,0:T(8,128)(2,1)}), bf16[32,64,256]{2,1,0:T(8,128)(2,1)}, u32[]{:S(2)}, u32[]{:S(2)}) async-start(bf16[32,64,256]{2,1,0:T(8,128)(2,1)} %regroup.1), calls=%async_computation.2 | async-start | bytes 2097152 | tf_op jit(solution)/shard_map/all_to_all | solution.py:397
  115.3 1.0 copy-start.4
  116.3 0.7 copy-start.7
  129.8 21.3 %all-to-all-start.3 = ((bf16[32,64,256]{2,1,0:T(8,128)(2,1)}), bf16[32,64,256]{2,1,0:T(8,128)(2,1)S(1)}, u32[]{:S(2)}, u32[]{:S(2)}) async-start(bf16[32,64,256]{2,1,0:T(8,128)(2,1)} %copy-done.4), calls=%async_computation.3 | async-start | bytes 2097152 | tf_op jit(solution)/shard_map/all_to_all | solution.py:397
  136.3 0.9 copy-start.10
  151.1 1.2 copy-start.1
  152.3 0.9 copy-start.8
  183.9 1.2 copy-start.23
  185.1 13.8 %copy-start.3 = (bf16[1024,1024]{1,0:T(8,128)(2,1)S(1)}, bf16[1024,1024]{1,0:T(8,128)(2,1)}, u32[]{:S(2)}) copy-start(bf16[1024,1024]{1,0:T(8,128)(2,1)} %copy-done.2) | copy-start | bytes 6291460
  187.2 0.9 copy-start.5
  188.1 26.8 %copy-start.18 = (s32[1,32,128]{2,1,0:T(8,128)S(1)}, s32[1,32,128]{2,1,0:T(8,128)}, u32[]{:S(2)}) copy-start(s32[1,32,128]{2,1,0:T(8,128)} %param.14) | copy-start | bytes 49156
  188.1 26.8 %all-to-all-start.5 = ((bf16[32,112,128]{2,1,0:T(8,128)(2,1)}), bf16[32,112,128]{2,1,0:T(8,128)(2,1)S(1)}, u32[]{:S(2)}, u32[]{:S(2)}) async-start(bf16[32,112,128]{2,1,0:T(8,128)(2,1)} %copy-done.5), calls=%async_computation.5 | async-start | bytes 1835008 | tf_op jit(solution)/shard_map/all_to_all | solution.py:397
  200.1 0.7 copy-start.11
  214.8 1.0 copy-start.12
  215.8 0.7 copy-start.20
  (1 other events, 0.7 us)
Sparse Core Ops, SparseCore 0:
  10.7 81.6 all-gather.1

commit v4 on v3

v4 whole, which is shorter than its diff:
```python
import jax
import jax.numpy as jnp
from jax import lax
from jax.experimental import pallas as pl
from jax.experimental.pallas import tpu as pltpu
from jax.sharding import PartitionSpec as P

NODES = 1024
FEATS = 64
PEERS = 32
SLOTS = 128
HUBS_OWN = 16
HUBS = 512
ROWS = 80
LAYERS = 16
OWN = 64
OUTS = 1024
BF16 = jnp.bfloat16
F32 = jnp.float32
NT = (((1,), (1,)), ((), ()))
NN = (((1,), (0,)), ((), ()))
MIB = 1 << 20


def params(mib):
    return pltpu.CompilerParams(vmem_limit_bytes=mib * MIB)


def cost(flops, moved):
    return pl.CostEstimate(flops=flops, bytes_accessed=moved, transcendentals=0)


def whole(shape):
    return pl.BlockSpec(shape, lambda *_: (0,) * len(shape))


HBM = pl.BlockSpec(memory_space=pltpu.HBM)
VMEM = pl.BlockSpec(memory_space=pltpu.VMEM)


def copies(sems, *pairs):
    started = []
    for i, (source, target) in enumerate(pairs):
        copy = pltpu.make_async_copy(source, target, sems.at[i])
        copy.start()
        started.append(copy)
    return started


def one_hot(mask):
    return jnp.where(mask, 1.0, 0.0).astype(BF16)


def matmul(a, b, dims):
    return lax.dot_general(a, b, dims, preferred_element_type=F32)


def pair_lanes(ref, pair):
    return jnp.concatenate([ref[2 * pair : 2 * pair + 1, :], ref[2 * pair + 1 : 2 * pair + 2, :]], axis=1)


def gather_kernel(x_hbm, send_hbm, hub_hbm, out_ref, x_ref, send_ref, hub_ref, sems):
    for copy in copies(sems, (x_hbm, x_ref), (send_hbm, send_ref), (hub_hbm, hub_ref)):
        copy.wait()
    x = x_ref[...]
    node = lax.broadcasted_iota(jnp.int32, (NODES, 2 * SLOTS), 0)
    hub_node = lax.broadcasted_iota(jnp.int32, (NODES, HUBS_OWN), 0)
    hub_feats = matmul(x, one_hot(hub_node == hub_ref[...]), NN)
    hub_rows = hub_feats.T
    hub_block = jnp.concatenate([hub_rows, jnp.zeros_like(hub_rows)], axis=1).astype(BF16)
    for pair in range(PEERS // 2):
        picked = matmul(x, one_hot(node == pair_lanes(send_ref, pair)), NN).astype(BF16)
        out_ref[2 * pair, :FEATS, :] = picked[:, :SLOTS]
        out_ref[2 * pair + 1, :FEATS, :] = picked[:, SLOTS:]
        out_ref[2 * pair, FEATS:, :] = hub_block
        out_ref[2 * pair + 1, FEATS:, :] = hub_block


def gather_slots(feats, send_lanes, hub_own):
    return pl.pallas_call(
        gather_kernel,
        in_specs=[HBM, HBM, HBM],
        out_shape=jax.ShapeDtypeStruct((PEERS, ROWS, SLOTS), BF16),
        scratch_shapes=[
            pltpu.VMEM((FEATS, NODES), BF16),
            pltpu.VMEM((PEERS, SLOTS), jnp.int32),
            pltpu.VMEM((1, HUBS_OWN), jnp.int32),
            pltpu.SemaphoreType.DMA((3,)),
        ],
        compiler_params=params(60),
        cost_estimate=cost(2 * 256 * 4096 * 1024, 1 << 20),
        name="gather_slots",
    )(feats, send_lanes, hub_own)


BUILD = 128


def build_kernel(loc_ref, hub_ref, local_ref, hubs_ref):
    lane = lax.broadcasted_iota(jnp.int32, (BUILD, NODES), 1)
    counts = jnp.zeros((BUILD, NODES), F32)
    for k in range(loc_ref.shape[1]):
        counts = counts + jnp.where(lane == loc_ref[:, k : k + 1], 1.0, 0.0)
    local_ref[...] = counts.astype(BF16)
    hub_lane = lax.broadcasted_iota(jnp.int32, (BUILD, HUBS), 1)
    hub_counts = jnp.zeros((BUILD, HUBS), F32)
    for k in range(hub_ref.shape[1]):
        hub_counts = hub_counts + jnp.where(hub_lane == hub_ref[:, k : k + 1], 1.0, 0.0)
    hubs_ref[...] = hub_counts.astype(BF16)


def build_counts(loc_nbr, hub_nbr):
    return pl.pallas_call(
        build_kernel,
        grid=(NODES // BUILD,),
        in_specs=[
            pl.BlockSpec((BUILD, loc_nbr.shape[1]), lambda i: (i, 0)),
            pl.BlockSpec((BUILD, hub_nbr.shape[1]), lambda i: (i, 0)),
        ],
        out_specs=[
            pl.BlockSpec((BUILD, NODES), lambda i: (i, 0)),
            pl.BlockSpec((BUILD, HUBS), lambda i: (i, 0)),
        ],
        out_shape=[
            jax.ShapeDtypeStruct((NODES, NODES), BF16),
            jax.ShapeDtypeStruct((NODES, HUBS), BF16),
        ],
        compiler_params=params(60),
        cost_estimate=cost(1 << 30, 12 << 20),
        name="build_counts",
    )(loc_nbr, hub_nbr)


AGG = 256


def fold_halves(block):
    return jnp.concatenate([block[: OWN // 2, :], block[OWN // 2 :, :]], axis=1)


NEIGHBOURS = 10.0


def aggregate_kernel(
    x_hbm, inc_ref, recv_hbm, local_hbm, hubs_hbm, cot_hbm, out_ref, degree_ref,
    slots, table, recv_ref, x_ref, local_ref, hubs_ref, cot_ref, sems,
):
    staged = copies(
        sems,
        (recv_hbm, recv_ref),
        (x_hbm, x_ref),
        (local_hbm, local_ref),
        (hubs_hbm, hubs_ref),
        (cot_hbm, cot_ref),
    )
    for peer in range(PEERS):
        slots[:FEATS, SLOTS * peer : SLOTS * (peer + 1)] = inc_ref[peer, :FEATS, :]
    slots[FEATS:, :] = jnp.ones((16, PEERS * SLOTS), BF16)
    rows = inc_ref[:, FEATS:, :].astype(F32).reshape(HUBS, SLOTS)
    table[...] = rows.T[:FEATS, :].astype(BF16)
    staged[0].wait()
    for tile in range(NODES // AGG):
        lanes = slice(AGG * tile, AGG * (tile + 1))
        node = lax.broadcasted_iota(jnp.int32, (AGG, 2 * SLOTS), 0) + AGG * tile
        remote = jnp.zeros((ROWS, AGG), F32)
        for pair in range(PEERS // 2):
            remote = remote + matmul(
                slots[:, 2 * SLOTS * pair : 2 * SLOTS * (pair + 1)],
                one_hot(node == pair_lanes(recv_ref, pair)),
                NT,
            )
        if tile == 0:
            for copy in staged[1:]:
                copy.wait()
        total = (
            remote[:FEATS, :]
            + matmul(x_ref[...], local_ref[lanes, :], NT)
            + matmul(table[...], hubs_ref[lanes, :], NT)
        )
        degree = remote[FEATS : FEATS + 8, :] + NEIGHBOURS
        degree_ref[:, lanes] = degree
        mean = (total / degree[0:1, :]).T
        nodes = jnp.concatenate([x_ref[:, lanes].astype(F32).T, mean], axis=1).astype(BF16)
        slopes = cot_ref[:, lanes].astype(F32).T
        for part in range(AGG // OWN):
            layer = AGG // OWN * tile + part
            out_ref[layer, :OWN, :] = nodes[OWN * part : OWN * (part + 1), :]
            out_ref[layer, OWN:, :] = fold_halves(slopes[OWN * part : OWN * (part + 1), :]).astype(BF16)


def aggregate(feats, incoming, recv_lanes, local, hubs, cotangent):
    return pl.pallas_call(
        aggregate_kernel,
        out_shape=[
            jax.ShapeDtypeStruct((LAYERS, 96, SLOTS), BF16),
            jax.ShapeDtypeStruct((8, NODES), F32),
        ],
        in_specs=[HBM, VMEM, HBM, HBM, HBM, HBM],
        scratch_shapes=[
            pltpu.VMEM((ROWS, PEERS * SLOTS), BF16),
            pltpu.VMEM((FEATS, HUBS), BF16),
            pltpu.VMEM((PEERS, SLOTS), jnp.int32),
            pltpu.VMEM((FEATS, NODES), BF16),
            pltpu.VMEM((NODES, NODES), BF16),
            pltpu.VMEM((NODES, HUBS), BF16),
            pltpu.VMEM((FEATS, NODES), BF16),
            pltpu.SemaphoreType.DMA((5,)),
        ],
        compiler_params=params(16),
        cost_estimate=cost(2 * 256 * 5632 * 1024, 5 << 20),
        name="aggregate",
    )(feats, incoming, recv_lanes, local, hubs, cotangent)


PIECE = 16
TILE = 256


def regroup_kernel(inc_ref, out_ref):
    group = lax.broadcasted_iota(jnp.int32, (OWN, SLOTS), 1) // PIECE
    for half in range(2):
        blocks = [inc_ref[8 * half + i, :OWN, :].astype(F32) for i in range(8)]
        for slice_of in range(8):
            tile = jnp.zeros((OWN, SLOTS), F32)
            for i in range(8):
                moved = blocks[i]
                if i != slice_of:
                    moved = pltpu.roll(moved, (PIECE * (i - slice_of)) % SLOTS, 1)
                tile = jnp.where(group == i, moved, tile)
            tile = tile.astype(BF16)
            for outs in range(4):
                out_ref[4 * slice_of + outs, :, SLOTS * half : SLOTS * (half + 1)] = tile


def regroup(node_block):
    return pl.pallas_call(
        regroup_kernel,
        out_shape=jax.ShapeDtypeStruct((PEERS, OWN, TILE), BF16),
        compiler_params=params(16),
        cost_estimate=cost(1 << 24, 2 << 20),
        name="regroup",
    )(node_block)


HALF = OUTS // 2
CHIPS = PEERS // 2


def forward_kernel(
    own_hbm, other_hbm, weights_hbm, slopes_hbm, flat_hbm, hidden_hbm,
    own_block, other_block, weights, blocks, cots, out_tile, flat, hidden, in_sems, out_sems,
):
    core = lax.axis_index("row") % 2
    staged = copies(
        in_sems, (own_hbm, own_block), (other_hbm, other_block), (weights_hbm, weights)
    )
    staged[0].wait()
    staged[1].wait()
    for layer in range(LAYERS):
        lanes = slice(SLOTS * layer, SLOTS * (layer + 1))
        blocks[core, :, lanes] = own_block[layer, :OWN, :]
        blocks[1 - core, :, lanes] = other_block[layer, :OWN, :]
    for layer in range(LAYERS // 2):
        cots[core, layer] = own_block[8 * core + layer, OWN:, :]
        cots[1 - core, layer] = other_block[8 * core + layer, OWN:, :]
    staged[2].wait()
    preacts = matmul(blocks[...].reshape(2 * OWN, 2 * OUTS), weights[...], NN)
    for block in range(2):
        for pair in range(4):
            lanes = slice(SLOTS * pair, SLOTS * (pair + 1))
            preact = preacts[OWN * block : OWN * (block + 1), lanes]
            sigmoid_part = jax.nn.sigmoid(preact)
            silu = preact * sigmoid_part
            slope = sigmoid_part * (1.0 + preact * (1.0 - sigmoid_part))
            even = cots[block, 2 * pair].astype(F32)
            odd = cots[block, 2 * pair + 1].astype(F32)
            top = jnp.concatenate([even[:, :FEATS], odd[:, :FEATS]], axis=1)
            bottom = jnp.concatenate([even[:, FEATS:], odd[:, FEATS:]], axis=1)
            slopes = (jnp.concatenate([top, bottom], axis=0) * slope).astype(BF16)
            column = SLOTS * (pair % 2)
            out_tile[pair // 2, OWN * block : OWN * (block + 1), column : column + SLOTS] = slopes
            flat[OWN * block : OWN * (block + 1), lanes] = slopes
            hidden[block, 2 * pair] = fold_halves(silu[:, :FEATS]).astype(BF16)
            hidden[block, 2 * pair + 1] = fold_halves(silu[:, FEATS:]).astype(BF16)
    sent = copies(
        out_sems,
        *[(out_tile.at[chip % 2], slopes_hbm.at[chip]) for chip in range(CHIPS)],
        (flat, flat_hbm),
        (hidden, hidden_hbm),
    )
    for copy in sent:
        copy.wait()


def forward(own_block, other_block, weights):
    return pl.pallas_call(
        forward_kernel,
        in_specs=[HBM, HBM, HBM],
        out_specs=[HBM, HBM, HBM],
        out_shape=[
            jax.ShapeDtypeStruct((CHIPS, 2 * OWN, TILE), BF16),
            jax.ShapeDtypeStruct((2 * OWN, HALF), BF16),
            jax.ShapeDtypeStruct((2, LAYERS // 2, OWN // 2, SLOTS), BF16),
        ],
        scratch_shapes=[
            pltpu.VMEM((LAYERS, 96, SLOTS), BF16),
            pltpu.VMEM((LAYERS, 96, SLOTS), BF16),
            pltpu.VMEM((2 * OUTS, HALF), BF16),
            pltpu.VMEM((2, OWN, 2 * OUTS), BF16),
            pltpu.VMEM((2, LAYERS // 2, OWN // 2, SLOTS), BF16),
            pltpu.VMEM((2, 2 * OWN, TILE), BF16),
            pltpu.VMEM((2 * OWN, HALF), BF16),
            pltpu.VMEM((2, LAYERS // 2, OWN // 2, SLOTS), BF16),
            pltpu.SemaphoreType.DMA((3,)),
            pltpu.SemaphoreType.DMA((CHIPS + 2,)),
        ],
        compiler_params=params(60),
        cost_estimate=cost(2 * 256 * 2048 * 512, 4 << 20),
        name="forward",
    )(own_block, other_block, weights)


def backward_kernel(slopes_ref, hidden_ref, weights_ref, keep_ref, send_ref, keep_hidden, send_hidden, parts):
    core = lax.axis_index("row") % 2
    back = matmul(slopes_ref[...], weights_ref[...], NT)
    parts[0] = back[:OWN, :]
    parts[1] = back[OWN:, :]
    keep_ref[...] = parts[core]
    send_ref[...] = parts[1 - core]
    keep_hidden[...] = hidden_ref[core]
    send_hidden[...] = hidden_ref[1 - core]


def backward(slopes, hidden, weights):
    part = jax.ShapeDtypeStruct((OWN, 2 * OUTS), F32)
    block = jax.ShapeDtypeStruct((LAYERS // 2, OWN // 2, SLOTS), BF16)
    return pl.pallas_call(
        backward_kernel,
        out_shape=[part, part, block, block],
        scratch_shapes=[pltpu.VMEM((2, OWN, 2 * OUTS), F32)],
        compiler_params=params(60),
        cost_estimate=cost(2 * 256 * 2048 * 512, 4 << 20),
        name="backward",
    )(slopes, hidden, weights)


def combine_kernel(mine_ref, theirs_ref, my_hidden, their_hidden, degree_ref, out_ref):
    core = lax.axis_index("row") % 2
    direct = lax.broadcasted_iota(jnp.int32, (OWN, SLOTS), 1) < FEATS
    divisor = jnp.where(direct, 1.0, degree_ref[...])
    for layer in range(LAYERS):
        lanes = slice(SLOTS * layer, SLOTS * (layer + 1))
        back = mine_ref[:, lanes] + theirs_ref[:, lanes]
        out_ref[layer, :OWN, :] = (back / divisor).astype(BF16)
    for layer in range(LAYERS // 2):
        out_ref[8 * core + layer, OWN:, :] = my_hidden[layer]
        out_ref[8 * (1 - core) + layer, OWN:, :] = their_hidden[layer]


def combine(mine, theirs, my_hidden, their_hidden, own_degree):
    return pl.pallas_call(
        combine_kernel,
        out_shape=jax.ShapeDtypeStruct((LAYERS, 96, SLOTS), BF16),
        compiler_params=params(60),
        cost_estimate=cost(1 << 20, 2 << 20),
        name="combine",
    )(mine, theirs, my_hidden, their_hidden, own_degree)


STEPS = 4


def weight_kernel(joined_hbm, slopes_ref, back_hbm, out_ref, joined, back, sems):
    depth = PEERS * OWN // STEPS
    staged = copies(
        sems,
        *[
            (joined_hbm.at[:, depth * i : depth * (i + 1)], joined.at[:, depth * i : depth * (i + 1)])
            for i in range(STEPS)
        ],
        (back_hbm, back),
    )
    part = jnp.zeros((TILE, TILE), F32)
    for i in range(STEPS):
        staged[i].wait()
        rows = slice(depth * i, depth * (i + 1))
        part = part + matmul(joined[:, rows], slopes_ref[rows, :], NN)
    part = part.astype(BF16)
    for layer in range(LAYERS):
        out_ref[layer, 96:112, :] = part[PIECE * layer : PIECE * (layer + 1), :SLOTS]
        out_ref[layer, 112:, :] = part[PIECE * layer : PIECE * (layer + 1), SLOTS:]
    staged[STEPS].wait()
    out_ref[:, :96, :] = back[...]


def weight_parts(joined_cols, slopes_rows, back):
    return pl.pallas_call(
        weight_kernel,
        in_specs=[HBM, VMEM, HBM],
        out_shape=jax.ShapeDtypeStruct((LAYERS, SLOTS, SLOTS), BF16),
        scratch_shapes=[
            pltpu.VMEM((TILE, PEERS * OWN), BF16),
            pltpu.VMEM((LAYERS, 96, SLOTS), BF16),
            pltpu.SemaphoreType.DMA((STEPS + 1,)),
        ],
        compiler_params=params(16),
        cost_estimate=cost(2 * 256 * 2048 * 256, 3 << 20),
        name="weight_parts",
    )(joined_cols, slopes_rows, back)


RETURN_ROWS = 112


def return_kernel(back_ref, recv_hbm, hubs_hbm, out_hbm, recv_ref, hubs_ref, out_ref, in_sems, out_sems):
    staged = copies(in_sems, (recv_hbm, recv_ref), (hubs_hbm, hubs_ref))
    rows = back_ref[:, :OWN, :].astype(F32).reshape(NODES, SLOTS)
    share = rows.T[FEATS:, :].astype(BF16)
    sums = jnp.sum(back_ref[:, 96:, :].astype(F32), axis=0).astype(BF16)
    node = lax.broadcasted_iota(jnp.int32, (NODES, 2 * SLOTS), 0)
    staged[0].wait()
    sent = []
    for pair in range(PEERS // 2):
        values = matmul(share, one_hot(node == pair_lanes(recv_ref, pair)), NN).astype(BF16)
        for side in range(2):
            peer = 2 * pair + side
            out_ref[peer, :FEATS, :] = values[:, SLOTS * side : SLOTS * (side + 1)]
            out_ref[peer, ROWS:, :] = sums
        if pair == 0:
            staged[1].wait()
            terms = matmul(share, hubs_ref[...], NN).T
            high = terms.astype(BF16).astype(F32)
            both = jnp.concatenate([high, terms - high], axis=1)
            out_ref[:, FEATS:ROWS, :] = both.reshape(PEERS, HUBS_OWN, SLOTS).astype(BF16)
        if pair % 4 == 3:
            part = pl.ds(2 * pair - 6, 8)
            copy = pltpu.make_async_copy(out_ref.at[part], out_hbm.at[part], out_sems.at[pair // 4])
            copy.start()
            sent.append(copy)
    for copy in sent:
        copy.wait()


def return_slots(back_block, recv_lanes, hubs):
    return pl.pallas_call(
        return_kernel,
        in_specs=[VMEM, HBM, HBM],
        out_specs=HBM,
        out_shape=jax.ShapeDtypeStruct((PEERS, RETURN_ROWS, SLOTS), BF16),
        scratch_shapes=[
            pltpu.VMEM((PEERS, SLOTS), jnp.int32),
            pltpu.VMEM((NODES, HUBS), BF16),
            pltpu.VMEM((PEERS, RETURN_ROWS, SLOTS), BF16),
            pltpu.SemaphoreType.DMA((2,)),
            pltpu.SemaphoreType.DMA((4,)),
        ],
        compiler_params=params(60),
        cost_estimate=cost(2 * 256 * 4608 * 1024, 3 << 20),
        name="return_slots",
    )(back_block, recv_lanes, hubs)


def local_kernel(back_ref, local_ref, base_ref, hidden_ref):
    columns = back_ref[:, :OWN, :].astype(F32).reshape(NODES, SLOTS).T
    share = columns[FEATS:, :].astype(BF16)
    base_ref[...] = columns[:FEATS, :] + matmul(share, local_ref[...], NN)
    folded = back_ref[:, OWN:96, :].astype(F32)
    rows = jnp.concatenate([folded[:, :, :FEATS], folded[:, :, FEATS:]], axis=1)
    hidden_ref[...] = rows.reshape(NODES, FEATS).T.astype(BF16)


def local_grads(back_block, local):
    return pl.pallas_call(
        local_kernel,
        out_shape=[
            jax.ShapeDtypeStruct((FEATS, NODES), F32),
            jax.ShapeDtypeStruct((FEATS, NODES), BF16),
        ],
        compiler_params=params(60),
        cost_estimate=cost(2 * 256 * 1024 * 1024, 3 << 20),
        name="local_grads",
    )(back_block, local)


SPREAD = 256


def spread_kernel(
    back_ref, send_hbm, hub_hbm, base_hbm, out_ref, self_hbm, neigh_hbm,
    send_ref, hub_ref, base_ref, grads_ref, slots, in_sems, out_sems,
):
    staged = copies(in_sems, (send_hbm, send_ref), (hub_hbm, hub_ref), (base_hbm, base_ref))
    for peer in range(PEERS):
        slots[:, SLOTS * peer : SLOTS * (peer + 1)] = back_ref[peer, :FEATS, :]
        grads = back_ref[peer, ROWS:, :].astype(F32)
        slice_of, outs = peer // 4, 2 * (peer % 2) + peer // 2 % 2
        rows = slice(PIECE * slice_of, PIECE * (slice_of + 1))
        grads_ref[rows, TILE * outs : TILE * outs + SLOTS] = grads[:PIECE, :]
        grads_ref[rows, TILE * outs + SLOTS : TILE * (outs + 1)] = grads[PIECE:, :]
    sent = copies(
        out_sems, (grads_ref.at[:FEATS], self_hbm), (grads_ref.at[FEATS:], neigh_hbm)
    )
    sums = jnp.sum(back_ref[:, FEATS:ROWS, :].astype(F32), axis=0)
    total = sums[:, :FEATS] + sums[:, FEATS:]
    high = total.astype(BF16).astype(F32)
    hub_high = high.T.astype(BF16)
    hub_low = (total - high).T.astype(BF16)
    for copy in staged:
        copy.wait()
    for tile in range(NODES // SPREAD):
        lanes = slice(SPREAD * tile, SPREAD * (tile + 1))
        node = lax.broadcasted_iota(jnp.int32, (SPREAD, 2 * SLOTS), 0) + SPREAD * tile
        grad = base_ref[:, lanes]
        for pair in range(PEERS // 2):
            grad = grad + matmul(
                slots[:, 2 * SLOTS * pair : 2 * SLOTS * (pair + 1)],
                one_hot(node == pair_lanes(send_ref, pair)),
                NT,
            )
        hub_node = lax.broadcasted_iota(jnp.int32, (SPREAD, HUBS_OWN), 0) + SPREAD * tile
        hub_hot = one_hot(hub_node == hub_ref[...])
        grad = grad + matmul(hub_high, hub_hot, NT) + matmul(hub_low, hub_hot, NT)
        out_ref[:, lanes] = grad.astype(BF16)
    for copy in sent:
        copy.wait()


def spread_grads(returned, send_lanes, hub_own, base):
    return pl.pallas_call(
        spread_kernel,
        in_specs=[VMEM, HBM, HBM, HBM],
        out_specs=[VMEM, HBM, HBM],
        out_shape=[
            jax.ShapeDtypeStruct((FEATS, NODES), BF16),
            jax.ShapeDtypeStruct((FEATS, OUTS), F32),
            jax.ShapeDtypeStruct((FEATS, OUTS), F32),
        ],
        scratch_shapes=[
            pltpu.VMEM((PEERS, SLOTS), jnp.int32),
            pltpu.VMEM((1, HUBS_OWN), jnp.int32),
            pltpu.VMEM((FEATS, NODES), F32),
            pltpu.VMEM((2 * FEATS, OUTS), F32),
            pltpu.VMEM((FEATS, PEERS * SLOTS), BF16),
            pltpu.SemaphoreType.DMA((3,)),
            pltpu.SemaphoreType.DMA((2,)),
        ],
        compiler_params=params(16),
        cost_estimate=cost(2 * 256 * 4224 * 1024, 2 << 20),
        name="spread_grads",
    )(returned, send_lanes, hub_own, base)


SAME_CORE = [list(range(core, PEERS, 2)) for core in range(2)]


def exchange(blocks, axis, groups=None):
    return lax.all_to_all(blocks, axis, 0, 0, axis_index_groups=groups, tiled=True)


def other_core(block):
    return lax.ppermute(block, "row", [(i, i ^ 1) for i in range(PEERS)])


def per_device(feats, w_self, w_neigh, cotangent, loc_nbr, send_rows, recv_node, hub_rows, hub_nbr):
    send_lanes = send_rows.reshape(PEERS, SLOTS)
    recv_lanes = recv_node.reshape(PEERS, SLOTS)
    hub_own = hub_rows[None, :]
    half = HALF * (lax.axis_index("row") % 2)
    weights = lax.all_gather(
        lax.dynamic_slice_in_dim(jnp.concatenate([w_self, w_neigh], axis=0), half, HALF, 1),
        "col",
        axis=0,
        tiled=True,
    )
    incoming = exchange(gather_slots(feats, send_lanes, hub_own), "row")
    local, hubs = build_counts(loc_nbr, hub_nbr)
    outgoing, degree = aggregate(feats, incoming, recv_lanes, local, hubs, cotangent)
    node_block = exchange(outgoing, "col")
    own_degree = lax.dynamic_slice_in_dim(degree[0], OWN * lax.axis_index("col"), OWN)[:, None]
    joined_cols = exchange(regroup(node_block), "row").reshape(PEERS * OWN, TILE).T
    slopes_out, slopes, hidden = forward(node_block, other_core(node_block), weights)
    slopes_rows = exchange(slopes_out, "row", SAME_CORE).reshape(PEERS * OWN, TILE)
    mine, theirs, my_hidden, their_hidden = backward(slopes, hidden, weights)
    back = combine(mine, other_core(theirs), my_hidden, other_core(their_hidden), own_degree)
    back_block = exchange(weight_parts(joined_cols, slopes_rows, back), "col")
    returned = exchange(return_slots(back_block, recv_lanes, hubs), "row")
    base, hidden_out = local_grads(back_block, local)
    grad_feats, grad_self, grad_neigh = spread_grads(returned, send_lanes, hub_own, base)
    return (hidden_out, grad_feats, grad_self, grad_neigh)


def solution(mesh):
    return jax.shard_map(
        per_device,
        mesh=mesh,
        in_specs=(
            P("col", "row"),
            P("col", None),
            P("col", None),
            P("col", "row"),
            P("row", None),
            P("row", None, None),
            P("row", None, None),
            P("row"),
            P("row", None),
        ),
        out_specs=(P("col", "row"), P("col", "row"), P("col", None), P("col", None)),
        check_vma=False,
    )
```

time: 229 us -> 205 us (0.90)
  waiting for transfers between devices: 78 us -> 31.1 us
  blocking collectives: 30.2 us -> 62.1 us
  Pallas kernels: 27.4 us -> 40.6 us
  starting transfers between devices: 57 us -> 44.3 us
  local copies, waits for them, and re-layouts: 19 us -> 9.71 us
    all_gather x1, waiting for transfers between devices: 36.4 us -> 0.01 us  [per_device(): lax.all_gather(lax.dynamic_slice_in_dim(jnp.concatenate([w_self, w_neigh]...]
    all_to_all x1 -> x2, blocking collectives: 30.2 us -> 62.1 us  [exchange(): lax.all_to_all(blocks, axis, 0, 0, axis_index_groups=groups, tiled=True)]
    all_to_all x5 -> x4, waiting for transfers between devices: 41.6 us -> 29.8 us  [exchange(): lax.all_to_all(blocks, axis, 0, 0, axis_index_groups=groups, tiled=True)]
    unnamed x54 -> x30, local copies, waits for them, and re-layouts: 16.5 us -> 8.28 us
    pallas_call x6 -> x7, Pallas kernels: 14.7 us -> 22.5 us  [the longest x1 4.82 us: return_slots(): pl.pallas_call(return_kernel, in_specs=[VMEM, HBM, HBM], out_specs=HBM, o...]
    all_to_all x5 -> x4, starting transfers between devices: 45.3 us -> 37.7 us  [exchange(): lax.all_to_all(blocks, axis, 0, 0, axis_index_groups=groups, tiled=True)]
    ppermute x1 -> x3, starting transfers between devices: 11.6 us -> 6.57 us  [other_core(): return lax.ppermute(block, 'row', [(i, i ^ 1) for i in range(PEERS)])]
    pallas_call x1, Pallas kernels: 5.37 us -> 7.94 us  [build_counts(): pl.pallas_call(build_kernel, grid=(NODES // BUILD,), in_specs=[pl.BlockSp...]
  transfers between devices with their start and end apart: 7 -> 8, of which waited for: 5 -> 5; matrix products, arithmetic and copies ran while one was open for 2% -> 2% of each run, Pallas kernels for 9% -> 15%
where the time goes in v4:
time: 205 us; the launch traced here: 204 us
  blocking collectives  62.1 us (30%)
  starting transfers between devices  44.3 us (22%)
  Pallas kernels  40.6 us (20%)
  waiting for transfers between devices  31.1 us (15%)
  between operations  14.3 us (7%)
  local copies, waits for them, and re-layouts  9.71 us (5%)
    all_to_all x2, blocking collectives, exchange(): lax.all_to_all(blocks, axis, 0, 0, axis_index_groups=groups, tiled=True)  62.1 us
    all_to_all x4, starting transfers between devices, exchange(): lax.all_to_all(blocks, axis, 0, 0, axis_index_groups=groups, tiled=True)  37.7 us
    all_to_all x4, waiting for transfers between devices, exchange(): lax.all_to_all(blocks, axis, 0, 0, axis_index_groups=groups, tiled=True)  29.8 us
    unnamed x30, local copies, waits for them, and re-layouts  8.28 us
    pallas_call x1, Pallas kernels, build_counts(): pl.pallas_call(build_kernel, grid=(NODES // BUILD,), in_specs=[pl.BlockSp...  7.94 us
    ppermute x3, starting transfers between devices, other_core(): return lax.ppermute(block, 'row', [(i, i ^ 1) for i in range(PEERS)])  6.57 us
    pallas_call x1, Pallas kernels, aggregate(): pl.pallas_call(aggregate_kernel, out_shape=[jax.ShapeDtypeStruct((LAYERS,...  5.68 us
    pallas_call x1, Pallas kernels, return_slots(): pl.pallas_call(return_kernel, in_specs=[VMEM, HBM, HBM], out_specs=HBM, o...  4.82 us
  transfers between devices with their start and end apart: 8, of which 5 were waited for; matrix products, arithmetic and copies ran while one was open for 2% of the time, Pallas kernels for 15%

profile of v4, /device:TPU:1, one launch (start us, length us, event | category | flops | bytes accessed | tf_op | source)
XLA Modules:
  0.0 203.7 jit_solution(5415396544389766443)
XLA Ops:
  7.2 1.5 fusion
  8.8 3.4 %gather_slots.1 = bf16[32,80,128]{2,1,0:T(8,128)(2,1)} custom-call(bf16[64,1024]{1,0:T(8,128)(2,1)} %x_hbm.3, s32[32,128]{1,0:T(8,128)} %bitcast.12, s32[1,16]{1,0:T(1,128)} %bitcast.14), custom_call_target="tpu_custom_call" | custom-call | flops 2147483648 | bytes 1048576 | tf_op jit(solution)/shard_map/gather_slots/pallas_call | solution.py:80
  12.3 10.4 %all-to-all-start = ((bf16[32,80,128]{2,1,0:T(8,128)(2,1)}), bf16[32,80,128]{2,1,0:T(8,128)(2,1)S(1)}, u32[]{:S(2)}, u32[]{:S(2)}) async-start(bf16[32,80,128]{2,1,0:T(8,128)(2,1)} %gather_slots.1), calls=%async_computation | async-start | bytes 1310720 | tf_op jit(solution)/shard_map/all_to_all | solution.py:557
  22.7 1.0 copy.17.loc_ref
  23.7 1.0 copy.18.hub_ref
  24.8 7.9 %build_counts.1 = (bf16[1024,1024]{1,0:T(8,128)(2,1)}, bf16[1024,512]{1,0:T(8,128)(2,1)}) custom-call(s32[1024,8]{1,0:T(8,128)} %copy.17.loc_ref, s32[1024,2]{1,0:T(8,128)} %copy.18.hub_ref), custom_call_target="tpu_custom_call" | custom-call | flops 1073741824 | bytes 12582912 | tf_op jit(solution)/shard_map/build_counts/pallas_call | solution.py:113
  32.7 3.0 %all-to-all-done.inc_ref = bf16[32,80,128]{2,1,0:T(8,128)(2,1)S(1)} async-done(((bf16[32,80,128]{2,1,0:T(8,128)(2,1)}), bf16[32,80,128]{2,1,0:T(8,128)(2,1)S(1)}, u32[]{:S(2)}, u32[]{:S(2)}) %all-to-all-start) | async-done | bytes 655392 | tf_op jit(solution)/shard_map/all_to_all | solution.py:557
  35.7 1.6 copy-done.1
  37.3 1.2 copy-done.9
  38.6 5.7 %aggregate.1 = (bf16[16,96,128]{2,1,0:T(8,128)(2,1)S(1)}, f32[8,1024]{1,0:T(8,128)S(1)}) custom-call(bf16[64,1024]{1,0:T(8,128)(2,1)S(1)} %copy-done.4, bf16[32,80,128]{2,1,0:T(8,128)(2,1)S(1)} %all-to-all-done.inc_ref, s32[32,128]{1,0:T(8,128)S(1)} %bitcast.11, bf16[1024,1024]{1,0:T(8,128)(2,1)S(1)} %copy-done.1, bf16[1024,512]{1,0:T(8,128)(2,1)S(1)} %copy-done.9, ...), custom_call_target="tpu_custom_call" | custom-call | flops 2952790016 | bytes 5242880 | tf_op jit(solution)/shard_map/aggregate/pallas_call | solution.py:192
  44.3 34.8 %all_to_all.30.inc_ref.own_hbm = bf16[16,96,128]{2,1,0:T(8,128)(2,1)S(1)} all-to-all(bf16[16,96,128]{2,1,0:T(8,128)(2,1)S(1)} %get-tuple-element.22), channel_id=1, replica_groups=mesh['row'=32,'col'=16] {'col'}, dimensions={0} | all-to-all | bytes 786432 | tf_op jit(solution)/shard_map/all_to_all | solution.py:557
  79.0 1.5 regroup.1
  80.5 11.1 %all-to-all-start.2 = ((bf16[32,64,256]{2,1,0:T(8,128)(2,1)}), bf16[32,64,256]{2,1,0:T(8,128)(2,1)S(1)}, u32[]{:S(2)}, u32[]{:S(2)}) async-start(bf16[32,64,256]{2,1,0:T(8,128)(2,1)} %regroup.1), calls=%async_computation.2 | async-start | bytes 2097152 | tf_op jit(solution)/shard_map/all_to_all | solution.py:557
  91.7 2.3 %collective-permute-start = (bf16[16,96,128]{2,1,0:T(8,128)(2,1)S(1)}, bf16[16,96,128]{2,1,0:T(8,128)(2,1)S(1)}, u32[]{:S(2)}, u32[]{:S(2)}) collective-permute-start(bf16[16,96,128]{2,1,0:T(8,128)(2,1)S(1)} %all_to_all.30.inc_ref.own_hbm), channel_id=1, source_target_pairs={{0,16},{16,0},{32,48},{48,32},{64,80},{80,64},{96,112},{112,96},{1... | collective-permute-start | bytes 1179656 | tf_op jit(solution)/shard_map/ppermute | solution.py:561
  93.9 1.4 collective-permute-done.other_hbm
  96.1 3.6 %forward.1 = (bf16[16,128,256]{2,1,0:T(8,128)(2,1)}, bf16[128,512]{1,0:T(8,128)(2,1)}, bf16[2,8,32,128]{3,2,1,0:T(8,128)(2,1)}) custom-call(bf16[16,96,128]{2,1,0:T(8,128)(2,1)} %copy-done, bf16[16,96,128]{2,1,0:T(8,128)(2,1)} %copy-done.10, bf16[2048,512]{1,0:T(8,128)(2,1)} %all-gather.2.cloned.1.call-done.weights_hbm.weights_ref), custom_call_target="tpu_custom_call" | custom-call | flops 536870912 | bytes 4194304 | tf_op jit(solution)/shard_map/forward/pallas_call | solution.py:296
  99.7 9.3 %all-to-all-done.2 = bf16[32,64,256]{2,1,0:T(8,128)(2,1)S(1)} async-done(((bf16[32,64,256]{2,1,0:T(8,128)(2,1)}), bf16[32,64,256]{2,1,0:T(8,128)(2,1)S(1)}, u32[]{:S(2)}, u32[]{:S(2)}) %all-to-all-start.2) | async-done | bytes 1048608 | tf_op jit(solution)/shard_map/all_to_all | solution.py:557
  108.9 3.7 %all-to-all-start.3 = ((bf16[16,128,256]{2,1,0:T(8,128)(2,1)}), bf16[16,128,256]{2,1,0:T(8,128)(2,1)S(1)}, u32[]{:S(2)}, u32[]{:S(2)}) async-start(bf16[16,128,256]{2,1,0:T(8,128)(2,1)} %get-tuple-element.23), calls=%async_computation.3 | async-start | bytes 2097152 | tf_op jit(solution)/shard_map/all_to_all | solution.py:557
  112.6 3.6 %backward.1 = (f32[64,2048]{1,0:T(8,128)}, f32[64,2048]{1,0:T(8,128)}, bf16[8,32,128]{2,1,0:T(8,128)(2,1)}, bf16[8,32,128]{2,1,0:T(8,128)(2,1)}) custom-call(bf16[128,512]{1,0:T(8,128)(2,1)} %get-tuple-element.24.slopes_ref, bf16[2,8,32,128]{3,2,1,0:T(8,128)(2,1)} %get-tuple-element.25.hidden_ref, ...), custom_call_target="tpu_custom_call" | custom-call | flops 536870912 | bytes 4194304 | tf_op jit(solution)/shard_map/backward/pallas_call | solution.py:337
  116.2 2.3 %collective-permute-start.1 = (f32[64,2048]{1,0:T(8,128)}, f32[64,2048]{1,0:T(8,128)}, u32[]{:S(2)}, u32[]{:S(2)}) collective-permute-start(f32[64,2048]{1,0:T(8,128)} %get-tuple-element.27), channel_id=1, source_target_pairs={{0,16},{16,0},{32,48},{48,32},{64,80},{80,64},{96,112},{112,96},{1... | collective-permute-start | bytes 1572872 | tf_op jit(solution)/shard_map/ppermute | solution.py:561
  118.5 2.0 collective-permute-start.2
  122.6 2.1 %combine.1.back_hbm = bf16[16,96,128]{2,1,0:T(8,128)(2,1)} custom-call(f32[64,2048]{1,0:T(8,128)} %get-tuple-element.26.mine_ref, f32[64,2048]{1,0:T(8,128)} %collective-permute-done.1.theirs_ref, bf16[8,32,128]{2,1,0:T(8,128)(2,1)} %get-tuple-element.28.my_hidden, bf16[8,32,128]{2,1,0:T(8,128)(2,1)} %copy-done.11, f32[64,1]{1,0:T(8,128)} %copy.20.degree_ref), custom_call_target="tpu_custom_call" | custom-call | flops 1048576 | bytes 2097152 | tf_op jit(solution)/shard_map/combine/pallas_call | solution.py:361
  124.7 4.7 %all-to-all-done.3 = bf16[16,128,256]{2,1,0:T(8,128)(2,1)S(1)} async-done(((bf16[16,128,256]{2,1,0:T(8,128)(2,1)}), bf16[16,128,256]{2,1,0:T(8,128)(2,1)S(1)}, u32[]{:S(2)}, u32[]{:S(2)}) %all-to-all-start.3) | async-done | bytes 1048608 | tf_op jit(solution)/shard_map/all_to_all | solution.py:557
  129.5 1.0 copy-done.2
  130.5 1.2 weight_parts.1
  131.7 27.4 %all_to_all.31.back_ref = bf16[16,128,128]{2,1,0:T(8,128)(2,1)} all-to-all(bf16[16,128,128]{2,1,0:T(8,128)(2,1)S(1)} %weight_parts.1), channel_id=1, replica_groups=mesh['row'=32,'col'=16] {'col'}, dimensions={0} | all-to-all | bytes 1048576 | tf_op jit(solution)/shard_map/all_to_all | solution.py:557
  159.1 4.8 %return_slots.1 = bf16[32,112,128]{2,1,0:T(8,128)(2,1)} custom-call(bf16[16,128,128]{2,1,0:T(8,128)(2,1)} %all_to_all.31.back_ref, s32[32,128]{1,0:T(8,128)} %bitcast.10, bf16[1024,512]{1,0:T(8,128)(2,1)} %get-tuple-element.21.hubs_hbm), custom_call_target="tpu_custom_call" | custom-call | flops 2415919104 | bytes 3145728 | tf_op jit(solution)/shard_map/return_slots/pallas_call | solution.py:445
  163.9 12.4 %all-to-all-start.5 = ((bf16[32,112,128]{2,1,0:T(8,128)(2,1)}), bf16[32,112,128]{2,1,0:T(8,128)(2,1)S(1)}, u32[]{:S(2)}, u32[]{:S(2)}) async-start(bf16[32,112,128]{2,1,0:T(8,128)(2,1)} %return_slots.1), calls=%async_computation.5 | async-start | bytes 1835008 | tf_op jit(solution)/shard_map/all_to_all | solution.py:557
  176.4 3.0 %local_grads.1 = (f32[64,1024]{1,0:T(8,128)}, bf16[64,1024]{1,0:T(8,128)(2,1)}) custom-call(bf16[16,128,128]{2,1,0:T(8,128)(2,1)} %all_to_all.31.back_ref, bf16[1024,1024]{1,0:T(8,128)(2,1)} %get-tuple-element.20.local_hbm.local_ref), custom_call_target="tpu_custom_call" | custom-call | flops 536870912 | bytes 3145728 | tf_op jit(solution)/shard_map/local_grads/pallas_call | solution.py:473
  179.4 12.7 %all-to-all-done.5.back_ref = bf16[32,112,128]{2,1,0:T(8,128)(2,1)S(1)} async-done(((bf16[32,112,128]{2,1,0:T(8,128)(2,1)}), bf16[32,112,128]{2,1,0:T(8,128)(2,1)S(1)}, u32[]{:S(2)}, u32[]{:S(2)}) %all-to-all-start.5) | async-done | bytes 917536 | tf_op jit(solution)/shard_map/all_to_all | solution.py:557
  192.1 0.9 copy-done.3
  193.1 3.7 %spread_grads.1 = (bf16[64,1024]{1,0:T(8,128)(2,1)}, f32[64,1024]{1,0:T(8,128)}, f32[64,1024]{1,0:T(8,128)}) custom-call(bf16[32,112,128]{2,1,0:T(8,128)(2,1)S(1)} %all-to-all-done.5.back_ref, s32[32,128]{1,0:T(8,128)S(1)} %bitcast.13, s32[1,16]{1,0:T(1,128)S(1)} %bitcast.15, f32[64,1024]{1,0:T(8,128)S(1)} %copy-done.3), custom_call_target="tpu_custom_call" | custom-call | flops 2214592512 | bytes 2097152 | tf_op jit(solution)/shard_map/spread_grads/pallas_call | solution.py:529
  (33 shorter events, 2.9 us)
Async XLA Ops:
  7.2 88.1 %all-gather.2.cloned.1.call-start = ((), (), s32[]{:S(2)}) async-start(), calls=%async_computation.6 | async-start | bytes 2228224 | tf_op jit(solution)/shard_map/all_gather | solution.py:569
  8.8 13.9 %copy-start.12 = (s32[1024,8]{0,1:T(8,128)S(1)}, s32[1024,8]{0,1:T(8,128)}, u32[]{:S(2)}) copy-start(s32[1024,8]{0,1:T(8,128)} %param.13) | copy-start | bytes 98308
  8.8 14.9 %copy-start.13 = (s32[1024,2]{0,1:T(2,128)S(1)}, s32[1024,2]{0,1:T(2,128)}, u32[]{:S(2)}) copy-start(s32[1024,2]{0,1:T(2,128)} %param.17) | copy-start | bytes 24580
  12.3 23.5 %all-to-all-start = ((bf16[32,80,128]{2,1,0:T(8,128)(2,1)}), bf16[32,80,128]{2,1,0:T(8,128)(2,1)S(1)}, u32[]{:S(2)}, u32[]{:S(2)}) async-start(bf16[32,80,128]{2,1,0:T(8,128)(2,1)} %gather_slots.1), calls=%async_computation | async-start | bytes 1310720 | tf_op jit(solution)/shard_map/all_to_all | solution.py:557
  24.8 10.9 %copy-start.4 = (bf16[64,1024]{1,0:T(8,128)(2,1)S(1)}, bf16[64,1024]{1,0:T(8,128)(2,1)}, u32[]{:S(2)}) copy-start(bf16[64,1024]{1,0:T(8,128)(2,1)} %x_hbm.3) | copy-start | bytes 393220
  24.8 10.9 %copy-start.5 = (bf16[64,1024]{1,0:T(8,128)(2,1)S(1)}, bf16[64,1024]{1,0:T(8,128)(2,1)}, u32[]{:S(2)}) copy-start(bf16[64,1024]{1,0:T(8,128)(2,1)} %cot_hbm.1) | copy-start | bytes 393220
  24.8 10.9 %copy-start.6 = (s32[1,32,128]{2,1,0:T(8,128)S(1)}, s32[1,32,128]{2,1,0:T(8,128)}, u32[]{:S(2)}) copy-start(s32[1,32,128]{2,1,0:T(8,128)} %param.15) | copy-start | bytes 49156
  35.7 1.6 copy-start.1
  37.3 1.2 copy-start.9
  79.0 16.3 %copy-start = (bf16[16,96,128]{2,1,0:T(8,128)(2,1)}, bf16[16,96,128]{2,1,0:T(8,128)(2,1)S(1)}, u32[]{:S(2)}) copy-start(bf16[16,96,128]{2,1,0:T(8,128)(2,1)S(1)} %all_to_all.30.inc_ref.own_hbm) | copy-start | bytes 1179652
  80.5 28.4 %all-to-all-start.2 = ((bf16[32,64,256]{2,1,0:T(8,128)(2,1)}), bf16[32,64,256]{2,1,0:T(8,128)(2,1)S(1)}, u32[]{:S(2)}, u32[]{:S(2)}) async-start(bf16[32,64,256]{2,1,0:T(8,128)(2,1)} %regroup.1), calls=%async_computation.2 | async-start | bytes 2097152 | tf_op jit(solution)/shard_map/all_to_all | solution.py:557
  91.7 3.6 %collective-permute-start = (bf16[16,96,128]{2,1,0:T(8,128)(2,1)S(1)}, bf16[16,96,128]{2,1,0:T(8,128)(2,1)S(1)}, u32[]{:S(2)}, u32[]{:S(2)}) collective-permute-start(bf16[16,96,128]{2,1,0:T(8,128)(2,1)S(1)} %all_to_all.30.inc_ref.own_hbm), channel_id=1, source_target_pairs={{0,16},{16,0},{32,48},{48,32},{64,80},{80,64},{96,112},{112,96},{1... | collective-permute-start | bytes 1179656 | tf_op jit(solution)/shard_map/ppermute | solution.py:561
  95.3 0.8 copy-start.10
  108.9 20.5 %all-to-all-start.3 = ((bf16[16,128,256]{2,1,0:T(8,128)(2,1)}), bf16[16,128,256]{2,1,0:T(8,128)(2,1)S(1)}, u32[]{:S(2)}, u32[]{:S(2)}) async-start(bf16[16,128,256]{2,1,0:T(8,128)(2,1)} %get-tuple-element.23), calls=%async_computation.3 | async-start | bytes 2097152 | tf_op jit(solution)/shard_map/all_to_all | solution.py:557
  116.2 5.8 %collective-permute-start.1 = (f32[64,2048]{1,0:T(8,128)}, f32[64,2048]{1,0:T(8,128)}, u32[]{:S(2)}, u32[]{:S(2)}) collective-permute-start(f32[64,2048]{1,0:T(8,128)} %get-tuple-element.27), channel_id=1, source_target_pairs={{0,16},{16,0},{32,48},{48,32},{64,80},{80,64},{96,112},{112,96},{1... | collective-permute-start | bytes 1572872 | tf_op jit(solution)/shard_map/ppermute | solution.py:561
  118.5 3.5 %collective-permute-start.2 = (bf16[8,32,128]{2,1,0:T(8,128)(2,1)}, bf16[8,32,128]{2,1,0:T(8,128)(2,1)S(1)}, u32[]{:S(2)}, u32[]{:S(2)}) collective-permute-start(bf16[8,32,128]{2,1,0:T(8,128)(2,1)} %get-tuple-element.29), channel_id=1, source_target_pairs={{0,16},{16,0},{32,48},{48,32},{64,80},{80,64},{96,112},{112,96},{1... | collective-permute-start | bytes 196616 | tf_op jit(solution)/shard_map/ppermute | solution.py:561
  122.0 0.6 copy-start.11
  129.5 1.0 copy-start.2
  163.9 28.2 %copy-start.7 = (s32[1,32,128]{2,1,0:T(8,128)S(1)}, s32[1,32,128]{2,1,0:T(8,128)}, u32[]{:S(2)}) copy-start(s32[1,32,128]{2,1,0:T(8,128)} %param.14) | copy-start | bytes 49156
  163.9 28.2 %copy-start.8 = (s32[16]{0:T(128)S(1)}, s32[16]{0:T(128)}, u32[]{:S(2)}) copy-start(s32[16]{0:T(128)} %param.16) | copy-start | bytes 196
  163.9 28.2 %all-to-all-start.5 = ((bf16[32,112,128]{2,1,0:T(8,128)(2,1)}), bf16[32,112,128]{2,1,0:T(8,128)(2,1)S(1)}, u32[]{:S(2)}, u32[]{:S(2)}) async-start(bf16[32,112,128]{2,1,0:T(8,128)(2,1)} %return_slots.1), calls=%async_computation.5 | async-start | bytes 1835008 | tf_op jit(solution)/shard_map/all_to_all | solution.py:557
  192.1 1.0 copy-start.3
Sparse Core Ops, SparseCore 0:
  10.7 81.4 all-gather.1

commit v5 on v4

--- a/solution.py
+++ b/solution.py
@@ -93,42 +93,47 @@
     )(feats, send_lanes, hub_own)
 
 
-BUILD = 128
-
-
-def build_kernel(loc_ref, hub_ref, local_ref, hubs_ref):
-    lane = lax.broadcasted_iota(jnp.int32, (BUILD, NODES), 1)
-    counts = jnp.zeros((BUILD, NODES), F32)
-    for k in range(loc_ref.shape[1]):
-        counts = counts + jnp.where(lane == loc_ref[:, k : k + 1], 1.0, 0.0)
-    local_ref[...] = counts.astype(BF16)
-    hub_lane = lax.broadcasted_iota(jnp.int32, (BUILD, HUBS), 1)
-    hub_counts = jnp.zeros((BUILD, HUBS), F32)
-    for k in range(hub_ref.shape[1]):
-        hub_counts = hub_counts + jnp.where(hub_lane == hub_ref[:, k : k + 1], 1.0, 0.0)
-    hubs_ref[...] = hub_counts.astype(BF16)
-
-
-def build_counts(loc_nbr, hub_nbr):
+BUILD = 256
+
+
+def counts_of(nbr_ref, rows):
+    first = lax.broadcasted_iota(jnp.int32, (rows, nbr_ref.shape[1]), 0)
+    counts = jnp.zeros(first.shape, F32)
+    for k in range(nbr_ref.shape[0]):
+        counts = counts + jnp.where(first == nbr_ref[k : k + 1, :], 1.0, 0.0)
+    return counts.astype(BF16)
+
+
+def build_kernel(x_ref, loc_ref, hub_ref, local_ref, hubs_ref, sum_ref):
+    counts = counts_of(loc_ref, NODES)
+    local_ref[...] = counts
+    hubs_ref[...] = counts_of(hub_ref, HUBS)
+    sum_ref[...] = matmul(x_ref[...], counts, NN)
+
+
+def build_counts(feats, loc_lanes, hub_lanes):
     return pl.pallas_call(
         build_kernel,
         grid=(NODES // BUILD,),
         in_specs=[
-            pl.BlockSpec((BUILD, loc_nbr.shape[1]), lambda i: (i, 0)),
-            pl.BlockSpec((BUILD, hub_nbr.shape[1]), lambda i: (i, 0)),
+            whole((FEATS, NODES)),
+            pl.BlockSpec((loc_lanes.shape[0], BUILD), lambda i: (0, i)),
+            pl.BlockSpec((hub_lanes.shape[0], BUILD), lambda i: (0, i)),
         ],
         out_specs=[
-            pl.BlockSpec((BUILD, NODES), lambda i: (i, 0)),
-            pl.BlockSpec((BUILD, HUBS), lambda i: (i, 0)),
+            pl.BlockSpec((NODES, BUILD), lambda i: (0, i)),
+            pl.BlockSpec((HUBS, BUILD), lambda i: (0, i)),
+            pl.BlockSpec((FEATS, BUILD), lambda i: (0, i)),
         ],
         out_shape=[
             jax.ShapeDtypeStruct((NODES, NODES), BF16),
-            jax.ShapeDtypeStruct((NODES, HUBS), BF16),
+            jax.ShapeDtypeStruct((HUBS, NODES), BF16),
+            jax.ShapeDtypeStruct((FEATS, NODES), F32),
         ],
         compiler_params=params(60),
-        cost_estimate=cost(1 << 30, 12 << 20),
+        cost_estimate=cost(1 << 30, 4 << 20),
         name="build_counts",
-    )(loc_nbr, hub_nbr)
+    )(feats, loc_lanes, hub_lanes)
 
 
 AGG = 256
@@ -142,16 +147,16 @@
 
 
 def aggregate_kernel(
-    x_hbm, inc_ref, recv_hbm, local_hbm, hubs_hbm, cot_hbm, out_ref, degree_ref,
-    slots, table, recv_ref, x_ref, local_ref, hubs_ref, cot_ref, sems,
+    x_hbm, inc_ref, recv_hbm, sum_hbm, hub_hbm, cot_hbm, out_ref, degree_ref,
+    slots, table, recv_ref, hub_ref, x_ref, cot_ref, sum_ref, sems,
 ):
     staged = copies(
         sems,
         (recv_hbm, recv_ref),
+        (hub_hbm, hub_ref),
         (x_hbm, x_ref),
-        (local_hbm, local_ref),
-        (hubs_hbm, hubs_ref),
         (cot_hbm, cot_ref),
+        (sum_hbm, sum_ref),
     )
     for peer in range(PEERS):
         slots[:FEATS, SLOTS * peer : SLOTS * (peer + 1)] = inc_ref[peer, :FEATS, :]
@@ -172,11 +177,8 @@
         if tile == 0:
             for copy in staged[1:]:
                 copy.wait()
-        total = (
-            remote[:FEATS, :]
-            + matmul(x_ref[...], local_ref[lanes, :], NT)
-            + matmul(table[...], hubs_ref[lanes, :], NT)
-        )
+        hubs = counts_of(hub_ref[:, lanes], HUBS)
+        total = remote[:FEATS, :] + sum_ref[:, lanes] + matmul(table[...], hubs, NN)
         degree = remote[FEATS : FEATS + 8, :] + NEIGHBOURS
         degree_ref[:, lanes] = degree
         mean = (total / degree[0:1, :]).T
@@ -188,7 +190,7 @@
             out_ref[layer, OWN:, :] = fold_halves(slopes[OWN * part : OWN * (part + 1), :]).astype(BF16)
 
 
-def aggregate(feats, incoming, recv_lanes, local, hubs, cotangent):
+def aggregate(feats, incoming, recv_lanes, local_sum, hub_lanes, cotangent):
     return pl.pallas_call(
         aggregate_kernel,
         out_shape=[
@@ -200,16 +202,16 @@
             pltpu.VMEM((ROWS, PEERS * SLOTS), BF16),
             pltpu.VMEM((FEATS, HUBS), BF16),
             pltpu.VMEM((PEERS, SLOTS), jnp.int32),
+            pltpu.VMEM((2, NODES), jnp.int32),
             pltpu.VMEM((FEATS, NODES), BF16),
-            pltpu.VMEM((NODES, NODES), BF16),
-            pltpu.VMEM((NODES, HUBS), BF16),
             pltpu.VMEM((FEATS, NODES), BF16),
+            pltpu.VMEM((FEATS, NODES), F32),
             pltpu.SemaphoreType.DMA((5,)),
         ],
         compiler_params=params(16),
-        cost_estimate=cost(2 * 256 * 5632 * 1024, 5 << 20),
+        cost_estimate=cost(2 * 256 * 5632 * 1024, 3 << 20),
         name="aggregate",
-    )(feats, incoming, recv_lanes, local, hubs, cotangent)
+    )(feats, incoming, recv_lanes, local_sum, hub_lanes, cotangent)
 
 
 PIECE = 16
@@ -338,7 +340,7 @@
         backward_kernel,
         out_shape=[part, part, block, block],
         scratch_shapes=[pltpu.VMEM((2, OWN, 2 * OUTS), F32)],
-        compiler_params=params(60),
+        compiler_params=params(16),
         cost_estimate=cost(2 * 256 * 2048 * 512, 4 << 20),
         name="backward",
     )(slopes, hidden, weights)
@@ -361,7 +363,7 @@
     return pl.pallas_call(
         combine_kernel,
         out_shape=jax.ShapeDtypeStruct((LAYERS, 96, SLOTS), BF16),
-        compiler_params=params(60),
+        compiler_params=params(16),
         cost_estimate=cost(1 << 20, 2 << 20),
         name="combine",
     )(mine, theirs, my_hidden, their_hidden, own_degree)
@@ -426,9 +428,9 @@
             peer = 2 * pair + side
             out_ref[peer, :FEATS, :] = values[:, SLOTS * side : SLOTS * (side + 1)]
             out_ref[peer, ROWS:, :] = sums
-        if pair == 0:
+        if pair == 3:
             staged[1].wait()
-            terms = matmul(share, hubs_ref[...], NN).T
+            terms = matmul(share, hubs_ref[...], NT).T
             high = terms.astype(BF16).astype(F32)
             both = jnp.concatenate([high, terms - high], axis=1)
             out_ref[:, FEATS:ROWS, :] = both.reshape(PEERS, HUBS_OWN, SLOTS).astype(BF16)
@@ -449,7 +451,7 @@
         out_shape=jax.ShapeDtypeStruct((PEERS, RETURN_ROWS, SLOTS), BF16),
         scratch_shapes=[
             pltpu.VMEM((PEERS, SLOTS), jnp.int32),
-            pltpu.VMEM((NODES, HUBS), BF16),
+            pltpu.VMEM((HUBS, NODES), BF16),
             pltpu.VMEM((PEERS, RETURN_ROWS, SLOTS), BF16),
             pltpu.SemaphoreType.DMA((2,)),
             pltpu.SemaphoreType.DMA((4,)),
@@ -463,7 +465,7 @@
 def local_kernel(back_ref, local_ref, base_ref, hidden_ref):
     columns = back_ref[:, :OWN, :].astype(F32).reshape(NODES, SLOTS).T
     share = columns[FEATS:, :].astype(BF16)
-    base_ref[...] = columns[:FEATS, :] + matmul(share, local_ref[...], NN)
+    base_ref[...] = columns[:FEATS, :] + matmul(share, local_ref[...], NT)
     folded = back_ref[:, OWN:96, :].astype(F32)
     rows = jnp.concatenate([folded[:, :, :FEATS], folded[:, :, FEATS:]], axis=1)
     hidden_ref[...] = rows.reshape(NODES, FEATS).T.astype(BF16)
@@ -573,8 +575,9 @@
         tiled=True,
     )
     incoming = exchange(gather_slots(feats, send_lanes, hub_own), "row")
-    local, hubs = build_counts(loc_nbr, hub_nbr)
-    outgoing, degree = aggregate(feats, incoming, recv_lanes, local, hubs, cotangent)
+    hub_lanes = hub_nbr.T
+    local, hubs, local_sum = build_counts(feats, loc_nbr.T, hub_lanes)
+    outgoing, degree = aggregate(feats, incoming, recv_lanes, local_sum, hub_lanes, cotangent)
     node_block = exchange(outgoing, "col")
     own_degree = lax.dynamic_slice_in_dim(degree[0], OWN * lax.axis_index("col"), OWN)[:, None]
     joined_cols = exchange(regroup(node_block), "row").reshape(PEERS * OWN, TILE).T

time: 205 us -> 201 us (0.980)
  Pallas kernels: 40.6 us -> 34.7 us
  blocking collectives: 62.1 us -> 65.3 us
  local copies, waits for them, and re-layouts: 9.71 us -> 6.88 us
    all_to_all x2, blocking collectives: 62.1 us -> 65.3 us  [exchange(): lax.all_to_all(blocks, axis, 0, 0, axis_index_groups=groups, tiled=True)]
    unnamed x30 -> x36, local copies, waits for them, and re-layouts: 8.28 us -> 5.22 us
    ppermute x3, starting transfers between devices: 6.57 us -> 8.89 us  [other_core(): return lax.ppermute(block, 'row', [(i, i ^ 1) for i in range(PEERS)])]
  transfers between devices with their start and end apart: 8 -> 8, of which waited for: 5 -> 6; matrix products, arithmetic and copies ran while one was open for 2% -> 1% of each run, Pallas kernels for 15% -> 12%
where the time goes in v5:
time: 201 us; the launch traced here: 200 us
  blocking collectives  65.3 us (32%)
  starting transfers between devices  46 us (23%)
  Pallas kernels  34.7 us (17%)
  waiting for transfers between devices  31.6 us (16%)
  between operations  14.3 us (7%)
  local copies, waits for them, and re-layouts  6.88 us (3%)
    all_to_all x2, blocking collectives, exchange(): lax.all_to_all(blocks, axis, 0, 0, axis_index_groups=groups, tiled=True)  65.3 us
    all_to_all x4, starting transfers between devices, exchange(): lax.all_to_all(blocks, axis, 0, 0, axis_index_groups=groups, tiled=True)  37.1 us
    all_to_all x4, waiting for transfers between devices, exchange(): lax.all_to_all(blocks, axis, 0, 0, axis_index_groups=groups, tiled=True)  29.2 us
    ppermute x3, starting transfers between devices, other_core(): return lax.ppermute(block, 'row', [(i, i ^ 1) for i in range(PEERS)])  8.89 us
    pallas_call x1, Pallas kernels, build_counts(): pl.pallas_call(build_kernel, grid=(NODES // BUILD,), in_specs=[whole((FEA...  6.18 us
    unnamed x36, local copies, waits for them, and re-layouts  5.22 us
    pallas_call x1, Pallas kernels, aggregate(): pl.pallas_call(aggregate_kernel, out_shape=[jax.ShapeDtypeStruct((LAYERS,...  4.92 us
    pallas_call x1, Pallas kernels, return_slots(): pl.pallas_call(return_kernel, in_specs=[VMEM, HBM, HBM], out_specs=HBM, o...  4.82 us
  transfers between devices with their start and end apart: 8, of which 6 were waited for; matrix products, arithmetic and copies ran while one was open for 1% of the time, Pallas kernels for 12%

profile of v5, /device:TPU:1, one launch (start us, length us, event | category | flops | bytes accessed | tf_op | source)
XLA Modules:
  0.0 200.4 jit_solution(15919380836874410186)
XLA Ops:
  7.2 1.5 fusion
  8.8 3.4 %gather_slots.1 = bf16[32,80,128]{2,1,0:T(8,128)(2,1)} custom-call(bf16[64,1024]{1,0:T(8,128)(2,1)} %x_hbm.3, s32[32,128]{1,0:T(8,128)} %bitcast.14, s32[1,16]{1,0:T(1,128)} %bitcast.18), custom_call_target="tpu_custom_call" | custom-call | flops 2147483648 | bytes 1048576 | tf_op jit(solution)/shard_map/gather_slots/pallas_call | solution.py:80
  12.2 10.4 %all-to-all-start = ((bf16[32,80,128]{2,1,0:T(8,128)(2,1)}), bf16[32,80,128]{2,1,0:T(8,128)(2,1)S(1)}, u32[]{:S(2)}, u32[]{:S(2)}) async-start(bf16[32,80,128]{2,1,0:T(8,128)(2,1)} %gather_slots.1), calls=%async_computation | async-start | bytes 1310720 | tf_op jit(solution)/shard_map/all_to_all | solution.py:559
  22.7 6.2 %build_counts.1 = (bf16[1024,1024]{1,0:T(8,128)(2,1)}, bf16[512,1024]{1,0:T(8,128)(2,1)}, f32[64,1024]{1,0:T(8,128)}) custom-call(bf16[64,1024]{1,0:T(8,128)(2,1)} %x_hbm.3, s32[8,1024]{1,0:T(8,128)} %bitcast.20, s32[2,1024]{1,0:T(2,128)} %bitcast.16), custom_call_target="tpu_custom_call" | custom-call | flops 1073741824 | bytes 4194304 | tf_op jit(solution)/shard_map/build_counts/pallas_call | solution.py:115
  28.9 6.8 %all-to-all-done.inc_ref = bf16[32,80,128]{2,1,0:T(8,128)(2,1)S(1)} async-done(((bf16[32,80,128]{2,1,0:T(8,128)(2,1)}), bf16[32,80,128]{2,1,0:T(8,128)(2,1)S(1)}, u32[]{:S(2)}, u32[]{:S(2)}) %all-to-all-start) | async-done | bytes 655392 | tf_op jit(solution)/shard_map/all_to_all | solution.py:559
  35.7 0.9 copy-done.16
  36.7 4.9 %aggregate.1 = (bf16[16,96,128]{2,1,0:T(8,128)(2,1)S(1)}, f32[8,1024]{1,0:T(8,128)S(1)}) custom-call(bf16[64,1024]{1,0:T(8,128)(2,1)S(1)} %copy-done.9, bf16[32,80,128]{2,1,0:T(8,128)(2,1)S(1)} %all-to-all-done.inc_ref, s32[32,128]{1,0:T(8,128)S(1)} %bitcast.13, f32[64,1024]{1,0:T(8,128)S(1)} %copy-done.16, s32[2,1024]{1,0:T(2,128)S(1)} %bitcast.17, ...), custom_call_target="tpu_custom_call" | custom-call | flops 2952790016 | bytes 3145728 | tf_op jit(solution)/shard_map/aggregate/pallas_call | solution.py:194
  41.6 36.0 %all_to_all.30.inc_ref.own_hbm = bf16[16,96,128]{2,1,0:T(8,128)(2,1)S(1)} all-to-all(bf16[16,96,128]{2,1,0:T(8,128)(2,1)S(1)} %get-tuple-element.22), channel_id=1, replica_groups=mesh['row'=32,'col'=16] {'col'}, dimensions={0} | all-to-all | bytes 786432 | tf_op jit(solution)/shard_map/all_to_all | solution.py:559
  77.6 1.6 regroup.1
  79.2 9.8 %all-to-all-start.2 = ((bf16[32,64,256]{2,1,0:T(8,128)(2,1)}), bf16[32,64,256]{2,1,0:T(8,128)(2,1)}, u32[]{:S(2)}, u32[]{:S(2)}) async-start(bf16[32,64,256]{2,1,0:T(8,128)(2,1)} %regroup.1), calls=%async_computation.2 | async-start | bytes 2097152 | tf_op jit(solution)/shard_map/all_to_all | solution.py:559
  89.0 2.2 %collective-permute-start = (bf16[16,96,128]{2,1,0:T(8,128)(2,1)S(1)}, bf16[16,96,128]{2,1,0:T(8,128)(2,1)S(1)}, u32[]{:S(2)}, u32[]{:S(2)}) collective-permute-start(bf16[16,96,128]{2,1,0:T(8,128)(2,1)S(1)} %all_to_all.30.inc_ref.own_hbm), channel_id=1, source_target_pairs={{0,16},{16,0},{32,48},{48,32},{64,80},{80,64},{96,112},{112,96},{1... | collective-permute-start | bytes 1179656 | tf_op jit(solution)/shard_map/ppermute | solution.py:563
  91.2 1.4 collective-permute-done.other_hbm
  92.6 1.0 all-gather.2.cloned.1.call-done.weights_hbm.weights_ref
  93.6 3.7 %forward.1 = (bf16[16,128,256]{2,1,0:T(8,128)(2,1)}, bf16[128,512]{1,0:T(8,128)(2,1)}, bf16[2,8,32,128]{3,2,1,0:T(8,128)(2,1)}) custom-call(bf16[16,96,128]{2,1,0:T(8,128)(2,1)} %copy-done.1, bf16[16,96,128]{2,1,0:T(8,128)(2,1)} %copy-done.17, bf16[2048,512]{1,0:T(8,128)(2,1)} %all-gather.2.cloned.1.call-done.weights_hbm.weights_ref), custom_call_target="tpu_custom_call" | custom-call | flops 536870912 | bytes 4194304 | tf_op jit(solution)/shard_map/forward/pallas_call | solution.py:298
  97.4 8.8 %all-to-all-done.2 = bf16[32,64,256]{2,1,0:T(8,128)(2,1)} async-done(((bf16[32,64,256]{2,1,0:T(8,128)(2,1)}), bf16[32,64,256]{2,1,0:T(8,128)(2,1)}, u32[]{:S(2)}, u32[]{:S(2)}) %all-to-all-start.2) | async-done | bytes 1048608 | tf_op jit(solution)/shard_map/all_to_all | solution.py:559
  106.2 3.7 %all-to-all-start.3 = ((bf16[16,128,256]{2,1,0:T(8,128)(2,1)}), bf16[16,128,256]{2,1,0:T(8,128)(2,1)S(1)}, u32[]{:S(2)}, u32[]{:S(2)}) async-start(bf16[16,128,256]{2,1,0:T(8,128)(2,1)} %get-tuple-element.23), calls=%async_computation.3 | async-start | bytes 2097152 | tf_op jit(solution)/shard_map/all_to_all | solution.py:559
  109.9 1.7 backward.1
  111.5 0.8 copy-done.2
  113.0 4.8 %collective-permute-start.1 = (f32[64,2048]{1,0:T(8,128)}, f32[64,2048]{1,0:T(8,128)S(1)}, u32[]{:S(2)}, u32[]{:S(2)}) collective-permute-start(f32[64,2048]{1,0:T(8,128)} %get-tuple-element.27), channel_id=1, source_target_pairs={{0,16},{16,0},{32,48},{48,32},{64,80},{80,64},{96,112},{112,96},{1... | collective-permute-start | bytes 1572872 | tf_op jit(solution)/shard_map/ppermute | solution.py:563
  117.8 1.9 collective-permute-start.2
  119.9 1.5 copy.15
  121.4 0.8 copy-done.4
  122.2 1.0 copy-done.5
  123.3 1.1 all-to-all-done.3
  124.4 1.2 weight_parts.1
  125.7 29.4 %all_to_all.31.back_ref = bf16[16,128,128]{2,1,0:T(8,128)(2,1)} all-to-all(bf16[16,128,128]{2,1,0:T(8,128)(2,1)S(1)} %weight_parts.1), channel_id=1, replica_groups=mesh['row'=32,'col'=16] {'col'}, dimensions={0} | all-to-all | bytes 1048576 | tf_op jit(solution)/shard_map/all_to_all | solution.py:559
  155.0 4.8 %return_slots.1 = bf16[32,112,128]{2,1,0:T(8,128)(2,1)} custom-call(bf16[16,128,128]{2,1,0:T(8,128)(2,1)} %all_to_all.31.back_ref, s32[32,128]{1,0:T(8,128)} %bitcast.12, bf16[512,1024]{1,0:T(8,128)(2,1)} %get-tuple-element.33.hubs_hbm), custom_call_target="tpu_custom_call" | custom-call | flops 2415919104 | bytes 3145728 | tf_op jit(solution)/shard_map/return_slots/pallas_call | solution.py:447
  159.9 13.2 %all-to-all-start.5 = ((bf16[32,112,128]{2,1,0:T(8,128)(2,1)}), bf16[32,112,128]{2,1,0:T(8,128)(2,1)S(1)}, u32[]{:S(2)}, u32[]{:S(2)}) async-start(bf16[32,112,128]{2,1,0:T(8,128)(2,1)} %return_slots.1), calls=%async_computation.5 | async-start | bytes 1835008 | tf_op jit(solution)/shard_map/all_to_all | solution.py:559
  173.1 3.3 %local_grads.1 = (f32[64,1024]{1,0:T(8,128)}, bf16[64,1024]{1,0:T(8,128)(2,1)}) custom-call(bf16[16,128,128]{2,1,0:T(8,128)(2,1)} %all_to_all.31.back_ref, bf16[1024,1024]{1,0:T(8,128)(2,1)} %get-tuple-element.31.local_ref), custom_call_target="tpu_custom_call" | custom-call | flops 536870912 | bytes 3145728 | tf_op jit(solution)/shard_map/local_grads/pallas_call | solution.py:475
  176.4 12.5 %all-to-all-done.5.back_ref = bf16[32,112,128]{2,1,0:T(8,128)(2,1)S(1)} async-done(((bf16[32,112,128]{2,1,0:T(8,128)(2,1)}), bf16[32,112,128]{2,1,0:T(8,128)(2,1)S(1)}, u32[]{:S(2)}, u32[]{:S(2)}) %all-to-all-start.5) | async-done | bytes 917536 | tf_op jit(solution)/shard_map/all_to_all | solution.py:559
  188.9 0.9 copy-done.8
  189.8 3.7 %spread_grads.1 = (bf16[64,1024]{1,0:T(8,128)(2,1)}, f32[64,1024]{1,0:T(8,128)}, f32[64,1024]{1,0:T(8,128)}) custom-call(bf16[32,112,128]{2,1,0:T(8,128)(2,1)S(1)} %all-to-all-done.5.back_ref, s32[32,128]{1,0:T(8,128)S(1)} %bitcast.15, s32[1,16]{1,0:T(1,128)S(1)} %bitcast.19, f32[64,1024]{1,0:T(8,128)S(1)} %copy-done.8), custom_call_target="tpu_custom_call" | custom-call | flops 2214592512 | bytes 2097152 | tf_op jit(solution)/shard_map/spread_grads/pallas_call | solution.py:531
  (39 shorter events, 1.1 us)
Async XLA Ops:
  7.2 86.4 %all-gather.2.cloned.1.call-start = ((), (), s32[]{:S(2)}) async-start(), calls=%async_computation.6 | async-start | bytes 2228224 | tf_op jit(solution)/shard_map/all_gather | solution.py:571
  12.2 23.5 %all-to-all-start = ((bf16[32,80,128]{2,1,0:T(8,128)(2,1)}), bf16[32,80,128]{2,1,0:T(8,128)(2,1)S(1)}, u32[]{:S(2)}, u32[]{:S(2)}) async-start(bf16[32,80,128]{2,1,0:T(8,128)(2,1)} %gather_slots.1), calls=%async_computation | async-start | bytes 1310720 | tf_op jit(solution)/shard_map/all_to_all | solution.py:559
  22.7 13.0 %copy-start.9 = (bf16[64,1024]{1,0:T(8,128)(2,1)S(1)}, bf16[64,1024]{1,0:T(8,128)(2,1)}, u32[]{:S(2)}) copy-start(bf16[64,1024]{1,0:T(8,128)(2,1)} %x_hbm.3) | copy-start | bytes 393220
  22.7 13.0 %copy-start.10 = (bf16[64,1024]{1,0:T(8,128)(2,1)S(1)}, bf16[64,1024]{1,0:T(8,128)(2,1)}, u32[]{:S(2)}) copy-start(bf16[64,1024]{1,0:T(8,128)(2,1)} %cot_hbm.1) | copy-start | bytes 393220
  22.7 13.0 %copy-start.12 = (s32[1,32,128]{2,1,0:T(8,128)S(1)}, s32[1,32,128]{2,1,0:T(8,128)}, u32[]{:S(2)}) copy-start(s32[1,32,128]{2,1,0:T(8,128)} %param.15) | copy-start | bytes 49156
  22.7 13.0 %copy-start.14 = (s32[1024,2]{0,1:T(2,128)S(1)}, s32[1024,2]{0,1:T(2,128)}, u32[]{:S(2)}) copy-start(s32[1024,2]{0,1:T(2,128)} %param.17) | copy-start | bytes 24580
  35.7 1.0 copy-start.16
  77.6 16.0 %copy-start.1 = (bf16[16,96,128]{2,1,0:T(8,128)(2,1)}, bf16[16,96,128]{2,1,0:T(8,128)(2,1)S(1)}, u32[]{:S(2)}) copy-start(bf16[16,96,128]{2,1,0:T(8,128)(2,1)S(1)} %all_to_all.30.inc_ref.own_hbm) | copy-start | bytes 1179652
  79.2 27.0 %all-to-all-start.2 = ((bf16[32,64,256]{2,1,0:T(8,128)(2,1)}), bf16[32,64,256]{2,1,0:T(8,128)(2,1)}, u32[]{:S(2)}, u32[]{:S(2)}) async-start(bf16[32,64,256]{2,1,0:T(8,128)(2,1)} %regroup.1), calls=%async_computation.2 | async-start | bytes 2097152 | tf_op jit(solution)/shard_map/all_to_all | solution.py:559
  89.0 3.6 %collective-permute-start = (bf16[16,96,128]{2,1,0:T(8,128)(2,1)S(1)}, bf16[16,96,128]{2,1,0:T(8,128)(2,1)S(1)}, u32[]{:S(2)}, u32[]{:S(2)}) collective-permute-start(bf16[16,96,128]{2,1,0:T(8,128)(2,1)S(1)} %all_to_all.30.inc_ref.own_hbm), channel_id=1, source_target_pairs={{0,16},{16,0},{32,48},{48,32},{64,80},{80,64},{96,112},{112,96},{1... | collective-permute-start | bytes 1179656 | tf_op jit(solution)/shard_map/ppermute | solution.py:563
  92.6 1.0 copy-start.17
  93.6 16.2 %copy-start = (bf16[2048,512]{1,0:T(8,128)(2,1)S(1)}, bf16[2048,512]{1,0:T(8,128)(2,1)}, u32[]{:S(2)}) copy-start(bf16[2048,512]{1,0:T(8,128)(2,1)} %all-gather.2.cloned.1.call-done.weights_hbm.weights_ref) | copy-start | bytes 6291460
  97.3 12.5 %copy-start.6 = (bf16[128,512]{1,0:T(8,128)(2,1)S(1)}, bf16[128,512]{1,0:T(8,128)(2,1)}, u32[]{:S(2)}) copy-start(bf16[128,512]{1,0:T(8,128)(2,1)} %get-tuple-element.24.slopes_ref) | copy-start | bytes 393220
  97.3 12.5 %copy-start.7 = (bf16[2,8,32,128]{3,2,1,0:T(8,128)(2,1)S(1)}, bf16[2,8,32,128]{3,2,1,0:T(8,128)(2,1)}, u32[]{:S(2)}) copy-start(bf16[2,8,32,128]{3,2,1,0:T(8,128)(2,1)} %get-tuple-element.25.hidden_ref) | copy-start | bytes 393220
  106.2 18.2 %all-to-all-start.3 = ((bf16[16,128,256]{2,1,0:T(8,128)(2,1)}), bf16[16,128,256]{2,1,0:T(8,128)(2,1)S(1)}, u32[]{:S(2)}, u32[]{:S(2)}) async-start(bf16[16,128,256]{2,1,0:T(8,128)(2,1)} %get-tuple-element.23), calls=%async_computation.3 | async-start | bytes 2097152 | tf_op jit(solution)/shard_map/all_to_all | solution.py:559
  111.5 0.8 copy-start.2
  112.3 0.6 copy-start.11
  113.0 9.2 %copy-start.3 = (f32[64,2048]{1,0:T(8,128)S(1)}, f32[64,2048]{1,0:T(8,128)}, u32[]{:S(2)}) copy-start(f32[64,2048]{1,0:T(8,128)} %copy-done.2) | copy-start | bytes 1572868
  113.0 8.4 %collective-permute-start.1 = (f32[64,2048]{1,0:T(8,128)}, f32[64,2048]{1,0:T(8,128)S(1)}, u32[]{:S(2)}, u32[]{:S(2)}) collective-permute-start(f32[64,2048]{1,0:T(8,128)} %get-tuple-element.27), channel_id=1, source_target_pairs={{0,16},{16,0},{32,48},{48,32},{64,80},{80,64},{96,112},{112,96},{1... | collective-permute-start | bytes 1572872 | tf_op jit(solution)/shard_map/ppermute | solution.py:563
  117.8 3.6 %collective-permute-start.2 = (bf16[8,32,128]{2,1,0:T(8,128)(2,1)}, bf16[8,32,128]{2,1,0:T(8,128)(2,1)S(1)}, u32[]{:S(2)}, u32[]{:S(2)}) collective-permute-start(bf16[8,32,128]{2,1,0:T(8,128)(2,1)} %copy-done.11), channel_id=1, source_target_pairs={{0,16},{16,0},{32,48},{48,32},{64,80},{80,64},{96,112},{112,96},{1... | collective-permute-start | bytes 196616 | tf_op jit(solution)/shard_map/ppermute | solution.py:563
  121.4 0.8 copy-start.4
  122.2 1.0 copy-start.5
  159.8 29.0 %copy-start.13 = (s32[1,32,128]{2,1,0:T(8,128)S(1)}, s32[1,32,128]{2,1,0:T(8,128)}, u32[]{:S(2)}) copy-start(s32[1,32,128]{2,1,0:T(8,128)} %param.14) | copy-start | bytes 49156
  159.9 29.0 %copy-start.15 = (s32[16]{0:T(128)S(1)}, s32[16]{0:T(128)}, u32[]{:S(2)}) copy-start(s32[16]{0:T(128)} %param.16) | copy-start | bytes 196
  159.9 29.0 %all-to-all-start.5 = ((bf16[32,112,128]{2,1,0:T(8,128)(2,1)}), bf16[32,112,128]{2,1,0:T(8,128)(2,1)S(1)}, u32[]{:S(2)}, u32[]{:S(2)}) async-start(bf16[32,112,128]{2,1,0:T(8,128)(2,1)} %return_slots.1), calls=%async_computation.5 | async-start | bytes 1835008 | tf_op jit(solution)/shard_map/all_to_all | solution.py:559
  188.9 1.0 copy-start.8
Sparse Core Ops, SparseCore 0:
  10.7 82.8 all-gather.1

commit v6 on v5

--- a/solution.py
+++ b/solution.py
@@ -94,6 +94,7 @@
 
 
 BUILD = 256
+KEPT = 512
 
 
 def counts_of(nbr_ref, rows):
@@ -128,7 +129,7 @@
         out_shape=[
             jax.ShapeDtypeStruct((NODES, NODES), BF16),
             jax.ShapeDtypeStruct((HUBS, NODES), BF16),
-            jax.ShapeDtypeStruct((FEATS, NODES), F32),
+            jax.ShapeDtypeStruct((KEPT, NODES), F32),
         ],
         compiler_params=params(60),
         cost_estimate=cost(1 << 30, 4 << 20),
@@ -156,7 +157,7 @@
         (hub_hbm, hub_ref),
         (x_hbm, x_ref),
         (cot_hbm, cot_ref),
-        (sum_hbm, sum_ref),
+        (sum_hbm.at[:FEATS], sum_ref),
     )
     for peer in range(PEERS):
         slots[:FEATS, SLOTS * peer : SLOTS * (peer + 1)] = inc_ref[peer, :FEATS, :]
@@ -208,7 +209,7 @@
             pltpu.VMEM((FEATS, NODES), F32),
             pltpu.SemaphoreType.DMA((5,)),
         ],
-        compiler_params=params(16),
+        compiler_params=params(52),
         cost_estimate=cost(2 * 256 * 5632 * 1024, 3 << 20),
         name="aggregate",
     )(feats, incoming, recv_lanes, local_sum, hub_lanes, cotangent)
@@ -248,53 +249,79 @@
 CHIPS = PEERS // 2
 
 
+def prepare_kernel(own_block, other_block, joined_ref, cot_ref):
+    core = lax.axis_index("row") % 2
+    for layer in range(LAYERS):
+        lanes = slice(SLOTS * layer, SLOTS * (layer + 1))
+        joined_ref[core, :, lanes] = own_block[layer, :OWN, :]
+        joined_ref[1 - core, :, lanes] = other_block[layer, :OWN, :]
+    for side, block in ((core, own_block), (1 - core, other_block)):
+        for pair in range(LAYERS // 4):
+            even = block[8 * core + 2 * pair, OWN:, :].astype(F32)
+            odd = block[8 * core + 2 * pair + 1, OWN:, :].astype(F32)
+            top = jnp.concatenate([even[:, :FEATS], odd[:, :FEATS]], axis=1)
+            bottom = jnp.concatenate([even[:, FEATS:], odd[:, FEATS:]], axis=1)
+            cot_ref[side, :, SLOTS * pair : SLOTS * (pair + 1)] = jnp.concatenate(
+                [top, bottom], axis=0
+            ).astype(BF16)
+
+
+def prepare(own_block, other_block):
+    return pl.pallas_call(
+        prepare_kernel,
+        out_shape=[
+            jax.ShapeDtypeStruct((2, OWN, 2 * OUTS), BF16),
+            jax.ShapeDtypeStruct((2, OWN, HALF), BF16),
+        ],
+        compiler_params=params(16),
+        cost_estimate=cost(1 << 20, 2 << 20),
+        name="prepare",
+    )(own_block, other_block)
+
+
 def forward_kernel(
-    own_hbm, other_hbm, weights_hbm, slopes_hbm, flat_hbm, hidden_hbm,
-    own_block, other_block, weights, blocks, cots, out_tile, flat, hidden, in_sems, out_sems,
+    joined_hbm, cot_hbm, weights_hbm, slopes_hbm, flat_hbm, hidden_hbm,
+    joined, cots, weights, out_tile, flat, hidden, in_sems, out_sems,
 ):
-    core = lax.axis_index("row") % 2
     staged = copies(
-        in_sems, (own_hbm, own_block), (other_hbm, other_block), (weights_hbm, weights)
+        in_sems,
+        (joined_hbm, joined),
+        (weights_hbm.at[:, :TILE], weights.at[:, :TILE]),
+        (cot_hbm, cots),
+        (weights_hbm.at[:, TILE:], weights.at[:, TILE:]),
     )
     staged[0].wait()
-    staged[1].wait()
-    for layer in range(LAYERS):
-        lanes = slice(SLOTS * layer, SLOTS * (layer + 1))
-        blocks[core, :, lanes] = own_block[layer, :OWN, :]
-        blocks[1 - core, :, lanes] = other_block[layer, :OWN, :]
-    for layer in range(LAYERS // 2):
-        cots[core, layer] = own_block[8 * core + layer, OWN:, :]
-        cots[1 - core, layer] = other_block[8 * core + layer, OWN:, :]
-    staged[2].wait()
-    preacts = matmul(blocks[...].reshape(2 * OWN, 2 * OUTS), weights[...], NN)
-    for block in range(2):
-        for pair in range(4):
-            lanes = slice(SLOTS * pair, SLOTS * (pair + 1))
-            preact = preacts[OWN * block : OWN * (block + 1), lanes]
-            sigmoid_part = jax.nn.sigmoid(preact)
-            silu = preact * sigmoid_part
-            slope = sigmoid_part * (1.0 + preact * (1.0 - sigmoid_part))
-            even = cots[block, 2 * pair].astype(F32)
-            odd = cots[block, 2 * pair + 1].astype(F32)
-            top = jnp.concatenate([even[:, :FEATS], odd[:, :FEATS]], axis=1)
-            bottom = jnp.concatenate([even[:, FEATS:], odd[:, FEATS:]], axis=1)
-            slopes = (jnp.concatenate([top, bottom], axis=0) * slope).astype(BF16)
-            column = SLOTS * (pair % 2)
-            out_tile[pair // 2, OWN * block : OWN * (block + 1), column : column + SLOTS] = slopes
-            flat[OWN * block : OWN * (block + 1), lanes] = slopes
-            hidden[block, 2 * pair] = fold_halves(silu[:, :FEATS]).astype(BF16)
-            hidden[block, 2 * pair + 1] = fold_halves(silu[:, FEATS:]).astype(BF16)
-    sent = copies(
-        out_sems,
-        *[(out_tile.at[chip % 2], slopes_hbm.at[chip]) for chip in range(CHIPS)],
-        (flat, flat_hbm),
-        (hidden, hidden_hbm),
-    )
+    sent = []
+    for side in range(2):
+        staged[2 * side + 1].wait()
+        columns = slice(TILE * side, TILE * (side + 1))
+        preact = matmul(joined[...].reshape(2 * OWN, 2 * OUTS), weights[:, columns], NN)
+        if side == 0:
+            staged[2].wait()
+        sigmoid_part = jax.nn.sigmoid(preact)
+        silu = preact * sigmoid_part
+        slope = sigmoid_part * (1.0 + preact * (1.0 - sigmoid_part))
+        cot = cots[:, :, columns].reshape(2 * OWN, TILE).astype(F32)
+        slopes = (cot * slope).astype(BF16)
+        out_tile[side] = slopes
+        for chip in range(side, CHIPS, 2):
+            copy = pltpu.make_async_copy(out_tile.at[side], slopes_hbm.at[chip], out_sems.at[chip])
+            copy.start()
+            sent.append(copy)
+        flat[:, columns] = slopes
+        for block in range(2):
+            for layer in range(4):
+                tile = silu[OWN * block : OWN * (block + 1), FEATS * layer : FEATS * (layer + 1)]
+                hidden[block, 4 * side + layer] = fold_halves(tile).astype(BF16)
+    for i, (source, target) in enumerate(((flat, flat_hbm), (hidden, hidden_hbm))):
+        copy = pltpu.make_async_copy(source, target, out_sems.at[CHIPS + i])
+        copy.start()
+        sent.append(copy)
     for copy in sent:
         copy.wait()
 
 
-def forward(own_block, other_block, weights):
+def forward(joined, cots, weights):
     return pl.pallas_call(
         forward_kernel,
         in_specs=[HBM, HBM, HBM],
@@ -305,21 +332,19 @@
             jax.ShapeDtypeStruct((2, LAYERS // 2, OWN // 2, SLOTS), BF16),
         ],
         scratch_shapes=[
-            pltpu.VMEM((LAYERS, 96, SLOTS), BF16),
-            pltpu.VMEM((LAYERS, 96, SLOTS), BF16),
+            pltpu.VMEM((2, OWN, 2 * OUTS), BF16),
+            pltpu.VMEM((2, OWN, HALF), BF16),
             pltpu.VMEM((2 * OUTS, HALF), BF16),
-            pltpu.VMEM((2, OWN, 2 * OUTS), BF16),
-            pltpu.VMEM((2, LAYERS // 2, OWN // 2, SLOTS), BF16),
             pltpu.VMEM((2, 2 * OWN, TILE), BF16),
             pltpu.VMEM((2 * OWN, HALF), BF16),
             pltpu.VMEM((2, LAYERS // 2, OWN // 2, SLOTS), BF16),
-            pltpu.SemaphoreType.DMA((3,)),
+            pltpu.SemaphoreType.DMA((4,)),
             pltpu.SemaphoreType.DMA((CHIPS + 2,)),
         ],
         compiler_params=params(60),
         cost_estimate=cost(2 * 256 * 2048 * 512, 4 << 20),
         name="forward",
-    )(own_block, other_block, weights)
+    )(joined, cots, weights)
 
 
 def backward_kernel(slopes_ref, hidden_ref, weights_ref, keep_ref, send_ref, keep_hidden, send_hidden, parts):
@@ -414,13 +439,23 @@
 RETURN_ROWS = 112
 
 
-def return_kernel(back_ref, recv_hbm, hubs_hbm, out_hbm, recv_ref, hubs_ref, out_ref, in_sems, out_sems):
-    staged = copies(in_sems, (recv_hbm, recv_ref), (hubs_hbm, hubs_ref))
-    rows = back_ref[:, :OWN, :].astype(F32).reshape(NODES, SLOTS)
-    share = rows.T[FEATS:, :].astype(BF16)
-    sums = jnp.sum(back_ref[:, 96:, :].astype(F32), axis=0).astype(BF16)
+def return_kernel(
+    back_hbm, recv_hbm, hubs_hbm, out_hbm,
+    back_ref, part_ref, recv_ref, hubs_ref, out_ref, in_sems, out_sems,
+):
+    staged = copies(
+        in_sems,
+        (recv_hbm, recv_ref),
+        (hubs_hbm, hubs_ref),
+        (back_hbm.at[:, :OWN, :], back_ref),
+        (back_hbm.at[:, 96:, :], part_ref),
+    )
     node = lax.broadcasted_iota(jnp.int32, (NODES, 2 * SLOTS), 0)
+    staged[2].wait()
+    share = back_ref[...].astype(F32).reshape(NODES, SLOTS).T[FEATS:, :].astype(BF16)
     staged[0].wait()
+    staged[3].wait()
+    sums = jnp.sum(part_ref[...].astype(F32), axis=0).astype(BF16)
     sent = []
     for pair in range(PEERS // 2):
         values = matmul(share, one_hot(node == pair_lanes(recv_ref, pair)), NN).astype(BF16)
@@ -446,14 +481,16 @@
 def return_slots(back_block, recv_lanes, hubs):
     return pl.pallas_call(
         return_kernel,
-        in_specs=[VMEM, HBM, HBM],
+        in_specs=[HBM, HBM, HBM],
         out_specs=HBM,
         out_shape=jax.ShapeDtypeStruct((PEERS, RETURN_ROWS, SLOTS), BF16),
         scratch_shapes=[
+            pltpu.VMEM((LAYERS, OWN, SLOTS), BF16),
+            pltpu.VMEM((LAYERS, 32, SLOTS), BF16),
             pltpu.VMEM((PEERS, SLOTS), jnp.int32),
             pltpu.VMEM((HUBS, NODES), BF16),
             pltpu.VMEM((PEERS, RETURN_ROWS, SLOTS), BF16),
-            pltpu.SemaphoreType.DMA((2,)),
+            pltpu.SemaphoreType.DMA((4,)),
             pltpu.SemaphoreType.DMA((4,)),
         ],
         compiler_params=params(60),
@@ -462,22 +499,26 @@
     )(back_block, recv_lanes, hubs)
 
 
-def local_kernel(back_ref, local_ref, base_ref, hidden_ref):
+def local_kernel(back_ref, local_ref, base_hbm, hidden_ref, base_ref, sems):
     columns = back_ref[:, :OWN, :].astype(F32).reshape(NODES, SLOTS).T
     share = columns[FEATS:, :].astype(BF16)
     base_ref[...] = columns[:FEATS, :] + matmul(share, local_ref[...], NT)
+    (sent,) = copies(sems, (base_ref, base_hbm.at[:FEATS]))
     folded = back_ref[:, OWN:96, :].astype(F32)
     rows = jnp.concatenate([folded[:, :, :FEATS], folded[:, :, FEATS:]], axis=1)
     hidden_ref[...] = rows.reshape(NODES, FEATS).T.astype(BF16)
+    sent.wait()
 
 
 def local_grads(back_block, local):
     return pl.pallas_call(
         local_kernel,
+        out_specs=[HBM, VMEM],
         out_shape=[
-            jax.ShapeDtypeStruct((FEATS, NODES), F32),
+            jax.ShapeDtypeStruct((KEPT, NODES), F32),
             jax.ShapeDtypeStruct((FEATS, NODES), BF16),
         ],
+        scratch_shapes=[pltpu.VMEM((FEATS, NODES), F32), pltpu.SemaphoreType.DMA((1,))],
         compiler_params=params(60),
         cost_estimate=cost(2 * 256 * 1024 * 1024, 3 << 20),
         name="local_grads",
@@ -491,7 +532,7 @@
     back_ref, send_hbm, hub_hbm, base_hbm, out_ref, self_hbm, neigh_hbm,
     send_ref, hub_ref, base_ref, grads_ref, slots, in_sems, out_sems,
 ):
-    staged = copies(in_sems, (send_hbm, send_ref), (hub_hbm, hub_ref), (base_hbm, base_ref))
+    staged = copies(in_sems, (send_hbm, send_ref), (hub_hbm, hub_ref), (base_hbm.at[:FEATS], base_ref))
     for peer in range(PEERS):
         slots[:, SLOTS * peer : SLOTS * (peer + 1)] = back_ref[peer, :FEATS, :]
         grads = back_ref[peer, ROWS:, :].astype(F32)
@@ -546,7 +587,7 @@
             pltpu.SemaphoreType.DMA((3,)),
             pltpu.SemaphoreType.DMA((2,)),
         ],
-        compiler_params=params(16),
+        compiler_params=params(52),
         cost_estimate=cost(2 * 256 * 4224 * 1024, 2 << 20),
         name="spread_grads",
     )(returned, send_lanes, hub_own, base)
@@ -581,7 +622,8 @@
     node_block = exchange(outgoing, "col")
     own_degree = lax.dynamic_slice_in_dim(degree[0], OWN * lax.axis_index("col"), OWN)[:, None]
     joined_cols = exchange(regroup(node_block), "row").reshape(PEERS * OWN, TILE).T
-    slopes_out, slopes, hidden = forward(node_block, other_core(node_block), weights)
+    joined, cots = prepare(node_block, other_core(node_block))
+    slopes_out, slopes, hidden = forward(joined, cots, weights)
     slopes_rows = exchange(slopes_out, "row", SAME_CORE).reshape(PEERS * OWN, TILE)
     mine, theirs, my_hidden, their_hidden = backward(slopes, hidden, weights)
     back = combine(mine, other_core(theirs), my_hidden, other_core(their_hidden), own_degree)

time: 201 us -> 201 us (level)
  starting transfers between devices: 46 us -> 50.1 us
  waiting for transfers between devices: 31.6 us -> 28.3 us
  blocking collectives: 65.3 us -> 63.2 us
    all_to_all x4, starting transfers between devices: 37.1 us -> 40.5 us  [exchange(): lax.all_to_all(blocks, axis, 0, 0, axis_index_groups=groups, tiled=True)]
    all_to_all x4, waiting for transfers between devices: 29.2 us -> 26.9 us  [exchange(): lax.all_to_all(blocks, axis, 0, 0, axis_index_groups=groups, tiled=True)]
    all_to_all x2, blocking collectives: 65.3 us -> 63.2 us  [exchange(): lax.all_to_all(blocks, axis, 0, 0, axis_index_groups=groups, tiled=True)]
    pallas_call x2 -> x3, Pallas kernels: 8.08 us -> 8.6 us  [the longest x1 4.5 us: return_slots(): pl.pallas_call(return_kernel, in_specs=[HBM, HBM, HBM], out_specs=HBM, ou...]
    unnamed x36 -> x32, local copies, waits for them, and re-layouts: 5.22 us -> 4.8 us
  transfers between devices with their start and end apart: 8 -> 8, of which waited for: 6 -> 4; matrix products, arithmetic and copies ran while one was open for 1% -> 1% of each run, Pallas kernels for 12% -> 13%
where the time goes in v6:
time: 201 us; the launch traced here: 200 us
  blocking collectives  63.2 us (31%)
  starting transfers between devices  50.1 us (25%)
  Pallas kernels  35.9 us (18%)
  waiting for transfers between devices  28.3 us (14%)
  between operations  14.3 us (7%)
  local copies, waits for them, and re-layouts  6.47 us (3%)
    all_to_all x2, blocking collectives, exchange(): lax.all_to_all(blocks, axis, 0, 0, axis_index_groups=groups, tiled=True)  63.2 us
    all_to_all x4, starting transfers between devices, exchange(): lax.all_to_all(blocks, axis, 0, 0, axis_index_groups=groups, tiled=True)  40.5 us
    all_to_all x4, waiting for transfers between devices, exchange(): lax.all_to_all(blocks, axis, 0, 0, axis_index_groups=groups, tiled=True)  26.9 us
    ppermute x3, starting transfers between devices, other_core(): return lax.ppermute(block, 'row', [(i, i ^ 1) for i in range(PEERS)])  9.57 us
    pallas_call x1, Pallas kernels, build_counts(): pl.pallas_call(build_kernel, grid=(NODES // BUILD,), in_specs=[whole((FEA...  6.2 us
    pallas_call x1, Pallas kernels, aggregate(): pl.pallas_call(aggregate_kernel, out_shape=[jax.ShapeDtypeStruct((LAYERS,...  4.94 us
    unnamed x32, local copies, waits for them, and re-layouts  4.8 us
    pallas_call x1, Pallas kernels, spread_grads(): pl.pallas_call(spread_kernel, in_specs=[VMEM, HBM, HBM, HBM], out_specs=[...  4.52 us
  transfers between devices with their start and end apart: 8, of which 4 were waited for; matrix products, arithmetic and copies ran while one was open for 1% of the time, Pallas kernels for 13%

profile of v6, /device:TPU:1, one launch (start us, length us, event | category | flops | bytes accessed | tf_op | source)
XLA Modules:
  0.0 200.0 jit_solution(14369383782647522638)
XLA Ops:
  7.2 1.5 fusion
  8.8 3.5 %gather_slots.1 = bf16[32,80,128]{2,1,0:T(8,128)(2,1)} custom-call(bf16[64,1024]{1,0:T(8,128)(2,1)} %x_hbm.3, s32[32,128]{1,0:T(8,128)} %bitcast.14, s32[1,16]{1,0:T(1,128)} %bitcast.18), custom_call_target="tpu_custom_call" | custom-call | flops 2147483648 | bytes 1048576 | tf_op jit(solution)/shard_map/gather_slots/pallas_call | solution.py:80
  12.3 10.4 %all-to-all-start = ((bf16[32,80,128]{2,1,0:T(8,128)(2,1)}), bf16[32,80,128]{2,1,0:T(8,128)(2,1)S(1)}, u32[]{:S(2)}, u32[]{:S(2)}) async-start(bf16[32,80,128]{2,1,0:T(8,128)(2,1)} %gather_slots.1), calls=%async_computation | async-start | bytes 1310720 | tf_op jit(solution)/shard_map/all_to_all | solution.py:600
  22.8 6.2 %build_counts.1 = (bf16[1024,1024]{1,0:T(8,128)(2,1)}, bf16[512,1024]{1,0:T(8,128)(2,1)}, f32[512,1024]{1,0:T(8,128)}) custom-call(bf16[64,1024]{1,0:T(8,128)(2,1)} %x_hbm.3, s32[8,1024]{1,0:T(8,128)} %bitcast.20, s32[2,1024]{1,0:T(2,128)} %bitcast.16), custom_call_target="tpu_custom_call" | custom-call | flops 1073741824 | bytes 4194304 | tf_op jit(solution)/shard_map/build_counts/pallas_call | solution.py:116
  29.0 6.8 %all-to-all-done.inc_ref = bf16[32,80,128]{2,1,0:T(8,128)(2,1)S(1)} async-done(((bf16[32,80,128]{2,1,0:T(8,128)(2,1)}), bf16[32,80,128]{2,1,0:T(8,128)(2,1)S(1)}, u32[]{:S(2)}, u32[]{:S(2)}) %all-to-all-start) | async-done | bytes 655392 | tf_op jit(solution)/shard_map/all_to_all | solution.py:600
  35.8 4.9 %aggregate.1 = (bf16[16,96,128]{2,1,0:T(8,128)(2,1)S(1)}, f32[8,1024]{1,0:T(8,128)S(1)}) custom-call(bf16[64,1024]{1,0:T(8,128)(2,1)S(1)} %copy-done.9, bf16[32,80,128]{2,1,0:T(8,128)(2,1)S(1)} %all-to-all-done.inc_ref, s32[32,128]{1,0:T(8,128)S(1)} %bitcast.13, f32[512,1024]{1,0:T(8,128)} %get-tuple-element.23.sum_hbm, s32[2,1024]{1,0:T(2,128)S(1)} %bitcast.17, ...), custom_call_target="tpu_custom_call" | custom-call | flops 2952790016 | bytes 3145728 | tf_op jit(solution)/shard_map/aggregate/pallas_call | solution.py:195
  40.7 35.5 %all_to_all.30.inc_ref.own_block = bf16[16,96,128]{2,1,0:T(8,128)(2,1)S(1)} all-to-all(bf16[16,96,128]{2,1,0:T(8,128)(2,1)S(1)} %get-tuple-element.24), channel_id=1, replica_groups=mesh['row'=32,'col'=16] {'col'}, dimensions={0} | all-to-all | bytes 786432 | tf_op jit(solution)/shard_map/all_to_all | solution.py:600
  76.3 1.6 regroup.1
  77.9 10.0 %all-to-all-start.2 = ((bf16[32,64,256]{2,1,0:T(8,128)(2,1)}), bf16[32,64,256]{2,1,0:T(8,128)(2,1)}, u32[]{:S(2)}, u32[]{:S(2)}) async-start(bf16[32,64,256]{2,1,0:T(8,128)(2,1)} %regroup.1), calls=%async_computation.2 | async-start | bytes 2097152 | tf_op jit(solution)/shard_map/all_to_all | solution.py:600
  87.9 2.2 %collective-permute-start = (bf16[16,96,128]{2,1,0:T(8,128)(2,1)S(1)}, bf16[16,96,128]{2,1,0:T(8,128)(2,1)S(1)}, u32[]{:S(2)}, u32[]{:S(2)}) collective-permute-start(bf16[16,96,128]{2,1,0:T(8,128)(2,1)S(1)} %all_to_all.30.inc_ref.own_block), channel_id=1, source_target_pairs={{0,16},{16,0},{32,48},{48,32},{64,80},{80,64},{96,112},{112,96},{1... | collective-permute-start | bytes 1179656 | tf_op jit(solution)/shard_map/ppermute | solution.py:604
  90.2 1.4 collective-permute-done.other_block
  91.6 0.2 prepare.1
  91.8 0.8 copy-done.5
  92.6 0.7 copy-done.8
  93.2 3.6 %forward.1 = (bf16[16,128,256]{2,1,0:T(8,128)(2,1)}, bf16[128,512]{1,0:T(8,128)(2,1)}, bf16[2,8,32,128]{3,2,1,0:T(8,128)(2,1)}) custom-call(bf16[2,64,2048]{2,1,0:T(8,128)(2,1)} %copy-done.5, bf16[2,64,512]{2,1,0:T(8,128)(2,1)} %copy-done.8, bf16[2048,512]{1,0:T(8,128)(2,1)} %all-gather.2.cloned.1.call-done.weights_hbm.weights_ref), custom_call_target="tpu_custom_call" | custom-call | flops 536870912 | bytes 4194304 | tf_op jit(solution)/shard_map/forward/pallas_call | solution.py:325
  96.8 8.3 %all-to-all-done.2 = bf16[32,64,256]{2,1,0:T(8,128)(2,1)} async-done(((bf16[32,64,256]{2,1,0:T(8,128)(2,1)}), bf16[32,64,256]{2,1,0:T(8,128)(2,1)}, u32[]{:S(2)}, u32[]{:S(2)}) %all-to-all-start.2) | async-done | bytes 1048608 | tf_op jit(solution)/shard_map/all_to_all | solution.py:600
  105.2 3.7 %all-to-all-start.3 = ((bf16[16,128,256]{2,1,0:T(8,128)(2,1)}), bf16[16,128,256]{2,1,0:T(8,128)(2,1)S(1)}, u32[]{:S(2)}, u32[]{:S(2)}) async-start(bf16[16,128,256]{2,1,0:T(8,128)(2,1)} %get-tuple-element.27), calls=%async_computation.3 | async-start | bytes 2097152 | tf_op jit(solution)/shard_map/all_to_all | solution.py:600
  108.9 1.7 backward.1
  110.5 0.8 copy-done.1
  111.3 0.6 copy-done.11
  112.0 5.4 %collective-permute-start.1 = (f32[64,2048]{1,0:T(8,128)}, f32[64,2048]{1,0:T(8,128)S(1)}, u32[]{:S(2)}, u32[]{:S(2)}) collective-permute-start(f32[64,2048]{1,0:T(8,128)} %get-tuple-element.31), channel_id=1, source_target_pairs={{0,16},{16,0},{32,48},{48,32},{64,80},{80,64},{96,112},{112,96},{1... | collective-permute-start | bytes 1572872 | tf_op jit(solution)/shard_map/ppermute | solution.py:604
  117.4 1.9 collective-permute-start.2
  119.5 1.5 copy.15
  121.0 0.8 copy-done.3
  121.8 1.0 copy-done.4
  123.0 1.2 weight_parts.1
  124.2 27.7 %all_to_all.31.back_ref.back_hbm = bf16[16,128,128]{2,1,0:T(8,128)(2,1)} all-to-all(bf16[16,128,128]{2,1,0:T(8,128)(2,1)S(1)} %weight_parts.1), channel_id=1, replica_groups=mesh['row'=32,'col'=16] {'col'}, dimensions={0} | all-to-all | bytes 1048576 | tf_op jit(solution)/shard_map/all_to_all | solution.py:600
  151.9 4.5 %return_slots.1 = bf16[32,112,128]{2,1,0:T(8,128)(2,1)} custom-call(bf16[16,128,128]{2,1,0:T(8,128)(2,1)} %all_to_all.31.back_ref.back_hbm, s32[32,128]{1,0:T(8,128)} %bitcast.12, bf16[512,1024]{1,0:T(8,128)(2,1)} %get-tuple-element.37.hubs_hbm), custom_call_target="tpu_custom_call" | custom-call | flops 2415919104 | bytes 3145728 | tf_op jit(solution)/shard_map/return_slots/pallas_call | solution.py:482
  156.4 16.4 %all-to-all-start.5 = ((bf16[32,112,128]{2,1,0:T(8,128)(2,1)}), bf16[32,112,128]{2,1,0:T(8,128)(2,1)S(1)}, u32[]{:S(2)}, u32[]{:S(2)}) async-start(bf16[32,112,128]{2,1,0:T(8,128)(2,1)} %return_slots.1), calls=%async_computation.5 | async-start | bytes 1835008 | tf_op jit(solution)/shard_map/all_to_all | solution.py:600
  172.8 3.9 %local_grads.1 = (f32[512,1024]{1,0:T(8,128)}, bf16[64,1024]{1,0:T(8,128)(2,1)}) custom-call(bf16[16,128,128]{2,1,0:T(8,128)(2,1)} %all_to_all.31.back_ref.back_hbm, bf16[1024,1024]{1,0:T(8,128)(2,1)} %get-tuple-element.35.local_ref), custom_call_target="tpu_custom_call" | custom-call | flops 536870912 | bytes 3145728 | tf_op jit(solution)/shard_map/local_grads/pallas_call | solution.py:514
  176.7 11.8 %all-to-all-done.5.back_ref = bf16[32,112,128]{2,1,0:T(8,128)(2,1)S(1)} async-done(((bf16[32,112,128]{2,1,0:T(8,128)(2,1)}), bf16[32,112,128]{2,1,0:T(8,128)(2,1)S(1)}, u32[]{:S(2)}, u32[]{:S(2)}) %all-to-all-start.5) | async-done | bytes 917536 | tf_op jit(solution)/shard_map/all_to_all | solution.py:600
  188.6 4.5 %spread_grads.1 = (bf16[64,1024]{1,0:T(8,128)(2,1)}, f32[64,1024]{1,0:T(8,128)}, f32[64,1024]{1,0:T(8,128)}) custom-call(bf16[32,112,128]{2,1,0:T(8,128)(2,1)S(1)} %all-to-all-done.5.back_ref, s32[32,128]{1,0:T(8,128)S(1)} %bitcast.15, s32[1,16]{1,0:T(1,128)S(1)} %bitcast.19, f32[512,1024]{1,0:T(8,128)} %get-tuple-element.38.base_hbm), custom_call_target="tpu_custom_call" | custom-call | flops 2214592512 | bytes 2097152 | tf_op jit(solution)/shard_map/spread_grads/pallas_call | solution.py:572
  (36 shorter events, 0.4 us)
Async XLA Ops:
  7.2 86.1 %all-gather.2.cloned.1.call-start = ((), (), s32[]{:S(2)}) async-start(), calls=%async_computation.6 | async-start | bytes 2228224 | tf_op jit(solution)/shard_map/all_gather | solution.py:612
  12.3 23.5 %all-to-all-start = ((bf16[32,80,128]{2,1,0:T(8,128)(2,1)}), bf16[32,80,128]{2,1,0:T(8,128)(2,1)S(1)}, u32[]{:S(2)}, u32[]{:S(2)}) async-start(bf16[32,80,128]{2,1,0:T(8,128)(2,1)} %gather_slots.1), calls=%async_computation | async-start | bytes 1310720 | tf_op jit(solution)/shard_map/all_to_all | solution.py:600
  22.7 13.0 %copy-start.9 = (bf16[64,1024]{1,0:T(8,128)(2,1)S(1)}, bf16[64,1024]{1,0:T(8,128)(2,1)}, u32[]{:S(2)}) copy-start(bf16[64,1024]{1,0:T(8,128)(2,1)} %x_hbm.3) | copy-start | bytes 393220
  22.7 13.0 %copy-start.10 = (bf16[64,1024]{1,0:T(8,128)(2,1)S(1)}, bf16[64,1024]{1,0:T(8,128)(2,1)}, u32[]{:S(2)}) copy-start(bf16[64,1024]{1,0:T(8,128)(2,1)} %cot_hbm.1) | copy-start | bytes 393220
  22.7 13.0 %copy-start.12 = (s32[1,32,128]{2,1,0:T(8,128)S(1)}, s32[1,32,128]{2,1,0:T(8,128)}, u32[]{:S(2)}) copy-start(s32[1,32,128]{2,1,0:T(8,128)} %param.15) | copy-start | bytes 49156
  22.8 13.0 %copy-start.14 = (s32[1024,2]{0,1:T(2,128)S(1)}, s32[1024,2]{0,1:T(2,128)}, u32[]{:S(2)}) copy-start(s32[1024,2]{0,1:T(2,128)} %param.17) | copy-start | bytes 24580
  77.9 27.3 %all-to-all-start.2 = ((bf16[32,64,256]{2,1,0:T(8,128)(2,1)}), bf16[32,64,256]{2,1,0:T(8,128)(2,1)}, u32[]{:S(2)}, u32[]{:S(2)}) async-start(bf16[32,64,256]{2,1,0:T(8,128)(2,1)} %regroup.1), calls=%async_computation.2 | async-start | bytes 2097152 | tf_op jit(solution)/shard_map/all_to_all | solution.py:600
  87.9 3.6 %collective-permute-start = (bf16[16,96,128]{2,1,0:T(8,128)(2,1)S(1)}, bf16[16,96,128]{2,1,0:T(8,128)(2,1)S(1)}, u32[]{:S(2)}, u32[]{:S(2)}) collective-permute-start(bf16[16,96,128]{2,1,0:T(8,128)(2,1)S(1)} %all_to_all.30.inc_ref.own_block), channel_id=1, source_target_pairs={{0,16},{16,0},{32,48},{48,32},{64,80},{80,64},{96,112},{112,96},{1... | collective-permute-start | bytes 1179656 | tf_op jit(solution)/shard_map/ppermute | solution.py:604
  91.8 0.8 copy-start.5
  92.6 0.7 copy-start.8
  93.2 15.6 %copy-start = (bf16[2048,512]{1,0:T(8,128)(2,1)S(1)}, bf16[2048,512]{1,0:T(8,128)(2,1)}, u32[]{:S(2)}) copy-start(bf16[2048,512]{1,0:T(8,128)(2,1)} %all-gather.2.cloned.1.call-done.weights_hbm.weights_ref) | copy-start | bytes 6291460
  96.8 12.0 %copy-start.6 = (bf16[128,512]{1,0:T(8,128)(2,1)S(1)}, bf16[128,512]{1,0:T(8,128)(2,1)}, u32[]{:S(2)}) copy-start(bf16[128,512]{1,0:T(8,128)(2,1)} %get-tuple-element.28.slopes_ref) | copy-start | bytes 393220
  96.8 12.0 %copy-start.7 = (bf16[2,8,32,128]{3,2,1,0:T(8,128)(2,1)S(1)}, bf16[2,8,32,128]{3,2,1,0:T(8,128)(2,1)}, u32[]{:S(2)}) copy-start(bf16[2,8,32,128]{3,2,1,0:T(8,128)(2,1)} %get-tuple-element.29.hidden_ref) | copy-start | bytes 393220
  105.2 17.8 %all-to-all-start.3 = ((bf16[16,128,256]{2,1,0:T(8,128)(2,1)}), bf16[16,128,256]{2,1,0:T(8,128)(2,1)S(1)}, u32[]{:S(2)}, u32[]{:S(2)}) async-start(bf16[16,128,256]{2,1,0:T(8,128)(2,1)} %get-tuple-element.27), calls=%async_computation.3 | async-start | bytes 2097152 | tf_op jit(solution)/shard_map/all_to_all | solution.py:600
  110.5 0.8 copy-start.1
  111.3 0.6 copy-start.11
  112.0 9.9 %copy-start.2 = (f32[64,2048]{1,0:T(8,128)S(1)}, f32[64,2048]{1,0:T(8,128)}, u32[]{:S(2)}) copy-start(f32[64,2048]{1,0:T(8,128)} %copy-done.1) | copy-start | bytes 1572868
  112.0 9.1 %collective-permute-start.1 = (f32[64,2048]{1,0:T(8,128)}, f32[64,2048]{1,0:T(8,128)S(1)}, u32[]{:S(2)}, u32[]{:S(2)}) collective-permute-start(f32[64,2048]{1,0:T(8,128)} %get-tuple-element.31), channel_id=1, source_target_pairs={{0,16},{16,0},{32,48},{48,32},{64,80},{80,64},{96,112},{112,96},{1... | collective-permute-start | bytes 1572872 | tf_op jit(solution)/shard_map/ppermute | solution.py:604
  117.4 3.6 %collective-permute-start.2 = (bf16[8,32,128]{2,1,0:T(8,128)(2,1)}, bf16[8,32,128]{2,1,0:T(8,128)(2,1)S(1)}, u32[]{:S(2)}, u32[]{:S(2)}) collective-permute-start(bf16[8,32,128]{2,1,0:T(8,128)(2,1)} %copy-done.11), channel_id=1, source_target_pairs={{0,16},{16,0},{32,48},{48,32},{64,80},{80,64},{96,112},{112,96},{1... | collective-permute-start | bytes 196616 | tf_op jit(solution)/shard_map/ppermute | solution.py:604
  121.0 0.8 copy-start.3
  121.8 1.0 copy-start.4
  156.4 32.2 %copy-start.13 = (s32[1,32,128]{2,1,0:T(8,128)S(1)}, s32[1,32,128]{2,1,0:T(8,128)}, u32[]{:S(2)}) copy-start(s32[1,32,128]{2,1,0:T(8,128)} %param.14) | copy-start | bytes 49156
  156.4 32.1 %copy-start.15 = (s32[16]{0:T(128)S(1)}, s32[16]{0:T(128)}, u32[]{:S(2)}) copy-start(s32[16]{0:T(128)} %param.16) | copy-start | bytes 196
  156.4 32.1 %all-to-all-start.5 = ((bf16[32,112,128]{2,1,0:T(8,128)(2,1)}), bf16[32,112,128]{2,1,0:T(8,128)(2,1)S(1)}, u32[]{:S(2)}, u32[]{:S(2)}) async-start(bf16[32,112,128]{2,1,0:T(8,128)(2,1)} %return_slots.1), calls=%async_computation.5 | async-start | bytes 1835008 | tf_op jit(solution)/shard_map/all_to_all | solution.py:600
Sparse Core Ops, SparseCore 0:
  10.7 82.3 all-gather.1

commit v7 on v6

--- a/solution.py
+++ b/solution.py
@@ -249,6 +249,45 @@
 CHIPS = PEERS // 2
 
 
+SIDE = 4
+BAND = 16
+
+
+def place_kernel(*refs):
+    stacks, out_hbm, sems = refs[:SIDE], refs[SIDE], refs[SIDE + 1]
+    chip = lax.axis_index("row") // 2
+    y, x = chip // SIDE, chip % SIDE
+    pairs = []
+    for shift_y in range(SIDE):
+        for shift_x in range(SIDE):
+            source = (y + SIDE - shift_y) % SIDE * SIDE + (x + SIDE - shift_x) % SIDE
+            band = pl.ds(pl.multiple_of(BAND * (source % 8), BAND), BAND)
+            pairs.append((stacks[shift_y].at[shift_x], out_hbm.at[source // 8, :, band, :]))
+    for copy in copies(sems, *pairs):
+        copy.wait()
+
+
+def place_weights(stacks):
+    return pl.pallas_call(
+        place_kernel,
+        in_specs=[HBM] * SIDE,
+        out_specs=HBM,
+        out_shape=jax.ShapeDtypeStruct((2, LAYERS, SLOTS, TILE), BF16),
+        scratch_shapes=[pltpu.SemaphoreType.DMA((SIDE * SIDE,))],
+        compiler_params=params(60),
+        cost_estimate=cost(0, 4 << 20),
+        name="place_weights",
+    )(*stacks)
+
+
+def chip_shift(block, shift_y, shift_x):
+    moves = []
+    for device in range(PEERS):
+        y, x, core = device // 8, device // 2 % SIDE, device % 2
+        moves.append((device, (y + shift_y) % SIDE * 8 + (x + shift_x) % SIDE * 2 + core))
+    return lax.ppermute(block, "row", moves)
+
+
 def prepare_kernel(own_block, other_block, joined_ref, cot_ref):
     core = lax.axis_index("row") % 2
     for layer in range(LAYERS):
@@ -286,16 +325,16 @@
     staged = copies(
         in_sems,
         (joined_hbm, joined),
-        (weights_hbm.at[:, :TILE], weights.at[:, :TILE]),
+        (weights_hbm.at[0], weights.at[0]),
         (cot_hbm, cots),
-        (weights_hbm.at[:, TILE:], weights.at[:, TILE:]),
+        (weights_hbm.at[1], weights.at[1]),
     )
     staged[0].wait()
     sent = []
     for side in range(2):
         staged[2 * side + 1].wait()
         columns = slice(TILE * side, TILE * (side + 1))
-        preact = matmul(joined[...].reshape(2 * OWN, 2 * OUTS), weights[:, columns], NN)
+        preact = matmul(joined[...].reshape(2 * OWN, 2 * OUTS), weights[side].reshape(2 * OUTS, TILE), NN)
         if side == 0:
             staged[2].wait()
         sigmoid_part = jax.nn.sigmoid(preact)
@@ -334,7 +373,7 @@
         scratch_shapes=[
             pltpu.VMEM((2, OWN, 2 * OUTS), BF16),
             pltpu.VMEM((2, OWN, HALF), BF16),
-            pltpu.VMEM((2 * OUTS, HALF), BF16),
+            pltpu.VMEM((2, LAYERS, SLOTS, TILE), BF16),
             pltpu.VMEM((2, 2 * OWN, TILE), BF16),
             pltpu.VMEM((2 * OWN, HALF), BF16),
             pltpu.VMEM((2, LAYERS // 2, OWN // 2, SLOTS), BF16),
@@ -349,7 +388,9 @@
 
 def backward_kernel(slopes_ref, hidden_ref, weights_ref, keep_ref, send_ref, keep_hidden, send_hidden, parts):
     core = lax.axis_index("row") % 2
-    back = matmul(slopes_ref[...], weights_ref[...], NT)
+    back = matmul(slopes_ref[:, :TILE], weights_ref[0].reshape(2 * OUTS, TILE), NT) + matmul(
+        slopes_ref[:, TILE:], weights_ref[1].reshape(2 * OUTS, TILE), NT
+    )
     parts[0] = back[:OWN, :]
     parts[1] = back[OWN:, :]
     keep_ref[...] = parts[core]
@@ -608,18 +649,25 @@
     send_lanes = send_rows.reshape(PEERS, SLOTS)
     recv_lanes = recv_node.reshape(PEERS, SLOTS)
     hub_own = hub_rows[None, :]
-    half = HALF * (lax.axis_index("row") % 2)
-    weights = lax.all_gather(
-        lax.dynamic_slice_in_dim(jnp.concatenate([w_self, w_neigh], axis=0), half, HALF, 1),
-        "col",
-        axis=0,
-        tiled=True,
+    device = lax.axis_index("row")
+    piece = lax.dynamic_slice(
+        jnp.concatenate([w_self, w_neigh], axis=0),
+        (BAND * (device // 2 % 8), HALF * (device % 2) + TILE * (device // 16)),
+        (BAND, TILE),
     )
-    incoming = exchange(gather_slots(feats, send_lanes, hub_own), "row")
+    piece = exchange(jnp.broadcast_to(piece[None], (LAYERS, BAND, TILE)), "col")
+    slots_out = gather_slots(feats, send_lanes, hub_own)
+    slots_out, piece = lax.optimization_barrier((slots_out, piece))
+    stack = jnp.stack([piece] + [chip_shift(piece, 0, shift) for shift in range(1, SIDE)])
+    incoming = exchange(slots_out, "row")
+    incoming, stack = lax.optimization_barrier((incoming, stack))
+    stacks = [stack] + [chip_shift(stack, shift, 0) for shift in range(1, SIDE)]
     hub_lanes = hub_nbr.T
     local, hubs, local_sum = build_counts(feats, loc_nbr.T, hub_lanes)
     outgoing, degree = aggregate(feats, incoming, recv_lanes, local_sum, hub_lanes, cotangent)
     node_block = exchange(outgoing, "col")
+    node_block, stacks = lax.optimization_barrier((node_block, stacks))
+    weights = place_weights(stacks)
     own_degree = lax.dynamic_slice_in_dim(degree[0], OWN * lax.axis_index("col"), OWN)[:, None]
     joined_cols = exchange(regroup(node_block), "row").reshape(PEERS * OWN, TILE).T
     joined, cots = prepare(node_block, other_core(node_block))

time: 201 us -> 274 us (1.36)
  Pallas kernels: 35.9 us -> 101 us
  starting transfers between devices: 50.1 us -> 83.3 us
  blocking collectives: 63.2 us -> 33.4 us
  waiting for transfers between devices: 28.3 us -> 46 us
  between operations: 14.3 us -> 1.28 us
    pallas_call x0 -> x1, Pallas kernels: none -> 64.8 us  [place_weights(): pl.pallas_call(place_kernel, in_specs=[HBM] * SIDE, out_specs=HBM, out_sh...]
    all_to_all x2 -> x1, blocking collectives: 63.2 us -> 33.4 us  [exchange(): lax.all_to_all(blocks, axis, 0, 0, axis_index_groups=groups, tiled=True)]
    ppermute x0 -> x6, starting transfers between devices: none -> 21.2 us  [chip_shift(): return lax.ppermute(block, 'row', moves)]
    ppermute x0 -> x6, waiting for transfers between devices: none -> 19.1 us  [chip_shift(): return lax.ppermute(block, 'row', moves)]
    all_to_all x4 -> x6, starting transfers between devices: 40.5 us -> 55.6 us  [exchange(): lax.all_to_all(blocks, axis, 0, 0, axis_index_groups=groups, tiled=True)]
    ppermute x3, starting transfers between devices: 9.57 us -> 6.53 us  [other_core(): return lax.ppermute(block, 'row', [(i, i ^ 1) for i in range(PEERS)])]
    all_to_all x4 -> x6, waiting for transfers between devices: 26.9 us -> 25.6 us  [exchange(): lax.all_to_all(blocks, axis, 0, 0, axis_index_groups=groups, tiled=True)]
  transfers between devices with their start and end apart: 8 -> 15, of which waited for: 4 -> 7; matrix products, arithmetic and copies ran while one was open for 1% -> 1% of each run, Pallas kernels for 13% -> 31%
where the time goes in v7:
time: 274 us; the launch traced here: 273 us
  Pallas kernels  101 us (37%)
  starting transfers between devices  83.3 us (30%)
  waiting for transfers between devices  46 us (17%)
  blocking collectives  33.4 us (12%)
  local copies, waits for them, and re-layouts  6.34 us (2%)
    pallas_call x1, Pallas kernels, place_weights(): pl.pallas_call(place_kernel, in_specs=[HBM] * SIDE, out_specs=HBM, out_sh...  64.8 us
    all_to_all x6, starting transfers between devices, exchange(): lax.all_to_all(blocks, axis, 0, 0, axis_index_groups=groups, tiled=True)  55.6 us
    all_to_all x1, blocking collectives, exchange(): lax.all_to_all(blocks, axis, 0, 0, axis_index_groups=groups, tiled=True)  33.4 us
    all_to_all x6, waiting for transfers between devices, exchange(): lax.all_to_all(blocks, axis, 0, 0, axis_index_groups=groups, tiled=True)  25.6 us
    ppermute x6, starting transfers between devices, chip_shift(): return lax.ppermute(block, 'row', moves)  21.2 us
    ppermute x6, waiting for transfers between devices, chip_shift(): return lax.ppermute(block, 'row', moves)  19.1 us
    ppermute x3, starting transfers between devices, other_core(): return lax.ppermute(block, 'row', [(i, i ^ 1) for i in range(PEERS)])  6.53 us
    pallas_call x1, Pallas kernels, build_counts(): pl.pallas_call(build_kernel, grid=(NODES // BUILD,), in_specs=[whole((FEA...  6.17 us
  transfers between devices with their start and end apart: 15, of which 7 were waited for; matrix products, arithmetic and copies ran while one was open for 1% of the time, Pallas kernels for 31%

profile of v7, /device:TPU:1, one launch (start us, length us, event | category | flops | bytes accessed | tf_op | source)
XLA Modules:
  0.0 272.5 jit_solution(12724857526185986064)
XLA Ops:
  2.1 15.7 %all-to-all-start = ((bf16[16,16,256]{2,1,0:T(8,128)(2,1)}), bf16[16,16,256]{2,1,0:T(8,128)(2,1)S(1)}, u32[]{:S(2)}, u32[]{:S(2)}) async-start(bf16[16,16,256]{2,1,0:T(8,128)(2,1)} %broadcast_in_dim.13), calls=%async_computation | async-start | bytes 262144 | tf_op jit(solution)/shard_map/all_to_all | solution.py:641
  17.8 3.4 %gather_slots.1 = bf16[32,80,128]{2,1,0:T(8,128)(2,1)} custom-call(bf16[64,1024]{1,0:T(8,128)(2,1)} %x_hbm.3, s32[32,128]{1,0:T(8,128)} %bitcast.18, s32[1,16]{1,0:T(1,128)} %bitcast.22), custom_call_target="tpu_custom_call" | custom-call | flops 2147483648 | bytes 1048576 | tf_op jit(solution)/shard_map/gather_slots/pallas_call | solution.py:80
  21.3 8.6 %all-to-all-done = bf16[16,16,256]{2,1,0:T(8,128)(2,1)S(1)} async-done(((bf16[16,16,256]{2,1,0:T(8,128)(2,1)}), bf16[16,16,256]{2,1,0:T(8,128)(2,1)S(1)}, u32[]{:S(2)}, u32[]{:S(2)}) %all-to-all-start) | async-done | bytes 131104 | tf_op jit(solution)/shard_map/all_to_all | solution.py:641
  29.8 10.7 %all-to-all-start.1 = ((bf16[32,80,128]{2,1,0:T(8,128)(2,1)}), bf16[32,80,128]{2,1,0:T(8,128)(2,1)S(1)}, u32[]{:S(2)}, u32[]{:S(2)}) async-start(bf16[32,80,128]{2,1,0:T(8,128)(2,1)} %gather_slots.1), calls=%async_computation.1 | async-start | bytes 1310720 | tf_op jit(solution)/shard_map/all_to_all | solution.py:641
  40.6 3.3 %collective-permute-start = (bf16[16,16,256]{2,1,0:T(8,128)(2,1)S(1)}, bf16[16,16,256]{2,1,0:T(8,128)(2,1)S(1)}, u32[]{:S(2)}, u32[]{:S(2)}) collective-permute-start(bf16[16,16,256]{2,1,0:T(8,128)(2,1)S(1)} %all-to-all-done), channel_id=1, source_target_pairs={{0,32},{16,48},{32,64},{48,80},{64,96},{80,112},{96,0},{112,16},{1... | collective-permute-start | bytes 393224 | tf_op jit(solution)/shard_map/ppermute | solution.py:288
  43.9 4.3 %collective-permute-start.1 = (bf16[16,16,256]{2,1,0:T(8,128)(2,1)S(1)}, bf16[16,16,256]{2,1,0:T(8,128)(2,1)S(1)}, u32[]{:S(2)}, u32[]{:S(2)}) collective-permute-start(bf16[16,16,256]{2,1,0:T(8,128)(2,1)S(1)} %all-to-all-done), channel_id=1, source_target_pairs={{0,64},{16,80},{32,96},{48,112},{64,0},{80,16},{96,32},{112,48},{1... | collective-permute-start | bytes 393224 | tf_op jit(solution)/shard_map/ppermute | solution.py:288
  48.2 3.1 %collective-permute-start.2 = (bf16[16,16,256]{2,1,0:T(8,128)(2,1)S(1)}, bf16[16,16,256]{2,1,0:T(8,128)(2,1)S(1)}, u32[]{:S(2)}, u32[]{:S(2)}) collective-permute-start(bf16[16,16,256]{2,1,0:T(8,128)(2,1)S(1)} %all-to-all-done), channel_id=1, source_target_pairs={{0,96},{16,112},{32,0},{48,16},{64,32},{80,48},{96,64},{112,80},{1... | collective-permute-start | bytes 393224 | tf_op jit(solution)/shard_map/ppermute | solution.py:288
  51.3 6.2 %build_counts.1 = (bf16[1024,1024]{1,0:T(8,128)(2,1)}, bf16[512,1024]{1,0:T(8,128)(2,1)}, f32[512,1024]{1,0:T(8,128)}) custom-call(bf16[64,1024]{1,0:T(8,128)(2,1)} %x_hbm.3, s32[8,1024]{1,0:T(8,128)} %bitcast.28, s32[2,1024]{1,0:T(2,128)} %bitcast.20), custom_call_target="tpu_custom_call" | custom-call | flops 1073741824 | bytes 4194304 | tf_op jit(solution)/shard_map/build_counts/pallas_call | solution.py:116
  57.7 5.7 %aggregate.1 = (bf16[16,96,128]{2,1,0:T(8,128)(2,1)}, f32[8,1024]{1,0:T(8,128)S(1)}) custom-call(bf16[64,1024]{1,0:T(8,128)(2,1)S(1)} %copy-done.7, bf16[32,80,128]{2,1,0:T(8,128)(2,1)S(1)} %all-to-all-done.1.inc_ref, s32[32,128]{1,0:T(8,128)S(1)} %bitcast.17, f32[512,1024]{1,0:T(8,128)} %get-tuple-element.35.sum_hbm, s32[2,1024]{1,0:T(2,128)S(1)} %bitcast.21, ...), custom_call_target="tpu_custom_call" | custom-call | flops 2952790016 | bytes 3145728 | tf_op jit(solution)/shard_map/aggregate/pallas_call | solution.py:195
  63.3 3.6 %all-to-all-start.2 = ((bf16[16,96,128]{2,1,0:T(8,128)(2,1)}), bf16[16,96,128]{2,1,0:T(8,128)(2,1)S(1)}, u32[]{:S(2)}, u32[]{:S(2)}) async-start(bf16[16,96,128]{2,1,0:T(8,128)(2,1)} %get-tuple-element.36), calls=%async_computation.2 | async-start | bytes 786432 | tf_op jit(solution)/shard_map/all_to_all | solution.py:641
  66.9 3.1 %collective-permute-start.3 = (bf16[4,16,16,256]{3,2,1,0:T(8,128)(2,1)S(1)}, bf16[4,16,16,256]{3,2,1,0:T(8,128)(2,1)S(1)}, u32[]{:S(2)}, u32[]{:S(2)}) collective-permute-start(bf16[4,16,16,256]{3,2,1,0:T(8,128)(2,1)S(1)} %pad_maximum_fusion.refs_0_), channel_id=1, source_target_pairs={{0,128},{16,144},{32,160},{48,176},{64,192},{80,208},{96,224},{112... | collective-permute-start | bytes 1572872 | tf_op jit(solution)/shard_map/ppermute | solution.py:288
  70.0 4.4 %collective-permute-start.4 = (bf16[4,16,16,256]{3,2,1,0:T(8,128)(2,1)S(1)}, bf16[4,16,16,256]{3,2,1,0:T(8,128)(2,1)S(1)}, u32[]{:S(2)}, u32[]{:S(2)}) collective-permute-start(bf16[4,16,16,256]{3,2,1,0:T(8,128)(2,1)S(1)} %pad_maximum_fusion.refs_0_), channel_id=1, source_target_pairs={{0,256},{16,272},{32,288},{48,304},{64,320},{80,336},{96,352},{112... | collective-permute-start | bytes 1572872 | tf_op jit(solution)/shard_map/ppermute | solution.py:288
  74.4 3.0 %collective-permute-start.5 = (bf16[4,16,16,256]{3,2,1,0:T(8,128)(2,1)S(1)}, bf16[4,16,16,256]{3,2,1,0:T(8,128)(2,1)S(1)}, u32[]{:S(2)}, u32[]{:S(2)}) collective-permute-start(bf16[4,16,16,256]{3,2,1,0:T(8,128)(2,1)S(1)} %pad_maximum_fusion.refs_0_), channel_id=1, source_target_pairs={{0,384},{16,400},{32,416},{48,432},{64,448},{80,464},{96,480},{112... | collective-permute-start | bytes 1572872 | tf_op jit(solution)/shard_map/ppermute | solution.py:288
  77.5 4.5 %collective-permute-done.3.refs_1_ = bf16[4,16,16,256]{3,2,1,0:T(8,128)(2,1)S(1)} collective-permute-done((bf16[4,16,16,256]{3,2,1,0:T(8,128)(2,1)S(1)}, bf16[4,16,16,256]{3,2,1,0:T(8,128)(2,1)S(1)}, u32[]{:S(2)}, u32[]{:S(2)}) %collective-permute-start.3) | collective-permute-done | bytes 524320 | tf_op jit(solution)/shard_map/ppermute | solution.py:288
  82.0 12.2 %collective-permute-done.4.refs_2_ = bf16[4,16,16,256]{3,2,1,0:T(8,128)(2,1)S(1)} collective-permute-done((bf16[4,16,16,256]{3,2,1,0:T(8,128)(2,1)S(1)}, bf16[4,16,16,256]{3,2,1,0:T(8,128)(2,1)S(1)}, u32[]{:S(2)}, u32[]{:S(2)}) %collective-permute-start.4) | collective-permute-done | bytes 524320 | tf_op jit(solution)/shard_map/ppermute | solution.py:288
  94.2 2.4 collective-permute-done.5.refs_3_
  96.6 1.5 regroup.1
  98.1 6.1 %all-to-all-start.3 = ((bf16[32,64,256]{2,1,0:T(8,128)(2,1)}), bf16[32,64,256]{2,1,0:T(8,128)(2,1)}, u32[]{:S(2)}, u32[]{:S(2)}) async-start(bf16[32,64,256]{2,1,0:T(8,128)(2,1)} %regroup.1), calls=%async_computation.3 | async-start | bytes 2097152 | tf_op jit(solution)/shard_map/all_to_all | solution.py:641
  104.2 2.2 collective-permute-start.6
  106.5 64.8 %place_weights.1.weights_hbm.weights_ref = bf16[2,16,128,256]{3,2,1,0:T(8,128)(2,1)} custom-call(bf16[4,16,16,256]{3,2,1,0:T(8,128)(2,1)} %copy-done.14, bf16[4,16,16,256]{3,2,1,0:T(8,128)(2,1)} %copy-done.15, bf16[4,16,16,256]{3,2,1,0:T(8,128)(2,1)} %copy-done.16, bf16[4,16,16,256]{3,2,1,0:T(8,128)(2,1)} %copy-done.17), custom_call_target="tpu_custom_call" | custom-call | bytes 4194304 | tf_op jit(solution)/shard_map/place_weights/pallas_call | solution.py:271
  173.0 3.6 %forward.1 = (bf16[16,128,256]{2,1,0:T(8,128)(2,1)}, bf16[128,512]{1,0:T(8,128)(2,1)}, bf16[2,8,32,128]{3,2,1,0:T(8,128)(2,1)}) custom-call(bf16[2,64,2048]{2,1,0:T(8,128)(2,1)} %copy-done.3, bf16[2,64,512]{2,1,0:T(8,128)(2,1)} %copy-done.6, bf16[2,16,128,256]{3,2,1,0:T(8,128)(2,1)} %place_weights.1.weights_hbm.weights_ref), custom_call_target="tpu_custom_call" | custom-call | flops 536870912 | bytes 4194304 | tf_op jit(solution)/shard_map/forward/pallas_call | solution.py:364
  176.7 6.9 %all-to-all-start.4 = ((bf16[16,128,256]{2,1,0:T(8,128)(2,1)}), bf16[16,128,256]{2,1,0:T(8,128)(2,1)S(1)}, u32[]{:S(2)}, u32[]{:S(2)}) async-start(bf16[16,128,256]{2,1,0:T(8,128)(2,1)} %get-tuple-element.45), calls=%async_computation.4 | async-start | bytes 2097152 | tf_op jit(solution)/shard_map/all_to_all | solution.py:641
  183.6 1.6 backward.1
  186.6 2.4 collective-permute-start.7
  189.0 2.0 collective-permute-start.8
  195.0 5.2 %all-to-all-done.4 = bf16[16,128,256]{2,1,0:T(8,128)(2,1)S(1)} async-done(((bf16[16,128,256]{2,1,0:T(8,128)(2,1)}), bf16[16,128,256]{2,1,0:T(8,128)(2,1)S(1)}, u32[]{:S(2)}, u32[]{:S(2)}) %all-to-all-start.4) | async-done | bytes 1048608 | tf_op jit(solution)/shard_map/all_to_all | solution.py:641
  201.5 33.4 %all_to_all.35.back_ref.back_hbm = bf16[16,128,128]{2,1,0:T(8,128)(2,1)} all-to-all(bf16[16,128,128]{2,1,0:T(8,128)(2,1)S(1)} %weight_parts.1), channel_id=1, replica_groups=mesh['row'=32,'col'=16] {'col'}, dimensions={0} | all-to-all | bytes 1048576 | tf_op jit(solution)/shard_map/all_to_all | solution.py:641
  234.9 4.5 %return_slots.1 = bf16[32,112,128]{2,1,0:T(8,128)(2,1)} custom-call(bf16[16,128,128]{2,1,0:T(8,128)(2,1)} %all_to_all.35.back_ref.back_hbm, s32[32,128]{1,0:T(8,128)} %bitcast.16, bf16[512,1024]{1,0:T(8,128)(2,1)} %get-tuple-element.55.hubs_hbm), custom_call_target="tpu_custom_call" | custom-call | flops 2415919104 | bytes 3145728 | tf_op jit(solution)/shard_map/return_slots/pallas_call | solution.py:523
  239.4 12.6 %all-to-all-start.6 = ((bf16[32,112,128]{2,1,0:T(8,128)(2,1)}), bf16[32,112,128]{2,1,0:T(8,128)(2,1)S(1)}, u32[]{:S(2)}, u32[]{:S(2)}) async-start(bf16[32,112,128]{2,1,0:T(8,128)(2,1)} %return_slots.1), calls=%async_computation.6 | async-start | bytes 1835008 | tf_op jit(solution)/shard_map/all_to_all | solution.py:641
  252.0 3.9 %local_grads.1 = (f32[512,1024]{1,0:T(8,128)}, bf16[64,1024]{1,0:T(8,128)(2,1)}) custom-call(bf16[16,128,128]{2,1,0:T(8,128)(2,1)} %all_to_all.35.back_ref.back_hbm, bf16[1024,1024]{1,0:T(8,128)(2,1)} %get-tuple-element.53.local_ref), custom_call_target="tpu_custom_call" | custom-call | flops 536870912 | bytes 3145728 | tf_op jit(solution)/shard_map/local_grads/pallas_call | solution.py:555
  256.0 11.8 %all-to-all-done.6.back_ref = bf16[32,112,128]{2,1,0:T(8,128)(2,1)S(1)} async-done(((bf16[32,112,128]{2,1,0:T(8,128)(2,1)}), bf16[32,112,128]{2,1,0:T(8,128)(2,1)S(1)}, u32[]{:S(2)}, u32[]{:S(2)}) %all-to-all-start.6) | async-done | bytes 917536 | tf_op jit(solution)/shard_map/all_to_all | solution.py:641
  267.8 4.5 %spread_grads.1 = (bf16[64,1024]{1,0:T(8,128)(2,1)}, f32[64,1024]{1,0:T(8,128)}, f32[64,1024]{1,0:T(8,128)}) custom-call(bf16[32,112,128]{2,1,0:T(8,128)(2,1)S(1)} %all-to-all-done.6.back_ref, s32[32,128]{1,0:T(8,128)S(1)} %bitcast.19, s32[1,16]{1,0:T(1,128)S(1)} %bitcast.23, f32[512,1024]{1,0:T(8,128)} %get-tuple-element.56.base_hbm), custom_call_target="tpu_custom_call" | custom-call | flops 2214592512 | bytes 2097152 | tf_op jit(solution)/shard_map/spread_grads/pallas_call | solution.py:613
  (55 shorter events, 9.9 us)
Async XLA Ops:
  2.1 27.8 %all-to-all-start = ((bf16[16,16,256]{2,1,0:T(8,128)(2,1)}), bf16[16,16,256]{2,1,0:T(8,128)(2,1)S(1)}, u32[]{:S(2)}, u32[]{:S(2)}) async-start(bf16[16,16,256]{2,1,0:T(8,128)(2,1)} %broadcast_in_dim.13), calls=%async_computation | async-start | bytes 262144 | tf_op jit(solution)/shard_map/all_to_all | solution.py:641
  29.8 27.8 %all-to-all-start.1 = ((bf16[32,80,128]{2,1,0:T(8,128)(2,1)}), bf16[32,80,128]{2,1,0:T(8,128)(2,1)S(1)}, u32[]{:S(2)}, u32[]{:S(2)}) async-start(bf16[32,80,128]{2,1,0:T(8,128)(2,1)} %gather_slots.1), calls=%async_computation.1 | async-start | bytes 1310720 | tf_op jit(solution)/shard_map/all_to_all | solution.py:641
  40.6 16.9 %collective-permute-start = (bf16[16,16,256]{2,1,0:T(8,128)(2,1)S(1)}, bf16[16,16,256]{2,1,0:T(8,128)(2,1)S(1)}, u32[]{:S(2)}, u32[]{:S(2)}) collective-permute-start(bf16[16,16,256]{2,1,0:T(8,128)(2,1)S(1)} %all-to-all-done), channel_id=1, source_target_pairs={{0,32},{16,48},{32,64},{48,80},{64,96},{80,112},{96,0},{112,16},{1... | collective-permute-start | bytes 393224 | tf_op jit(solution)/shard_map/ppermute | solution.py:288
  43.9 13.6 %collective-permute-start.1 = (bf16[16,16,256]{2,1,0:T(8,128)(2,1)S(1)}, bf16[16,16,256]{2,1,0:T(8,128)(2,1)S(1)}, u32[]{:S(2)}, u32[]{:S(2)}) collective-permute-start(bf16[16,16,256]{2,1,0:T(8,128)(2,1)S(1)} %all-to-all-done), channel_id=1, source_target_pairs={{0,64},{16,80},{32,96},{48,112},{64,0},{80,16},{96,32},{112,48},{1... | collective-permute-start | bytes 393224 | tf_op jit(solution)/shard_map/ppermute | solution.py:288
  48.2 9.3 %collective-permute-start.2 = (bf16[16,16,256]{2,1,0:T(8,128)(2,1)S(1)}, bf16[16,16,256]{2,1,0:T(8,128)(2,1)S(1)}, u32[]{:S(2)}, u32[]{:S(2)}) collective-permute-start(bf16[16,16,256]{2,1,0:T(8,128)(2,1)S(1)} %all-to-all-done), channel_id=1, source_target_pairs={{0,96},{16,112},{32,0},{48,16},{64,32},{80,48},{96,64},{112,80},{1... | collective-permute-start | bytes 393224 | tf_op jit(solution)/shard_map/ppermute | solution.py:288
  51.3 6.3 %copy-start.7 = (bf16[64,1024]{1,0:T(8,128)(2,1)S(1)}, bf16[64,1024]{1,0:T(8,128)(2,1)}, u32[]{:S(2)}) copy-start(bf16[64,1024]{1,0:T(8,128)(2,1)} %x_hbm.3) | copy-start | bytes 393220
  51.3 6.3 %copy-start.8 = (bf16[64,1024]{1,0:T(8,128)(2,1)S(1)}, bf16[64,1024]{1,0:T(8,128)(2,1)}, u32[]{:S(2)}) copy-start(bf16[64,1024]{1,0:T(8,128)(2,1)} %cot_hbm.1) | copy-start | bytes 393220
  51.3 6.3 %copy-start.10 = (s32[1,32,128]{2,1,0:T(8,128)S(1)}, s32[1,32,128]{2,1,0:T(8,128)}, u32[]{:S(2)}) copy-start(s32[1,32,128]{2,1,0:T(8,128)} %param.15) | copy-start | bytes 49156
  51.3 6.3 %copy-start.12 = (s32[1024,2]{0,1:T(2,128)S(1)}, s32[1024,2]{0,1:T(2,128)}, u32[]{:S(2)}) copy-start(s32[1024,2]{0,1:T(2,128)} %param.17) | copy-start | bytes 24580
  57.6 16.8 %copy-start.14 = (bf16[4,16,16,256]{3,2,1,0:T(8,128)(2,1)}, bf16[4,16,16,256]{3,2,1,0:T(8,128)(2,1)S(1)}, u32[]{:S(2)}) copy-start(bf16[4,16,16,256]{3,2,1,0:T(8,128)(2,1)S(1)} %pad_maximum_fusion.refs_0_) | copy-start | bytes 1572868
  63.3 33.2 %all-to-all-start.2 = ((bf16[16,96,128]{2,1,0:T(8,128)(2,1)}), bf16[16,96,128]{2,1,0:T(8,128)(2,1)S(1)}, u32[]{:S(2)}, u32[]{:S(2)}) async-start(bf16[16,96,128]{2,1,0:T(8,128)(2,1)} %get-tuple-element.36), calls=%async_computation.2 | async-start | bytes 786432 | tf_op jit(solution)/shard_map/all_to_all | solution.py:641
  66.9 15.0 %collective-permute-start.3 = (bf16[4,16,16,256]{3,2,1,0:T(8,128)(2,1)S(1)}, bf16[4,16,16,256]{3,2,1,0:T(8,128)(2,1)S(1)}, u32[]{:S(2)}, u32[]{:S(2)}) collective-permute-start(bf16[4,16,16,256]{3,2,1,0:T(8,128)(2,1)S(1)} %pad_maximum_fusion.refs_0_), channel_id=1, source_target_pairs={{0,128},{16,144},{32,160},{48,176},{64,192},{80,208},{96,224},{112... | collective-permute-start | bytes 1572872 | tf_op jit(solution)/shard_map/ppermute | solution.py:288
  70.0 24.1 %collective-permute-start.4 = (bf16[4,16,16,256]{3,2,1,0:T(8,128)(2,1)S(1)}, bf16[4,16,16,256]{3,2,1,0:T(8,128)(2,1)S(1)}, u32[]{:S(2)}, u32[]{:S(2)}) collective-permute-start(bf16[4,16,16,256]{3,2,1,0:T(8,128)(2,1)S(1)} %pad_maximum_fusion.refs_0_), channel_id=1, source_target_pairs={{0,256},{16,272},{32,288},{48,304},{64,320},{80,336},{96,352},{112... | collective-permute-start | bytes 1572872 | tf_op jit(solution)/shard_map/ppermute | solution.py:288
  74.4 22.2 %collective-permute-start.5 = (bf16[4,16,16,256]{3,2,1,0:T(8,128)(2,1)S(1)}, bf16[4,16,16,256]{3,2,1,0:T(8,128)(2,1)S(1)}, u32[]{:S(2)}, u32[]{:S(2)}) collective-permute-start(bf16[4,16,16,256]{3,2,1,0:T(8,128)(2,1)S(1)} %pad_maximum_fusion.refs_0_), channel_id=1, source_target_pairs={{0,384},{16,400},{32,416},{48,432},{64,448},{80,464},{96,480},{112... | collective-permute-start | bytes 1572872 | tf_op jit(solution)/shard_map/ppermute | solution.py:288
  82.0 24.5 %copy-start.15 = (bf16[4,16,16,256]{3,2,1,0:T(8,128)(2,1)}, bf16[4,16,16,256]{3,2,1,0:T(8,128)(2,1)S(1)}, u32[]{:S(2)}) copy-start(bf16[4,16,16,256]{3,2,1,0:T(8,128)(2,1)S(1)} %collective-permute-done.3.refs_1_) | copy-start | bytes 1572868
  94.2 12.3 %copy-start.16 = (bf16[4,16,16,256]{3,2,1,0:T(8,128)(2,1)}, bf16[4,16,16,256]{3,2,1,0:T(8,128)(2,1)S(1)}, u32[]{:S(2)}) copy-start(bf16[4,16,16,256]{3,2,1,0:T(8,128)(2,1)S(1)} %collective-permute-done.4.refs_2_) | copy-start | bytes 1572868
  96.6 9.9 %copy-start.17 = (bf16[4,16,16,256]{3,2,1,0:T(8,128)(2,1)}, bf16[4,16,16,256]{3,2,1,0:T(8,128)(2,1)S(1)}, u32[]{:S(2)}) copy-start(bf16[4,16,16,256]{3,2,1,0:T(8,128)(2,1)S(1)} %collective-permute-done.5.refs_3_) | copy-start | bytes 1572868
  98.1 78.5 %all-to-all-start.3 = ((bf16[32,64,256]{2,1,0:T(8,128)(2,1)}), bf16[32,64,256]{2,1,0:T(8,128)(2,1)}, u32[]{:S(2)}, u32[]{:S(2)}) async-start(bf16[32,64,256]{2,1,0:T(8,128)(2,1)} %regroup.1), calls=%async_computation.3 | async-start | bytes 2097152 | tf_op jit(solution)/shard_map/all_to_all | solution.py:641
  104.2 67.1 %collective-permute-start.6 = (bf16[16,96,128]{2,1,0:T(8,128)(2,1)S(1)}, bf16[16,96,128]{2,1,0:T(8,128)(2,1)S(1)}, u32[]{:S(2)}, u32[]{:S(2)}) collective-permute-start(bf16[16,96,128]{2,1,0:T(8,128)(2,1)S(1)} %all-to-all-done.2.inc_ref.own_block), channel_id=1, source_target_pairs={{0,16},{16,0},{32,48},{48,32},{64,80},{80,64},{96,112},{112,96},{1... | collective-permute-start | bytes 1179656 | tf_op jit(solution)/shard_map/ppermute | solution.py:645
  171.5 0.8 copy-start.3
  172.3 0.7 copy-start.6
  173.0 10.6 %copy-start = (bf16[2,16,128,256]{3,2,1,0:T(8,128)(2,1)S(1)}, bf16[2,16,128,256]{3,2,1,0:T(8,128)(2,1)}, u32[]{:S(2)}) copy-start(bf16[2,16,128,256]{3,2,1,0:T(8,128)(2,1)} %place_weights.1.weights_hbm.weights_ref) | copy-start | bytes 6291460
  176.6 6.9 %copy-start.4 = (bf16[128,512]{1,0:T(8,128)(2,1)S(1)}, bf16[128,512]{1,0:T(8,128)(2,1)}, u32[]{:S(2)}) copy-start(bf16[128,512]{1,0:T(8,128)(2,1)} %get-tuple-element.46.slopes_ref) | copy-start | bytes 393220
  176.6 6.9 %copy-start.5 = (bf16[2,8,32,128]{3,2,1,0:T(8,128)(2,1)S(1)}, bf16[2,8,32,128]{3,2,1,0:T(8,128)(2,1)}, u32[]{:S(2)}) copy-start(bf16[2,8,32,128]{3,2,1,0:T(8,128)(2,1)} %get-tuple-element.47.hidden_ref) | copy-start | bytes 393220
  176.7 23.6 %all-to-all-start.4 = ((bf16[16,128,256]{2,1,0:T(8,128)(2,1)}), bf16[16,128,256]{2,1,0:T(8,128)(2,1)S(1)}, u32[]{:S(2)}, u32[]{:S(2)}) async-start(bf16[16,128,256]{2,1,0:T(8,128)(2,1)} %get-tuple-element.45), calls=%async_computation.4 | async-start | bytes 2097152 | tf_op jit(solution)/shard_map/all_to_all | solution.py:641
  185.2 0.8 copy-start.1
  186.6 5.7 %collective-permute-start.7 = (f32[64,2048]{1,0:T(8,128)}, f32[64,2048]{1,0:T(8,128)S(1)}, u32[]{:S(2)}, u32[]{:S(2)}) collective-permute-start(f32[64,2048]{1,0:T(8,128)} %get-tuple-element.49), channel_id=1, source_target_pairs={{0,16},{16,0},{32,48},{48,32},{64,80},{80,64},{96,112},{112,96},{1... | collective-permute-start | bytes 1572872 | tf_op jit(solution)/shard_map/ppermute | solution.py:645
  189.0 3.4 %collective-permute-start.8 = (bf16[8,32,128]{2,1,0:T(8,128)(2,1)}, bf16[8,32,128]{2,1,0:T(8,128)(2,1)S(1)}, u32[]{:S(2)}, u32[]{:S(2)}) collective-permute-start(bf16[8,32,128]{2,1,0:T(8,128)(2,1)} %copy-done.9), channel_id=1, source_target_pairs={{0,16},{16,0},{32,48},{48,32},{64,80},{80,64},{96,112},{112,96},{1... | collective-permute-start | bytes 196616 | tf_op jit(solution)/shard_map/ppermute | solution.py:645
  192.4 1.0 copy-start.2
  239.4 28.4 %copy-start.11 = (s32[1,32,128]{2,1,0:T(8,128)S(1)}, s32[1,32,128]{2,1,0:T(8,128)}, u32[]{:S(2)}) copy-start(s32[1,32,128]{2,1,0:T(8,128)} %param.14) | copy-start | bytes 49156
  239.4 28.4 %copy-start.13 = (s32[16]{0:T(128)S(1)}, s32[16]{0:T(128)}, u32[]{:S(2)}) copy-start(s32[16]{0:T(128)} %param.16) | copy-start | bytes 196
  239.4 28.4 %all-to-all-start.6 = ((bf16[32,112,128]{2,1,0:T(8,128)(2,1)}), bf16[32,112,128]{2,1,0:T(8,128)(2,1)S(1)}, u32[]{:S(2)}, u32[]{:S(2)}) async-start(bf16[32,112,128]{2,1,0:T(8,128)(2,1)} %return_slots.1), calls=%async_computation.6 | async-start | bytes 1835008 | tf_op jit(solution)/shard_map/all_to_all | solution.py:641
  (1 other events, 0.6 us)

commit v8 on v6

--- a/solution.py
+++ b/solution.py
@@ -215,30 +215,32 @@
     )(feats, incoming, recv_lanes, local_sum, hub_lanes, cotangent)
 
 
-PIECE = 16
+PIECE = 32
 TILE = 256
+CHIPS = PEERS // 2
+SLICE = LAYERS * PIECE
 
 
 def regroup_kernel(inc_ref, out_ref):
     group = lax.broadcasted_iota(jnp.int32, (OWN, SLOTS), 1) // PIECE
-    for half in range(2):
-        blocks = [inc_ref[8 * half + i, :OWN, :].astype(F32) for i in range(8)]
-        for slice_of in range(8):
+    for part in range(4):
+        blocks = [inc_ref[4 * part + i, :OWN, :].astype(F32) for i in range(4)]
+        for slice_of in range(4):
             tile = jnp.zeros((OWN, SLOTS), F32)
-            for i in range(8):
+            for i in range(4):
                 moved = blocks[i]
                 if i != slice_of:
                     moved = pltpu.roll(moved, (PIECE * (i - slice_of)) % SLOTS, 1)
                 tile = jnp.where(group == i, moved, tile)
             tile = tile.astype(BF16)
             for outs in range(4):
-                out_ref[4 * slice_of + outs, :, SLOTS * half : SLOTS * (half + 1)] = tile
+                out_ref[4 * slice_of + outs, :, SLOTS * part : SLOTS * (part + 1)] = tile
 
 
 def regroup(node_block):
     return pl.pallas_call(
         regroup_kernel,
-        out_shape=jax.ShapeDtypeStruct((PEERS, OWN, TILE), BF16),
+        out_shape=jax.ShapeDtypeStruct((CHIPS, OWN, SLICE), BF16),
         compiler_params=params(16),
         cost_estimate=cost(1 << 24, 2 << 20),
         name="regroup",
@@ -246,16 +248,15 @@
 
 
 HALF = OUTS // 2
-CHIPS = PEERS // 2
 
 
 def prepare_kernel(own_block, other_block, joined_ref, cot_ref):
     core = lax.axis_index("row") % 2
     for layer in range(LAYERS):
         lanes = slice(SLOTS * layer, SLOTS * (layer + 1))
-        joined_ref[core, :, lanes] = own_block[layer, :OWN, :]
-        joined_ref[1 - core, :, lanes] = other_block[layer, :OWN, :]
-    for side, block in ((core, own_block), (1 - core, other_block)):
+        joined_ref[0, :, lanes] = own_block[layer, :OWN, :]
+        joined_ref[1, :, lanes] = other_block[layer, :OWN, :]
+    for side, block in enumerate((own_block, other_block)):
         for pair in range(LAYERS // 4):
             even = block[8 * core + 2 * pair, OWN:, :].astype(F32)
             odd = block[8 * core + 2 * pair + 1, OWN:, :].astype(F32)
@@ -303,11 +304,15 @@
         slope = sigmoid_part * (1.0 + preact * (1.0 - sigmoid_part))
         cot = cots[:, :, columns].reshape(2 * OWN, TILE).astype(F32)
         slopes = (cot * slope).astype(BF16)
-        out_tile[side] = slopes
-        for chip in range(side, CHIPS, 2):
-            copy = pltpu.make_async_copy(out_tile.at[side], slopes_hbm.at[chip], out_sems.at[chip])
-            copy.start()
-            sent.append(copy)
+        for outs in range(2):
+            out_tile[2 * side + outs] = slopes[:, SLOTS * outs : SLOTS * (outs + 1)]
+        for chip in range(CHIPS):
+            if chip % 4 // 2 == side:
+                copy = pltpu.make_async_copy(
+                    out_tile.at[chip % 4], slopes_hbm.at[chip], out_sems.at[chip]
+                )
+                copy.start()
+                sent.append(copy)
         flat[:, columns] = slopes
         for block in range(2):
             for layer in range(4):
@@ -327,7 +332,7 @@
         in_specs=[HBM, HBM, HBM],
         out_specs=[HBM, HBM, HBM],
         out_shape=[
-            jax.ShapeDtypeStruct((CHIPS, 2 * OWN, TILE), BF16),
+            jax.ShapeDtypeStruct((CHIPS, 2 * OWN, SLOTS), BF16),
             jax.ShapeDtypeStruct((2 * OWN, HALF), BF16),
             jax.ShapeDtypeStruct((2, LAYERS // 2, OWN // 2, SLOTS), BF16),
         ],
@@ -335,7 +340,7 @@
             pltpu.VMEM((2, OWN, 2 * OUTS), BF16),
             pltpu.VMEM((2, OWN, HALF), BF16),
             pltpu.VMEM((2 * OUTS, HALF), BF16),
-            pltpu.VMEM((2, 2 * OWN, TILE), BF16),
+            pltpu.VMEM((4, 2 * OWN, SLOTS), BF16),
             pltpu.VMEM((2 * OWN, HALF), BF16),
             pltpu.VMEM((2, LAYERS // 2, OWN // 2, SLOTS), BF16),
             pltpu.SemaphoreType.DMA((4,)),
@@ -347,15 +352,12 @@
     )(joined, cots, weights)
 
 
-def backward_kernel(slopes_ref, hidden_ref, weights_ref, keep_ref, send_ref, keep_hidden, send_hidden, parts):
-    core = lax.axis_index("row") % 2
+def backward_kernel(slopes_ref, hidden_ref, weights_ref, keep_ref, send_ref, keep_hidden, send_hidden):
     back = matmul(slopes_ref[...], weights_ref[...], NT)
-    parts[0] = back[:OWN, :]
-    parts[1] = back[OWN:, :]
-    keep_ref[...] = parts[core]
-    send_ref[...] = parts[1 - core]
-    keep_hidden[...] = hidden_ref[core]
-    send_hidden[...] = hidden_ref[1 - core]
+    keep_ref[...] = back[:OWN, :]
+    send_ref[...] = back[OWN:, :].astype(BF16)
+    keep_hidden[...] = hidden_ref[0]
+    send_hidden[...] = hidden_ref[1]
 
 
 def backward(slopes, hidden, weights):
@@ -363,9 +365,8 @@
     block = jax.ShapeDtypeStruct((LAYERS // 2, OWN // 2, SLOTS), BF16)
     return pl.pallas_call(
         backward_kernel,
-        out_shape=[part, part, block, block],
-        scratch_shapes=[pltpu.VMEM((2, OWN, 2 * OUTS), F32)],
-        compiler_params=params(16),
+        out_shape=[part, jax.ShapeDtypeStruct((OWN, 2 * OUTS), BF16), block, block],
+        compiler_params=params(60),
         cost_estimate=cost(2 * 256 * 2048 * 512, 4 << 20),
         name="backward",
     )(slopes, hidden, weights)
@@ -377,7 +378,7 @@
     divisor = jnp.where(direct, 1.0, degree_ref[...])
     for layer in range(LAYERS):
         lanes = slice(SLOTS * layer, SLOTS * (layer + 1))
-        back = mine_ref[:, lanes] + theirs_ref[:, lanes]
+        back = mine_ref[:, lanes] + theirs_ref[:, lanes].astype(F32)
         out_ref[layer, :OWN, :] = (back / divisor).astype(BF16)
     for layer in range(LAYERS // 2):
         out_ref[8 * core + layer, OWN:, :] = my_hidden[layer]
@@ -394,46 +395,36 @@
     )(mine, theirs, my_hidden, their_hidden, own_degree)
 
 
-STEPS = 4
-
-
-def weight_kernel(joined_hbm, slopes_ref, back_hbm, out_ref, joined, back, sems):
-    depth = PEERS * OWN // STEPS
-    staged = copies(
-        sems,
-        *[
-            (joined_hbm.at[:, depth * i : depth * (i + 1)], joined.at[:, depth * i : depth * (i + 1)])
-            for i in range(STEPS)
-        ],
-        (back_hbm, back),
-    )
-    part = jnp.zeros((TILE, TILE), F32)
-    for i in range(STEPS):
-        staged[i].wait()
-        rows = slice(depth * i, depth * (i + 1))
-        part = part + matmul(joined[:, rows], slopes_ref[rows, :], NN)
-    part = part.astype(BF16)
+def weight_kernel(mine_hbm, theirs_hbm, slopes_ref, back_hbm, out_ref, mine, theirs, back, sems):
+    staged = copies(sems, (mine_hbm, mine), (theirs_hbm, theirs), (back_hbm, back))
+    part = jnp.zeros((SLOTS, SLICE), F32)
+    for side, rows in enumerate((mine, theirs)):
+        slopes = slopes_ref[:, OWN * side : OWN * (side + 1), :].astype(F32)
+        columns = slopes.reshape(CHIPS * OWN, SLOTS).T.astype(BF16)
+        staged[side].wait()
+        part = part + matmul(columns, rows[...].reshape(CHIPS * OWN, SLICE), NN)
+    part = part.T.astype(BF16)
     for layer in range(LAYERS):
-        out_ref[layer, 96:112, :] = part[PIECE * layer : PIECE * (layer + 1), :SLOTS]
-        out_ref[layer, 112:, :] = part[PIECE * layer : PIECE * (layer + 1), SLOTS:]
-    staged[STEPS].wait()
+        out_ref[layer, 96:, :] = part[PIECE * layer : PIECE * (layer + 1), :]
+    staged[2].wait()
     out_ref[:, :96, :] = back[...]
 
 
-def weight_parts(joined_cols, slopes_rows, back):
+def weight_parts(mine, theirs, slopes_rows, back):
     return pl.pallas_call(
         weight_kernel,
-        in_specs=[HBM, VMEM, HBM],
+        in_specs=[HBM, HBM, VMEM, HBM],
         out_shape=jax.ShapeDtypeStruct((LAYERS, SLOTS, SLOTS), BF16),
         scratch_shapes=[
-            pltpu.VMEM((TILE, PEERS * OWN), BF16),
+            pltpu.VMEM((CHIPS, OWN, SLICE), BF16),
+            pltpu.VMEM((CHIPS, OWN, SLICE), BF16),
             pltpu.VMEM((LAYERS, 96, SLOTS), BF16),
-            pltpu.SemaphoreType.DMA((STEPS + 1,)),
+            pltpu.SemaphoreType.DMA((3,)),
         ],
         compiler_params=params(16),
         cost_estimate=cost(2 * 256 * 2048 * 256, 3 << 20),
         name="weight_parts",
-    )(joined_cols, slopes_rows, back)
+    )(mine, theirs, slopes_rows, back)
 
 
 RETURN_ROWS = 112
@@ -536,10 +527,8 @@
     for peer in range(PEERS):
         slots[:, SLOTS * peer : SLOTS * (peer + 1)] = back_ref[peer, :FEATS, :]
         grads = back_ref[peer, ROWS:, :].astype(F32)
-        slice_of, outs = peer // 4, 2 * (peer % 2) + peer // 2 % 2
-        rows = slice(PIECE * slice_of, PIECE * (slice_of + 1))
-        grads_ref[rows, TILE * outs : TILE * outs + SLOTS] = grads[:PIECE, :]
-        grads_ref[rows, TILE * outs + SLOTS : TILE * (outs + 1)] = grads[PIECE:, :]
+        slice_of, start = peer // 8, HALF * (peer % 2) + SLOTS * (peer // 2 % 4)
+        grads_ref[PIECE * slice_of : PIECE * (slice_of + 1), start : start + SLOTS] = grads
     sent = copies(
         out_sems, (grads_ref.at[:FEATS], self_hbm), (grads_ref.at[FEATS:], neigh_hbm)
     )
@@ -621,13 +610,15 @@
     outgoing, degree = aggregate(feats, incoming, recv_lanes, local_sum, hub_lanes, cotangent)
     node_block = exchange(outgoing, "col")
     own_degree = lax.dynamic_slice_in_dim(degree[0], OWN * lax.axis_index("col"), OWN)[:, None]
-    joined_cols = exchange(regroup(node_block), "row").reshape(PEERS * OWN, TILE).T
+    joined_mine = exchange(regroup(node_block), "row", SAME_CORE)
     joined, cots = prepare(node_block, other_core(node_block))
     slopes_out, slopes, hidden = forward(joined, cots, weights)
-    slopes_rows = exchange(slopes_out, "row", SAME_CORE).reshape(PEERS * OWN, TILE)
+    slopes_rows = exchange(slopes_out, "row", SAME_CORE)
+    joined_mine, slopes = lax.optimization_barrier((joined_mine, slopes))
+    joined_theirs = other_core(joined_mine)
     mine, theirs, my_hidden, their_hidden = backward(slopes, hidden, weights)
     back = combine(mine, other_core(theirs), my_hidden, other_core(their_hidden), own_degree)
-    back_block = exchange(weight_parts(joined_cols, slopes_rows, back), "col")
+    back_block = exchange(weight_parts(joined_mine, joined_theirs, slopes_rows, back), "col")
     returned = exchange(return_slots(back_block, recv_lanes, hubs), "row")
     base, hidden_out = local_grads(back_block, local)
     grad_feats, grad_self, grad_neigh = spread_grads(returned, send_lanes, hub_own, base)

time: 201 us -> 202 us (level)
  starting transfers between devices: 50.1 us -> 55.2 us
  waiting for transfers between devices: 28.3 us -> 23.6 us
  local copies, waits for them, and re-layouts: 6.47 us -> 3.56 us
  blocking collectives: 63.2 us -> 65.9 us
    ppermute x3 -> x4, starting transfers between devices: 9.57 us -> 17.3 us  [other_core(): return lax.ppermute(block, 'row', [(i, i ^ 1) for i in range(PEERS)])]
    all_to_all x4, waiting for transfers between devices: 26.9 us -> 20.7 us  [exchange(): lax.all_to_all(blocks, axis, 0, 0, axis_index_groups=groups, tiled=True)]
    all_to_all x4, starting transfers between devices: 40.5 us -> 37.8 us  [exchange(): lax.all_to_all(blocks, axis, 0, 0, axis_index_groups=groups, tiled=True)]
    all_to_all x2, blocking collectives: 63.2 us -> 65.9 us  [exchange(): lax.all_to_all(blocks, axis, 0, 0, axis_index_groups=groups, tiled=True)]
    unnamed x32 -> x20, local copies, waits for them, and re-layouts: 4.8 us -> 3.37 us
  transfers between devices with their start and end apart: 8 -> 9, of which waited for: 4 -> 7; matrix products, arithmetic and copies ran while one was open for 1% -> 0% of each run, Pallas kernels for 13% -> 13%
where the time goes in v8:
time: 202 us; the launch traced here: 201 us
  blocking collectives  65.9 us (33%)
  starting transfers between devices  55.2 us (27%)
  Pallas kernels  37.2 us (18%)
  waiting for transfers between devices  23.6 us (12%)
  between operations  14.3 us (7%)
  local copies, waits for them, and re-layouts  3.56 us (2%)
    all_to_all x2, blocking collectives, exchange(): lax.all_to_all(blocks, axis, 0, 0, axis_index_groups=groups, tiled=True)  65.9 us
    all_to_all x4, starting transfers between devices, exchange(): lax.all_to_all(blocks, axis, 0, 0, axis_index_groups=groups, tiled=True)  37.8 us
    all_to_all x4, waiting for transfers between devices, exchange(): lax.all_to_all(blocks, axis, 0, 0, axis_index_groups=groups, tiled=True)  20.7 us
    ppermute x4, starting transfers between devices, other_core(): return lax.ppermute(block, 'row', [(i, i ^ 1) for i in range(PEERS)])  17.3 us
    pallas_call x1, Pallas kernels, build_counts(): pl.pallas_call(build_kernel, grid=(NODES // BUILD,), in_specs=[whole((FEA...  6.23 us
    pallas_call x1, Pallas kernels, aggregate(): pl.pallas_call(aggregate_kernel, out_shape=[jax.ShapeDtypeStruct((LAYERS,...  4.94 us
    pallas_call x1, Pallas kernels, spread_grads(): pl.pallas_call(spread_kernel, in_specs=[VMEM, HBM, HBM, HBM], out_specs=[...  4.53 us
    pallas_call x1, Pallas kernels, return_slots(): pl.pallas_call(return_kernel, in_specs=[HBM, HBM, HBM], out_specs=HBM, ou...  4.49 us
  transfers between devices with their start and end apart: 9, of which 7 were waited for; matrix products, arithmetic and copies ran while one was open for 0% of the time, Pallas kernels for 13%

profile of v8, /device:TPU:1, one launch (start us, length us, event | category | flops | bytes accessed | tf_op | source)
XLA Modules:
  0.0 201.2 jit_solution(12105220858249455773)
XLA Ops:
  7.2 1.5 fusion
  8.8 3.5 %gather_slots.1 = bf16[32,80,128]{2,1,0:T(8,128)(2,1)} custom-call(bf16[64,1024]{1,0:T(8,128)(2,1)} %x_hbm.3, s32[32,128]{1,0:T(8,128)} %bitcast.9, s32[1,16]{1,0:T(1,128)} %bitcast.13), custom_call_target="tpu_custom_call" | custom-call | flops 2147483648 | bytes 1048576 | tf_op jit(solution)/shard_map/gather_slots/pallas_call | solution.py:80
  12.3 10.4 %all-to-all-start = ((bf16[32,80,128]{2,1,0:T(8,128)(2,1)}), bf16[32,80,128]{2,1,0:T(8,128)(2,1)S(1)}, u32[]{:S(2)}, u32[]{:S(2)}) async-start(bf16[32,80,128]{2,1,0:T(8,128)(2,1)} %gather_slots.1), calls=%async_computation | async-start | bytes 1310720 | tf_op jit(solution)/shard_map/all_to_all | solution.py:589
  22.8 6.2 %build_counts.1 = (bf16[1024,1024]{1,0:T(8,128)(2,1)}, bf16[512,1024]{1,0:T(8,128)(2,1)}, f32[512,1024]{1,0:T(8,128)}) custom-call(bf16[64,1024]{1,0:T(8,128)(2,1)} %x_hbm.3, s32[8,1024]{1,0:T(8,128)} %bitcast.15, s32[2,1024]{1,0:T(2,128)} %bitcast.11), custom_call_target="tpu_custom_call" | custom-call | flops 1073741824 | bytes 4194304 | tf_op jit(solution)/shard_map/build_counts/pallas_call | solution.py:116
  29.0 6.7 %all-to-all-done.inc_ref = bf16[32,80,128]{2,1,0:T(8,128)(2,1)S(1)} async-done(((bf16[32,80,128]{2,1,0:T(8,128)(2,1)}), bf16[32,80,128]{2,1,0:T(8,128)(2,1)S(1)}, u32[]{:S(2)}, u32[]{:S(2)}) %all-to-all-start) | async-done | bytes 655392 | tf_op jit(solution)/shard_map/all_to_all | solution.py:589
  35.8 4.9 %aggregate.1 = (bf16[16,96,128]{2,1,0:T(8,128)(2,1)S(1)}, f32[8,1024]{1,0:T(8,128)S(1)}) custom-call(bf16[64,1024]{1,0:T(8,128)(2,1)S(1)} %copy-done.4, bf16[32,80,128]{2,1,0:T(8,128)(2,1)S(1)} %all-to-all-done.inc_ref, s32[32,128]{1,0:T(8,128)S(1)} %bitcast.8, f32[512,1024]{1,0:T(8,128)} %get-tuple-element.25.sum_hbm, s32[2,1024]{1,0:T(2,128)S(1)} %bitcast.12, ...), custom_call_target="tpu_custom_call" | custom-call | flops 2952790016 | bytes 3145728 | tf_op jit(solution)/shard_map/aggregate/pallas_call | solution.py:195
  40.7 36.4 %all_to_all.30.inc_ref.own_block = bf16[16,96,128]{2,1,0:T(8,128)(2,1)S(1)} all-to-all(bf16[16,96,128]{2,1,0:T(8,128)(2,1)S(1)} %get-tuple-element.26), channel_id=1, replica_groups=mesh['row'=32,'col'=16] {'col'}, dimensions={0} | all-to-all | bytes 786432 | tf_op jit(solution)/shard_map/all_to_all | solution.py:589
  77.1 1.3 regroup.1
  78.4 6.0 %all-to-all-start.2 = ((bf16[16,64,512]{2,1,0:T(8,128)(2,1)}), bf16[16,64,512]{2,1,0:T(8,128)(2,1)S(1)}, u32[]{:S(2)}, u32[]{:S(2)}) async-start(bf16[16,64,512]{2,1,0:T(8,128)(2,1)} %regroup.1), calls=%async_computation.2 | async-start | bytes 2097152 | tf_op jit(solution)/shard_map/all_to_all | solution.py:589
  84.4 5.2 %collective-permute-start = (bf16[16,96,128]{2,1,0:T(8,128)(2,1)S(1)}, bf16[16,96,128]{2,1,0:T(8,128)(2,1)S(1)}, u32[]{:S(2)}, u32[]{:S(2)}) collective-permute-start(bf16[16,96,128]{2,1,0:T(8,128)(2,1)S(1)} %all_to_all.30.inc_ref.own_block), channel_id=1, source_target_pairs={{0,16},{16,0},{32,48},{48,32},{64,80},{80,64},{96,112},{112,96},{1... | collective-permute-start | bytes 1179656 | tf_op jit(solution)/shard_map/ppermute | solution.py:593
  89.5 1.3 collective-permute-done.other_block
  90.9 0.2 prepare.1
  91.1 0.8 copy-done.1
  91.9 0.7 copy-done.2
  92.5 0.4 all-gather.2.cloned.1.call-done.weights_hbm.weights_ref
  93.0 3.3 %forward.1 = (bf16[16,128,128]{2,1,0:T(8,128)(2,1)}, bf16[128,512]{1,0:T(8,128)(2,1)}, bf16[2,8,32,128]{3,2,1,0:T(8,128)(2,1)}) custom-call(bf16[2,64,2048]{2,1,0:T(8,128)(2,1)} %copy-done.1, bf16[2,64,512]{2,1,0:T(8,128)(2,1)} %copy-done.2, bf16[2048,512]{1,0:T(8,128)(2,1)} %all-gather.2.cloned.1.call-done.weights_hbm.weights_ref), custom_call_target="tpu_custom_call" | custom-call | flops 536870912 | bytes 4194304 | tf_op jit(solution)/shard_map/forward/pallas_call | solution.py:330
  96.3 2.1 %all-to-all-done.2.mine_hbm = bf16[16,64,512]{2,1,0:T(8,128)(2,1)S(1)} async-done(((bf16[16,64,512]{2,1,0:T(8,128)(2,1)}), bf16[16,64,512]{2,1,0:T(8,128)(2,1)S(1)}, u32[]{:S(2)}, u32[]{:S(2)}) %all-to-all-start.2) | async-done | bytes 1048608 | tf_op jit(solution)/shard_map/all_to_all | solution.py:589
  98.4 7.9 %collective-permute-start.1 = (bf16[16,64,512]{2,1,0:T(8,128)(2,1)S(1)}, bf16[16,64,512]{2,1,0:T(8,128)(2,1)S(1)}, u32[]{:S(2)}, u32[]{:S(2)}) collective-permute-start(bf16[16,64,512]{2,1,0:T(8,128)(2,1)S(1)} %all-to-all-done.2.mine_hbm), channel_id=1, source_target_pairs={{0,16},{16,0},{32,48},{48,32},{64,80},{80,64},{96,112},{112,96},{1... | collective-permute-start | bytes 3145736 | tf_op jit(solution)/shard_map/ppermute | solution.py:593
  106.3 7.2 %all-to-all-start.3 = ((bf16[16,128,128]{2,1,0:T(8,128)(2,1)}), bf16[16,128,128]{2,1,0:T(8,128)(2,1)S(1)}, u32[]{:S(2)}, u32[]{:S(2)}) async-start(bf16[16,128,128]{2,1,0:T(8,128)(2,1)} %get-tuple-element.31), calls=%async_computation.3 | async-start | bytes 1048576 | tf_op jit(solution)/shard_map/all_to_all | solution.py:589
  113.5 3.4 %backward.1 = (f32[64,2048]{1,0:T(8,128)}, bf16[64,2048]{1,0:T(8,128)(2,1)}, bf16[8,32,128]{2,1,0:T(8,128)(2,1)}, bf16[8,32,128]{2,1,0:T(8,128)(2,1)}) custom-call(bf16[128,512]{1,0:T(8,128)(2,1)} %get-tuple-element.32.slopes_ref, bf16[2,8,32,128]{3,2,1,0:T(8,128)(2,1)} %get-tuple-element.33.hidden_ref, ...), custom_call_target="tpu_custom_call" | custom-call | flops 536870912 | bytes 4194304 | tf_op jit(solution)/shard_map/backward/pallas_call | solution.py:366
  116.9 2.2 %collective-permute-start.2 = (bf16[64,2048]{1,0:T(8,128)(2,1)}, bf16[64,2048]{1,0:T(8,128)(2,1)S(1)}, u32[]{:S(2)}, u32[]{:S(2)}) collective-permute-start(bf16[64,2048]{1,0:T(8,128)(2,1)} %get-tuple-element.35), channel_id=1, source_target_pairs={{0,16},{16,0},{32,48},{48,32},{64,80},{80,64},{96,112},{112,96},{1... | collective-permute-start | bytes 786440 | tf_op jit(solution)/shard_map/ppermute | solution.py:593
  119.1 2.1 %collective-permute-start.3 = (bf16[8,32,128]{2,1,0:T(8,128)(2,1)}, bf16[8,32,128]{2,1,0:T(8,128)(2,1)S(1)}, u32[]{:S(2)}, u32[]{:S(2)}) collective-permute-start(bf16[8,32,128]{2,1,0:T(8,128)(2,1)} %get-tuple-element.37), channel_id=1, source_target_pairs={{0,16},{16,0},{32,48},{48,32},{64,80},{80,64},{96,112},{112,96},{1... | collective-permute-start | bytes 196616 | tf_op jit(solution)/shard_map/ppermute | solution.py:593
  121.4 1.1 collective-permute-done.3.their_hidden
  122.5 1.0 copy-done
  123.5 0.8 copy-done.3
  124.6 1.2 weight_parts.1
  125.8 29.5 %all_to_all.31.back_ref.back_hbm = bf16[16,128,128]{2,1,0:T(8,128)(2,1)} all-to-all(bf16[16,128,128]{2,1,0:T(8,128)(2,1)S(1)} %weight_parts.1), channel_id=1, replica_groups=mesh['row'=32,'col'=16] {'col'}, dimensions={0} | all-to-all | bytes 1048576 | tf_op jit(solution)/shard_map/all_to_all | solution.py:589
  155.3 4.5 %return_slots.1 = bf16[32,112,128]{2,1,0:T(8,128)(2,1)} custom-call(bf16[16,128,128]{2,1,0:T(8,128)(2,1)} %all_to_all.31.back_ref.back_hbm, s32[32,128]{1,0:T(8,128)} %bitcast.7, bf16[512,1024]{1,0:T(8,128)(2,1)} %get-tuple-element.41.hubs_hbm), custom_call_target="tpu_custom_call" | custom-call | flops 2415919104 | bytes 3145728 | tf_op jit(solution)/shard_map/return_slots/pallas_call | solution.py:473
  159.8 14.2 %all-to-all-start.5 = ((bf16[32,112,128]{2,1,0:T(8,128)(2,1)}), bf16[32,112,128]{2,1,0:T(8,128)(2,1)S(1)}, u32[]{:S(2)}, u32[]{:S(2)}) async-start(bf16[32,112,128]{2,1,0:T(8,128)(2,1)} %return_slots.1), calls=%async_computation.5 | async-start | bytes 1835008 | tf_op jit(solution)/shard_map/all_to_all | solution.py:589
  174.0 3.9 %local_grads.1 = (f32[512,1024]{1,0:T(8,128)}, bf16[64,1024]{1,0:T(8,128)(2,1)}) custom-call(bf16[16,128,128]{2,1,0:T(8,128)(2,1)} %all_to_all.31.back_ref.back_hbm, bf16[1024,1024]{1,0:T(8,128)(2,1)} %get-tuple-element.39.local_ref), custom_call_target="tpu_custom_call" | custom-call | flops 536870912 | bytes 3145728 | tf_op jit(solution)/shard_map/local_grads/pallas_call | solution.py:505
  178.0 11.8 %all-to-all-done.5.back_ref = bf16[32,112,128]{2,1,0:T(8,128)(2,1)S(1)} async-done(((bf16[32,112,128]{2,1,0:T(8,128)(2,1)}), bf16[32,112,128]{2,1,0:T(8,128)(2,1)S(1)}, u32[]{:S(2)}, u32[]{:S(2)}) %all-to-all-start.5) | async-done | bytes 917536 | tf_op jit(solution)/shard_map/all_to_all | solution.py:589
  189.8 4.5 %spread_grads.1 = (bf16[64,1024]{1,0:T(8,128)(2,1)}, f32[64,1024]{1,0:T(8,128)}, f32[64,1024]{1,0:T(8,128)}) custom-call(bf16[32,112,128]{2,1,0:T(8,128)(2,1)S(1)} %all-to-all-done.5.back_ref, s32[32,128]{1,0:T(8,128)S(1)} %bitcast.10, s32[1,16]{1,0:T(1,128)S(1)} %bitcast.14, f32[512,1024]{1,0:T(8,128)} %get-tuple-element.42.base_hbm), custom_call_target="tpu_custom_call" | custom-call | flops 2214592512 | bytes 2097152 | tf_op jit(solution)/shard_map/spread_grads/pallas_call | solution.py:561
  (25 shorter events, 0.5 us)
Async XLA Ops:
  7.2 85.8 %all-gather.2.cloned.1.call-start = ((), (), s32[]{:S(2)}) async-start(), calls=%async_computation.6 | async-start | bytes 2228224 | tf_op jit(solution)/shard_map/all_gather | solution.py:601
  12.3 23.5 %all-to-all-start = ((bf16[32,80,128]{2,1,0:T(8,128)(2,1)}), bf16[32,80,128]{2,1,0:T(8,128)(2,1)S(1)}, u32[]{:S(2)}, u32[]{:S(2)}) async-start(bf16[32,80,128]{2,1,0:T(8,128)(2,1)} %gather_slots.1), calls=%async_computation | async-start | bytes 1310720 | tf_op jit(solution)/shard_map/all_to_all | solution.py:589
  22.7 13.0 %copy-start.4 = (bf16[64,1024]{1,0:T(8,128)(2,1)S(1)}, bf16[64,1024]{1,0:T(8,128)(2,1)}, u32[]{:S(2)}) copy-start(bf16[64,1024]{1,0:T(8,128)(2,1)} %x_hbm.3) | copy-start | bytes 393220
  22.7 13.0 %copy-start.5 = (bf16[64,1024]{1,0:T(8,128)(2,1)S(1)}, bf16[64,1024]{1,0:T(8,128)(2,1)}, u32[]{:S(2)}) copy-start(bf16[64,1024]{1,0:T(8,128)(2,1)} %cot_hbm.1) | copy-start | bytes 393220
  22.7 13.0 %copy-start.6 = (s32[1,32,128]{2,1,0:T(8,128)S(1)}, s32[1,32,128]{2,1,0:T(8,128)}, u32[]{:S(2)}) copy-start(s32[1,32,128]{2,1,0:T(8,128)} %param.15) | copy-start | bytes 49156
  22.7 13.0 %copy-start.8 = (s32[1024,2]{0,1:T(2,128)S(1)}, s32[1024,2]{0,1:T(2,128)}, u32[]{:S(2)}) copy-start(s32[1024,2]{0,1:T(2,128)} %param.17) | copy-start | bytes 24580
  78.4 20.0 %all-to-all-start.2 = ((bf16[16,64,512]{2,1,0:T(8,128)(2,1)}), bf16[16,64,512]{2,1,0:T(8,128)(2,1)S(1)}, u32[]{:S(2)}, u32[]{:S(2)}) async-start(bf16[16,64,512]{2,1,0:T(8,128)(2,1)} %regroup.1), calls=%async_computation.2 | async-start | bytes 2097152 | tf_op jit(solution)/shard_map/all_to_all | solution.py:589
  84.4 6.5 %collective-permute-start = (bf16[16,96,128]{2,1,0:T(8,128)(2,1)S(1)}, bf16[16,96,128]{2,1,0:T(8,128)(2,1)S(1)}, u32[]{:S(2)}, u32[]{:S(2)}) collective-permute-start(bf16[16,96,128]{2,1,0:T(8,128)(2,1)S(1)} %all_to_all.30.inc_ref.own_block), channel_id=1, source_target_pairs={{0,16},{16,0},{32,48},{48,32},{64,80},{80,64},{96,112},{112,96},{1... | collective-permute-start | bytes 1179656 | tf_op jit(solution)/shard_map/ppermute | solution.py:593
  91.1 0.8 copy-start.1
  91.9 0.7 copy-start.2
  98.4 26.2 %collective-permute-start.1 = (bf16[16,64,512]{2,1,0:T(8,128)(2,1)S(1)}, bf16[16,64,512]{2,1,0:T(8,128)(2,1)S(1)}, u32[]{:S(2)}, u32[]{:S(2)}) collective-permute-start(bf16[16,64,512]{2,1,0:T(8,128)(2,1)S(1)} %all-to-all-done.2.mine_hbm), channel_id=1, source_target_pairs={{0,16},{16,0},{32,48},{48,32},{64,80},{80,64},{96,112},{112,96},{1... | collective-permute-start | bytes 3145736 | tf_op jit(solution)/shard_map/ppermute | solution.py:593
  106.3 18.3 %all-to-all-start.3 = ((bf16[16,128,128]{2,1,0:T(8,128)(2,1)}), bf16[16,128,128]{2,1,0:T(8,128)(2,1)S(1)}, u32[]{:S(2)}, u32[]{:S(2)}) async-start(bf16[16,128,128]{2,1,0:T(8,128)(2,1)} %get-tuple-element.31), calls=%async_computation.3 | async-start | bytes 1048576 | tf_op jit(solution)/shard_map/all_to_all | solution.py:589
  116.9 5.6 %collective-permute-start.2 = (bf16[64,2048]{1,0:T(8,128)(2,1)}, bf16[64,2048]{1,0:T(8,128)(2,1)S(1)}, u32[]{:S(2)}, u32[]{:S(2)}) collective-permute-start(bf16[64,2048]{1,0:T(8,128)(2,1)} %get-tuple-element.35), channel_id=1, source_target_pairs={{0,16},{16,0},{32,48},{48,32},{64,80},{80,64},{96,112},{112,96},{1... | collective-permute-start | bytes 786440 | tf_op jit(solution)/shard_map/ppermute | solution.py:593
  119.1 3.4 %collective-permute-start.3 = (bf16[8,32,128]{2,1,0:T(8,128)(2,1)}, bf16[8,32,128]{2,1,0:T(8,128)(2,1)S(1)}, u32[]{:S(2)}, u32[]{:S(2)}) collective-permute-start(bf16[8,32,128]{2,1,0:T(8,128)(2,1)} %get-tuple-element.37), channel_id=1, source_target_pairs={{0,16},{16,0},{32,48},{48,32},{64,80},{80,64},{96,112},{112,96},{1... | collective-permute-start | bytes 196616 | tf_op jit(solution)/shard_map/ppermute | solution.py:593
  122.5 1.0 copy-start
  123.5 0.8 copy-start.3
  159.8 30.0 %copy-start.7 = (s32[1,32,128]{2,1,0:T(8,128)S(1)}, s32[1,32,128]{2,1,0:T(8,128)}, u32[]{:S(2)}) copy-start(s32[1,32,128]{2,1,0:T(8,128)} %param.14) | copy-start | bytes 49156
  159.8 30.0 %copy-start.9 = (s32[16]{0:T(128)S(1)}, s32[16]{0:T(128)}, u32[]{:S(2)}) copy-start(s32[16]{0:T(128)} %param.16) | copy-start | bytes 196
  159.8 30.0 %all-to-all-start.5 = ((bf16[32,112,128]{2,1,0:T(8,128)(2,1)}), bf16[32,112,128]{2,1,0:T(8,128)(2,1)S(1)}, u32[]{:S(2)}, u32[]{:S(2)}) async-start(bf16[32,112,128]{2,1,0:T(8,128)(2,1)} %return_slots.1), calls=%async_computation.5 | async-start | bytes 1835008 | tf_op jit(solution)/shard_map/all_to_all | solution.py:589
Sparse Core Ops, SparseCore 0:
  10.7 82.2 all-gather.1

commit v9 on v8

--- a/solution.py
+++ b/solution.py
@@ -352,79 +352,91 @@
     )(joined, cots, weights)
 
 
-def backward_kernel(slopes_ref, hidden_ref, weights_ref, keep_ref, send_ref, keep_hidden, send_hidden):
+SWAP = LAYERS + 4
+
+
+def backward_kernel(slopes_ref, hidden_ref, weights_ref, keep_ref, send_ref):
     back = matmul(slopes_ref[...], weights_ref[...], NT)
     keep_ref[...] = back[:OWN, :]
-    send_ref[...] = back[OWN:, :].astype(BF16)
-    keep_hidden[...] = hidden_ref[0]
-    send_hidden[...] = hidden_ref[1]
+    for layer in range(LAYERS):
+        send_ref[layer] = back[OWN:, SLOTS * layer : SLOTS * (layer + 1)].astype(BF16)
+    for pair in range(LAYERS // 4):
+        send_ref[LAYERS + pair] = hidden_ref[1, 2 * pair : 2 * pair + 2].reshape(OWN, SLOTS)
 
 
 def backward(slopes, hidden, weights):
-    part = jax.ShapeDtypeStruct((OWN, 2 * OUTS), F32)
-    block = jax.ShapeDtypeStruct((LAYERS // 2, OWN // 2, SLOTS), BF16)
     return pl.pallas_call(
         backward_kernel,
-        out_shape=[part, jax.ShapeDtypeStruct((OWN, 2 * OUTS), BF16), block, block],
-        compiler_params=params(60),
+        out_shape=[
+            jax.ShapeDtypeStruct((OWN, 2 * OUTS), F32),
+            jax.ShapeDtypeStruct((SWAP, OWN, SLOTS), BF16),
+        ],
+        compiler_params=params(16),
         cost_estimate=cost(2 * 256 * 2048 * 512, 4 << 20),
         name="backward",
     )(slopes, hidden, weights)
 
 
-def combine_kernel(mine_ref, theirs_ref, my_hidden, their_hidden, degree_ref, out_ref):
+def weight_kernel(
+    mine_hbm, theirs_hbm, slopes_ref, keep_hbm, swapped_hbm, hidden_hbm, degree_hbm, out_ref,
+    mine, theirs, keep, swapped, hidden, degree, sems,
+):
     core = lax.axis_index("row") % 2
+    staged = copies(
+        sems,
+        (degree_hbm, degree),
+        (keep_hbm, keep),
+        (swapped_hbm, swapped),
+        (hidden_hbm.at[0], hidden),
+        (mine_hbm, mine),
+        (theirs_hbm, theirs),
+    )
+    slopes = [
+        slopes_ref[:, OWN * side : OWN * (side + 1), :].astype(F32).reshape(CHIPS * OWN, SLOTS)
+        for side in range(2)
+    ]
+    columns = [rows.T.astype(BF16) for rows in slopes]
+    for copy in staged[:4]:
+        copy.wait()
     direct = lax.broadcasted_iota(jnp.int32, (OWN, SLOTS), 1) < FEATS
-    divisor = jnp.where(direct, 1.0, degree_ref[...])
+    divisor = jnp.where(direct, 1.0, degree[...])
     for layer in range(LAYERS):
-        lanes = slice(SLOTS * layer, SLOTS * (layer + 1))
-        back = mine_ref[:, lanes] + theirs_ref[:, lanes].astype(F32)
+        back = keep[:, SLOTS * layer : SLOTS * (layer + 1)] + swapped[layer].astype(F32)
         out_ref[layer, :OWN, :] = (back / divisor).astype(BF16)
-    for layer in range(LAYERS // 2):
-        out_ref[8 * core + layer, OWN:, :] = my_hidden[layer]
-        out_ref[8 * (1 - core) + layer, OWN:, :] = their_hidden[layer]
-
-
-def combine(mine, theirs, my_hidden, their_hidden, own_degree):
-    return pl.pallas_call(
-        combine_kernel,
-        out_shape=jax.ShapeDtypeStruct((LAYERS, 96, SLOTS), BF16),
-        compiler_params=params(16),
-        cost_estimate=cost(1 << 20, 2 << 20),
-        name="combine",
-    )(mine, theirs, my_hidden, their_hidden, own_degree)
-
-
-def weight_kernel(mine_hbm, theirs_hbm, slopes_ref, back_hbm, out_ref, mine, theirs, back, sems):
-    staged = copies(sems, (mine_hbm, mine), (theirs_hbm, theirs), (back_hbm, back))
+    for pair in range(LAYERS // 4):
+        for side in range(2):
+            layer = 2 * pair + side
+            out_ref[8 * core + layer, OWN:96, :] = hidden[layer]
+            out_ref[8 * (1 - core) + layer, OWN:96, :] = swapped[
+                LAYERS + pair, OWN // 2 * side : OWN // 2 * (side + 1), :
+            ]
     part = jnp.zeros((SLOTS, SLICE), F32)
     for side, rows in enumerate((mine, theirs)):
-        slopes = slopes_ref[:, OWN * side : OWN * (side + 1), :].astype(F32)
-        columns = slopes.reshape(CHIPS * OWN, SLOTS).T.astype(BF16)
-        staged[side].wait()
-        part = part + matmul(columns, rows[...].reshape(CHIPS * OWN, SLICE), NN)
+        staged[4 + side].wait()
+        part = part + matmul(columns[side], rows[...].reshape(CHIPS * OWN, SLICE), NN)
     part = part.T.astype(BF16)
     for layer in range(LAYERS):
         out_ref[layer, 96:, :] = part[PIECE * layer : PIECE * (layer + 1), :]
-    staged[2].wait()
-    out_ref[:, :96, :] = back[...]
-
-
-def weight_parts(mine, theirs, slopes_rows, back):
+
+
+def weight_parts(mine, theirs, slopes_rows, keep, swapped, hidden, own_degree):
     return pl.pallas_call(
         weight_kernel,
-        in_specs=[HBM, HBM, VMEM, HBM],
+        in_specs=[HBM, HBM, VMEM, HBM, HBM, HBM, HBM],
         out_shape=jax.ShapeDtypeStruct((LAYERS, SLOTS, SLOTS), BF16),
         scratch_shapes=[
             pltpu.VMEM((CHIPS, OWN, SLICE), BF16),
             pltpu.VMEM((CHIPS, OWN, SLICE), BF16),
-            pltpu.VMEM((LAYERS, 96, SLOTS), BF16),
-            pltpu.SemaphoreType.DMA((3,)),
-        ],
-        compiler_params=params(16),
-        cost_estimate=cost(2 * 256 * 2048 * 256, 3 << 20),
+            pltpu.VMEM((OWN, 2 * OUTS), F32),
+            pltpu.VMEM((SWAP, OWN, SLOTS), BF16),
+            pltpu.VMEM((LAYERS // 2, OWN // 2, SLOTS), BF16),
+            pltpu.VMEM((OWN, 1), F32),
+            pltpu.SemaphoreType.DMA((6,)),
+        ],
+        compiler_params=params(52),
+        cost_estimate=cost(2 * 256 * 2048 * 256, 4 << 20),
         name="weight_parts",
-    )(mine, theirs, slopes_rows, back)
+    )(mine, theirs, slopes_rows, keep, swapped, hidden, own_degree)
 
 
 RETURN_ROWS = 112
@@ -616,9 +628,11 @@
     slopes_rows = exchange(slopes_out, "row", SAME_CORE)
     joined_mine, slopes = lax.optimization_barrier((joined_mine, slopes))
     joined_theirs = other_core(joined_mine)
-    mine, theirs, my_hidden, their_hidden = backward(slopes, hidden, weights)
-    back = combine(mine, other_core(theirs), my_hidden, other_core(their_hidden), own_degree)
-    back_block = exchange(weight_parts(joined_mine, joined_theirs, slopes_rows, back), "col")
+    keep, sent = backward(slopes, hidden, weights)
+    parts = weight_parts(
+        joined_mine, joined_theirs, slopes_rows, keep, other_core(sent), hidden, own_degree
+    )
+    back_block = exchange(parts, "col")
     returned = exchange(return_slots(back_block, recv_lanes, hubs), "row")
     base, hidden_out = local_grads(back_block, local)
     grad_feats, grad_self, grad_neigh = spread_grads(returned, send_lanes, hub_own, base)

time: 202 us -> 200 us (0.990)
  starting transfers between devices: 55.2 us -> 50 us
  waiting for transfers between devices: 23.6 us -> 28.1 us
    all_to_all x4, waiting for transfers between devices: 20.7 us -> 25.6 us  [exchange(): lax.all_to_all(blocks, axis, 0, 0, axis_index_groups=groups, tiled=True)]
    ppermute x4 -> x3, starting transfers between devices: 17.3 us -> 14.3 us  [other_core(): return lax.ppermute(block, 'row', [(i, i ^ 1) for i in range(PEERS)])]
    all_to_all x4, starting transfers between devices: 37.8 us -> 35.6 us  [exchange(): lax.all_to_all(blocks, axis, 0, 0, axis_index_groups=groups, tiled=True)]
    pallas_call x3 -> x2, Pallas kernels: 4.79 us -> 3.29 us  [the longest x1 2.49 us: weight_parts(): pl.pallas_call(weight_kernel, in_specs=[HBM, HBM, VMEM, HBM, HBM, HBM, HB...]
    unnamed x20 -> x26, local copies, waits for them, and re-layouts: 3.37 us -> 4.14 us
  transfers between devices with their start and end apart: 9 -> 8, of which waited for: 7 -> 6; matrix products, arithmetic and copies ran while one was open for 0% -> 0% of each run, Pallas kernels for 13% -> 12%
where the time goes in v9:
time: 200 us
  blocking collectives  65.4 us (33%)
  starting transfers between devices  50 us (25%)
  Pallas kernels  35.8 us (18%)
  waiting for transfers between devices  28.1 us (14%)
  between operations  14.3 us (7%)
  local copies, waits for them, and re-layouts  4.33 us (2%)
    all_to_all x2, blocking collectives, exchange(): lax.all_to_all(blocks, axis, 0, 0, axis_index_groups=groups, tiled=True)  65.4 us
    all_to_all x4, starting transfers between devices, exchange(): lax.all_to_all(blocks, axis, 0, 0, axis_index_groups=groups, tiled=True)  35.6 us
    all_to_all x4, waiting for transfers between devices, exchange(): lax.all_to_all(blocks, axis, 0, 0, axis_index_groups=groups, tiled=True)  25.6 us
    ppermute x3, starting transfers between devices, other_core(): return lax.ppermute(block, 'row', [(i, i ^ 1) for i in range(PEERS)])  14.3 us
    pallas_call x1, Pallas kernels, build_counts(): pl.pallas_call(build_kernel, grid=(NODES // BUILD,), in_specs=[whole((FEA...  6.22 us
    pallas_call x1, Pallas kernels, aggregate(): pl.pallas_call(aggregate_kernel, out_shape=[jax.ShapeDtypeStruct((LAYERS,...  4.94 us
    pallas_call x1, Pallas kernels, spread_grads(): pl.pallas_call(spread_kernel, in_specs=[VMEM, HBM, HBM, HBM], out_specs=[...  4.53 us
    pallas_call x1, Pallas kernels, return_slots(): pl.pallas_call(return_kernel, in_specs=[HBM, HBM, HBM], out_specs=HBM, ou...  4.5 us
  transfers between devices with their start and end apart: 8, of which 6 were waited for; matrix products, arithmetic and copies ran while one was open for 0% of the time, Pallas kernels for 12%

profile of v9, /device:TPU:1, one launch (start us, length us, event | category | flops | bytes accessed | tf_op | source)
XLA Modules:
  0.0 199.6 jit_solution(15102463746530896897)
XLA Ops:
  7.2 1.5 fusion
  8.8 3.5 %gather_slots.1 = bf16[32,80,128]{2,1,0:T(8,128)(2,1)} custom-call(bf16[64,1024]{1,0:T(8,128)(2,1)} %x_hbm.3, s32[32,128]{1,0:T(8,128)} %bitcast.9, s32[1,16]{1,0:T(1,128)} %bitcast.13), custom_call_target="tpu_custom_call" | custom-call | flops 2147483648 | bytes 1048576 | tf_op jit(solution)/shard_map/gather_slots/pallas_call | solution.py:80
  12.3 10.4 %all-to-all-start = ((bf16[32,80,128]{2,1,0:T(8,128)(2,1)}), bf16[32,80,128]{2,1,0:T(8,128)(2,1)S(1)}, u32[]{:S(2)}, u32[]{:S(2)}) async-start(bf16[32,80,128]{2,1,0:T(8,128)(2,1)} %gather_slots.1), calls=%async_computation | async-start | bytes 1310720 | tf_op jit(solution)/shard_map/all_to_all | solution.py:601
  22.8 6.2 %build_counts.1 = (bf16[1024,1024]{1,0:T(8,128)(2,1)}, bf16[512,1024]{1,0:T(8,128)(2,1)}, f32[512,1024]{1,0:T(8,128)}) custom-call(bf16[64,1024]{1,0:T(8,128)(2,1)} %x_hbm.3, s32[8,1024]{1,0:T(8,128)} %bitcast.15, s32[2,1024]{1,0:T(2,128)} %bitcast.11), custom_call_target="tpu_custom_call" | custom-call | flops 1073741824 | bytes 4194304 | tf_op jit(solution)/shard_map/build_counts/pallas_call | solution.py:116
  29.0 6.7 %all-to-all-done.inc_ref = bf16[32,80,128]{2,1,0:T(8,128)(2,1)S(1)} async-done(((bf16[32,80,128]{2,1,0:T(8,128)(2,1)}), bf16[32,80,128]{2,1,0:T(8,128)(2,1)S(1)}, u32[]{:S(2)}, u32[]{:S(2)}) %all-to-all-start) | async-done | bytes 655392 | tf_op jit(solution)/shard_map/all_to_all | solution.py:601
  35.8 4.9 %aggregate.1 = (bf16[16,96,128]{2,1,0:T(8,128)(2,1)S(1)}, f32[8,1024]{1,0:T(8,128)S(1)}) custom-call(bf16[64,1024]{1,0:T(8,128)(2,1)S(1)} %copy-done.7, bf16[32,80,128]{2,1,0:T(8,128)(2,1)S(1)} %all-to-all-done.inc_ref, s32[32,128]{1,0:T(8,128)S(1)} %bitcast.8, f32[512,1024]{1,0:T(8,128)} %get-tuple-element.23.sum_hbm, s32[2,1024]{1,0:T(2,128)S(1)} %bitcast.12, ...), custom_call_target="tpu_custom_call" | custom-call | flops 2952790016 | bytes 3145728 | tf_op jit(solution)/shard_map/aggregate/pallas_call | solution.py:195
  40.7 35.4 %all_to_all.30.inc_ref.own_block = bf16[16,96,128]{2,1,0:T(8,128)(2,1)S(1)} all-to-all(bf16[16,96,128]{2,1,0:T(8,128)(2,1)S(1)} %get-tuple-element.24), channel_id=1, replica_groups=mesh['row'=32,'col'=16] {'col'}, dimensions={0} | all-to-all | bytes 786432 | tf_op jit(solution)/shard_map/all_to_all | solution.py:601
  76.1 1.3 regroup.1
  77.4 7.5 %all-to-all-start.2 = ((bf16[16,64,512]{2,1,0:T(8,128)(2,1)}), bf16[16,64,512]{2,1,0:T(8,128)(2,1)}, u32[]{:S(2)}, u32[]{:S(2)}) async-start(bf16[16,64,512]{2,1,0:T(8,128)(2,1)} %regroup.1), calls=%async_computation.2 | async-start | bytes 2097152 | tf_op jit(solution)/shard_map/all_to_all | solution.py:601
  84.9 4.9 %collective-permute-start = (bf16[16,96,128]{2,1,0:T(8,128)(2,1)S(1)}, bf16[16,96,128]{2,1,0:T(8,128)(2,1)S(1)}, u32[]{:S(2)}, u32[]{:S(2)}) collective-permute-start(bf16[16,96,128]{2,1,0:T(8,128)(2,1)S(1)} %all_to_all.30.inc_ref.own_block), channel_id=1, source_target_pairs={{0,16},{16,0},{32,48},{48,32},{64,80},{80,64},{96,112},{112,96},{1... | collective-permute-start | bytes 1179656 | tf_op jit(solution)/shard_map/ppermute | solution.py:605
  89.8 1.3 collective-permute-done.other_block
  91.1 0.2 prepare.1
  91.3 0.8 copy-done.3
  92.2 0.7 copy-done.6
  92.8 3.5 %forward.1 = (bf16[16,128,128]{2,1,0:T(8,128)(2,1)}, bf16[128,512]{1,0:T(8,128)(2,1)}, bf16[2,8,32,128]{3,2,1,0:T(8,128)(2,1)}) custom-call(bf16[2,64,2048]{2,1,0:T(8,128)(2,1)} %copy-done.3, bf16[2,64,512]{2,1,0:T(8,128)(2,1)} %copy-done.6, bf16[2048,512]{1,0:T(8,128)(2,1)} %all-gather.2.cloned.1.call-done.weights_hbm.weights_ref), custom_call_target="tpu_custom_call" | custom-call | flops 536870912 | bytes 4194304 | tf_op jit(solution)/shard_map/forward/pallas_call | solution.py:330
  96.3 2.9 %all-to-all-done.2.mine_hbm = bf16[16,64,512]{2,1,0:T(8,128)(2,1)} async-done(((bf16[16,64,512]{2,1,0:T(8,128)(2,1)}), bf16[16,64,512]{2,1,0:T(8,128)(2,1)}, u32[]{:S(2)}, u32[]{:S(2)}) %all-to-all-start.2) | async-done | bytes 1048608 | tf_op jit(solution)/shard_map/all_to_all | solution.py:601
  99.3 7.3 %collective-permute-start.1 = (bf16[16,64,512]{2,1,0:T(8,128)(2,1)}, bf16[16,64,512]{2,1,0:T(8,128)(2,1)}, u32[]{:S(2)}, u32[]{:S(2)}) collective-permute-start(bf16[16,64,512]{2,1,0:T(8,128)(2,1)} %all-to-all-done.2.mine_hbm), channel_id=1, source_target_pairs={{0,16},{16,0},{32,48},{48,32},{64,80},{80,64},{96,112},{112,96},{1... | collective-permute-start | bytes 3145736 | tf_op jit(solution)/shard_map/ppermute | solution.py:605
  106.5 7.0 %all-to-all-start.3 = ((bf16[16,128,128]{2,1,0:T(8,128)(2,1)}), bf16[16,128,128]{2,1,0:T(8,128)(2,1)S(1)}, u32[]{:S(2)}, u32[]{:S(2)}) async-start(bf16[16,128,128]{2,1,0:T(8,128)(2,1)} %get-tuple-element.29), calls=%async_computation.3 | async-start | bytes 1048576 | tf_op jit(solution)/shard_map/all_to_all | solution.py:601
  113.5 0.9 copy-done.1
  114.4 0.9 copy-done.5
  115.3 0.8 backward.1
  116.1 0.8 copy-done.4
  116.9 2.2 %collective-permute-start.2 = (bf16[20,64,128]{2,1,0:T(8,128)(2,1)S(1)}, bf16[20,64,128]{2,1,0:T(8,128)(2,1)S(1)}, u32[]{:S(2)}, u32[]{:S(2)}) collective-permute-start(bf16[20,64,128]{2,1,0:T(8,128)(2,1)S(1)} %get-tuple-element.33), channel_id=1, source_target_pairs={{0,16},{16,0},{32,48},{48,32},{64,80},{80,64},{96,112},{112,96},{1... | collective-permute-start | bytes 983048 | tf_op jit(solution)/shard_map/ppermute | solution.py:605
  119.3 1.1 collective-permute-done.2.swapped_hbm
  120.4 4.1 %all-to-all-done.3.slopes_ref = bf16[16,128,128]{2,1,0:T(8,128)(2,1)S(1)} async-done(((bf16[16,128,128]{2,1,0:T(8,128)(2,1)}), bf16[16,128,128]{2,1,0:T(8,128)(2,1)S(1)}, u32[]{:S(2)}, u32[]{:S(2)}) %all-to-all-start.3) | async-done | bytes 524320 | tf_op jit(solution)/shard_map/all_to_all | solution.py:601
  124.6 2.5 %weight_parts.1 = bf16[16,128,128]{2,1,0:T(8,128)(2,1)S(1)} custom-call(bf16[16,64,512]{2,1,0:T(8,128)(2,1)} %all-to-all-done.2.mine_hbm, bf16[16,64,512]{2,1,0:T(8,128)(2,1)} %collective-permute-done.1.theirs_hbm, bf16[16,128,128]{2,1,0:T(8,128)(2,1)S(1)} %all-to-all-done.3.slopes_ref, f32[64,2048]{1,0:T(8,128)} %copy-done.4, ...), custom_call_target="tpu_custom_call" | custom-call | flops 268435456 | bytes 4194304 | tf_op jit(solution)/shard_map/weight_parts/pallas_call | solution.py:423
  127.1 30.1 %all_to_all.31.back_ref.back_hbm = bf16[16,128,128]{2,1,0:T(8,128)(2,1)} all-to-all(bf16[16,128,128]{2,1,0:T(8,128)(2,1)S(1)} %weight_parts.1), channel_id=1, replica_groups=mesh['row'=32,'col'=16] {'col'}, dimensions={0} | all-to-all | bytes 1048576 | tf_op jit(solution)/shard_map/all_to_all | solution.py:601
  157.1 4.5 %return_slots.1 = bf16[32,112,128]{2,1,0:T(8,128)(2,1)} custom-call(bf16[16,128,128]{2,1,0:T(8,128)(2,1)} %all_to_all.31.back_ref.back_hbm, s32[32,128]{1,0:T(8,128)} %bitcast.7, bf16[512,1024]{1,0:T(8,128)(2,1)} %get-tuple-element.37.hubs_hbm), custom_call_target="tpu_custom_call" | custom-call | flops 2415919104 | bytes 3145728 | tf_op jit(solution)/shard_map/return_slots/pallas_call | solution.py:485
  161.7 10.7 %all-to-all-start.5 = ((bf16[32,112,128]{2,1,0:T(8,128)(2,1)}), bf16[32,112,128]{2,1,0:T(8,128)(2,1)S(1)}, u32[]{:S(2)}, u32[]{:S(2)}) async-start(bf16[32,112,128]{2,1,0:T(8,128)(2,1)} %return_slots.1), calls=%async_computation.5 | async-start | bytes 1835008 | tf_op jit(solution)/shard_map/all_to_all | solution.py:601
  172.4 3.9 %local_grads.1 = (f32[512,1024]{1,0:T(8,128)}, bf16[64,1024]{1,0:T(8,128)(2,1)}) custom-call(bf16[16,128,128]{2,1,0:T(8,128)(2,1)} %all_to_all.31.back_ref.back_hbm, bf16[1024,1024]{1,0:T(8,128)(2,1)} %get-tuple-element.35.local_ref), custom_call_target="tpu_custom_call" | custom-call | flops 536870912 | bytes 3145728 | tf_op jit(solution)/shard_map/local_grads/pallas_call | solution.py:517
  176.3 11.8 %all-to-all-done.5.back_ref = bf16[32,112,128]{2,1,0:T(8,128)(2,1)S(1)} async-done(((bf16[32,112,128]{2,1,0:T(8,128)(2,1)}), bf16[32,112,128]{2,1,0:T(8,128)(2,1)S(1)}, u32[]{:S(2)}, u32[]{:S(2)}) %all-to-all-start.5) | async-done | bytes 917536 | tf_op jit(solution)/shard_map/all_to_all | solution.py:601
  188.2 4.5 %spread_grads.1 = (bf16[64,1024]{1,0:T(8,128)(2,1)}, f32[64,1024]{1,0:T(8,128)}, f32[64,1024]{1,0:T(8,128)}) custom-call(bf16[32,112,128]{2,1,0:T(8,128)(2,1)S(1)} %all-to-all-done.5.back_ref, s32[32,128]{1,0:T(8,128)S(1)} %bitcast.10, s32[1,16]{1,0:T(1,128)S(1)} %bitcast.14, f32[512,1024]{1,0:T(8,128)} %get-tuple-element.38.base_hbm), custom_call_target="tpu_custom_call" | custom-call | flops 2214592512 | bytes 2097152 | tf_op jit(solution)/shard_map/spread_grads/pallas_call | solution.py:573
  (28 shorter events, 0.3 us)
Async XLA Ops:
  7.2 85.7 %all-gather.2.cloned.1.call-start = ((), (), s32[]{:S(2)}) async-start(), calls=%async_computation.6 | async-start | bytes 2228224 | tf_op jit(solution)/shard_map/all_gather | solution.py:613
  12.3 23.5 %all-to-all-start = ((bf16[32,80,128]{2,1,0:T(8,128)(2,1)}), bf16[32,80,128]{2,1,0:T(8,128)(2,1)S(1)}, u32[]{:S(2)}, u32[]{:S(2)}) async-start(bf16[32,80,128]{2,1,0:T(8,128)(2,1)} %gather_slots.1), calls=%async_computation | async-start | bytes 1310720 | tf_op jit(solution)/shard_map/all_to_all | solution.py:601
  22.7 13.0 %copy-start.7 = (bf16[64,1024]{1,0:T(8,128)(2,1)S(1)}, bf16[64,1024]{1,0:T(8,128)(2,1)}, u32[]{:S(2)}) copy-start(bf16[64,1024]{1,0:T(8,128)(2,1)} %x_hbm.3) | copy-start | bytes 393220
  22.7 13.0 %copy-start.8 = (bf16[64,1024]{1,0:T(8,128)(2,1)S(1)}, bf16[64,1024]{1,0:T(8,128)(2,1)}, u32[]{:S(2)}) copy-start(bf16[64,1024]{1,0:T(8,128)(2,1)} %cot_hbm.1) | copy-start | bytes 393220
  22.7 13.0 %copy-start.9 = (s32[1,32,128]{2,1,0:T(8,128)S(1)}, s32[1,32,128]{2,1,0:T(8,128)}, u32[]{:S(2)}) copy-start(s32[1,32,128]{2,1,0:T(8,128)} %param.15) | copy-start | bytes 49156
  22.8 13.0 %copy-start.11 = (s32[1024,2]{0,1:T(2,128)S(1)}, s32[1024,2]{0,1:T(2,128)}, u32[]{:S(2)}) copy-start(s32[1024,2]{0,1:T(2,128)} %param.17) | copy-start | bytes 24580
  77.4 21.9 %all-to-all-start.2 = ((bf16[16,64,512]{2,1,0:T(8,128)(2,1)}), bf16[16,64,512]{2,1,0:T(8,128)(2,1)}, u32[]{:S(2)}, u32[]{:S(2)}) async-start(bf16[16,64,512]{2,1,0:T(8,128)(2,1)} %regroup.1), calls=%async_computation.2 | async-start | bytes 2097152 | tf_op jit(solution)/shard_map/all_to_all | solution.py:601
  84.9 6.2 %collective-permute-start = (bf16[16,96,128]{2,1,0:T(8,128)(2,1)S(1)}, bf16[16,96,128]{2,1,0:T(8,128)(2,1)S(1)}, u32[]{:S(2)}, u32[]{:S(2)}) collective-permute-start(bf16[16,96,128]{2,1,0:T(8,128)(2,1)S(1)} %all_to_all.30.inc_ref.own_block), channel_id=1, source_target_pairs={{0,16},{16,0},{32,48},{48,32},{64,80},{80,64},{96,112},{112,96},{1... | collective-permute-start | bytes 1179656 | tf_op jit(solution)/shard_map/ppermute | solution.py:605
  91.3 0.9 copy-start.3
  92.2 0.7 copy-start.6
  92.8 20.7 %copy-start = (bf16[2048,512]{1,0:T(8,128)(2,1)S(1)}, bf16[2048,512]{1,0:T(8,128)(2,1)}, u32[]{:S(2)}) copy-start(bf16[2048,512]{1,0:T(8,128)(2,1)} %all-gather.2.cloned.1.call-done.weights_hbm.weights_ref) | copy-start | bytes 6291460
  96.3 28.3 %copy-start.2 = (bf16[2,8,32,128]{3,2,1,0:T(8,128)(2,1)S(1)}, bf16[2,8,32,128]{3,2,1,0:T(8,128)(2,1)}, u32[]{:S(2)}) copy-start(bf16[2,8,32,128]{3,2,1,0:T(8,128)(2,1)} %get-tuple-element.31.hidden_ref.hidden_hbm) | copy-start | bytes 393220
  99.3 25.3 %collective-permute-start.1 = (bf16[16,64,512]{2,1,0:T(8,128)(2,1)}, bf16[16,64,512]{2,1,0:T(8,128)(2,1)}, u32[]{:S(2)}, u32[]{:S(2)}) collective-permute-start(bf16[16,64,512]{2,1,0:T(8,128)(2,1)} %all-to-all-done.2.mine_hbm), channel_id=1, source_target_pairs={{0,16},{16,0},{32,48},{48,32},{64,80},{80,64},{96,112},{112,96},{1... | collective-permute-start | bytes 3145736 | tf_op jit(solution)/shard_map/ppermute | solution.py:605
  106.5 18.0 %all-to-all-start.3 = ((bf16[16,128,128]{2,1,0:T(8,128)(2,1)}), bf16[16,128,128]{2,1,0:T(8,128)(2,1)S(1)}, u32[]{:S(2)}, u32[]{:S(2)}) async-start(bf16[16,128,128]{2,1,0:T(8,128)(2,1)} %get-tuple-element.29), calls=%async_computation.3 | async-start | bytes 1048576 | tf_op jit(solution)/shard_map/all_to_all | solution.py:601
  113.5 0.9 copy-start.1
  114.4 0.9 copy-start.5
  116.1 0.8 copy-start.4
  116.9 3.5 %collective-permute-start.2 = (bf16[20,64,128]{2,1,0:T(8,128)(2,1)S(1)}, bf16[20,64,128]{2,1,0:T(8,128)(2,1)S(1)}, u32[]{:S(2)}, u32[]{:S(2)}) collective-permute-start(bf16[20,64,128]{2,1,0:T(8,128)(2,1)S(1)} %get-tuple-element.33), channel_id=1, source_target_pairs={{0,16},{16,0},{32,48},{48,32},{64,80},{80,64},{96,112},{112,96},{1... | collective-permute-start | bytes 983048 | tf_op jit(solution)/shard_map/ppermute | solution.py:605
  161.6 26.5 %copy-start.10 = (s32[1,32,128]{2,1,0:T(8,128)S(1)}, s32[1,32,128]{2,1,0:T(8,128)}, u32[]{:S(2)}) copy-start(s32[1,32,128]{2,1,0:T(8,128)} %param.14) | copy-start | bytes 49156
  161.7 26.5 %copy-start.12 = (s32[16]{0:T(128)S(1)}, s32[16]{0:T(128)}, u32[]{:S(2)}) copy-start(s32[16]{0:T(128)} %param.16) | copy-start | bytes 196
  161.7 26.5 %all-to-all-start.5 = ((bf16[32,112,128]{2,1,0:T(8,128)(2,1)}), bf16[32,112,128]{2,1,0:T(8,128)(2,1)S(1)}, u32[]{:S(2)}, u32[]{:S(2)}) async-start(bf16[32,112,128]{2,1,0:T(8,128)(2,1)} %return_slots.1), calls=%async_computation.5 | async-start | bytes 1835008 | tf_op jit(solution)/shard_map/all_to_all | solution.py:601
Sparse Core Ops, SparseCore 0:
  10.7 82.0 all-gather.1

commit v10 on v9

--- a/solution.py
+++ b/solution.py
@@ -248,6 +248,7 @@
 
 
 HALF = OUTS // 2
+STEPS = 4
 
 
 def prepare_kernel(own_block, other_block, joined_ref, cot_ref):
@@ -284,40 +285,37 @@
     joined_hbm, cot_hbm, weights_hbm, slopes_hbm, flat_hbm, hidden_hbm,
     joined, cots, weights, out_tile, flat, hidden, in_sems, out_sems,
 ):
+    depth = 2 * OUTS // STEPS
+    bands = [slice(depth * step, depth * (step + 1)) for step in range(STEPS)]
     staged = copies(
         in_sems,
         (joined_hbm, joined),
-        (weights_hbm.at[:, :TILE], weights.at[:, :TILE]),
+        *[(weights_hbm.at[band, :], weights.at[band, :]) for band in bands],
         (cot_hbm, cots),
-        (weights_hbm.at[:, TILE:], weights.at[:, TILE:]),
     )
     staged[0].wait()
+    preact = jnp.zeros((2 * OWN, HALF), F32)
+    for step, band in enumerate(bands):
+        staged[step + 1].wait()
+        rows = joined[:, :, band].reshape(2 * OWN, depth)
+        preact = preact + matmul(rows, weights[band, :], NN)
+    staged[STEPS + 1].wait()
+    sigmoid_part = jax.nn.sigmoid(preact)
+    silu = preact * sigmoid_part
+    slope = sigmoid_part * (1.0 + preact * (1.0 - sigmoid_part))
+    slopes = (cots[...].reshape(2 * OWN, HALF).astype(F32) * slope).astype(BF16)
+    for outs in range(4):
+        out_tile[outs] = slopes[:, SLOTS * outs : SLOTS * (outs + 1)]
     sent = []
-    for side in range(2):
-        staged[2 * side + 1].wait()
-        columns = slice(TILE * side, TILE * (side + 1))
-        preact = matmul(joined[...].reshape(2 * OWN, 2 * OUTS), weights[:, columns], NN)
-        if side == 0:
-            staged[2].wait()
-        sigmoid_part = jax.nn.sigmoid(preact)
-        silu = preact * sigmoid_part
-        slope = sigmoid_part * (1.0 + preact * (1.0 - sigmoid_part))
-        cot = cots[:, :, columns].reshape(2 * OWN, TILE).astype(F32)
-        slopes = (cot * slope).astype(BF16)
-        for outs in range(2):
-            out_tile[2 * side + outs] = slopes[:, SLOTS * outs : SLOTS * (outs + 1)]
-        for chip in range(CHIPS):
-            if chip % 4 // 2 == side:
-                copy = pltpu.make_async_copy(
-                    out_tile.at[chip % 4], slopes_hbm.at[chip], out_sems.at[chip]
-                )
-                copy.start()
-                sent.append(copy)
-        flat[:, columns] = slopes
-        for block in range(2):
-            for layer in range(4):
-                tile = silu[OWN * block : OWN * (block + 1), FEATS * layer : FEATS * (layer + 1)]
-                hidden[block, 4 * side + layer] = fold_halves(tile).astype(BF16)
+    for chip in range(CHIPS):
+        copy = pltpu.make_async_copy(out_tile.at[chip % 4], slopes_hbm.at[chip], out_sems.at[chip])
+        copy.start()
+        sent.append(copy)
+    flat[...] = slopes
+    for block in range(2):
+        for layer in range(LAYERS // 2):
+            tile = silu[OWN * block : OWN * (block + 1), FEATS * layer : FEATS * (layer + 1)]
+            hidden[block, layer] = fold_halves(tile).astype(BF16)
     for i, (source, target) in enumerate(((flat, flat_hbm), (hidden, hidden_hbm))):
         copy = pltpu.make_async_copy(source, target, out_sems.at[CHIPS + i])
         copy.start()
@@ -343,7 +341,7 @@
             pltpu.VMEM((4, 2 * OWN, SLOTS), BF16),
             pltpu.VMEM((2 * OWN, HALF), BF16),
             pltpu.VMEM((2, LAYERS // 2, OWN // 2, SLOTS), BF16),
-            pltpu.SemaphoreType.DMA((4,)),
+            pltpu.SemaphoreType.DMA((STEPS + 2,)),
             pltpu.SemaphoreType.DMA((CHIPS + 2,)),
         ],
         compiler_params=params(60),
@@ -549,12 +547,12 @@
     high = total.astype(BF16).astype(F32)
     hub_high = high.T.astype(BF16)
     hub_low = (total - high).T.astype(BF16)
-    for copy in staged:
-        copy.wait()
+    staged[0].wait()
+    staged[1].wait()
     for tile in range(NODES // SPREAD):
         lanes = slice(SPREAD * tile, SPREAD * (tile + 1))
         node = lax.broadcasted_iota(jnp.int32, (SPREAD, 2 * SLOTS), 0) + SPREAD * tile
-        grad = base_ref[:, lanes]
+        grad = jnp.zeros((FEATS, SPREAD), F32)
         for pair in range(PEERS // 2):
             grad = grad + matmul(
                 slots[:, 2 * SLOTS * pair : 2 * SLOTS * (pair + 1)],
@@ -564,7 +562,9 @@
         hub_node = lax.broadcasted_iota(jnp.int32, (SPREAD, HUBS_OWN), 0) + SPREAD * tile
         hub_hot = one_hot(hub_node == hub_ref[...])
         grad = grad + matmul(hub_high, hub_hot, NT) + matmul(hub_low, hub_hot, NT)
-        out_ref[:, lanes] = grad.astype(BF16)
+        if tile == 0:
+            staged[2].wait()
+        out_ref[:, lanes] = (grad + base_ref[:, lanes]).astype(BF16)
     for copy in sent:
         copy.wait()
 

time: 200 us -> 200 us (level)
  no operation moved by 1% of the time
where the time goes in v10:
time: 200 us
  blocking collectives  65.4 us (33%)
  starting transfers between devices  49.8 us (25%)
  Pallas kernels  35.8 us (18%)
  waiting for transfers between devices  28.3 us (14%)
  between operations  14.3 us (7%)
  local copies, waits for them, and re-layouts  4.33 us (2%)
    all_to_all x2, blocking collectives, exchange(): lax.all_to_all(blocks, axis, 0, 0, axis_index_groups=groups, tiled=True)  65.4 us
    all_to_all x4, starting transfers between devices, exchange(): lax.all_to_all(blocks, axis, 0, 0, axis_index_groups=groups, tiled=True)  35.7 us
    all_to_all x4, waiting for transfers between devices, exchange(): lax.all_to_all(blocks, axis, 0, 0, axis_index_groups=groups, tiled=True)  25.9 us
    ppermute x3, starting transfers between devices, other_core(): return lax.ppermute(block, 'row', [(i, i ^ 1) for i in range(PEERS)])  14.1 us
    pallas_call x1, Pallas kernels, build_counts(): pl.pallas_call(build_kernel, grid=(NODES // BUILD,), in_specs=[whole((FEA...  6.22 us
    pallas_call x1, Pallas kernels, aggregate(): pl.pallas_call(aggregate_kernel, out_shape=[jax.ShapeDtypeStruct((LAYERS,...  4.94 us
    pallas_call x1, Pallas kernels, spread_grads(): pl.pallas_call(spread_kernel, in_specs=[VMEM, HBM, HBM, HBM], out_specs=[...  4.74 us
    pallas_call x1, Pallas kernels, return_slots(): pl.pallas_call(return_kernel, in_specs=[HBM, HBM, HBM], out_specs=HBM, ou...  4.5 us
  transfers between devices with their start and end apart: 8, of which 6 were waited for; matrix products, arithmetic and copies ran while one was open for 0% of the time, Pallas kernels for 12%

profile of v10, /device:TPU:1, one launch (start us, length us, event | category | flops | bytes accessed | tf_op | source)
XLA Modules:
  0.0 199.6 jit_solution(13111131930867547037)
XLA Ops:
  7.2 1.5 fusion
  8.8 3.5 %gather_slots.1 = bf16[32,80,128]{2,1,0:T(8,128)(2,1)} custom-call(bf16[64,1024]{1,0:T(8,128)(2,1)} %x_hbm.3, s32[32,128]{1,0:T(8,128)} %bitcast.9, s32[1,16]{1,0:T(1,128)} %bitcast.13), custom_call_target="tpu_custom_call" | custom-call | flops 2147483648 | bytes 1048576 | tf_op jit(solution)/shard_map/gather_slots/pallas_call | solution.py:80
  12.3 10.4 %all-to-all-start = ((bf16[32,80,128]{2,1,0:T(8,128)(2,1)}), bf16[32,80,128]{2,1,0:T(8,128)(2,1)S(1)}, u32[]{:S(2)}, u32[]{:S(2)}) async-start(bf16[32,80,128]{2,1,0:T(8,128)(2,1)} %gather_slots.1), calls=%async_computation | async-start | bytes 1310720 | tf_op jit(solution)/shard_map/all_to_all | solution.py:601
  22.8 6.2 %build_counts.1 = (bf16[1024,1024]{1,0:T(8,128)(2,1)}, bf16[512,1024]{1,0:T(8,128)(2,1)}, f32[512,1024]{1,0:T(8,128)}) custom-call(bf16[64,1024]{1,0:T(8,128)(2,1)} %x_hbm.3, s32[8,1024]{1,0:T(8,128)} %bitcast.15, s32[2,1024]{1,0:T(2,128)} %bitcast.11), custom_call_target="tpu_custom_call" | custom-call | flops 1073741824 | bytes 4194304 | tf_op jit(solution)/shard_map/build_counts/pallas_call | solution.py:116
  29.0 6.7 %all-to-all-done.inc_ref = bf16[32,80,128]{2,1,0:T(8,128)(2,1)S(1)} async-done(((bf16[32,80,128]{2,1,0:T(8,128)(2,1)}), bf16[32,80,128]{2,1,0:T(8,128)(2,1)S(1)}, u32[]{:S(2)}, u32[]{:S(2)}) %all-to-all-start) | async-done | bytes 655392 | tf_op jit(solution)/shard_map/all_to_all | solution.py:601
  35.8 4.9 %aggregate.1 = (bf16[16,96,128]{2,1,0:T(8,128)(2,1)S(1)}, f32[8,1024]{1,0:T(8,128)S(1)}) custom-call(bf16[64,1024]{1,0:T(8,128)(2,1)S(1)} %copy-done.7, bf16[32,80,128]{2,1,0:T(8,128)(2,1)S(1)} %all-to-all-done.inc_ref, s32[32,128]{1,0:T(8,128)S(1)} %bitcast.8, f32[512,1024]{1,0:T(8,128)} %get-tuple-element.23.sum_hbm, s32[2,1024]{1,0:T(2,128)S(1)} %bitcast.12, ...), custom_call_target="tpu_custom_call" | custom-call | flops 2952790016 | bytes 3145728 | tf_op jit(solution)/shard_map/aggregate/pallas_call | solution.py:195
  40.7 35.4 %all_to_all.30.inc_ref.own_block = bf16[16,96,128]{2,1,0:T(8,128)(2,1)S(1)} all-to-all(bf16[16,96,128]{2,1,0:T(8,128)(2,1)S(1)} %get-tuple-element.24), channel_id=1, replica_groups=mesh['row'=32,'col'=16] {'col'}, dimensions={0} | all-to-all | bytes 786432 | tf_op jit(solution)/shard_map/all_to_all | solution.py:601
  76.1 1.3 regroup.1
  77.4 7.5 %all-to-all-start.2 = ((bf16[16,64,512]{2,1,0:T(8,128)(2,1)}), bf16[16,64,512]{2,1,0:T(8,128)(2,1)}, u32[]{:S(2)}, u32[]{:S(2)}) async-start(bf16[16,64,512]{2,1,0:T(8,128)(2,1)} %regroup.1), calls=%async_computation.2 | async-start | bytes 2097152 | tf_op jit(solution)/shard_map/all_to_all | solution.py:601
  84.9 4.9 %collective-permute-start = (bf16[16,96,128]{2,1,0:T(8,128)(2,1)S(1)}, bf16[16,96,128]{2,1,0:T(8,128)(2,1)S(1)}, u32[]{:S(2)}, u32[]{:S(2)}) collective-permute-start(bf16[16,96,128]{2,1,0:T(8,128)(2,1)S(1)} %all_to_all.30.inc_ref.own_block), channel_id=1, source_target_pairs={{0,16},{16,0},{32,48},{48,32},{64,80},{80,64},{96,112},{112,96},{1... | collective-permute-start | bytes 1179656 | tf_op jit(solution)/shard_map/ppermute | solution.py:605
  89.8 1.3 collective-permute-done.other_block
  91.1 0.2 prepare.1
  91.3 0.8 copy-done.3
  92.2 0.7 copy-done.6
  92.8 3.3 %forward.1 = (bf16[16,128,128]{2,1,0:T(8,128)(2,1)}, bf16[128,512]{1,0:T(8,128)(2,1)}, bf16[2,8,32,128]{3,2,1,0:T(8,128)(2,1)}) custom-call(bf16[2,64,2048]{2,1,0:T(8,128)(2,1)} %copy-done.3, bf16[2,64,512]{2,1,0:T(8,128)(2,1)} %copy-done.6, bf16[2048,512]{1,0:T(8,128)(2,1)} %all-gather.2.cloned.1.call-done.weights_hbm.weights_ref), custom_call_target="tpu_custom_call" | custom-call | flops 536870912 | bytes 4194304 | tf_op jit(solution)/shard_map/forward/pallas_call | solution.py:328
  96.1 3.2 %all-to-all-done.2.mine_hbm = bf16[16,64,512]{2,1,0:T(8,128)(2,1)} async-done(((bf16[16,64,512]{2,1,0:T(8,128)(2,1)}), bf16[16,64,512]{2,1,0:T(8,128)(2,1)}, u32[]{:S(2)}, u32[]{:S(2)}) %all-to-all-start.2) | async-done | bytes 1048608 | tf_op jit(solution)/shard_map/all_to_all | solution.py:601
  99.3 7.0 %collective-permute-start.1 = (bf16[16,64,512]{2,1,0:T(8,128)(2,1)}, bf16[16,64,512]{2,1,0:T(8,128)(2,1)}, u32[]{:S(2)}, u32[]{:S(2)}) collective-permute-start(bf16[16,64,512]{2,1,0:T(8,128)(2,1)} %all-to-all-done.2.mine_hbm), channel_id=1, source_target_pairs={{0,16},{16,0},{32,48},{48,32},{64,80},{80,64},{96,112},{112,96},{1... | collective-permute-start | bytes 3145736 | tf_op jit(solution)/shard_map/ppermute | solution.py:605
  106.3 7.0 %all-to-all-start.3 = ((bf16[16,128,128]{2,1,0:T(8,128)(2,1)}), bf16[16,128,128]{2,1,0:T(8,128)(2,1)S(1)}, u32[]{:S(2)}, u32[]{:S(2)}) async-start(bf16[16,128,128]{2,1,0:T(8,128)(2,1)} %get-tuple-element.29), calls=%async_computation.3 | async-start | bytes 1048576 | tf_op jit(solution)/shard_map/all_to_all | solution.py:601
  113.3 0.9 copy-done.1
  114.2 0.9 copy-done.5
  115.1 0.8 backward.1
  115.9 0.8 copy-done.4
  116.7 2.2 %collective-permute-start.2 = (bf16[20,64,128]{2,1,0:T(8,128)(2,1)S(1)}, bf16[20,64,128]{2,1,0:T(8,128)(2,1)S(1)}, u32[]{:S(2)}, u32[]{:S(2)}) collective-permute-start(bf16[20,64,128]{2,1,0:T(8,128)(2,1)S(1)} %get-tuple-element.33), channel_id=1, source_target_pairs={{0,16},{16,0},{32,48},{48,32},{64,80},{80,64},{96,112},{112,96},{1... | collective-permute-start | bytes 983048 | tf_op jit(solution)/shard_map/ppermute | solution.py:605
  119.1 1.1 collective-permute-done.2.swapped_hbm
  120.2 4.1 %all-to-all-done.3.slopes_ref = bf16[16,128,128]{2,1,0:T(8,128)(2,1)S(1)} async-done(((bf16[16,128,128]{2,1,0:T(8,128)(2,1)}), bf16[16,128,128]{2,1,0:T(8,128)(2,1)S(1)}, u32[]{:S(2)}, u32[]{:S(2)}) %all-to-all-start.3) | async-done | bytes 524320 | tf_op jit(solution)/shard_map/all_to_all | solution.py:601
  124.4 2.5 %weight_parts.1 = bf16[16,128,128]{2,1,0:T(8,128)(2,1)S(1)} custom-call(bf16[16,64,512]{2,1,0:T(8,128)(2,1)} %all-to-all-done.2.mine_hbm, bf16[16,64,512]{2,1,0:T(8,128)(2,1)} %collective-permute-done.1.theirs_hbm, bf16[16,128,128]{2,1,0:T(8,128)(2,1)S(1)} %all-to-all-done.3.slopes_ref, f32[64,2048]{1,0:T(8,128)} %copy-done.4, ...), custom_call_target="tpu_custom_call" | custom-call | flops 268435456 | bytes 4194304 | tf_op jit(solution)/shard_map/weight_parts/pallas_call | solution.py:421
  126.9 30.0 %all_to_all.31.back_ref.back_hbm = bf16[16,128,128]{2,1,0:T(8,128)(2,1)} all-to-all(bf16[16,128,128]{2,1,0:T(8,128)(2,1)S(1)} %weight_parts.1), channel_id=1, replica_groups=mesh['row'=32,'col'=16] {'col'}, dimensions={0} | all-to-all | bytes 1048576 | tf_op jit(solution)/shard_map/all_to_all | solution.py:601
  156.9 4.5 %return_slots.1 = bf16[32,112,128]{2,1,0:T(8,128)(2,1)} custom-call(bf16[16,128,128]{2,1,0:T(8,128)(2,1)} %all_to_all.31.back_ref.back_hbm, s32[32,128]{1,0:T(8,128)} %bitcast.7, bf16[512,1024]{1,0:T(8,128)(2,1)} %get-tuple-element.37.hubs_hbm), custom_call_target="tpu_custom_call" | custom-call | flops 2415919104 | bytes 3145728 | tf_op jit(solution)/shard_map/return_slots/pallas_call | solution.py:483
  161.4 10.7 %all-to-all-start.5 = ((bf16[32,112,128]{2,1,0:T(8,128)(2,1)}), bf16[32,112,128]{2,1,0:T(8,128)(2,1)S(1)}, u32[]{:S(2)}, u32[]{:S(2)}) async-start(bf16[32,112,128]{2,1,0:T(8,128)(2,1)} %return_slots.1), calls=%async_computation.5 | async-start | bytes 1835008 | tf_op jit(solution)/shard_map/all_to_all | solution.py:601
  172.2 3.9 %local_grads.1 = (f32[512,1024]{1,0:T(8,128)}, bf16[64,1024]{1,0:T(8,128)(2,1)}) custom-call(bf16[16,128,128]{2,1,0:T(8,128)(2,1)} %all_to_all.31.back_ref.back_hbm, bf16[1024,1024]{1,0:T(8,128)(2,1)} %get-tuple-element.35.local_ref), custom_call_target="tpu_custom_call" | custom-call | flops 536870912 | bytes 3145728 | tf_op jit(solution)/shard_map/local_grads/pallas_call | solution.py:515
  176.1 11.8 %all-to-all-done.5.back_ref = bf16[32,112,128]{2,1,0:T(8,128)(2,1)S(1)} async-done(((bf16[32,112,128]{2,1,0:T(8,128)(2,1)}), bf16[32,112,128]{2,1,0:T(8,128)(2,1)S(1)}, u32[]{:S(2)}, u32[]{:S(2)}) %all-to-all-start.5) | async-done | bytes 917536 | tf_op jit(solution)/shard_map/all_to_all | solution.py:601
  187.9 4.7 %spread_grads.1 = (bf16[64,1024]{1,0:T(8,128)(2,1)}, f32[64,1024]{1,0:T(8,128)}, f32[64,1024]{1,0:T(8,128)}) custom-call(bf16[32,112,128]{2,1,0:T(8,128)(2,1)S(1)} %all-to-all-done.5.back_ref, s32[32,128]{1,0:T(8,128)S(1)} %bitcast.10, s32[1,16]{1,0:T(1,128)S(1)} %bitcast.14, f32[512,1024]{1,0:T(8,128)} %get-tuple-element.38.base_hbm), custom_call_target="tpu_custom_call" | custom-call | flops 2214592512 | bytes 2097152 | tf_op jit(solution)/shard_map/spread_grads/pallas_call | solution.py:573
  (28 shorter events, 0.3 us)
Async XLA Ops:
  7.2 85.7 %all-gather.2.cloned.1.call-start = ((), (), s32[]{:S(2)}) async-start(), calls=%async_computation.6 | async-start | bytes 2228224 | tf_op jit(solution)/shard_map/all_gather | solution.py:613
  12.3 23.5 %all-to-all-start = ((bf16[32,80,128]{2,1,0:T(8,128)(2,1)}), bf16[32,80,128]{2,1,0:T(8,128)(2,1)S(1)}, u32[]{:S(2)}, u32[]{:S(2)}) async-start(bf16[32,80,128]{2,1,0:T(8,128)(2,1)} %gather_slots.1), calls=%async_computation | async-start | bytes 1310720 | tf_op jit(solution)/shard_map/all_to_all | solution.py:601
  22.7 13.0 %copy-start.7 = (bf16[64,1024]{1,0:T(8,128)(2,1)S(1)}, bf16[64,1024]{1,0:T(8,128)(2,1)}, u32[]{:S(2)}) copy-start(bf16[64,1024]{1,0:T(8,128)(2,1)} %x_hbm.3) | copy-start | bytes 393220
  22.7 13.0 %copy-start.8 = (bf16[64,1024]{1,0:T(8,128)(2,1)S(1)}, bf16[64,1024]{1,0:T(8,128)(2,1)}, u32[]{:S(2)}) copy-start(bf16[64,1024]{1,0:T(8,128)(2,1)} %cot_hbm.1) | copy-start | bytes 393220
  22.7 13.0 %copy-start.9 = (s32[1,32,128]{2,1,0:T(8,128)S(1)}, s32[1,32,128]{2,1,0:T(8,128)}, u32[]{:S(2)}) copy-start(s32[1,32,128]{2,1,0:T(8,128)} %param.15) | copy-start | bytes 49156
  22.8 13.0 %copy-start.11 = (s32[1024,2]{0,1:T(2,128)S(1)}, s32[1024,2]{0,1:T(2,128)}, u32[]{:S(2)}) copy-start(s32[1024,2]{0,1:T(2,128)} %param.17) | copy-start | bytes 24580
  77.4 21.9 %all-to-all-start.2 = ((bf16[16,64,512]{2,1,0:T(8,128)(2,1)}), bf16[16,64,512]{2,1,0:T(8,128)(2,1)}, u32[]{:S(2)}, u32[]{:S(2)}) async-start(bf16[16,64,512]{2,1,0:T(8,128)(2,1)} %regroup.1), calls=%async_computation.2 | async-start | bytes 2097152 | tf_op jit(solution)/shard_map/all_to_all | solution.py:601
  84.9 6.2 %collective-permute-start = (bf16[16,96,128]{2,1,0:T(8,128)(2,1)S(1)}, bf16[16,96,128]{2,1,0:T(8,128)(2,1)S(1)}, u32[]{:S(2)}, u32[]{:S(2)}) collective-permute-start(bf16[16,96,128]{2,1,0:T(8,128)(2,1)S(1)} %all_to_all.30.inc_ref.own_block), channel_id=1, source_target_pairs={{0,16},{16,0},{32,48},{48,32},{64,80},{80,64},{96,112},{112,96},{1... | collective-permute-start | bytes 1179656 | tf_op jit(solution)/shard_map/ppermute | solution.py:605
  91.3 0.9 copy-start.3
  92.2 0.7 copy-start.6
  92.8 20.4 %copy-start = (bf16[2048,512]{1,0:T(8,128)(2,1)S(1)}, bf16[2048,512]{1,0:T(8,128)(2,1)}, u32[]{:S(2)}) copy-start(bf16[2048,512]{1,0:T(8,128)(2,1)} %all-gather.2.cloned.1.call-done.weights_hbm.weights_ref) | copy-start | bytes 6291460
  96.1 28.3 %copy-start.2 = (bf16[2,8,32,128]{3,2,1,0:T(8,128)(2,1)S(1)}, bf16[2,8,32,128]{3,2,1,0:T(8,128)(2,1)}, u32[]{:S(2)}) copy-start(bf16[2,8,32,128]{3,2,1,0:T(8,128)(2,1)} %get-tuple-element.31.hidden_ref.hidden_hbm) | copy-start | bytes 393220
  99.3 25.1 %collective-permute-start.1 = (bf16[16,64,512]{2,1,0:T(8,128)(2,1)}, bf16[16,64,512]{2,1,0:T(8,128)(2,1)}, u32[]{:S(2)}, u32[]{:S(2)}) collective-permute-start(bf16[16,64,512]{2,1,0:T(8,128)(2,1)} %all-to-all-done.2.mine_hbm), channel_id=1, source_target_pairs={{0,16},{16,0},{32,48},{48,32},{64,80},{80,64},{96,112},{112,96},{1... | collective-permute-start | bytes 3145736 | tf_op jit(solution)/shard_map/ppermute | solution.py:605
  106.3 18.0 %all-to-all-start.3 = ((bf16[16,128,128]{2,1,0:T(8,128)(2,1)}), bf16[16,128,128]{2,1,0:T(8,128)(2,1)S(1)}, u32[]{:S(2)}, u32[]{:S(2)}) async-start(bf16[16,128,128]{2,1,0:T(8,128)(2,1)} %get-tuple-element.29), calls=%async_computation.3 | async-start | bytes 1048576 | tf_op jit(solution)/shard_map/all_to_all | solution.py:601
  113.3 0.9 copy-start.1
  114.2 0.9 copy-start.5
  115.9 0.8 copy-start.4
  116.7 3.5 %collective-permute-start.2 = (bf16[20,64,128]{2,1,0:T(8,128)(2,1)S(1)}, bf16[20,64,128]{2,1,0:T(8,128)(2,1)S(1)}, u32[]{:S(2)}, u32[]{:S(2)}) collective-permute-start(bf16[20,64,128]{2,1,0:T(8,128)(2,1)S(1)} %get-tuple-element.33), channel_id=1, source_target_pairs={{0,16},{16,0},{32,48},{48,32},{64,80},{80,64},{96,112},{112,96},{1... | collective-permute-start | bytes 983048 | tf_op jit(solution)/shard_map/ppermute | solution.py:605
  161.4 26.5 %copy-start.10 = (s32[1,32,128]{2,1,0:T(8,128)S(1)}, s32[1,32,128]{2,1,0:T(8,128)}, u32[]{:S(2)}) copy-start(s32[1,32,128]{2,1,0:T(8,128)} %param.14) | copy-start | bytes 49156
  161.4 26.5 %copy-start.12 = (s32[16]{0:T(128)S(1)}, s32[16]{0:T(128)}, u32[]{:S(2)}) copy-start(s32[16]{0:T(128)} %param.16) | copy-start | bytes 196
  161.4 26.5 %all-to-all-start.5 = ((bf16[32,112,128]{2,1,0:T(8,128)(2,1)}), bf16[32,112,128]{2,1,0:T(8,128)(2,1)S(1)}, u32[]{:S(2)}, u32[]{:S(2)}) async-start(bf16[32,112,128]{2,1,0:T(8,128)(2,1)} %return_slots.1), calls=%async_computation.5 | async-start | bytes 1835008 | tf_op jit(solution)/shard_map/all_to_all | solution.py:601
Sparse Core Ops, SparseCore 0:
  10.7 82.0 all-gather.1

commit v11 on v10

--- a/solution.py
+++ b/solution.py
@@ -494,7 +494,7 @@
             pltpu.SemaphoreType.DMA((4,)),
             pltpu.SemaphoreType.DMA((4,)),
         ],
-        compiler_params=params(60),
+        compiler_params=params(53),
         cost_estimate=cost(2 * 256 * 4608 * 1024, 3 << 20),
         name="return_slots",
     )(back_block, recv_lanes, hubs)

time: 200 us -> 200 us (level)
    unnamed x26 -> x28, local copies, waits for them, and re-layouts: 4.14 us -> 4.14 us
  transfers between devices with their start and end apart: 8 -> 8, of which waited for: 6 -> 7; matrix products, arithmetic and copies ran while one was open for 0% -> 0% of each run, Pallas kernels for 12% -> 12%
where the time goes in v11:
time: 200 us; the launch traced here: 199 us
  blocking collectives  65.9 us (33%)
  starting transfers between devices  48 us (24%)
  Pallas kernels  35.3 us (18%)
  waiting for transfers between devices  29.4 us (15%)
  between operations  14.3 us (7%)
  local copies, waits for them, and re-layouts  4.32 us (2%)
    all_to_all x2, blocking collectives, exchange(): lax.all_to_all(blocks, axis, 0, 0, axis_index_groups=groups, tiled=True)  65.9 us
    all_to_all x4, starting transfers between devices, exchange(): lax.all_to_all(blocks, axis, 0, 0, axis_index_groups=groups, tiled=True)  35 us
    all_to_all x4, waiting for transfers between devices, exchange(): lax.all_to_all(blocks, axis, 0, 0, axis_index_groups=groups, tiled=True)  26.9 us
    ppermute x3, starting transfers between devices, other_core(): return lax.ppermute(block, 'row', [(i, i ^ 1) for i in range(PEERS)])  13 us
    pallas_call x1, Pallas kernels, build_counts(): pl.pallas_call(build_kernel, grid=(NODES // BUILD,), in_specs=[whole((FEA...  6.22 us
    pallas_call x1, Pallas kernels, aggregate(): pl.pallas_call(aggregate_kernel, out_shape=[jax.ShapeDtypeStruct((LAYERS,...  4.94 us
    pallas_call x1, Pallas kernels, spread_grads(): pl.pallas_call(spread_kernel, in_specs=[VMEM, HBM, HBM, HBM], out_specs=[...  4.74 us
    unnamed x28, local copies, waits for them, and re-layouts  4.14 us
  transfers between devices with their start and end apart: 8, of which 7 were waited for; matrix products, arithmetic and copies ran while one was open for 0% of the time, Pallas kernels for 12%

profile of v11, /device:TPU:1, one launch (start us, length us, event | category | flops | bytes accessed | tf_op | source)
XLA Modules:
  0.0 198.8 jit_solution(8026475982678391105)
XLA Ops:
  7.2 1.5 fusion
  8.8 3.5 %gather_slots.1 = bf16[32,80,128]{2,1,0:T(8,128)(2,1)} custom-call(bf16[64,1024]{1,0:T(8,128)(2,1)} %x_hbm.3, s32[32,128]{1,0:T(8,128)} %bitcast.9, s32[1,16]{1,0:T(1,128)} %bitcast.13), custom_call_target="tpu_custom_call" | custom-call | flops 2147483648 | bytes 1048576 | tf_op jit(solution)/shard_map/gather_slots/pallas_call | solution.py:80
  12.3 10.4 %all-to-all-start = ((bf16[32,80,128]{2,1,0:T(8,128)(2,1)}), bf16[32,80,128]{2,1,0:T(8,128)(2,1)S(1)}, u32[]{:S(2)}, u32[]{:S(2)}) async-start(bf16[32,80,128]{2,1,0:T(8,128)(2,1)} %gather_slots.1), calls=%async_computation | async-start | bytes 1310720 | tf_op jit(solution)/shard_map/all_to_all | solution.py:601
  22.8 6.2 %build_counts.1 = (bf16[1024,1024]{1,0:T(8,128)(2,1)}, bf16[512,1024]{1,0:T(8,128)(2,1)}, f32[512,1024]{1,0:T(8,128)}) custom-call(bf16[64,1024]{1,0:T(8,128)(2,1)} %x_hbm.3, s32[8,1024]{1,0:T(8,128)} %bitcast.15, s32[2,1024]{1,0:T(2,128)} %bitcast.11), custom_call_target="tpu_custom_call" | custom-call | flops 1073741824 | bytes 4194304 | tf_op jit(solution)/shard_map/build_counts/pallas_call | solution.py:116
  29.0 6.8 %all-to-all-done.inc_ref = bf16[32,80,128]{2,1,0:T(8,128)(2,1)S(1)} async-done(((bf16[32,80,128]{2,1,0:T(8,128)(2,1)}), bf16[32,80,128]{2,1,0:T(8,128)(2,1)S(1)}, u32[]{:S(2)}, u32[]{:S(2)}) %all-to-all-start) | async-done | bytes 655392 | tf_op jit(solution)/shard_map/all_to_all | solution.py:601
  35.8 4.9 %aggregate.1 = (bf16[16,96,128]{2,1,0:T(8,128)(2,1)S(1)}, f32[8,1024]{1,0:T(8,128)S(1)}) custom-call(bf16[64,1024]{1,0:T(8,128)(2,1)S(1)} %copy-done.8, bf16[32,80,128]{2,1,0:T(8,128)(2,1)S(1)} %all-to-all-done.inc_ref, s32[32,128]{1,0:T(8,128)S(1)} %bitcast.7, f32[512,1024]{1,0:T(8,128)} %get-tuple-element.23.sum_hbm, s32[2,1024]{1,0:T(2,128)S(1)} %bitcast.12, ...), custom_call_target="tpu_custom_call" | custom-call | flops 2952790016 | bytes 3145728 | tf_op jit(solution)/shard_map/aggregate/pallas_call | solution.py:195
  40.7 36.4 %all_to_all.30.inc_ref.own_block = bf16[16,96,128]{2,1,0:T(8,128)(2,1)S(1)} all-to-all(bf16[16,96,128]{2,1,0:T(8,128)(2,1)S(1)} %get-tuple-element.24), channel_id=1, replica_groups=mesh['row'=32,'col'=16] {'col'}, dimensions={0} | all-to-all | bytes 786432 | tf_op jit(solution)/shard_map/all_to_all | solution.py:601
  77.1 1.3 regroup.1
  78.4 6.9 %all-to-all-start.2 = ((bf16[16,64,512]{2,1,0:T(8,128)(2,1)}), bf16[16,64,512]{2,1,0:T(8,128)(2,1)}, u32[]{:S(2)}, u32[]{:S(2)}) async-start(bf16[16,64,512]{2,1,0:T(8,128)(2,1)} %regroup.1), calls=%async_computation.2 | async-start | bytes 2097152 | tf_op jit(solution)/shard_map/all_to_all | solution.py:601
  85.3 4.5 %collective-permute-start = (bf16[16,96,128]{2,1,0:T(8,128)(2,1)S(1)}, bf16[16,96,128]{2,1,0:T(8,128)(2,1)S(1)}, u32[]{:S(2)}, u32[]{:S(2)}) collective-permute-start(bf16[16,96,128]{2,1,0:T(8,128)(2,1)S(1)} %all_to_all.30.inc_ref.own_block), channel_id=1, source_target_pairs={{0,16},{16,0},{32,48},{48,32},{64,80},{80,64},{96,112},{112,96},{1... | collective-permute-start | bytes 1179656 | tf_op jit(solution)/shard_map/ppermute | solution.py:605
  89.8 1.3 collective-permute-done.other_block
  91.1 0.2 prepare.1
  91.3 0.8 copy-done.4
  92.2 0.7 copy-done.7
  92.9 3.3 %forward.1 = (bf16[16,128,128]{2,1,0:T(8,128)(2,1)}, bf16[128,512]{1,0:T(8,128)(2,1)}, bf16[2,8,32,128]{3,2,1,0:T(8,128)(2,1)}) custom-call(bf16[2,64,2048]{2,1,0:T(8,128)(2,1)} %copy-done.4, bf16[2,64,512]{2,1,0:T(8,128)(2,1)} %copy-done.7, bf16[2048,512]{1,0:T(8,128)(2,1)} %all-gather.2.cloned.1.call-done.weights_hbm.weights_ref), custom_call_target="tpu_custom_call" | custom-call | flops 536870912 | bytes 4194304 | tf_op jit(solution)/shard_map/forward/pallas_call | solution.py:328
  96.2 4.1 %all-to-all-done.2.mine_hbm = bf16[16,64,512]{2,1,0:T(8,128)(2,1)} async-done(((bf16[16,64,512]{2,1,0:T(8,128)(2,1)}), bf16[16,64,512]{2,1,0:T(8,128)(2,1)}, u32[]{:S(2)}, u32[]{:S(2)}) %all-to-all-start.2) | async-done | bytes 1048608 | tf_op jit(solution)/shard_map/all_to_all | solution.py:601
  100.3 6.4 %collective-permute-start.1 = (bf16[16,64,512]{2,1,0:T(8,128)(2,1)}, bf16[16,64,512]{2,1,0:T(8,128)(2,1)}, u32[]{:S(2)}, u32[]{:S(2)}) collective-permute-start(bf16[16,64,512]{2,1,0:T(8,128)(2,1)} %all-to-all-done.2.mine_hbm), channel_id=1, source_target_pairs={{0,16},{16,0},{32,48},{48,32},{64,80},{80,64},{96,112},{112,96},{1... | collective-permute-start | bytes 3145736 | tf_op jit(solution)/shard_map/ppermute | solution.py:605
  106.7 6.9 %all-to-all-start.3 = ((bf16[16,128,128]{2,1,0:T(8,128)(2,1)}), bf16[16,128,128]{2,1,0:T(8,128)(2,1)S(1)}, u32[]{:S(2)}, u32[]{:S(2)}) async-start(bf16[16,128,128]{2,1,0:T(8,128)(2,1)} %get-tuple-element.29), calls=%async_computation.3 | async-start | bytes 1048576 | tf_op jit(solution)/shard_map/all_to_all | solution.py:601
  113.6 0.9 copy-done.2
  114.5 0.9 copy-done.6
  115.4 0.8 backward.1
  116.3 0.8 copy-done.5
  117.0 2.2 %collective-permute-start.2 = (bf16[20,64,128]{2,1,0:T(8,128)(2,1)S(1)}, bf16[20,64,128]{2,1,0:T(8,128)(2,1)S(1)}, u32[]{:S(2)}, u32[]{:S(2)}) collective-permute-start(bf16[20,64,128]{2,1,0:T(8,128)(2,1)S(1)} %get-tuple-element.33), channel_id=1, source_target_pairs={{0,16},{16,0},{32,48},{48,32},{64,80},{80,64},{96,112},{112,96},{1... | collective-permute-start | bytes 983048 | tf_op jit(solution)/shard_map/ppermute | solution.py:605
  119.4 1.1 collective-permute-done.2.swapped_hbm
  120.6 4.1 %all-to-all-done.3.slopes_ref = bf16[16,128,128]{2,1,0:T(8,128)(2,1)S(1)} async-done(((bf16[16,128,128]{2,1,0:T(8,128)(2,1)}), bf16[16,128,128]{2,1,0:T(8,128)(2,1)S(1)}, u32[]{:S(2)}, u32[]{:S(2)}) %all-to-all-start.3) | async-done | bytes 524320 | tf_op jit(solution)/shard_map/all_to_all | solution.py:601
  124.7 2.5 %weight_parts.1 = bf16[16,128,128]{2,1,0:T(8,128)(2,1)S(1)} custom-call(bf16[16,64,512]{2,1,0:T(8,128)(2,1)} %all-to-all-done.2.mine_hbm, bf16[16,64,512]{2,1,0:T(8,128)(2,1)} %collective-permute-done.1.theirs_hbm, bf16[16,128,128]{2,1,0:T(8,128)(2,1)S(1)} %all-to-all-done.3.slopes_ref, f32[64,2048]{1,0:T(8,128)} %copy-done.5, ...), custom_call_target="tpu_custom_call" | custom-call | flops 268435456 | bytes 4194304 | tf_op jit(solution)/shard_map/weight_parts/pallas_call | solution.py:421
  127.2 29.5 %all_to_all.31.back_ref.back_hbm = bf16[16,128,128]{2,1,0:T(8,128)(2,1)S(1)} all-to-all(bf16[16,128,128]{2,1,0:T(8,128)(2,1)S(1)} %weight_parts.1), channel_id=1, replica_groups=mesh['row'=32,'col'=16] {'col'}, dimensions={0} | all-to-all | bytes 1048576 | tf_op jit(solution)/shard_map/all_to_all | solution.py:601
  156.7 4.0 %return_slots.1 = bf16[32,112,128]{2,1,0:T(8,128)(2,1)} custom-call(bf16[16,128,128]{2,1,0:T(8,128)(2,1)S(1)} %all_to_all.31.back_ref.back_hbm, s32[32,128]{1,0:T(8,128)S(1)} %bitcast.8, bf16[512,1024]{1,0:T(8,128)(2,1)} %get-tuple-element.37.hubs_hbm), custom_call_target="tpu_custom_call" | custom-call | flops 2415919104 | bytes 3145728 | tf_op jit(solution)/shard_map/return_slots/pallas_call | solution.py:483
  160.7 10.7 %all-to-all-start.5 = ((bf16[32,112,128]{2,1,0:T(8,128)(2,1)}), bf16[32,112,128]{2,1,0:T(8,128)(2,1)S(1)}, u32[]{:S(2)}, u32[]{:S(2)}) async-start(bf16[32,112,128]{2,1,0:T(8,128)(2,1)} %return_slots.1), calls=%async_computation.5 | async-start | bytes 1835008 | tf_op jit(solution)/shard_map/all_to_all | solution.py:601
  171.5 3.9 %local_grads.1 = (f32[512,1024]{1,0:T(8,128)}, bf16[64,1024]{1,0:T(8,128)(2,1)}) custom-call(bf16[16,128,128]{2,1,0:T(8,128)(2,1)} %copy-done.1, bf16[1024,1024]{1,0:T(8,128)(2,1)} %get-tuple-element.35.local_ref), custom_call_target="tpu_custom_call" | custom-call | flops 536870912 | bytes 3145728 | tf_op jit(solution)/shard_map/local_grads/pallas_call | solution.py:515
  175.4 11.8 %all-to-all-done.5.back_ref = bf16[32,112,128]{2,1,0:T(8,128)(2,1)S(1)} async-done(((bf16[32,112,128]{2,1,0:T(8,128)(2,1)}), bf16[32,112,128]{2,1,0:T(8,128)(2,1)S(1)}, u32[]{:S(2)}, u32[]{:S(2)}) %all-to-all-start.5) | async-done | bytes 917536 | tf_op jit(solution)/shard_map/all_to_all | solution.py:601
  187.2 4.7 %spread_grads.1 = (bf16[64,1024]{1,0:T(8,128)(2,1)}, f32[64,1024]{1,0:T(8,128)}, f32[64,1024]{1,0:T(8,128)}) custom-call(bf16[32,112,128]{2,1,0:T(8,128)(2,1)S(1)} %all-to-all-done.5.back_ref, s32[32,128]{1,0:T(8,128)S(1)} %bitcast.10, s32[1,16]{1,0:T(1,128)S(1)} %bitcast.14, f32[512,1024]{1,0:T(8,128)} %get-tuple-element.38.base_hbm), custom_call_target="tpu_custom_call" | custom-call | flops 2214592512 | bytes 2097152 | tf_op jit(solution)/shard_map/spread_grads/pallas_call | solution.py:573
  (30 shorter events, 0.4 us)
Async XLA Ops:
  7.2 85.8 %all-gather.2.cloned.1.call-start = ((), (), s32[]{:S(2)}) async-start(), calls=%async_computation.6 | async-start | bytes 2228224 | tf_op jit(solution)/shard_map/all_gather | solution.py:613
  12.3 23.5 %all-to-all-start = ((bf16[32,80,128]{2,1,0:T(8,128)(2,1)}), bf16[32,80,128]{2,1,0:T(8,128)(2,1)S(1)}, u32[]{:S(2)}, u32[]{:S(2)}) async-start(bf16[32,80,128]{2,1,0:T(8,128)(2,1)} %gather_slots.1), calls=%async_computation | async-start | bytes 1310720 | tf_op jit(solution)/shard_map/all_to_all | solution.py:601
  22.7 13.0 %copy-start.8 = (bf16[64,1024]{1,0:T(8,128)(2,1)S(1)}, bf16[64,1024]{1,0:T(8,128)(2,1)}, u32[]{:S(2)}) copy-start(bf16[64,1024]{1,0:T(8,128)(2,1)} %x_hbm.3) | copy-start | bytes 393220
  22.8 13.0 %copy-start.9 = (bf16[64,1024]{1,0:T(8,128)(2,1)S(1)}, bf16[64,1024]{1,0:T(8,128)(2,1)}, u32[]{:S(2)}) copy-start(bf16[64,1024]{1,0:T(8,128)(2,1)} %cot_hbm.1) | copy-start | bytes 393220
  22.8 13.0 %copy-start.10 = (s32[1,32,128]{2,1,0:T(8,128)S(1)}, s32[1,32,128]{2,1,0:T(8,128)}, u32[]{:S(2)}) copy-start(s32[1,32,128]{2,1,0:T(8,128)} %param.15) | copy-start | bytes 49156
  22.8 13.0 %copy-start.12 = (s32[1024,2]{0,1:T(2,128)S(1)}, s32[1024,2]{0,1:T(2,128)}, u32[]{:S(2)}) copy-start(s32[1024,2]{0,1:T(2,128)} %param.17) | copy-start | bytes 24580
  78.4 21.9 %all-to-all-start.2 = ((bf16[16,64,512]{2,1,0:T(8,128)(2,1)}), bf16[16,64,512]{2,1,0:T(8,128)(2,1)}, u32[]{:S(2)}, u32[]{:S(2)}) async-start(bf16[16,64,512]{2,1,0:T(8,128)(2,1)} %regroup.1), calls=%async_computation.2 | async-start | bytes 2097152 | tf_op jit(solution)/shard_map/all_to_all | solution.py:601
  85.3 5.8 %collective-permute-start = (bf16[16,96,128]{2,1,0:T(8,128)(2,1)S(1)}, bf16[16,96,128]{2,1,0:T(8,128)(2,1)S(1)}, u32[]{:S(2)}, u32[]{:S(2)}) collective-permute-start(bf16[16,96,128]{2,1,0:T(8,128)(2,1)S(1)} %all_to_all.30.inc_ref.own_block), channel_id=1, source_target_pairs={{0,16},{16,0},{32,48},{48,32},{64,80},{80,64},{96,112},{112,96},{1... | collective-permute-start | bytes 1179656 | tf_op jit(solution)/shard_map/ppermute | solution.py:605
  91.3 0.8 copy-start.4
  92.2 0.7 copy-start.7
  92.9 20.7 %copy-start = (bf16[2048,512]{1,0:T(8,128)(2,1)S(1)}, bf16[2048,512]{1,0:T(8,128)(2,1)}, u32[]{:S(2)}) copy-start(bf16[2048,512]{1,0:T(8,128)(2,1)} %all-gather.2.cloned.1.call-done.weights_hbm.weights_ref) | copy-start | bytes 6291460
  96.2 28.5 %copy-start.3 = (bf16[2,8,32,128]{3,2,1,0:T(8,128)(2,1)S(1)}, bf16[2,8,32,128]{3,2,1,0:T(8,128)(2,1)}, u32[]{:S(2)}) copy-start(bf16[2,8,32,128]{3,2,1,0:T(8,128)(2,1)} %get-tuple-element.31.hidden_ref.hidden_hbm) | copy-start | bytes 393220
  100.3 24.4 %collective-permute-start.1 = (bf16[16,64,512]{2,1,0:T(8,128)(2,1)}, bf16[16,64,512]{2,1,0:T(8,128)(2,1)}, u32[]{:S(2)}, u32[]{:S(2)}) collective-permute-start(bf16[16,64,512]{2,1,0:T(8,128)(2,1)} %all-to-all-done.2.mine_hbm), channel_id=1, source_target_pairs={{0,16},{16,0},{32,48},{48,32},{64,80},{80,64},{96,112},{112,96},{1... | collective-permute-start | bytes 3145736 | tf_op jit(solution)/shard_map/ppermute | solution.py:605
  106.7 18.0 %all-to-all-start.3 = ((bf16[16,128,128]{2,1,0:T(8,128)(2,1)}), bf16[16,128,128]{2,1,0:T(8,128)(2,1)S(1)}, u32[]{:S(2)}, u32[]{:S(2)}) async-start(bf16[16,128,128]{2,1,0:T(8,128)(2,1)} %get-tuple-element.29), calls=%async_computation.3 | async-start | bytes 1048576 | tf_op jit(solution)/shard_map/all_to_all | solution.py:601
  113.6 0.9 copy-start.2
  114.5 0.9 copy-start.6
  116.2 0.8 copy-start.5
  117.0 3.5 %collective-permute-start.2 = (bf16[20,64,128]{2,1,0:T(8,128)(2,1)S(1)}, bf16[20,64,128]{2,1,0:T(8,128)(2,1)S(1)}, u32[]{:S(2)}, u32[]{:S(2)}) collective-permute-start(bf16[20,64,128]{2,1,0:T(8,128)(2,1)S(1)} %get-tuple-element.33), channel_id=1, source_target_pairs={{0,16},{16,0},{32,48},{48,32},{64,80},{80,64},{96,112},{112,96},{1... | collective-permute-start | bytes 983048 | tf_op jit(solution)/shard_map/ppermute | solution.py:605
  156.7 4.0 %copy-start.1 = (bf16[16,128,128]{2,1,0:T(8,128)(2,1)}, bf16[16,128,128]{2,1,0:T(8,128)(2,1)S(1)}, u32[]{:S(2)}) copy-start(bf16[16,128,128]{2,1,0:T(8,128)(2,1)S(1)} %all_to_all.31.back_ref.back_hbm) | copy-start | bytes 1572868
  160.7 26.5 %copy-start.11 = (s32[1,32,128]{2,1,0:T(8,128)S(1)}, s32[1,32,128]{2,1,0:T(8,128)}, u32[]{:S(2)}) copy-start(s32[1,32,128]{2,1,0:T(8,128)} %param.14) | copy-start | bytes 49156
  160.7 26.5 %copy-start.13 = (s32[16]{0:T(128)S(1)}, s32[16]{0:T(128)}, u32[]{:S(2)}) copy-start(s32[16]{0:T(128)} %param.16) | copy-start | bytes 196
  160.7 26.5 %all-to-all-start.5 = ((bf16[32,112,128]{2,1,0:T(8,128)(2,1)}), bf16[32,112,128]{2,1,0:T(8,128)(2,1)S(1)}, u32[]{:S(2)}, u32[]{:S(2)}) async-start(bf16[32,112,128]{2,1,0:T(8,128)(2,1)} %return_slots.1), calls=%async_computation.5 | async-start | bytes 1835008 | tf_op jit(solution)/shard_map/all_to_all | solution.py:601
Sparse Core Ops, SparseCore 0:
  10.7 82.2 all-gather.1

commit v12 on v11

--- a/solution.py
+++ b/solution.py
@@ -441,22 +441,13 @@
 
 
 def return_kernel(
-    back_hbm, recv_hbm, hubs_hbm, out_hbm,
-    back_ref, part_ref, recv_ref, hubs_ref, out_ref, in_sems, out_sems,
+    back_ref, recv_hbm, hubs_hbm, out_hbm, recv_ref, hubs_ref, out_ref, in_sems, out_sems
 ):
-    staged = copies(
-        in_sems,
-        (recv_hbm, recv_ref),
-        (hubs_hbm, hubs_ref),
-        (back_hbm.at[:, :OWN, :], back_ref),
-        (back_hbm.at[:, 96:, :], part_ref),
-    )
+    staged = copies(in_sems, (recv_hbm, recv_ref), (hubs_hbm, hubs_ref))
     node = lax.broadcasted_iota(jnp.int32, (NODES, 2 * SLOTS), 0)
-    staged[2].wait()
-    share = back_ref[...].astype(F32).reshape(NODES, SLOTS).T[FEATS:, :].astype(BF16)
+    share = back_ref[:, :OWN, :].astype(F32).reshape(NODES, SLOTS).T[FEATS:, :].astype(BF16)
     staged[0].wait()
-    staged[3].wait()
-    sums = jnp.sum(part_ref[...].astype(F32), axis=0).astype(BF16)
+    sums = jnp.sum(back_ref[:, 96:, :].astype(F32), axis=0).astype(BF16)
     sent = []
     for pair in range(PEERS // 2):
         values = matmul(share, one_hot(node == pair_lanes(recv_ref, pair)), NN).astype(BF16)
@@ -482,16 +473,14 @@
 def return_slots(back_block, recv_lanes, hubs):
     return pl.pallas_call(
         return_kernel,
-        in_specs=[HBM, HBM, HBM],
+        in_specs=[VMEM, HBM, HBM],
         out_specs=HBM,
         out_shape=jax.ShapeDtypeStruct((PEERS, RETURN_ROWS, SLOTS), BF16),
         scratch_shapes=[
-            pltpu.VMEM((LAYERS, OWN, SLOTS), BF16),
-            pltpu.VMEM((LAYERS, 32, SLOTS), BF16),
             pltpu.VMEM((PEERS, SLOTS), jnp.int32),
             pltpu.VMEM((HUBS, NODES), BF16),
             pltpu.VMEM((PEERS, RETURN_ROWS, SLOTS), BF16),
-            pltpu.SemaphoreType.DMA((4,)),
+            pltpu.SemaphoreType.DMA((2,)),
             pltpu.SemaphoreType.DMA((4,)),
         ],
         compiler_params=params(53),

time: 200 us -> 200 us (level)
  no operation moved by 1% of the time
where the time goes in v12:
time: 200 us; the launch traced here: 199 us
  blocking collectives  65.9 us (33%)
  starting transfers between devices  48 us (24%)
  Pallas kernels  35.3 us (18%)
  waiting for transfers between devices  29.4 us (15%)
  between operations  14.3 us (7%)
  local copies, waits for them, and re-layouts  4.32 us (2%)
    all_to_all x2, blocking collectives, exchange(): lax.all_to_all(blocks, axis, 0, 0, axis_index_groups=groups, tiled=True)  65.9 us
    all_to_all x4, starting transfers between devices, exchange(): lax.all_to_all(blocks, axis, 0, 0, axis_index_groups=groups, tiled=True)  35 us
    all_to_all x4, waiting for transfers between devices, exchange(): lax.all_to_all(blocks, axis, 0, 0, axis_index_groups=groups, tiled=True)  26.9 us
    ppermute x3, starting transfers between devices, other_core(): return lax.ppermute(block, 'row', [(i, i ^ 1) for i in range(PEERS)])  13 us
    pallas_call x1, Pallas kernels, build_counts(): pl.pallas_call(build_kernel, grid=(NODES // BUILD,), in_specs=[whole((FEA...  6.22 us
    pallas_call x1, Pallas kernels, aggregate(): pl.pallas_call(aggregate_kernel, out_shape=[jax.ShapeDtypeStruct((LAYERS,...  4.94 us
    pallas_call x1, Pallas kernels, spread_grads(): pl.pallas_call(spread_kernel, in_specs=[VMEM, HBM, HBM, HBM], out_specs=[...  4.74 us
    unnamed x28, local copies, waits for them, and re-layouts  4.14 us
  transfers between devices with their start and end apart: 8, of which 7 were waited for; matrix products, arithmetic and copies ran while one was open for 0% of the time, Pallas kernels for 12%

profile of v12, /device:TPU:1, one launch (start us, length us, event | category | flops | bytes accessed | tf_op | source)
XLA Modules:
  0.0 198.8 jit_solution(12603890754551371284)
XLA Ops:
  7.2 1.5 fusion
  8.8 3.5 %gather_slots.1 = bf16[32,80,128]{2,1,0:T(8,128)(2,1)} custom-call(bf16[64,1024]{1,0:T(8,128)(2,1)} %x_hbm.3, s32[32,128]{1,0:T(8,128)} %bitcast.9, s32[1,16]{1,0:T(1,128)} %bitcast.13), custom_call_target="tpu_custom_call" | custom-call | flops 2147483648 | bytes 1048576 | tf_op jit(solution)/shard_map/gather_slots/pallas_call | solution.py:80
  12.3 10.4 %all-to-all-start = ((bf16[32,80,128]{2,1,0:T(8,128)(2,1)}), bf16[32,80,128]{2,1,0:T(8,128)(2,1)S(1)}, u32[]{:S(2)}, u32[]{:S(2)}) async-start(bf16[32,80,128]{2,1,0:T(8,128)(2,1)} %gather_slots.1), calls=%async_computation | async-start | bytes 1310720 | tf_op jit(solution)/shard_map/all_to_all | solution.py:590
  22.8 6.2 %build_counts.1 = (bf16[1024,1024]{1,0:T(8,128)(2,1)}, bf16[512,1024]{1,0:T(8,128)(2,1)}, f32[512,1024]{1,0:T(8,128)}) custom-call(bf16[64,1024]{1,0:T(8,128)(2,1)} %x_hbm.3, s32[8,1024]{1,0:T(8,128)} %bitcast.15, s32[2,1024]{1,0:T(2,128)} %bitcast.11), custom_call_target="tpu_custom_call" | custom-call | flops 1073741824 | bytes 4194304 | tf_op jit(solution)/shard_map/build_counts/pallas_call | solution.py:116
  29.0 6.8 %all-to-all-done.inc_ref = bf16[32,80,128]{2,1,0:T(8,128)(2,1)S(1)} async-done(((bf16[32,80,128]{2,1,0:T(8,128)(2,1)}), bf16[32,80,128]{2,1,0:T(8,128)(2,1)S(1)}, u32[]{:S(2)}, u32[]{:S(2)}) %all-to-all-start) | async-done | bytes 655392 | tf_op jit(solution)/shard_map/all_to_all | solution.py:590
  35.8 4.9 %aggregate.1 = (bf16[16,96,128]{2,1,0:T(8,128)(2,1)S(1)}, f32[8,1024]{1,0:T(8,128)S(1)}) custom-call(bf16[64,1024]{1,0:T(8,128)(2,1)S(1)} %copy-done.8, bf16[32,80,128]{2,1,0:T(8,128)(2,1)S(1)} %all-to-all-done.inc_ref, s32[32,128]{1,0:T(8,128)S(1)} %bitcast.7, f32[512,1024]{1,0:T(8,128)} %get-tuple-element.23.sum_hbm, s32[2,1024]{1,0:T(2,128)S(1)} %bitcast.12, ...), custom_call_target="tpu_custom_call" | custom-call | flops 2952790016 | bytes 3145728 | tf_op jit(solution)/shard_map/aggregate/pallas_call | solution.py:195
  40.7 36.4 %all_to_all.30.inc_ref.own_block = bf16[16,96,128]{2,1,0:T(8,128)(2,1)S(1)} all-to-all(bf16[16,96,128]{2,1,0:T(8,128)(2,1)S(1)} %get-tuple-element.24), channel_id=1, replica_groups=mesh['row'=32,'col'=16] {'col'}, dimensions={0} | all-to-all | bytes 786432 | tf_op jit(solution)/shard_map/all_to_all | solution.py:590
  77.1 1.3 regroup.1
  78.4 6.9 %all-to-all-start.2 = ((bf16[16,64,512]{2,1,0:T(8,128)(2,1)}), bf16[16,64,512]{2,1,0:T(8,128)(2,1)}, u32[]{:S(2)}, u32[]{:S(2)}) async-start(bf16[16,64,512]{2,1,0:T(8,128)(2,1)} %regroup.1), calls=%async_computation.2 | async-start | bytes 2097152 | tf_op jit(solution)/shard_map/all_to_all | solution.py:590
  85.3 4.5 %collective-permute-start = (bf16[16,96,128]{2,1,0:T(8,128)(2,1)S(1)}, bf16[16,96,128]{2,1,0:T(8,128)(2,1)S(1)}, u32[]{:S(2)}, u32[]{:S(2)}) collective-permute-start(bf16[16,96,128]{2,1,0:T(8,128)(2,1)S(1)} %all_to_all.30.inc_ref.own_block), channel_id=1, source_target_pairs={{0,16},{16,0},{32,48},{48,32},{64,80},{80,64},{96,112},{112,96},{1... | collective-permute-start | bytes 1179656 | tf_op jit(solution)/shard_map/ppermute | solution.py:594
  89.8 1.3 collective-permute-done.other_block
  91.1 0.2 prepare.1
  91.3 0.8 copy-done.4
  92.2 0.7 copy-done.7
  92.9 3.3 %forward.1 = (bf16[16,128,128]{2,1,0:T(8,128)(2,1)}, bf16[128,512]{1,0:T(8,128)(2,1)}, bf16[2,8,32,128]{3,2,1,0:T(8,128)(2,1)}) custom-call(bf16[2,64,2048]{2,1,0:T(8,128)(2,1)} %copy-done.4, bf16[2,64,512]{2,1,0:T(8,128)(2,1)} %copy-done.7, bf16[2048,512]{1,0:T(8,128)(2,1)} %all-gather.2.cloned.1.call-done.weights_hbm.weights_ref), custom_call_target="tpu_custom_call" | custom-call | flops 536870912 | bytes 4194304 | tf_op jit(solution)/shard_map/forward/pallas_call | solution.py:328
  96.2 4.1 %all-to-all-done.2.mine_hbm = bf16[16,64,512]{2,1,0:T(8,128)(2,1)} async-done(((bf16[16,64,512]{2,1,0:T(8,128)(2,1)}), bf16[16,64,512]{2,1,0:T(8,128)(2,1)}, u32[]{:S(2)}, u32[]{:S(2)}) %all-to-all-start.2) | async-done | bytes 1048608 | tf_op jit(solution)/shard_map/all_to_all | solution.py:590
  100.3 6.4 %collective-permute-start.1 = (bf16[16,64,512]{2,1,0:T(8,128)(2,1)}, bf16[16,64,512]{2,1,0:T(8,128)(2,1)}, u32[]{:S(2)}, u32[]{:S(2)}) collective-permute-start(bf16[16,64,512]{2,1,0:T(8,128)(2,1)} %all-to-all-done.2.mine_hbm), channel_id=1, source_target_pairs={{0,16},{16,0},{32,48},{48,32},{64,80},{80,64},{96,112},{112,96},{1... | collective-permute-start | bytes 3145736 | tf_op jit(solution)/shard_map/ppermute | solution.py:594
  106.7 6.9 %all-to-all-start.3 = ((bf16[16,128,128]{2,1,0:T(8,128)(2,1)}), bf16[16,128,128]{2,1,0:T(8,128)(2,1)S(1)}, u32[]{:S(2)}, u32[]{:S(2)}) async-start(bf16[16,128,128]{2,1,0:T(8,128)(2,1)} %get-tuple-element.29), calls=%async_computation.3 | async-start | bytes 1048576 | tf_op jit(solution)/shard_map/all_to_all | solution.py:590
  113.6 0.9 copy-done.2
  114.5 0.9 copy-done.6
  115.4 0.8 backward.1
  116.3 0.8 copy-done.5
  117.0 2.2 %collective-permute-start.2 = (bf16[20,64,128]{2,1,0:T(8,128)(2,1)S(1)}, bf16[20,64,128]{2,1,0:T(8,128)(2,1)S(1)}, u32[]{:S(2)}, u32[]{:S(2)}) collective-permute-start(bf16[20,64,128]{2,1,0:T(8,128)(2,1)S(1)} %get-tuple-element.33), channel_id=1, source_target_pairs={{0,16},{16,0},{32,48},{48,32},{64,80},{80,64},{96,112},{112,96},{1... | collective-permute-start | bytes 983048 | tf_op jit(solution)/shard_map/ppermute | solution.py:594
  119.4 1.1 collective-permute-done.2.swapped_hbm
  120.6 4.1 %all-to-all-done.3.slopes_ref = bf16[16,128,128]{2,1,0:T(8,128)(2,1)S(1)} async-done(((bf16[16,128,128]{2,1,0:T(8,128)(2,1)}), bf16[16,128,128]{2,1,0:T(8,128)(2,1)S(1)}, u32[]{:S(2)}, u32[]{:S(2)}) %all-to-all-start.3) | async-done | bytes 524320 | tf_op jit(solution)/shard_map/all_to_all | solution.py:590
  124.7 2.5 %weight_parts.1 = bf16[16,128,128]{2,1,0:T(8,128)(2,1)S(1)} custom-call(bf16[16,64,512]{2,1,0:T(8,128)(2,1)} %all-to-all-done.2.mine_hbm, bf16[16,64,512]{2,1,0:T(8,128)(2,1)} %collective-permute-done.1.theirs_hbm, bf16[16,128,128]{2,1,0:T(8,128)(2,1)S(1)} %all-to-all-done.3.slopes_ref, f32[64,2048]{1,0:T(8,128)} %copy-done.5, ...), custom_call_target="tpu_custom_call" | custom-call | flops 268435456 | bytes 4194304 | tf_op jit(solution)/shard_map/weight_parts/pallas_call | solution.py:421
  127.2 29.5 %all_to_all.31.back_ref = bf16[16,128,128]{2,1,0:T(8,128)(2,1)S(1)} all-to-all(bf16[16,128,128]{2,1,0:T(8,128)(2,1)S(1)} %weight_parts.1), channel_id=1, replica_groups=mesh['row'=32,'col'=16] {'col'}, dimensions={0} | all-to-all | bytes 1048576 | tf_op jit(solution)/shard_map/all_to_all | solution.py:590
  156.7 4.0 %return_slots.1 = bf16[32,112,128]{2,1,0:T(8,128)(2,1)} custom-call(bf16[16,128,128]{2,1,0:T(8,128)(2,1)S(1)} %all_to_all.31.back_ref, s32[32,128]{1,0:T(8,128)S(1)} %bitcast.8, bf16[512,1024]{1,0:T(8,128)(2,1)} %get-tuple-element.37.hubs_hbm), custom_call_target="tpu_custom_call" | custom-call | flops 2415919104 | bytes 3145728 | tf_op jit(solution)/shard_map/return_slots/pallas_call | solution.py:474
  160.7 10.7 %all-to-all-start.5 = ((bf16[32,112,128]{2,1,0:T(8,128)(2,1)}), bf16[32,112,128]{2,1,0:T(8,128)(2,1)S(1)}, u32[]{:S(2)}, u32[]{:S(2)}) async-start(bf16[32,112,128]{2,1,0:T(8,128)(2,1)} %return_slots.1), calls=%async_computation.5 | async-start | bytes 1835008 | tf_op jit(solution)/shard_map/all_to_all | solution.py:590
  171.4 3.9 %local_grads.1 = (f32[512,1024]{1,0:T(8,128)}, bf16[64,1024]{1,0:T(8,128)(2,1)}) custom-call(bf16[16,128,128]{2,1,0:T(8,128)(2,1)} %copy-done.1, bf16[1024,1024]{1,0:T(8,128)(2,1)} %get-tuple-element.35.local_ref), custom_call_target="tpu_custom_call" | custom-call | flops 536870912 | bytes 3145728 | tf_op jit(solution)/shard_map/local_grads/pallas_call | solution.py:504
  175.4 11.8 %all-to-all-done.5.back_ref = bf16[32,112,128]{2,1,0:T(8,128)(2,1)S(1)} async-done(((bf16[32,112,128]{2,1,0:T(8,128)(2,1)}), bf16[32,112,128]{2,1,0:T(8,128)(2,1)S(1)}, u32[]{:S(2)}, u32[]{:S(2)}) %all-to-all-start.5) | async-done | bytes 917536 | tf_op jit(solution)/shard_map/all_to_all | solution.py:590
  187.2 4.7 %spread_grads.1 = (bf16[64,1024]{1,0:T(8,128)(2,1)}, f32[64,1024]{1,0:T(8,128)}, f32[64,1024]{1,0:T(8,128)}) custom-call(bf16[32,112,128]{2,1,0:T(8,128)(2,1)S(1)} %all-to-all-done.5.back_ref, s32[32,128]{1,0:T(8,128)S(1)} %bitcast.10, s32[1,16]{1,0:T(1,128)S(1)} %bitcast.14, f32[512,1024]{1,0:T(8,128)} %get-tuple-element.38.base_hbm), custom_call_target="tpu_custom_call" | custom-call | flops 2214592512 | bytes 2097152 | tf_op jit(solution)/shard_map/spread_grads/pallas_call | solution.py:562
  (30 shorter events, 0.4 us)
Async XLA Ops:
  7.2 85.8 %all-gather.2.cloned.1.call-start = ((), (), s32[]{:S(2)}) async-start(), calls=%async_computation.6 | async-start | bytes 2228224 | tf_op jit(solution)/shard_map/all_gather | solution.py:602
  12.3 23.5 %all-to-all-start = ((bf16[32,80,128]{2,1,0:T(8,128)(2,1)}), bf16[32,80,128]{2,1,0:T(8,128)(2,1)S(1)}, u32[]{:S(2)}, u32[]{:S(2)}) async-start(bf16[32,80,128]{2,1,0:T(8,128)(2,1)} %gather_slots.1), calls=%async_computation | async-start | bytes 1310720 | tf_op jit(solution)/shard_map/all_to_all | solution.py:590
  22.7 13.0 %copy-start.8 = (bf16[64,1024]{1,0:T(8,128)(2,1)S(1)}, bf16[64,1024]{1,0:T(8,128)(2,1)}, u32[]{:S(2)}) copy-start(bf16[64,1024]{1,0:T(8,128)(2,1)} %x_hbm.3) | copy-start | bytes 393220
  22.8 13.0 %copy-start.9 = (bf16[64,1024]{1,0:T(8,128)(2,1)S(1)}, bf16[64,1024]{1,0:T(8,128)(2,1)}, u32[]{:S(2)}) copy-start(bf16[64,1024]{1,0:T(8,128)(2,1)} %cot_hbm.1) | copy-start | bytes 393220
  22.8 13.0 %copy-start.10 = (s32[1,32,128]{2,1,0:T(8,128)S(1)}, s32[1,32,128]{2,1,0:T(8,128)}, u32[]{:S(2)}) copy-start(s32[1,32,128]{2,1,0:T(8,128)} %param.15) | copy-start | bytes 49156
  22.8 13.0 %copy-start.12 = (s32[1024,2]{0,1:T(2,128)S(1)}, s32[1024,2]{0,1:T(2,128)}, u32[]{:S(2)}) copy-start(s32[1024,2]{0,1:T(2,128)} %param.17) | copy-start | bytes 24580
  78.4 21.9 %all-to-all-start.2 = ((bf16[16,64,512]{2,1,0:T(8,128)(2,1)}), bf16[16,64,512]{2,1,0:T(8,128)(2,1)}, u32[]{:S(2)}, u32[]{:S(2)}) async-start(bf16[16,64,512]{2,1,0:T(8,128)(2,1)} %regroup.1), calls=%async_computation.2 | async-start | bytes 2097152 | tf_op jit(solution)/shard_map/all_to_all | solution.py:590
  85.3 5.8 %collective-permute-start = (bf16[16,96,128]{2,1,0:T(8,128)(2,1)S(1)}, bf16[16,96,128]{2,1,0:T(8,128)(2,1)S(1)}, u32[]{:S(2)}, u32[]{:S(2)}) collective-permute-start(bf16[16,96,128]{2,1,0:T(8,128)(2,1)S(1)} %all_to_all.30.inc_ref.own_block), channel_id=1, source_target_pairs={{0,16},{16,0},{32,48},{48,32},{64,80},{80,64},{96,112},{112,96},{1... | collective-permute-start | bytes 1179656 | tf_op jit(solution)/shard_map/ppermute | solution.py:594
  91.3 0.8 copy-start.4
  92.2 0.7 copy-start.7
  92.9 20.7 %copy-start = (bf16[2048,512]{1,0:T(8,128)(2,1)S(1)}, bf16[2048,512]{1,0:T(8,128)(2,1)}, u32[]{:S(2)}) copy-start(bf16[2048,512]{1,0:T(8,128)(2,1)} %all-gather.2.cloned.1.call-done.weights_hbm.weights_ref) | copy-start | bytes 6291460
  96.2 28.5 %copy-start.3 = (bf16[2,8,32,128]{3,2,1,0:T(8,128)(2,1)S(1)}, bf16[2,8,32,128]{3,2,1,0:T(8,128)(2,1)}, u32[]{:S(2)}) copy-start(bf16[2,8,32,128]{3,2,1,0:T(8,128)(2,1)} %get-tuple-element.31.hidden_ref.hidden_hbm) | copy-start | bytes 393220
  100.3 24.4 %collective-permute-start.1 = (bf16[16,64,512]{2,1,0:T(8,128)(2,1)}, bf16[16,64,512]{2,1,0:T(8,128)(2,1)}, u32[]{:S(2)}, u32[]{:S(2)}) collective-permute-start(bf16[16,64,512]{2,1,0:T(8,128)(2,1)} %all-to-all-done.2.mine_hbm), channel_id=1, source_target_pairs={{0,16},{16,0},{32,48},{48,32},{64,80},{80,64},{96,112},{112,96},{1... | collective-permute-start | bytes 3145736 | tf_op jit(solution)/shard_map/ppermute | solution.py:594
  106.7 18.0 %all-to-all-start.3 = ((bf16[16,128,128]{2,1,0:T(8,128)(2,1)}), bf16[16,128,128]{2,1,0:T(8,128)(2,1)S(1)}, u32[]{:S(2)}, u32[]{:S(2)}) async-start(bf16[16,128,128]{2,1,0:T(8,128)(2,1)} %get-tuple-element.29), calls=%async_computation.3 | async-start | bytes 1048576 | tf_op jit(solution)/shard_map/all_to_all | solution.py:590
  113.6 0.9 copy-start.2
  114.5 0.9 copy-start.6
  116.2 0.8 copy-start.5
  117.0 3.5 %collective-permute-start.2 = (bf16[20,64,128]{2,1,0:T(8,128)(2,1)S(1)}, bf16[20,64,128]{2,1,0:T(8,128)(2,1)S(1)}, u32[]{:S(2)}, u32[]{:S(2)}) collective-permute-start(bf16[20,64,128]{2,1,0:T(8,128)(2,1)S(1)} %get-tuple-element.33), channel_id=1, source_target_pairs={{0,16},{16,0},{32,48},{48,32},{64,80},{80,64},{96,112},{112,96},{1... | collective-permute-start | bytes 983048 | tf_op jit(solution)/shard_map/ppermute | solution.py:594
  156.7 4.0 %copy-start.1 = (bf16[16,128,128]{2,1,0:T(8,128)(2,1)}, bf16[16,128,128]{2,1,0:T(8,128)(2,1)S(1)}, u32[]{:S(2)}) copy-start(bf16[16,128,128]{2,1,0:T(8,128)(2,1)S(1)} %all_to_all.31.back_ref) | copy-start | bytes 1572868
  160.7 26.5 %copy-start.11 = (s32[1,32,128]{2,1,0:T(8,128)S(1)}, s32[1,32,128]{2,1,0:T(8,128)}, u32[]{:S(2)}) copy-start(s32[1,32,128]{2,1,0:T(8,128)} %param.14) | copy-start | bytes 49156
  160.7 26.5 %copy-start.13 = (s32[16]{0:T(128)S(1)}, s32[16]{0:T(128)}, u32[]{:S(2)}) copy-start(s32[16]{0:T(128)} %param.16) | copy-start | bytes 196
  160.7 26.5 %all-to-all-start.5 = ((bf16[32,112,128]{2,1,0:T(8,128)(2,1)}), bf16[32,112,128]{2,1,0:T(8,128)(2,1)S(1)}, u32[]{:S(2)}, u32[]{:S(2)}) async-start(bf16[32,112,128]{2,1,0:T(8,128)(2,1)} %return_slots.1), calls=%async_computation.5 | async-start | bytes 1835008 | tf_op jit(solution)/shard_map/all_to_all | solution.py:590
Sparse Core Ops, SparseCore 0:
  10.7 82.2 all-gather.1

commit v13 on v11

--- a/solution.py
+++ b/solution.py
@@ -536,12 +536,6 @@
     staged = copies(in_sems, (send_hbm, send_ref), (hub_hbm, hub_ref), (base_hbm.at[:FEATS], base_ref))
     for peer in range(PEERS):
         slots[:, SLOTS * peer : SLOTS * (peer + 1)] = back_ref[peer, :FEATS, :]
-        grads = back_ref[peer, ROWS:, :].astype(F32)
-        slice_of, start = peer // 8, HALF * (peer % 2) + SLOTS * (peer // 2 % 4)
-        grads_ref[PIECE * slice_of : PIECE * (slice_of + 1), start : start + SLOTS] = grads
-    sent = copies(
-        out_sems, (grads_ref.at[:FEATS], self_hbm), (grads_ref.at[FEATS:], neigh_hbm)
-    )
     sums = jnp.sum(back_ref[:, FEATS:ROWS, :].astype(F32), axis=0)
     total = sums[:, :FEATS] + sums[:, FEATS:]
     high = total.astype(BF16).astype(F32)
@@ -563,6 +557,14 @@
         hub_hot = one_hot(hub_node == hub_ref[...])
         grad = grad + matmul(hub_high, hub_hot, NT) + matmul(hub_low, hub_hot, NT)
         if tile == 0:
+            for peer in range(PEERS):
+                slice_of, start = peer // 8, HALF * (peer % 2) + SLOTS * (peer // 2 % 4)
+                grads_ref[
+                    PIECE * slice_of : PIECE * (slice_of + 1), start : start + SLOTS
+                ] = back_ref[peer, ROWS:, :].astype(F32)
+            sent = copies(
+                out_sems, (grads_ref.at[:FEATS], self_hbm), (grads_ref.at[FEATS:], neigh_hbm)
+            )
             staged[2].wait()
         out_ref[:, lanes] = (grad + base_ref[:, lanes]).astype(BF16)
     for copy in sent:

time: 200 us -> 200 us (level)
  no operation moved by 1% of the time
where the time goes in v13:
time: 200 us; the launch traced here: 199 us
  blocking collectives  65.9 us (33%)
  starting transfers between devices  48 us (24%)
  Pallas kernels  35.3 us (18%)
  waiting for transfers between devices  29.4 us (15%)
  between operations  14.3 us (7%)
  local copies, waits for them, and re-layouts  4.32 us (2%)
    all_to_all x2, blocking collectives, exchange(): lax.all_to_all(blocks, axis, 0, 0, axis_index_groups=groups, tiled=True)  65.9 us
    all_to_all x4, starting transfers between devices, exchange(): lax.all_to_all(blocks, axis, 0, 0, axis_index_groups=groups, tiled=True)  35 us
    all_to_all x4, waiting for transfers between devices, exchange(): lax.all_to_all(blocks, axis, 0, 0, axis_index_groups=groups, tiled=True)  26.9 us
    ppermute x3, starting transfers between devices, other_core(): return lax.ppermute(block, 'row', [(i, i ^ 1) for i in range(PEERS)])  13 us
    pallas_call x1, Pallas kernels, build_counts(): pl.pallas_call(build_kernel, grid=(NODES // BUILD,), in_specs=[whole((FEA...  6.22 us
    pallas_call x1, Pallas kernels, aggregate(): pl.pallas_call(aggregate_kernel, out_shape=[jax.ShapeDtypeStruct((LAYERS,...  4.94 us
    pallas_call x1, Pallas kernels, spread_grads(): pl.pallas_call(spread_kernel, in_specs=[VMEM, HBM, HBM, HBM], out_specs=[...  4.72 us
    unnamed x28, local copies, waits for them, and re-layouts  4.14 us
  transfers between devices with their start and end apart: 8, of which 7 were waited for; matrix products, arithmetic and copies ran while one was open for 0% of the time, Pallas kernels for 12%

profile of v13, /device:TPU:1, one launch (start us, length us, event | category | flops | bytes accessed | tf_op | source)
XLA Modules:
  0.0 198.8 jit_solution(2634789462818180089)
XLA Ops:
  7.2 1.5 fusion
  8.8 3.5 %gather_slots.1 = bf16[32,80,128]{2,1,0:T(8,128)(2,1)} custom-call(bf16[64,1024]{1,0:T(8,128)(2,1)} %x_hbm.3, s32[32,128]{1,0:T(8,128)} %bitcast.9, s32[1,16]{1,0:T(1,128)} %bitcast.13), custom_call_target="tpu_custom_call" | custom-call | flops 2147483648 | bytes 1048576 | tf_op jit(solution)/shard_map/gather_slots/pallas_call | solution.py:80
  12.3 10.4 %all-to-all-start = ((bf16[32,80,128]{2,1,0:T(8,128)(2,1)}), bf16[32,80,128]{2,1,0:T(8,128)(2,1)S(1)}, u32[]{:S(2)}, u32[]{:S(2)}) async-start(bf16[32,80,128]{2,1,0:T(8,128)(2,1)} %gather_slots.1), calls=%async_computation | async-start | bytes 1310720 | tf_op jit(solution)/shard_map/all_to_all | solution.py:603
  22.8 6.2 %build_counts.1 = (bf16[1024,1024]{1,0:T(8,128)(2,1)}, bf16[512,1024]{1,0:T(8,128)(2,1)}, f32[512,1024]{1,0:T(8,128)}) custom-call(bf16[64,1024]{1,0:T(8,128)(2,1)} %x_hbm.3, s32[8,1024]{1,0:T(8,128)} %bitcast.15, s32[2,1024]{1,0:T(2,128)} %bitcast.11), custom_call_target="tpu_custom_call" | custom-call | flops 1073741824 | bytes 4194304 | tf_op jit(solution)/shard_map/build_counts/pallas_call | solution.py:116
  29.0 6.8 %all-to-all-done.inc_ref = bf16[32,80,128]{2,1,0:T(8,128)(2,1)S(1)} async-done(((bf16[32,80,128]{2,1,0:T(8,128)(2,1)}), bf16[32,80,128]{2,1,0:T(8,128)(2,1)S(1)}, u32[]{:S(2)}, u32[]{:S(2)}) %all-to-all-start) | async-done | bytes 655392 | tf_op jit(solution)/shard_map/all_to_all | solution.py:603
  35.8 4.9 %aggregate.1 = (bf16[16,96,128]{2,1,0:T(8,128)(2,1)S(1)}, f32[8,1024]{1,0:T(8,128)S(1)}) custom-call(bf16[64,1024]{1,0:T(8,128)(2,1)S(1)} %copy-done.8, bf16[32,80,128]{2,1,0:T(8,128)(2,1)S(1)} %all-to-all-done.inc_ref, s32[32,128]{1,0:T(8,128)S(1)} %bitcast.7, f32[512,1024]{1,0:T(8,128)} %get-tuple-element.23.sum_hbm, s32[2,1024]{1,0:T(2,128)S(1)} %bitcast.12, ...), custom_call_target="tpu_custom_call" | custom-call | flops 2952790016 | bytes 3145728 | tf_op jit(solution)/shard_map/aggregate/pallas_call | solution.py:195
  40.7 36.4 %all_to_all.30.inc_ref.own_block = bf16[16,96,128]{2,1,0:T(8,128)(2,1)S(1)} all-to-all(bf16[16,96,128]{2,1,0:T(8,128)(2,1)S(1)} %get-tuple-element.24), channel_id=1, replica_groups=mesh['row'=32,'col'=16] {'col'}, dimensions={0} | all-to-all | bytes 786432 | tf_op jit(solution)/shard_map/all_to_all | solution.py:603
  77.1 1.3 regroup.1
  78.4 6.9 %all-to-all-start.2 = ((bf16[16,64,512]{2,1,0:T(8,128)(2,1)}), bf16[16,64,512]{2,1,0:T(8,128)(2,1)}, u32[]{:S(2)}, u32[]{:S(2)}) async-start(bf16[16,64,512]{2,1,0:T(8,128)(2,1)} %regroup.1), calls=%async_computation.2 | async-start | bytes 2097152 | tf_op jit(solution)/shard_map/all_to_all | solution.py:603
  85.3 4.5 %collective-permute-start = (bf16[16,96,128]{2,1,0:T(8,128)(2,1)S(1)}, bf16[16,96,128]{2,1,0:T(8,128)(2,1)S(1)}, u32[]{:S(2)}, u32[]{:S(2)}) collective-permute-start(bf16[16,96,128]{2,1,0:T(8,128)(2,1)S(1)} %all_to_all.30.inc_ref.own_block), channel_id=1, source_target_pairs={{0,16},{16,0},{32,48},{48,32},{64,80},{80,64},{96,112},{112,96},{1... | collective-permute-start | bytes 1179656 | tf_op jit(solution)/shard_map/ppermute | solution.py:607
  89.8 1.3 collective-permute-done.other_block
  91.1 0.2 prepare.1
  91.3 0.8 copy-done.4
  92.2 0.7 copy-done.7
  92.9 3.3 %forward.1 = (bf16[16,128,128]{2,1,0:T(8,128)(2,1)}, bf16[128,512]{1,0:T(8,128)(2,1)}, bf16[2,8,32,128]{3,2,1,0:T(8,128)(2,1)}) custom-call(bf16[2,64,2048]{2,1,0:T(8,128)(2,1)} %copy-done.4, bf16[2,64,512]{2,1,0:T(8,128)(2,1)} %copy-done.7, bf16[2048,512]{1,0:T(8,128)(2,1)} %all-gather.2.cloned.1.call-done.weights_hbm.weights_ref), custom_call_target="tpu_custom_call" | custom-call | flops 536870912 | bytes 4194304 | tf_op jit(solution)/shard_map/forward/pallas_call | solution.py:328
  96.2 4.1 %all-to-all-done.2.mine_hbm = bf16[16,64,512]{2,1,0:T(8,128)(2,1)} async-done(((bf16[16,64,512]{2,1,0:T(8,128)(2,1)}), bf16[16,64,512]{2,1,0:T(8,128)(2,1)}, u32[]{:S(2)}, u32[]{:S(2)}) %all-to-all-start.2) | async-done | bytes 1048608 | tf_op jit(solution)/shard_map/all_to_all | solution.py:603
  100.3 6.4 %collective-permute-start.1 = (bf16[16,64,512]{2,1,0:T(8,128)(2,1)}, bf16[16,64,512]{2,1,0:T(8,128)(2,1)}, u32[]{:S(2)}, u32[]{:S(2)}) collective-permute-start(bf16[16,64,512]{2,1,0:T(8,128)(2,1)} %all-to-all-done.2.mine_hbm), channel_id=1, source_target_pairs={{0,16},{16,0},{32,48},{48,32},{64,80},{80,64},{96,112},{112,96},{1... | collective-permute-start | bytes 3145736 | tf_op jit(solution)/shard_map/ppermute | solution.py:607
  106.7 6.9 %all-to-all-start.3 = ((bf16[16,128,128]{2,1,0:T(8,128)(2,1)}), bf16[16,128,128]{2,1,0:T(8,128)(2,1)S(1)}, u32[]{:S(2)}, u32[]{:S(2)}) async-start(bf16[16,128,128]{2,1,0:T(8,128)(2,1)} %get-tuple-element.29), calls=%async_computation.3 | async-start | bytes 1048576 | tf_op jit(solution)/shard_map/all_to_all | solution.py:603
  113.6 0.9 copy-done.2
  114.5 0.9 copy-done.6
  115.4 0.8 backward.1
  116.3 0.8 copy-done.5
  117.0 2.2 %collective-permute-start.2 = (bf16[20,64,128]{2,1,0:T(8,128)(2,1)S(1)}, bf16[20,64,128]{2,1,0:T(8,128)(2,1)S(1)}, u32[]{:S(2)}, u32[]{:S(2)}) collective-permute-start(bf16[20,64,128]{2,1,0:T(8,128)(2,1)S(1)} %get-tuple-element.33), channel_id=1, source_target_pairs={{0,16},{16,0},{32,48},{48,32},{64,80},{80,64},{96,112},{112,96},{1... | collective-permute-start | bytes 983048 | tf_op jit(solution)/shard_map/ppermute | solution.py:607
  119.4 1.1 collective-permute-done.2.swapped_hbm
  120.6 4.1 %all-to-all-done.3.slopes_ref = bf16[16,128,128]{2,1,0:T(8,128)(2,1)S(1)} async-done(((bf16[16,128,128]{2,1,0:T(8,128)(2,1)}), bf16[16,128,128]{2,1,0:T(8,128)(2,1)S(1)}, u32[]{:S(2)}, u32[]{:S(2)}) %all-to-all-start.3) | async-done | bytes 524320 | tf_op jit(solution)/shard_map/all_to_all | solution.py:603
  124.7 2.5 %weight_parts.1 = bf16[16,128,128]{2,1,0:T(8,128)(2,1)S(1)} custom-call(bf16[16,64,512]{2,1,0:T(8,128)(2,1)} %all-to-all-done.2.mine_hbm, bf16[16,64,512]{2,1,0:T(8,128)(2,1)} %collective-permute-done.1.theirs_hbm, bf16[16,128,128]{2,1,0:T(8,128)(2,1)S(1)} %all-to-all-done.3.slopes_ref, f32[64,2048]{1,0:T(8,128)} %copy-done.5, ...), custom_call_target="tpu_custom_call" | custom-call | flops 268435456 | bytes 4194304 | tf_op jit(solution)/shard_map/weight_parts/pallas_call | solution.py:421
  127.2 29.5 %all_to_all.31.back_ref.back_hbm = bf16[16,128,128]{2,1,0:T(8,128)(2,1)S(1)} all-to-all(bf16[16,128,128]{2,1,0:T(8,128)(2,1)S(1)} %weight_parts.1), channel_id=1, replica_groups=mesh['row'=32,'col'=16] {'col'}, dimensions={0} | all-to-all | bytes 1048576 | tf_op jit(solution)/shard_map/all_to_all | solution.py:603
  156.7 4.0 %return_slots.1 = bf16[32,112,128]{2,1,0:T(8,128)(2,1)} custom-call(bf16[16,128,128]{2,1,0:T(8,128)(2,1)S(1)} %all_to_all.31.back_ref.back_hbm, s32[32,128]{1,0:T(8,128)S(1)} %bitcast.8, bf16[512,1024]{1,0:T(8,128)(2,1)} %get-tuple-element.37.hubs_hbm), custom_call_target="tpu_custom_call" | custom-call | flops 2415919104 | bytes 3145728 | tf_op jit(solution)/shard_map/return_slots/pallas_call | solution.py:483
  160.7 10.7 %all-to-all-start.5 = ((bf16[32,112,128]{2,1,0:T(8,128)(2,1)}), bf16[32,112,128]{2,1,0:T(8,128)(2,1)S(1)}, u32[]{:S(2)}, u32[]{:S(2)}) async-start(bf16[32,112,128]{2,1,0:T(8,128)(2,1)} %return_slots.1), calls=%async_computation.5 | async-start | bytes 1835008 | tf_op jit(solution)/shard_map/all_to_all | solution.py:603
  171.5 3.9 %local_grads.1 = (f32[512,1024]{1,0:T(8,128)}, bf16[64,1024]{1,0:T(8,128)(2,1)}) custom-call(bf16[16,128,128]{2,1,0:T(8,128)(2,1)} %copy-done.1, bf16[1024,1024]{1,0:T(8,128)(2,1)} %get-tuple-element.35.local_ref), custom_call_target="tpu_custom_call" | custom-call | flops 536870912 | bytes 3145728 | tf_op jit(solution)/shard_map/local_grads/pallas_call | solution.py:515
  175.4 11.8 %all-to-all-done.5.back_ref = bf16[32,112,128]{2,1,0:T(8,128)(2,1)S(1)} async-done(((bf16[32,112,128]{2,1,0:T(8,128)(2,1)}), bf16[32,112,128]{2,1,0:T(8,128)(2,1)S(1)}, u32[]{:S(2)}, u32[]{:S(2)}) %all-to-all-start.5) | async-done | bytes 917536 | tf_op jit(solution)/shard_map/all_to_all | solution.py:603
  187.2 4.7 %spread_grads.1 = (bf16[64,1024]{1,0:T(8,128)(2,1)}, f32[64,1024]{1,0:T(8,128)}, f32[64,1024]{1,0:T(8,128)}) custom-call(bf16[32,112,128]{2,1,0:T(8,128)(2,1)S(1)} %all-to-all-done.5.back_ref, s32[32,128]{1,0:T(8,128)S(1)} %bitcast.10, s32[1,16]{1,0:T(1,128)S(1)} %bitcast.14, f32[512,1024]{1,0:T(8,128)} %get-tuple-element.38.base_hbm), custom_call_target="tpu_custom_call" | custom-call | flops 2214592512 | bytes 2097152 | tf_op jit(solution)/shard_map/spread_grads/pallas_call | solution.py:575
  (30 shorter events, 0.4 us)
Async XLA Ops:
  7.2 85.8 %all-gather.2.cloned.1.call-start = ((), (), s32[]{:S(2)}) async-start(), calls=%async_computation.6 | async-start | bytes 2228224 | tf_op jit(solution)/shard_map/all_gather | solution.py:615
  12.3 23.5 %all-to-all-start = ((bf16[32,80,128]{2,1,0:T(8,128)(2,1)}), bf16[32,80,128]{2,1,0:T(8,128)(2,1)S(1)}, u32[]{:S(2)}, u32[]{:S(2)}) async-start(bf16[32,80,128]{2,1,0:T(8,128)(2,1)} %gather_slots.1), calls=%async_computation | async-start | bytes 1310720 | tf_op jit(solution)/shard_map/all_to_all | solution.py:603
  22.7 13.0 %copy-start.8 = (bf16[64,1024]{1,0:T(8,128)(2,1)S(1)}, bf16[64,1024]{1,0:T(8,128)(2,1)}, u32[]{:S(2)}) copy-start(bf16[64,1024]{1,0:T(8,128)(2,1)} %x_hbm.3) | copy-start | bytes 393220
  22.8 13.0 %copy-start.9 = (bf16[64,1024]{1,0:T(8,128)(2,1)S(1)}, bf16[64,1024]{1,0:T(8,128)(2,1)}, u32[]{:S(2)}) copy-start(bf16[64,1024]{1,0:T(8,128)(2,1)} %cot_hbm.1) | copy-start | bytes 393220
  22.8 13.0 %copy-start.10 = (s32[1,32,128]{2,1,0:T(8,128)S(1)}, s32[1,32,128]{2,1,0:T(8,128)}, u32[]{:S(2)}) copy-start(s32[1,32,128]{2,1,0:T(8,128)} %param.15) | copy-start | bytes 49156
  22.8 13.0 %copy-start.12 = (s32[1024,2]{0,1:T(2,128)S(1)}, s32[1024,2]{0,1:T(2,128)}, u32[]{:S(2)}) copy-start(s32[1024,2]{0,1:T(2,128)} %param.17) | copy-start | bytes 24580
  78.4 21.9 %all-to-all-start.2 = ((bf16[16,64,512]{2,1,0:T(8,128)(2,1)}), bf16[16,64,512]{2,1,0:T(8,128)(2,1)}, u32[]{:S(2)}, u32[]{:S(2)}) async-start(bf16[16,64,512]{2,1,0:T(8,128)(2,1)} %regroup.1), calls=%async_computation.2 | async-start | bytes 2097152 | tf_op jit(solution)/shard_map/all_to_all | solution.py:603
  85.3 5.8 %collective-permute-start = (bf16[16,96,128]{2,1,0:T(8,128)(2,1)S(1)}, bf16[16,96,128]{2,1,0:T(8,128)(2,1)S(1)}, u32[]{:S(2)}, u32[]{:S(2)}) collective-permute-start(bf16[16,96,128]{2,1,0:T(8,128)(2,1)S(1)} %all_to_all.30.inc_ref.own_block), channel_id=1, source_target_pairs={{0,16},{16,0},{32,48},{48,32},{64,80},{80,64},{96,112},{112,96},{1... | collective-permute-start | bytes 1179656 | tf_op jit(solution)/shard_map/ppermute | solution.py:607
  91.3 0.8 copy-start.4
  92.2 0.7 copy-start.7
  92.9 20.7 %copy-start = (bf16[2048,512]{1,0:T(8,128)(2,1)S(1)}, bf16[2048,512]{1,0:T(8,128)(2,1)}, u32[]{:S(2)}) copy-start(bf16[2048,512]{1,0:T(8,128)(2,1)} %all-gather.2.cloned.1.call-done.weights_hbm.weights_ref) | copy-start | bytes 6291460
  96.2 28.5 %copy-start.3 = (bf16[2,8,32,128]{3,2,1,0:T(8,128)(2,1)S(1)}, bf16[2,8,32,128]{3,2,1,0:T(8,128)(2,1)}, u32[]{:S(2)}) copy-start(bf16[2,8,32,128]{3,2,1,0:T(8,128)(2,1)} %get-tuple-element.31.hidden_ref.hidden_hbm) | copy-start | bytes 393220
  100.3 24.4 %collective-permute-start.1 = (bf16[16,64,512]{2,1,0:T(8,128)(2,1)}, bf16[16,64,512]{2,1,0:T(8,128)(2,1)}, u32[]{:S(2)}, u32[]{:S(2)}) collective-permute-start(bf16[16,64,512]{2,1,0:T(8,128)(2,1)} %all-to-all-done.2.mine_hbm), channel_id=1, source_target_pairs={{0,16},{16,0},{32,48},{48,32},{64,80},{80,64},{96,112},{112,96},{1... | collective-permute-start | bytes 3145736 | tf_op jit(solution)/shard_map/ppermute | solution.py:607
  106.7 18.0 %all-to-all-start.3 = ((bf16[16,128,128]{2,1,0:T(8,128)(2,1)}), bf16[16,128,128]{2,1,0:T(8,128)(2,1)S(1)}, u32[]{:S(2)}, u32[]{:S(2)}) async-start(bf16[16,128,128]{2,1,0:T(8,128)(2,1)} %get-tuple-element.29), calls=%async_computation.3 | async-start | bytes 1048576 | tf_op jit(solution)/shard_map/all_to_all | solution.py:603
  113.6 0.9 copy-start.2
  114.5 0.9 copy-start.6
  116.2 0.8 copy-start.5
  117.0 3.5 %collective-permute-start.2 = (bf16[20,64,128]{2,1,0:T(8,128)(2,1)S(1)}, bf16[20,64,128]{2,1,0:T(8,128)(2,1)S(1)}, u32[]{:S(2)}, u32[]{:S(2)}) collective-permute-start(bf16[20,64,128]{2,1,0:T(8,128)(2,1)S(1)} %get-tuple-element.33), channel_id=1, source_target_pairs={{0,16},{16,0},{32,48},{48,32},{64,80},{80,64},{96,112},{112,96},{1... | collective-permute-start | bytes 983048 | tf_op jit(solution)/shard_map/ppermute | solution.py:607
  156.7 4.0 %copy-start.1 = (bf16[16,128,128]{2,1,0:T(8,128)(2,1)}, bf16[16,128,128]{2,1,0:T(8,128)(2,1)S(1)}, u32[]{:S(2)}) copy-start(bf16[16,128,128]{2,1,0:T(8,128)(2,1)S(1)} %all_to_all.31.back_ref.back_hbm) | copy-start | bytes 1572868
  160.7 26.5 %copy-start.11 = (s32[1,32,128]{2,1,0:T(8,128)S(1)}, s32[1,32,128]{2,1,0:T(8,128)}, u32[]{:S(2)}) copy-start(s32[1,32,128]{2,1,0:T(8,128)} %param.14) | copy-start | bytes 49156
  160.7 26.5 %copy-start.13 = (s32[16]{0:T(128)S(1)}, s32[16]{0:T(128)}, u32[]{:S(2)}) copy-start(s32[16]{0:T(128)} %param.16) | copy-start | bytes 196
  160.7 26.5 %all-to-all-start.5 = ((bf16[32,112,128]{2,1,0:T(8,128)(2,1)}), bf16[32,112,128]{2,1,0:T(8,128)(2,1)S(1)}, u32[]{:S(2)}, u32[]{:S(2)}) async-start(bf16[32,112,128]{2,1,0:T(8,128)(2,1)} %return_slots.1), calls=%async_computation.5 | async-start | bytes 1835008 | tf_op jit(solution)/shard_map/all_to_all | solution.py:603
Sparse Core Ops, SparseCore 0:
  10.7 82.2 all-gather.1
